TPU v7x, 256 devices: a whole 4x4x8 slice. The times are simulated.
256 devices in a mesh: dp: 32 (over y, x, core), mp: 8 (over z).
Axes of the slice: x: 4, y: 4, z: 8, core: 2. Of those that a mesh axis runs over, the one named last changes fastest.
Arguments:
- tile_features: bfloat16 [6144, 1536], P('dp'), may hold values from -6 to 6
- tile_slide: int32 [6144, 1], P('dp'), may hold values from 0 to 31; in each aligned block of 192 rows (0 to 191, 192 to 383, ...) at most 12 rows name the same one
- slide_pair: int32 [32], replicated, may hold values from 0 to 31, each once
- reports: bfloat16 [32, 1536], P('dp'), may hold values from -6 to 6
- w_one: bfloat16 [1536, 6144], P(None, 'mp'), may hold values from -0.15625 to 0.15625
- w_two: bfloat16 [6144, 1536], P('mp'), may hold values from -0.078125 to 0.078125
- w_query: bfloat16 [1536, 1536], P(None, 'mp'), may hold values from -0.15625 to 0.15625
- w_key: bfloat16 [1536, 1536], P(None, 'mp'), may hold values from -0.15625 to 0.15625
- w_value: bfloat16 [1536, 1536], P(None, 'mp'), may hold values from -0.15625 to 0.15625
- w_out: bfloat16 [1536, 1536], P('mp'), may hold values from -0.15625 to 0.15625
Outputs:
- contrast_loss: float32 [], replicated
- grad_one: float32 [1536, 6144], P('dp', 'mp')
- grad_two: float32 [6144, 1536], P('mp', 'dp')
- grad_query: float32 [1536, 1536], P('dp', 'mp')
- grad_key: float32 [1536, 1536], P('dp', 'mp')
- grad_value: float32 [1536, 1536], P('dp', 'mp')
- grad_out: float32 [1536, 1536], P('mp', 'dp')
Inputs may be any that keep to these rules, and one draw needn't show every extreme that they name: `tile_slide`: within the 192 tiles of one device (aligned blocks) no slide has more than 12 tiles, and some slide has exactly 12; every slide has at least one tile. `slide_pair`: each report is paired with exactly one slide.
All inputs are finite; a program needn't handle non-finite values.
Results may differ from a plain program's by a relative error of at most 0.039.
Values may be sent and summed in bfloat16 or wider, within the bound.
No kernel may reach another device: no remote copies, remote signals or barrier semaphores. Data moves between devices by JAX's collectives and lax.ppermute only.
A program may use at most 128 MiB of HBM per device.

v0:
```python
import jax
import jax.numpy as jnp
from jax import lax
from jax.experimental import pallas as pl
from jax.experimental.pallas import tpu as pltpu
from jax.sharding import Mesh, PartitionSpec as P

HEAD = 96
CORES = 2
ROWS = 16
EXTRA = 16

eps = 1e-05
contrast_divisor_factor = 0.07
score_scale = 10.0
loss_scale = 4096.0
exact = lax.Precision.HIGHEST
f32 = jnp.float32
bf16 = jnp.bfloat16
i32 = jnp.int32
DP = ("chip", "core")


def contract(left, right, left_dim, right_dim, **kw):
    return lax.dot_general(
        left, right, (((left_dim,), (right_dim,)), ((), ())), preferred_element_type=f32, **kw
    )


def exchange(values, axis):
    return lax.all_to_all(values, axis, 0, 0, tiled=True)


def pick(values, index, axis):
    return lax.dynamic_index_in_dim(values, index, axis, keepdims=False)


def call(body, outs, *args, scalars=(), scratch=(), anchors=(), limit=16):
    count = len(scalars)
    skip = len(anchors)

    def kernel(*refs):
        body(*refs[skip:])

    return pl.pallas_call(
        kernel if skip else body,
        out_shape=[jax.ShapeDtypeStruct(shape, kind) for shape, kind in outs],
        in_specs=[pl.BlockSpec(memory_space=pl.ANY)] * skip
        + [pl.BlockSpec(memory_space=pltpu.SMEM)] * count
        + [pl.BlockSpec(memory_space=pltpu.VMEM)] * len(args),
        out_specs=[pl.BlockSpec(memory_space=pltpu.VMEM)] * len(outs),
        scratch_shapes=[pltpu.VMEM(shape, kind) for shape, kind in scratch],
        compiler_params=pltpu.CompilerParams(vmem_limit_bytes=limit * 1024 * 1024),
    )(*anchors, *[jnp.reshape(s, (1,)).astype(i32) for s in scalars], *args)


def turn(count, step):
    return [(index, (index + step) % count) for index in range(count)]


def scatter_ring(pieces, count):
    return [pieces[0]] + [
        lax.ppermute(pieces[k], "mp", turn(count, k)) for k in range(1, count)
    ]


def gather_ring(piece, count):
    found = [piece]
    back = ahead = piece
    for _ in range(count // 2 - 1):
        back = lax.ppermute(back, "mp", turn(count, 1))
        ahead = lax.ppermute(ahead, "mp", turn(count, count - 1))
        found += [back, ahead]
    half = (piece.shape[0] // 2 + ROWS - 1) // ROWS * ROWS
    found.append(lax.ppermute(back[:half], "mp", turn(count, 1)))
    found.append(lax.ppermute(ahead[half:], "mp", turn(count, count - 1)))
    return found


def place(refs, here, count, store):
    half = count // 2
    store(here, refs[0][...])
    for step in range(1, half):
        for ref, sign in ((refs[2 * step - 1], -1), (refs[2 * step], 1)):
            store(lax.rem(here + sign * step + count, count), ref[...])
    store(
        lax.rem(here + half, count), jnp.concatenate([refs[-2][...], refs[-1][...]], 0)
    )


def pack(square):
    half = square.shape[0] // 2
    side = square[:, 128:]
    return jnp.concatenate(
        [square[:, :128], jnp.concatenate([side[:half], side[half:]], 1)], 0
    )


def unpack(packed):
    rows = packed.shape[0] // 3 * 2
    side = packed[rows:]
    return jnp.concatenate(
        [packed[:rows], jnp.concatenate([side[:, :64], side[:, 64:]], 0)], 1
    )


def tile_forward(x_ref, one_ref, two_ref, norm_ref, hidden_ref, slope_ref, out_ref):
    x = x_ref[...].astype(f32)
    centred = x - jnp.mean(x, -1, keepdims=True)
    normed = centred * lax.rsqrt(jnp.mean(centred * centred, -1, keepdims=True) + eps)
    normed = normed.astype(bf16)
    norm_ref[...] = normed
    pre = jnp.dot(normed, one_ref[...], preferred_element_type=f32)
    bell = 0.5 * (1.0 + lax.erf(pre * 0.7071067811865476))
    hidden = (pre * bell).astype(bf16)
    hidden_ref[...] = hidden
    slope_ref[...] = bell + pre * jnp.exp(-0.5 * pre * pre) * 0.3989422804014327
    partial = jnp.dot(hidden, two_ref[...], preferred_element_type=f32).astype(bf16)
    count = out_ref.shape[0]
    block = partial.shape[1] // count
    for j in range(count):
        out_ref[j] = pack(partial[:, j * block : (j + 1) * block])


def tile_dispatch(own_ref, report_ref, dispatch_ref, flags_ref, parts_ref, out_ref):
    total = parts_ref[0].astype(f32)
    for j in range(1, parts_ref.shape[0]):
        total = total + parts_ref[j].astype(f32)
    embedding = (own_ref[...].astype(f32) + unpack(total)).astype(bf16)
    rows = jnp.dot(dispatch_ref[...], embedding, preferred_element_type=f32)
    slot = lax.broadcasted_iota(i32, rows.shape, 0)
    rows = jnp.where(lax.rem(slot, ROWS) == ROWS - 1, report_ref[...].astype(f32), rows)
    out_ref[...] = jnp.concatenate([rows.astype(bf16), flags_ref[...]], 1)


def slot_rows(arrived_ref, select_ref, report_select_ref, chunk_ref, valid_ref):
    arrived = arrived_ref[...]
    chunk = contract(arrived, select_ref[...], 0, 0)
    block = chunk_ref.shape[0] - EXTRA
    chunk_ref[0:block, :] = chunk[:block].astype(bf16)
    valid_ref[...] = chunk[block : block + 1]
    reports = jnp.dot(report_select_ref[...], arrived, preferred_element_type=f32)
    reports = reports[:, :block].astype(bf16)
    chunk_ref[block : block + EXTRA, :] = jnp.concatenate(
        [reports[:EXTRA], reports[EXTRA:]], 1
    )


def slide_forward(
    here,
    valid_ref,
    query_weights_ref,
    key_weights_ref,
    value_weights_ref,
    out_weights_ref,
    *rest,
):
    pieces = rest[:9]
    (
        norm_ref,
        stat_ref,
        query_ref,
        key_ref,
        value_ref,
        scale_ref,
        attention_ref,
        mass_ref,
        attended_ref,
        pooled_ref,
        reports_ref,
        slide_ref,
    ) = rest[9:]
    count, owners, block = reports_ref.shape

    def store(index, piece):
        start = pl.multiple_of(index * block, 16)
        slide_ref[pl.ds(start, block), :] = piece[:block]
        reports = piece[block:]
        reports_ref[index] = jnp.concatenate([reports[:, :block], reports[:, block:]], 0)

    place(pieces, here[0], count, store)
    valid = valid_ref[...]
    valid_low = valid.astype(bf16)
    low = slide_ref[...]
    slide = low.astype(f32)
    mean = jnp.mean(slide, 0, keepdims=True)
    centred = slide - mean
    inverse = lax.rsqrt(jnp.mean(centred * centred, 0, keepdims=True) + eps)
    stat_ref[...] = jnp.concatenate([mean, inverse], 0)
    norm_ref[...] = (centred * inverse).astype(bf16)
    normed = norm_ref[...]
    all_query = jnp.dot(query_weights_ref[...], normed, preferred_element_type=f32)
    all_keys = jnp.dot(key_weights_ref[...], normed, preferred_element_type=f32)
    all_values = jnp.dot(value_weights_ref[...], normed, preferred_element_type=f32)
    heads = all_query.shape[0] // HEAD
    attended = []
    for h in range(heads):
        low_rows, high_rows = h * HEAD, (h + 1) * HEAD
        query = all_query[low_rows:high_rows]
        keys = all_keys[low_rows:high_rows]
        values = all_values[low_rows:high_rows]
        query_scale = lax.rsqrt(jnp.mean(query * query, 0, keepdims=True) + eps)
        key_scale = lax.rsqrt(jnp.mean(keys * keys, 0, keepdims=True) + eps)
        query_unit = query * query_scale
        key_unit = keys * key_scale
        query_ref[h] = query_unit
        key_ref[h] = key_unit
        value_ref[h] = values
        scale_ref[h] = jnp.concatenate([query_scale, key_scale], 0)
        scores = contract(query_unit.astype(bf16), key_unit.astype(bf16), 0, 0)
        weights = jnp.exp(scores * (score_scale / HEAD)) * valid
        weights = weights * (1.0 / jnp.sum(weights, 1, keepdims=True))
        attention_ref[h] = weights
        weights_low = weights.astype(bf16)
        mass_ref[h : h + 1, :] = jnp.dot(valid_low, weights_low, preferred_element_type=f32)
        attended.append(contract(values.astype(bf16), weights_low, 1, 1))
    attended = jnp.concatenate(attended, 0).astype(bf16)
    attended_sum = contract(valid_low, attended, 1, 1)
    attended_ref[...] = attended_sum
    high = attended_sum.astype(bf16)
    rest_low = (attended_sum - high.astype(f32)).astype(bf16)
    part = jnp.dot(high, out_weights_ref[...], preferred_element_type=f32)
    part = part + jnp.dot(rest_low, out_weights_ref[...], preferred_element_type=f32)
    slide_sum = contract(valid_low, low, 1, 1)
    pooled = (part + slide_sum * (1.0 / count)) / jnp.sum(valid)
    pooled_ref[...] = jnp.broadcast_to(pooled[None], pooled_ref.shape)


def logits_row(parts_ref, reports_ref, unit_ref, report_ref, row_ref):
    pooled = jnp.sum(parts_ref[...], 0)
    inverse = lax.rsqrt(jnp.sum(pooled * pooled, -1, keepdims=True) + eps)
    unit = pooled * inverse
    unit_ref[...] = jnp.concatenate([unit, jnp.broadcast_to(inverse, unit.shape)], 0)
    count, owners, block = reports_ref.shape
    squares = jnp.zeros((owners, 1), f32)
    for j in range(count):
        reports = reports_ref[j].astype(f32)
        report_ref[:, j * block : (j + 1) * block] = reports
        squares = squares + jnp.sum(reports * reports, -1, keepdims=True)
    report = report_ref[...] * lax.rsqrt(squares + eps)
    report_ref[...] = report
    row = contract(unit, report, 1, 1, precision=exact) / contrast_divisor_factor
    pad = row_ref.shape[2] - row.shape[1]
    row = jnp.concatenate([row, jnp.zeros((1, pad), f32)], 1)
    row_ref[...] = jnp.broadcast_to(row[None], row_ref.shape)


def slide_backward(
    here,
    owner,
    logits_ref,
    pair_ref,
    unit_ref,
    report_ref,
    valid_ref,
    out_weights_ref,
    query_weights_ref,
    key_weights_ref,
    value_weights_ref,
    norm_ref,
    query_ref,
    key_ref,
    value_ref,
    scale_ref,
    attention_ref,
    mass_ref,
    loss_ref,
    grad_ref,
    up_ref,
    grads_ref,
    *outs,
):
    owners = report_ref.shape[0]
    valid = valid_ref[...]
    logits = logits_ref[...]
    shape = logits.shape
    columns = lax.broadcasted_iota(i32, shape, 1)
    rows = lax.broadcasted_iota(i32, shape, 0)
    real = columns < owners
    expo = jnp.where(real, jnp.exp(logits), 0.0)
    row_total = jnp.sum(expo, 1, keepdims=True)
    column_total = jnp.where(real[:1], jnp.sum(expo, 0, keepdims=True), 1.0)
    target = jnp.where(pair_ref[...] == columns, 1.0, 0.0)
    loss = jnp.sum(
        0.5 * jnp.log(row_total) - jnp.sum(logits * target, 1, keepdims=True), 0, keepdims=True
    )
    loss = loss + 0.5 * jnp.sum(jnp.log(column_total), 1, keepdims=True)
    loss_ref[...] = loss * (1.0 / owners)
    grad_logits = (0.5 * expo / row_total + 0.5 * expo / column_total - target) * (
        loss_scale / owners
    )
    grad_row = jnp.sum(jnp.where(rows == owner[0], grad_logits, 0.0), 0, keepdims=True)
    grad_unit = (
        jnp.dot(grad_row[:, :owners], report_ref[...], precision=exact, preferred_element_type=f32)
        / contrast_divisor_factor
    )
    unit = unit_ref[0:1]
    inverse = unit_ref[1:2]
    grad_pooled = (grad_unit - unit * jnp.sum(unit * grad_unit, -1, keepdims=True)) * inverse
    grad = grad_pooled / jnp.sum(valid)
    grad_ref[...] = grad
    low = grad.astype(bf16)
    out_weights = out_weights_ref[...]
    up_ref[...] = contract(low, out_weights, 1, 1)
    up = jnp.sum(out_weights.astype(f32) * low.astype(f32), 1, keepdims=True)
    heads = query_ref.shape[0]
    inner = heads * HEAD
    for h in range(heads):
        up_head = up[h * HEAD : (h + 1) * HEAD]
        values = value_ref[h]
        weights = attention_ref[h]
        pull = jnp.sum(up_head * values, 0, keepdims=True)
        pull_mean = jnp.sum(weights * pull, 1, keepdims=True)
        grad_scores = (weights * (pull - pull_mean) * (score_scale / HEAD)).astype(bf16)
        query_unit = query_ref[h]
        key_unit = key_ref[h]
        grad_query = contract(key_unit.astype(bf16), grad_scores, 1, 1) * valid
        grad_key = jnp.dot(query_unit.astype(bf16), grad_scores, preferred_element_type=f32)
        grad_query = scale_ref[h, 0:1] * (
            grad_query - query_unit * jnp.mean(query_unit * grad_query, 0, keepdims=True)
        )
        grad_key = scale_ref[h, 1:2] * (
            grad_key - key_unit * jnp.mean(key_unit * grad_key, 0, keepdims=True)
        )
        grad_value = up_head * mass_ref[h : h + 1]
        for part, values in enumerate((grad_query, grad_key, grad_value)):
            start = part * inner + h * HEAD
            grads_ref[start : start + HEAD, :] = values.astype(bf16)
    grad_query = grads_ref[0:inner, :]
    grad_key = grads_ref[inner : 2 * inner, :]
    grad_value = grads_ref[2 * inner : 3 * inner, :]
    count = len(outs)
    block = norm_ref.shape[0] // count
    first = jnp.zeros_like(valid)
    second = jnp.zeros_like(valid)
    for k in range(count):
        start = pl.multiple_of(lax.rem(here[0] + k, count) * block, 16)
        rows = pl.ds(start, block)
        part = jnp.dot(query_weights_ref[rows, :], grad_query, preferred_element_type=f32)
        part = part + jnp.dot(key_weights_ref[rows, :], grad_key, preferred_element_type=f32)
        part = part + jnp.dot(value_weights_ref[rows, :], grad_value, preferred_element_type=f32)
        outs[k][0:block, :] = part.astype(bf16)
        first = first + jnp.sum(part, 0, keepdims=True)
        second = second + jnp.sum(part * norm_ref[rows, :].astype(f32), 0, keepdims=True)
    width = norm_ref.shape[0]
    stats = jnp.concatenate([first, second], 0) * (1.0 / width)
    high = stats.astype(bf16).astype(f32)
    stats = jnp.concatenate(
        [high, stats - high, jnp.zeros((EXTRA - 4, stats.shape[1]), f32)], 0
    ).astype(bf16)
    for k in range(count):
        outs[k][block : block + EXTRA, :] = stats


def slot_grads(own_ref, valid_ref, stat_ref, chunk_ref, select_ref, extra_ref, *rest):
    refs, out_ref = rest[:-1], rest[-1]
    total = refs[0][...].astype(f32)
    for ref in refs[1:]:
        total = total + ref[...].astype(f32)
    block = chunk_ref.shape[0] - EXTRA
    first = total[block : block + 1] + total[block + 2 : block + 3]
    second = total[block + 1 : block + 2] + total[block + 3 : block + 4]
    mean = stat_ref[0:1]
    inverse = stat_ref[1:2]
    normed = (chunk_ref[0:block, :].astype(f32) - mean) * inverse
    rows = own_ref[...] * valid_ref[...] + (total[:block] - first - normed * second) * inverse
    rows = contract(select_ref[...], rows.astype(bf16), 1, 1).astype(bf16)
    out_ref[...] = rows + extra_ref[...]


def tile_grads(back_ref, dispatch_ref, out_ref):
    piece = pack(contract(back_ref[...], dispatch_ref[...], 0, 0).astype(bf16))
    out_ref[...] = jnp.broadcast_to(piece[None], out_ref.shape)


def other_grads(
    other, two_ref, slope_ref, norm_ref, hidden_ref, parts_ref, grad_ref, hidden_grad_ref, out_ref
):
    count = parts_ref.shape[0]
    rows = grad_ref.shape[0] // count
    for j in range(count):
        grad_ref[j * rows : (j + 1) * rows, :] = unpack(parts_ref[j])
    grad_hidden = jnp.dot(two_ref[...], grad_ref[...], preferred_element_type=f32)
    hidden_grad_ref[...] = (grad_hidden * slope_ref[...]).astype(bf16)

    def store(rows, values):
        out_ref[rows] = values.astype(bf16)

    both_layers(other[0], norm_ref, hidden_ref, grad_ref, hidden_grad_ref, out_ref.shape, store)


def own_grads(own, norm_ref, hidden_ref, grad_ref, hidden_grad_ref, got_ref, out_ref):
    def store(rows, values):
        out_ref[rows] = (values + got_ref[rows].astype(f32)).astype(bf16)

    both_layers(own[0], norm_ref, hidden_ref, grad_ref, hidden_grad_ref, out_ref.shape, store)


def both_layers(which, norm_ref, hidden_ref, grad_ref, hidden_grad_ref, shape, store):
    chips, share = shape[0], shape[1] // 2
    rows = [
        grad_ref[pl.ds(pl.multiple_of((CORES * chip + which) * share, 16), share), :]
        for chip in range(chips)
    ]
    two = jnp.dot(jnp.concatenate(rows, 0), hidden_ref[...], preferred_element_type=f32)
    one = contract(norm_ref[...], hidden_grad_ref[...], 1, 1)
    for chip in range(chips):
        start = chip * share
        store((chip, slice(0, share)), one[start : start + share])
        store((chip, slice(share, 2 * share)), two[start : start + share])


def last_sums(values_ref, one_ref, two_ref):
    share = one_ref.shape[0]
    total = values_ref[0].astype(f32)
    for chip in range(1, values_ref.shape[0]):
        total = total + values_ref[chip].astype(f32)
    one_ref[...] = total[:share]
    two_ref[...] = total[share:]


def per_device(
    tile_features, tile_slide, slide_pair, reports, w_one, w_two, w_query, w_key, w_value, w_out
):
    chips = lax.axis_size("chip")
    owners = chips * CORES
    parts = lax.axis_size("mp")
    core = lax.axis_index("core")
    owner = lax.axis_index(DP)
    here = lax.axis_index("mp")
    tiles, width = tile_features.shape
    units = w_one.shape[1]
    capacity = 2 * tiles // owners
    length = owners * capacity
    slots = owners * ROWS
    block = width // parts
    share = width // owners
    inner = w_query.shape[1]
    heads = inner // HEAD
    packed = (block // 2 * 3, 128)

    def halves(values):
        rest = values.shape[1:]
        values = values.reshape((chips, CORES, share) + rest)
        own = pick(values, core, 1).reshape((chips * share,) + rest)
        other = pick(values, 1 - core, 1).reshape((chips * share,) + rest)
        return own, other

    tile_norm, hidden, slope, partial = call(
        tile_forward,
        [
            ((tiles, width), bf16),
            ((tiles, units), bf16),
            ((tiles, units), f32),
            ((parts,) + packed, bf16),
        ],
        tile_features,
        w_one,
        w_two,
        limit=24,
    )
    partial = exchange(partial, "mp")

    slide_ids = tile_slide[:, 0]
    matches = (slide_ids[:, None] == jnp.arange(owners, dtype=i32)[None, :]).astype(i32)
    ordinal = jnp.sum(matches * (jnp.cumsum(matches, 0) - 1), 1)
    position = slide_ids * ROWS + ordinal
    dispatch = jnp.arange(slots, dtype=i32)[:, None] == position[None, :]
    flags = jnp.sum(dispatch.astype(f32), 1, keepdims=True).astype(bf16)
    flags = jnp.pad(flags, ((0, 0), (0, 256 - block - 1)))
    dispatch = dispatch.astype(bf16)
    slot = jnp.arange(slots, dtype=i32)
    row_of_slot = jnp.where(slot % ROWS < capacity, slot // ROWS * capacity + slot % ROWS, -1)
    select = (row_of_slot[:, None] == jnp.arange(length, dtype=i32)[None, :]).astype(bf16)
    last_slot = jnp.arange(owners, dtype=i32)[:, None] * ROWS + ROWS - 1
    report_select = (last_slot == slot[None, :]).astype(bf16)
    own_columns = pick(tile_features.reshape(tiles, parts, block), here, 1)
    own_report = pick(reports.reshape(1, parts, block), here, 1)
    tile_own, tile_other = halves(tile_norm.T)
    slope = slope.T

    (outgoing,) = call(
        tile_dispatch,
        [((slots, 256), bf16)],
        own_columns,
        own_report,
        dispatch,
        flags,
        partial,
        anchors=(select, report_select, tile_own, tile_other, slope),
    )
    arrived = exchange(outgoing.reshape(owners, ROWS, 256), DP).reshape(slots, 256)
    chunk, valid = call(
        slot_rows,
        [((block + EXTRA, length), bf16), ((1, length), f32)],
        arrived,
        select,
        report_select,
    )
    pieces = gather_ring(chunk, parts)

    (
        slide_norm,
        stat,
        query,
        keys,
        values,
        scales,
        attention,
        mass,
        attended_sum,
        pooled,
        all_reports,
    ) = call(
        slide_forward,
        [
            ((width, length), bf16),
            ((2, length), f32),
            ((heads, HEAD, length), f32),
            ((heads, HEAD, length), f32),
            ((heads, HEAD, length), f32),
            ((heads, 2, length), f32),
            ((heads, length, length), f32),
            ((heads, length), f32),
            ((1, inner), f32),
            ((parts, 1, width), f32),
            ((parts, owners, block), bf16),
        ],
        valid,
        w_query.T,
        w_key.T,
        w_value.T,
        w_out,
        *pieces,
        scalars=(here,),
        scratch=[((width, length), bf16)],
        limit=28,
    )
    pooled = exchange(pooled, "mp")
    unit, report_unit, row = call(
        logits_row,
        [((2, width), f32), ((owners, width), f32), ((owners, 1, 128), f32)],
        pooled,
        all_reports,
    )
    logits = exchange(row, DP).reshape(owners, 128)
    loss, grad, up, grads, *pieces = call(
        slide_backward,
        [((1, 1), f32), ((1, width), f32), ((1, inner), f32), ((3 * inner, length), bf16)]
        + [((block + EXTRA, length), bf16)] * parts,
        logits,
        slide_pair[:, None],
        unit,
        report_unit,
        valid,
        w_out,
        w_query,
        w_key,
        w_value,
        slide_norm,
        query,
        keys,
        values,
        scales,
        attention,
        mass,
        scalars=(here, owner),
        limit=24,
    )
    pieces = scatter_ring(pieces, parts)

    norm_own, norm_other = halves(slide_norm)
    wide = (chips, share, 2 * inner)
    wide_other = contract(norm_other, grads[: 2 * inner], 1, 1).astype(bf16).reshape(wide)
    wide_got = lax.ppermute(wide_other, "core", [(0, 1), (1, 0)])
    wide_own = contract(norm_own, grads[: 2 * inner], 1, 1).reshape(wide)
    wide_sent = (wide_own + wide_got.astype(f32)).astype(bf16)
    grad_wide = jnp.sum(exchange(wide_sent, "chip").astype(f32), 0)
    value_rows = contract(mass.astype(bf16), slide_norm, 1, 1)
    extra = jnp.concatenate(
        [
            value_rows.reshape(heads, owners, share).transpose(1, 0, 2).reshape(owners, -1),
            grad.reshape(owners, share),
            jnp.broadcast_to(up, (owners, inner)),
            jnp.broadcast_to(attended_sum, (owners, inner)),
        ],
        1,
    ).astype(bf16)
    spare = ROWS - capacity
    extra = jnp.pad(extra, ((0, 0), (0, spare * block - extra.shape[1])))
    extra = extra.reshape(owners, spare, block)
    extra = jnp.pad(extra, ((0, 0), (capacity, 0), (0, 0))).reshape(slots, block)

    own_grad = lax.dynamic_slice_in_dim(grad, here * block, block, 1).reshape(block, 1)
    (going,) = call(
        slot_grads,
        [((slots, block), bf16)],
        own_grad,
        valid,
        stat,
        chunk,
        select,
        extra,
        *pieces,
        anchors=(grad_wide,),
    )
    back = exchange(going.reshape(owners, ROWS, block), DP).reshape(slots, block)
    (spreading,) = call(tile_grads, [((parts,) + packed, bf16)], back, dispatch)

    size = (chips, 2 * share, units)
    grad_embedding, grad_hidden, sent = call(
        other_grads,
        [((width, tiles), bf16), ((units, tiles), bf16), (size, bf16)],
        w_two,
        slope,
        tile_other,
        hidden,
        exchange(spreading, "mp"),
        scalars=(1 - core,),
        limit=24,
    )
    got = lax.ppermute(sent, "core", [(0, 1), (1, 0)])
    (both,) = call(
        own_grads,
        [(size, bf16)],
        tile_own,
        hidden,
        grad_embedding,
        grad_hidden,
        got,
        scalars=(core,),
        limit=24,
    )
    grad_one, grad_two = call(
        last_sums, [((share, units), f32), ((share, units), f32)], exchange(both, "chip")
    )
    grad_two = grad_two.T

    terms = back.reshape(owners, ROWS, block)[:, capacity:].reshape(owners, -1).astype(f32)
    edge = heads * share
    from_values = terms[:, :edge].reshape(owners, heads, share)
    from_grads = terms[:, edge : edge + share]
    edge = edge + share
    from_up = terms[:, edge : edge + inner].reshape(owners, heads, HEAD)
    edge = edge + inner
    from_attended = terms[:, edge : edge + inner]
    grad_value = jnp.einsum("ohs,ohd->shd", from_values, from_up, precision=exact)
    grad_value = grad_value.reshape(share, inner)
    grad_out = contract(from_attended, from_grads, 0, 0, precision=exact)
    return (
        loss[0, 0],
        grad_one,
        grad_two,
        grad_wide[:, :inner],
        grad_wide[:, inner:],
        grad_value,
        grad_out,
    )


def solution(mesh):
    owners, parts = mesh.devices.shape
    split = Mesh(
        mesh.devices.reshape(owners // CORES, CORES, parts), ("chip", "core", "mp")
    )
    return jax.shard_map(
        per_device,
        mesh=split,
        in_specs=(
            P(DP, None),
            P(DP, None),
            P(),
            P(DP, None),
            P(None, "mp"),
            P("mp", None),
            P(None, "mp"),
            P(None, "mp"),
            P(None, "mp"),
            P("mp", None),
        ),
        out_specs=(
            P(),
            P(DP, "mp"),
            P("mp", DP),
            P(DP, "mp"),
            P(DP, "mp"),
            P(DP, "mp"),
            P("mp", DP),
        ),
        check_vma=False,
    )
```

profile of v0, /device:TPU:8, one launch (start us, length us, event | category | flops | bytes accessed | tf_op | source)
XLA Modules:
  0.0 266.6 jit_solution(3599062715547738652)
XLA Ops:
  0.6 1.7 copy-done.1
  2.3 1.7 copy-done.11
  5.0 2.7 %shard_map.153 = (bf16[192,1536]{1,0:T(8,128)(2,1)S(1)}, bf16[192,768]{1,0:T(8,128)(2,1)S(1)}, f32[192,768]{1,0:T(8,128)S(1)}, bf16[8,288,128]{2,1,0:T(8,128)(2,1)}) custom-call(bf16[192,1536]{1,0:T(8,128)(2,1)S(1)} %copy-done.12, bf16[1536,768]{1,0:T(8,128)(2,1)S(1)} %copy-done.11, bf16[768,1536]{1,0:T(8,128)(2,1)S(1)} %copy-done.1), custom_call_target="tpu_custom_call" | custom-call | tf_op jit(solution)/shard_map/pallas_call | solution.py:45
  8.5 8.6 %all-to-all-start = ((bf16[8,288,128]{2,1,0:T(8,128)(2,1)}), bf16[8,288,128]{2,1,0:T(8,128)(2,1)S(1)}, u32[]{:S(2)}, u32[]{:S(2)}) async-start(bf16[8,288,128]{2,1,0:T(8,128)(2,1)} %get-tuple-element.46), calls=%async_computation | async-start | bytes 1179648 | tf_op jit(solution)/shard_map/all_to_all | solution.py:31
  21.0 1.2 constant_dynamic-slice_fusion.4
  22.5 13.5 %all-to-all-done.refs_9_ = bf16[8,288,128]{2,1,0:T(8,128)(2,1)S(1)} async-done(((bf16[8,288,128]{2,1,0:T(8,128)(2,1)}), bf16[8,288,128]{2,1,0:T(8,128)(2,1)S(1)}, u32[]{:S(2)}, u32[]{:S(2)}) %all-to-all-start) | async-done | bytes 589856 | tf_op jit(solution)/shard_map/all_to_all | solution.py:31
  36.3 14.9 %all_to_all.40 = bf16[32,16,256]{2,1,0:T(8,128)(2,1)S(1)} all-to-all(bf16[32,16,256]{2,1,0:T(8,128)(2,1)S(1)} %bitcast.71), channel_id=1, replica_groups=mesh['chip'=16,'core'=2,'mp'=8] {'chip','core'}, dimensions={0} | all-to-all | bytes 524288 | tf_op jit(solution)/shard_map/all_to_all | solution.py:31
  52.2 2.7 %collective-permute-start.1 = (bf16[208,384]{1,0:T(8,128)(2,1)S(1)}, bf16[208,384]{1,0:T(8,128)(2,1)S(1)}, u32[]{:S(2)}, u32[]{:S(2)}) collective-permute-start(bf16[208,384]{1,0:T(8,128)(2,1)S(1)} %get-tuple-element.48.rest_0_.refs_4_), channel_id=1, source_target_pairs={{0,7},{1,0},{2,1},{3,2},{4,3},{5,4},{6,5},{7,6},{8,15},{9,8},{10,9... | collective-permute-start | bytes 479240 | tf_op jit(solution)/shard_map/ppermute | solution.py:72
  54.9 4.5 %collective-permute-done.rest_1_ = bf16[208,384]{1,0:T(8,128)(2,1)S(1)} collective-permute-done((bf16[208,384]{1,0:T(8,128)(2,1)S(1)}, bf16[208,384]{1,0:T(8,128)(2,1)S(1)}, u32[]{:S(2)}, u32[]{:S(2)}) %collective-permute-start) | collective-permute-done | bytes 159776 | tf_op jit(solution)/shard_map/ppermute | solution.py:71
  59.5 3.2 %collective-permute-start.3 = (bf16[208,384]{1,0:T(8,128)(2,1)S(1)}, bf16[208,384]{1,0:T(8,128)(2,1)S(1)}, u32[]{:S(2)}, u32[]{:S(2)}) collective-permute-start(bf16[208,384]{1,0:T(8,128)(2,1)S(1)} %collective-permute-done.1.rest_2_), channel_id=1, source_target_pairs={{0,7},{1,0},{2,1},{3,2},{4,3},{5,4},{6,5},{7,6},{8,15},{9,8},{10,9... | collective-permute-start | bytes 479240 | tf_op jit(solution)/shard_map/ppermute | solution.py:72
  62.7 3.8 %collective-permute-done.2.rest_3_ = bf16[208,384]{1,0:T(8,128)(2,1)S(1)} collective-permute-done((bf16[208,384]{1,0:T(8,128)(2,1)S(1)}, bf16[208,384]{1,0:T(8,128)(2,1)S(1)}, u32[]{:S(2)}, u32[]{:S(2)}) %collective-permute-start.2) | collective-permute-done | bytes 159776 | tf_op jit(solution)/shard_map/ppermute | solution.py:71
  66.4 3.2 %collective-permute-start.5 = (bf16[208,384]{1,0:T(8,128)(2,1)S(1)}, bf16[208,384]{1,0:T(8,128)(2,1)S(1)}, u32[]{:S(2)}, u32[]{:S(2)}) collective-permute-start(bf16[208,384]{1,0:T(8,128)(2,1)S(1)} %collective-permute-done.3.rest_4_), channel_id=1, source_target_pairs={{0,7},{1,0},{2,1},{3,2},{4,3},{5,4},{6,5},{7,6},{8,15},{9,8},{10,9... | collective-permute-start | bytes 479240 | tf_op jit(solution)/shard_map/ppermute | solution.py:72
  69.7 3.2 %collective-permute-done.4.rest_5_ = bf16[208,384]{1,0:T(8,128)(2,1)S(1)} collective-permute-done((bf16[208,384]{1,0:T(8,128)(2,1)S(1)}, bf16[208,384]{1,0:T(8,128)(2,1)S(1)}, u32[]{:S(2)}, u32[]{:S(2)}) %collective-permute-start.4) | collective-permute-done | bytes 159776 | tf_op jit(solution)/shard_map/ppermute | solution.py:71
  73.1 3.5 %collective-permute-start.7 = (bf16[96,384]{1,0:T(8,128)(2,1)S(1)}, bf16[96,384]{1,0:T(8,128)(2,1)S(1)}, u32[]{:S(2)}, u32[]{:S(2)}) collective-permute-start(bf16[96,384]{1,0:T(8,128)(2,1)S(1)} %slice.56), channel_id=1, source_target_pairs={{0,7},{1,0},{2,1},{3,2},{4,3},{5,4},{6,5},{7,6},{8,15},{9,8},{10,9... | collective-permute-start | bytes 221192 | tf_op jit(solution)/shard_map/ppermute | solution.py:76
  76.5 2.0 collective-permute-done.7.rest_8_
  78.7 4.0 %shard_map.156 = (bf16[1536,384]{1,0:T(8,128)(2,1)S(1)}, f32[2,384]{1,0:T(2,128)S(1)}, f32[2,96,384]{2,1,0:T(8,128)S(1)}, f32[2,96,384]{2,1,0:T(8,128)S(1)}, f32...) custom-call(s32[1]{0:T(128)} %bitcast.here, ...), custom_call_target="tpu_custom_call" | custom-call | tf_op jit(solution)/shard_map/pallas_call | solution.py:45
  86.6 4.7 %all-to-all-start.2 = ((f32[8,1,1536]{2,1,0:T(1,128)}), f32[8,1,1536]{2,1,0:T(1,128)S(1)}, u32[]{:S(2)}, u32[]{:S(2)}) async-start(f32[8,1,1536]{2,1,0:T(1,128)} %get-tuple-element.49), calls=%async_computation.2 | async-start | bytes 98304 | tf_op jit(solution)/shard_map/all_to_all | solution.py:31
  91.3 2.2 copy.49.query_weights_ref
  93.5 2.3 copy.50.key_weights_ref
  95.8 2.2 copy.51.value_weights_ref
  98.1 1.4 all-to-all-done.2.parts_ref
  102.1 4.9 %all-to-all-start.3 = ((f32[32,1,128]{2,1,0:T(1,128)}), f32[32,1,128]{2,1,0:T(1,128)S(1)}, u32[]{:S(2)}, u32[]{:S(2)}) async-start(f32[32,1,128]{2,1,0:T(1,128)} %get-tuple-element.51), calls=%async_computation.3 | async-start | bytes 32768 | tf_op jit(solution)/shard_map/all_to_all | solution.py:31
  107.9 5.2 %all-to-all-done.3 = f32[32,1,128]{2,1,0:T(1,128)S(1)} async-done(((f32[32,1,128]{2,1,0:T(1,128)}), f32[32,1,128]{2,1,0:T(1,128)S(1)}, u32[]{:S(2)}, u32[]{:S(2)}) %all-to-all-start.3) | async-done | bytes 16416 | tf_op jit(solution)/shard_map/all_to_all | solution.py:31
  117.6 1.3 copy-done.16
  122.6 3.0 %shard_map.158 = (f32[1,1]{1,0:T(1,128)}, f32[1,1536]{1,0:T(1,128)S(1)}, f32[1,192]{1,0:T(1,128)S(1)}, bf16[576,384]{1,0:T(8,128)(2,1)S(1)}, bf16[208,384]{1,0:T...) custom-call(s32[1]{0:T(128)} %bitcast.here, ...), custom_call_target="tpu_custom_call" | custom-call | tf_op jit(solution)/shard_map/pallas_call | solution.py:45
  126.4 1.3 convolution_convert_fusion.1
  128.6 1.6 collective-permute-done.8
  130.3 2.5 add_convert_fusion
  132.8 5.6 %all-to-all-start.4 = ((bf16[16,48,384]{2,1,0:T(8,128)(2,1)}), bf16[16,48,384]{2,1,0:T(8,128)(2,1)}, u32[]{:S(2)}, u32[]{:S(2)}) async-start(bf16[16,48,384]{2,1,0:T(8,128)(2,1)} %add_convert_fusion), calls=%async_computation.4 | async-start | bytes 1179648 | tf_op jit(solution)/shard_map/all_to_all | solution.py:31
  139.2 2.4 collective-permute-start.10
  141.6 2.7 %collective-permute-start.11 = (bf16[208,384]{1,0:T(8,128)(2,1)}, bf16[208,384]{1,0:T(8,128)(2,1)S(1)}, u32[]{:S(2)}, u32[]{:S(2)}) collective-permute-start(bf16[208,384]{1,0:T(8,128)(2,1)} %copy-done.38), channel_id=1, source_target_pairs={{0,3},{1,4},{2,5},{3,6},{4,7},{5,0},{6,1},{7,2},{8,11},{9,12},{10,... | collective-permute-start | bytes 479240 | tf_op jit(solution)/shard_map/ppermute | solution.py:63
  144.2 2.3 collective-permute-start.12
  146.6 2.7 %collective-permute-start.13 = (bf16[208,384]{1,0:T(8,128)(2,1)}, bf16[208,384]{1,0:T(8,128)(2,1)}, u32[]{:S(2)}, u32[]{:S(2)}) collective-permute-start(bf16[208,384]{1,0:T(8,128)(2,1)} %copy-done.36), channel_id=1, source_target_pairs={{0,5},{1,6},{2,7},{3,0},{4,1},{5,2},{6,3},{7,4},{8,13},{9,14},{10,... | collective-permute-start | bytes 479240 | tf_op jit(solution)/shard_map/ppermute | solution.py:63
  149.3 3.7 %collective-permute-start.14 = (bf16[208,384]{1,0:T(8,128)(2,1)}, bf16[208,384]{1,0:T(8,128)(2,1)}, u32[]{:S(2)}, u32[]{:S(2)}) collective-permute-start(bf16[208,384]{1,0:T(8,128)(2,1)} %copy-done.35), channel_id=1, source_target_pairs={{0,6},{1,7},{2,0},{3,1},{4,2},{5,3},{6,4},{7,5},{8,14},{9,15},{10,... | collective-permute-start | bytes 479240 | tf_op jit(solution)/shard_map/ppermute | solution.py:63
  153.0 3.0 %collective-permute-done.10.refs_9_ = bf16[208,384]{1,0:T(8,128)(2,1)S(1)} collective-permute-done((bf16[208,384]{1,0:T(8,128)(2,1)}, bf16[208,384]{1,0:T(8,128)(2,1)S(1)}, u32[]{:S(2)}, u32[]{:S(2)}) %collective-permute-start.10) | collective-permute-done | bytes 159776 | tf_op jit(solution)/shard_map/ppermute | solution.py:63
  156.0 2.1 collective-permute-start.15
  159.7 4.2 %collective-permute-done.11.refs_10_ = bf16[208,384]{1,0:T(8,128)(2,1)S(1)} collective-permute-done((bf16[208,384]{1,0:T(8,128)(2,1)}, bf16[208,384]{1,0:T(8,128)(2,1)S(1)}, u32[]{:S(2)}, u32[]{:S(2)}) %collective-permute-start.11) | collective-permute-done | bytes 159776 | tf_op jit(solution)/shard_map/ppermute | solution.py:63
  163.8 3.3 %collective-permute-done.12.refs_11_ = bf16[208,384]{1,0:T(8,128)(2,1)} collective-permute-done((bf16[208,384]{1,0:T(8,128)(2,1)}, bf16[208,384]{1,0:T(8,128)(2,1)}, u32[]{:S(2)}, u32[]{:S(2)}) %collective-permute-start.12) | collective-permute-done | bytes 159776 | tf_op jit(solution)/shard_map/ppermute | solution.py:63
  168.1 5.5 %collective-permute-done.14.refs_13_ = bf16[208,384]{1,0:T(8,128)(2,1)} collective-permute-done((bf16[208,384]{1,0:T(8,128)(2,1)}, bf16[208,384]{1,0:T(8,128)(2,1)}, u32[]{:S(2)}, u32[]{:S(2)}) %collective-permute-start.14) | collective-permute-done | bytes 159776 | tf_op jit(solution)/shard_map/ppermute | solution.py:63
  173.5 2.0 collective-permute-done.15.refs_14_
  175.6 1.7 shard_map.159
  177.3 14.8 %all_to_all.41 = bf16[32,16,192]{2,1,0:T(8,128)(2,1)S(1)} all-to-all(bf16[32,16,192]{2,1,0:T(8,128)(2,1)S(1)} %bitcast.74), channel_id=1, replica_groups=mesh['chip'=16,'core'=2,'mp'=8] {'chip','core'}, dimensions={0} | all-to-all | bytes 393216 | tf_op jit(solution)/shard_map/all_to_all | solution.py:31
  192.4 23.2 %all_to_all.42.parts_ref = bf16[8,288,128]{2,1,0:T(8,128)(2,1)S(1)} all-to-all(bf16[8,288,128]{2,1,0:T(8,128)(2,1)S(1)} %shard_map.160), channel_id=1, replica_groups=mesh['chip'=16,'core'=2,'mp'=8] {'mp'}, dimensions={0} | all-to-all | bytes 1179648 | tf_op jit(solution)/shard_map/all_to_all | solution.py:31
  215.6 2.1 shard_map.161
  217.9 4.5 %collective-permute-done.16.got_ref = bf16[16,96,768]{2,1,0:T(8,128)(2,1)S(1)} collective-permute-done((bf16[16,96,768]{2,1,0:T(8,128)(2,1)S(1)}, bf16[16,96,768]{2,1,0:T(8,128)(2,1)S(1)}, u32[]{:S(2)}, u32[]{:S(2)}) %collective-permute-start.16) | collective-permute-done | bytes 2359328 | tf_op jit(solution)/shard_map/ppermute | solution.py:622
  223.2 1.4 copy-done
  224.6 4.9 %all-to-all-start.7 = ((bf16[16,96,768]{2,1,0:T(8,128)(2,1)}), bf16[16,96,768]{2,1,0:T(8,128)(2,1)S(1)}, u32[]{:S(2)}, u32[]{:S(2)}) async-start(bf16[16,96,768]{2,1,0:T(8,128)(2,1)} %copy-done), calls=%async_computation.7 | async-start | bytes 4718592 | tf_op jit(solution)/shard_map/all_to_all | solution.py:31
  233.4 32.3 %all-to-all-done.7.values_ref = bf16[16,96,768]{2,1,0:T(8,128)(2,1)S(1)} async-done(((bf16[16,96,768]{2,1,0:T(8,128)(2,1)}), bf16[16,96,768]{2,1,0:T(8,128)(2,1)S(1)}, u32[]{:S(2)}, u32[]{:S(2)}) %all-to-all-start.7) | async-done | bytes 2359328 | tf_op jit(solution)/shard_map/all_to_all | solution.py:31
  (163 shorter events, 34.4 us)
Async XLA Ops:
  0.6 1.7 copy-start.1
  2.3 1.7 copy-start.11
  8.5 8.6 %copy-start.13 = (bf16[192,1536]{1,0:T(8,128)(2,1)S(1)}, bf16[192,1536]{1,0:T(8,128)(2,1)}, u32[]{:S(2)}) copy-start(bf16[192,1536]{1,0:T(8,128)(2,1)} %x_ref.1) | copy-start | bytes 1769476
  8.5 27.5 %all-to-all-start = ((bf16[8,288,128]{2,1,0:T(8,128)(2,1)}), bf16[8,288,128]{2,1,0:T(8,128)(2,1)S(1)}, u32[]{:S(2)}, u32[]{:S(2)}) async-start(bf16[8,288,128]{2,1,0:T(8,128)(2,1)} %get-tuple-element.46), calls=%async_computation | async-start | bytes 1179648 | tf_op jit(solution)/shard_map/all_to_all | solution.py:31
  36.0 42.7 %copy-start.9 = (bf16[1536,192]{0,1:T(8,128)(2,1)S(1)}, bf16[1536,192]{0,1:T(8,128)(2,1)}, u32[]{:S(2)}) copy-start(bf16[1536,192]{0,1:T(8,128)(2,1)} %param.17) | copy-start | bytes 1769476
  36.0 42.7 %copy-start.10 = (bf16[1536,192]{0,1:T(8,128)(2,1)S(1)}, bf16[1536,192]{0,1:T(8,128)(2,1)}, u32[]{:S(2)}) copy-start(bf16[1536,192]{0,1:T(8,128)(2,1)} %param.18) | copy-start | bytes 1769476
  36.3 42.4 %copy-start.6 = (bf16[192,1536]{1,0:T(8,128)(2,1)S(1)}, bf16[192,1536]{1,0:T(8,128)(2,1)}, u32[]{:S(2)}) copy-start(bf16[192,1536]{1,0:T(8,128)(2,1)} %out_weights_ref.3) | copy-start | bytes 1769476
  36.3 42.4 %copy-start.8 = (bf16[1536,192]{0,1:T(8,128)(2,1)S(1)}, bf16[1536,192]{0,1:T(8,128)(2,1)}, u32[]{:S(2)}) copy-start(bf16[1536,192]{0,1:T(8,128)(2,1)} %param.16) | copy-start | bytes 1769476
  51.6 31.1 %copy-start.20 = (bf16[208,384]{1,0:T(8,128)(2,1)}, bf16[208,384]{1,0:T(8,128)(2,1)S(1)}, u32[]{:S(2)}) copy-start(bf16[208,384]{1,0:T(8,128)(2,1)S(1)} %get-tuple-element.48.rest_0_.refs_4_) | copy-start | bytes 479236
  51.6 7.8 %collective-permute-start = (bf16[208,384]{1,0:T(8,128)(2,1)S(1)}, bf16[208,384]{1,0:T(8,128)(2,1)S(1)}, u32[]{:S(2)}, u32[]{:S(2)}) collective-permute-start(bf16[208,384]{1,0:T(8,128)(2,1)S(1)} %get-tuple-element.48.rest_0_.refs_4_), channel_id=1, source_target_pairs={{0,1},{1,2},{2,3},{3,4},{4,5},{5,6},{6,7},{7,0},{8,9},{9,10},{10,1... | collective-permute-start | bytes 479240 | tf_op jit(solution)/shard_map/ppermute | solution.py:71
  52.2 7.2 %collective-permute-start.1 = (bf16[208,384]{1,0:T(8,128)(2,1)S(1)}, bf16[208,384]{1,0:T(8,128)(2,1)S(1)}, u32[]{:S(2)}, u32[]{:S(2)}) collective-permute-start(bf16[208,384]{1,0:T(8,128)(2,1)S(1)} %get-tuple-element.48.rest_0_.refs_4_), channel_id=1, source_target_pairs={{0,7},{1,0},{2,1},{3,2},{4,3},{5,4},{6,5},{7,6},{8,15},{9,8},{10,9... | collective-permute-start | bytes 479240 | tf_op jit(solution)/shard_map/ppermute | solution.py:72
  59.4 7.0 %collective-permute-start.2 = (bf16[208,384]{1,0:T(8,128)(2,1)S(1)}, bf16[208,384]{1,0:T(8,128)(2,1)S(1)}, u32[]{:S(2)}, u32[]{:S(2)}) collective-permute-start(bf16[208,384]{1,0:T(8,128)(2,1)S(1)} %collective-permute-done.rest_1_), channel_id=1, source_target_pairs={{0,1},{1,2},{2,3},{3,4},{4,5},{5,6},{6,7},{7,0},{8,9},{9,10},{10,1... | collective-permute-start | bytes 479240 | tf_op jit(solution)/shard_map/ppermute | solution.py:71
  59.5 7.0 %collective-permute-start.3 = (bf16[208,384]{1,0:T(8,128)(2,1)S(1)}, bf16[208,384]{1,0:T(8,128)(2,1)S(1)}, u32[]{:S(2)}, u32[]{:S(2)}) collective-permute-start(bf16[208,384]{1,0:T(8,128)(2,1)S(1)} %collective-permute-done.1.rest_2_), channel_id=1, source_target_pairs={{0,7},{1,0},{2,1},{3,2},{4,3},{5,4},{6,5},{7,6},{8,15},{9,8},{10,9... | collective-permute-start | bytes 479240 | tf_op jit(solution)/shard_map/ppermute | solution.py:72
  66.4 6.5 %collective-permute-start.4 = (bf16[208,384]{1,0:T(8,128)(2,1)S(1)}, bf16[208,384]{1,0:T(8,128)(2,1)S(1)}, u32[]{:S(2)}, u32[]{:S(2)}) collective-permute-start(bf16[208,384]{1,0:T(8,128)(2,1)S(1)} %collective-permute-done.2.rest_3_), channel_id=1, source_target_pairs={{0,1},{1,2},{2,3},{3,4},{4,5},{5,6},{6,7},{7,0},{8,9},{9,10},{10,1... | collective-permute-start | bytes 479240 | tf_op jit(solution)/shard_map/ppermute | solution.py:71
  66.4 6.6 %collective-permute-start.5 = (bf16[208,384]{1,0:T(8,128)(2,1)S(1)}, bf16[208,384]{1,0:T(8,128)(2,1)S(1)}, u32[]{:S(2)}, u32[]{:S(2)}) collective-permute-start(bf16[208,384]{1,0:T(8,128)(2,1)S(1)} %collective-permute-done.3.rest_4_), channel_id=1, source_target_pairs={{0,7},{1,0},{2,1},{3,2},{4,3},{5,4},{6,5},{7,6},{8,15},{9,8},{10,9... | collective-permute-start | bytes 479240 | tf_op jit(solution)/shard_map/ppermute | solution.py:72
  72.9 5.8 %collective-permute-start.6 = (bf16[112,384]{1,0:T(8,128)(2,1)S(1)}, bf16[112,384]{1,0:T(8,128)(2,1)S(1)}, u32[]{:S(2)}, u32[]{:S(2)}) collective-permute-start(bf16[112,384]{1,0:T(8,128)(2,1)S(1)} %slice.55), channel_id=1, source_target_pairs={{0,1},{1,2},{2,3},{3,4},{4,5},{5,6},{6,7},{7,0},{8,9},{9,10},{10,1... | collective-permute-start | bytes 258056 | tf_op jit(solution)/shard_map/ppermute | solution.py:75
  73.1 5.5 %collective-permute-start.7 = (bf16[96,384]{1,0:T(8,128)(2,1)S(1)}, bf16[96,384]{1,0:T(8,128)(2,1)S(1)}, u32[]{:S(2)}, u32[]{:S(2)}) collective-permute-start(bf16[96,384]{1,0:T(8,128)(2,1)S(1)} %slice.56), channel_id=1, source_target_pairs={{0,7},{1,0},{2,1},{3,2},{4,3},{5,4},{6,5},{7,6},{8,15},{9,8},{10,9... | collective-permute-start | bytes 221192 | tf_op jit(solution)/shard_map/ppermute | solution.py:76
  86.6 12.9 %all-to-all-start.2 = ((f32[8,1,1536]{2,1,0:T(1,128)}), f32[8,1,1536]{2,1,0:T(1,128)S(1)}, u32[]{:S(2)}, u32[]{:S(2)}) async-start(f32[8,1,1536]{2,1,0:T(1,128)} %get-tuple-element.49), calls=%async_computation.2 | async-start | bytes 98304 | tf_op jit(solution)/shard_map/all_to_all | solution.py:31
  93.5 4.5 %copy-start.44 = (s32[32]{0:T(128)S(1)}, s32[32]{0:T(128)}, u32[]{:S(2)}) copy-start(s32[32]{0:T(128)} %param.12) | copy-start | bytes 388
  102.1 11.0 %all-to-all-start.3 = ((f32[32,1,128]{2,1,0:T(1,128)}), f32[32,1,128]{2,1,0:T(1,128)S(1)}, u32[]{:S(2)}, u32[]{:S(2)}) async-start(f32[32,1,128]{2,1,0:T(1,128)} %get-tuple-element.51), calls=%async_computation.3 | async-start | bytes 32768 | tf_op jit(solution)/shard_map/all_to_all | solution.py:31
  113.1 1.1 copy-start.3
  117.6 1.3 copy-start.16
  122.6 3.8 %copy-start.41 = (bf16[16,1,48,384]{3,2,1,0:T(8,128)(2,1)S(1)}, bf16[16,1,48,384]{3,2,1,0:T(8,128)(2,1)}, u32[]{:S(2)}) copy-start(bf16[16,1,48,384]{3,2,1,0:T(8,128)(2,1)} %constant_dynamic-slice_fusion.1) | copy-start | bytes 1769476
  125.6 2.1 copy-start.30
  125.6 2.1 copy-start.34
  125.6 2.1 copy-start.35
  125.6 2.1 copy-start.36
  125.7 2.1 copy-start.37
  125.7 2.1 copy-start.38
  125.7 2.1 copy-start.39
  125.7 2.1 copy-start.40
  127.8 2.4 collective-permute-start.8
  132.8 42.8 %copy-start.21 = (bf16[208,384]{1,0:T(8,128)(2,1)S(1)}, bf16[208,384]{1,0:T(8,128)(2,1)}, u32[]{:S(2)}) copy-start(bf16[208,384]{1,0:T(8,128)(2,1)} %copy-done.20) | copy-start | bytes 479236
  132.8 42.8 %copy-start.31 = (bf16[208,384]{1,0:T(8,128)(2,1)S(1)}, bf16[208,384]{1,0:T(8,128)(2,1)}, u32[]{:S(2)}) copy-start(bf16[208,384]{1,0:T(8,128)(2,1)} %copy-done.30) | copy-start | bytes 479236
  132.8 25.7 %all-to-all-start.4 = ((bf16[16,48,384]{2,1,0:T(8,128)(2,1)}), bf16[16,48,384]{2,1,0:T(8,128)(2,1)}, u32[]{:S(2)}, u32[]{:S(2)}) async-start(bf16[16,48,384]{2,1,0:T(8,128)(2,1)} %add_convert_fusion), calls=%async_computation.4 | async-start | bytes 1179648 | tf_op jit(solution)/shard_map/all_to_all | solution.py:31
  138.5 10.8 %collective-permute-start.9 = (bf16[208,384]{1,0:T(8,128)(2,1)}, bf16[208,384]{1,0:T(8,128)(2,1)S(1)}, u32[]{:S(2)}, u32[]{:S(2)}) collective-permute-start(bf16[208,384]{1,0:T(8,128)(2,1)} %copy-done.40), channel_id=1, source_target_pairs={{0,1},{1,2},{2,3},{3,4},{4,5},{5,6},{6,7},{7,0},{8,9},{9,10},{10,1... | collective-permute-start | bytes 479240 | tf_op jit(solution)/shard_map/ppermute | solution.py:63
  139.2 16.8 %collective-permute-start.10 = (bf16[208,384]{1,0:T(8,128)(2,1)}, bf16[208,384]{1,0:T(8,128)(2,1)S(1)}, u32[]{:S(2)}, u32[]{:S(2)}) collective-permute-start(bf16[208,384]{1,0:T(8,128)(2,1)} %copy-done.39), channel_id=1, source_target_pairs={{0,2},{1,3},{2,4},{3,5},{4,6},{5,7},{6,0},{7,1},{8,10},{9,11},{10,... | collective-permute-start | bytes 479240 | tf_op jit(solution)/shard_map/ppermute | solution.py:63
  141.6 22.3 %collective-permute-start.11 = (bf16[208,384]{1,0:T(8,128)(2,1)}, bf16[208,384]{1,0:T(8,128)(2,1)S(1)}, u32[]{:S(2)}, u32[]{:S(2)}) collective-permute-start(bf16[208,384]{1,0:T(8,128)(2,1)} %copy-done.38), channel_id=1, source_target_pairs={{0,3},{1,4},{2,5},{3,6},{4,7},{5,0},{6,1},{7,2},{8,11},{9,12},{10,... | collective-permute-start | bytes 479240 | tf_op jit(solution)/shard_map/ppermute | solution.py:63
  144.2 22.9 %collective-permute-start.12 = (bf16[208,384]{1,0:T(8,128)(2,1)}, bf16[208,384]{1,0:T(8,128)(2,1)}, u32[]{:S(2)}, u32[]{:S(2)}) collective-permute-start(bf16[208,384]{1,0:T(8,128)(2,1)} %copy-done.37), channel_id=1, source_target_pairs={{0,4},{1,5},{2,6},{3,7},{4,0},{5,1},{6,2},{7,3},{8,12},{9,13},{10,... | collective-permute-start | bytes 479240 | tf_op jit(solution)/shard_map/ppermute | solution.py:63
  146.6 21.5 %collective-permute-start.13 = (bf16[208,384]{1,0:T(8,128)(2,1)}, bf16[208,384]{1,0:T(8,128)(2,1)}, u32[]{:S(2)}, u32[]{:S(2)}) collective-permute-start(bf16[208,384]{1,0:T(8,128)(2,1)} %copy-done.36), channel_id=1, source_target_pairs={{0,5},{1,6},{2,7},{3,0},{4,1},{5,2},{6,3},{7,4},{8,13},{9,14},{10,... | collective-permute-start | bytes 479240 | tf_op jit(solution)/shard_map/ppermute | solution.py:63
  149.3 24.2 %collective-permute-start.14 = (bf16[208,384]{1,0:T(8,128)(2,1)}, bf16[208,384]{1,0:T(8,128)(2,1)}, u32[]{:S(2)}, u32[]{:S(2)}) collective-permute-start(bf16[208,384]{1,0:T(8,128)(2,1)} %copy-done.35), channel_id=1, source_target_pairs={{0,6},{1,7},{2,0},{3,1},{4,2},{5,3},{6,4},{7,5},{8,14},{9,15},{10,... | collective-permute-start | bytes 479240 | tf_op jit(solution)/shard_map/ppermute | solution.py:63
  156.0 19.6 %collective-permute-start.15 = (bf16[208,384]{1,0:T(8,128)(2,1)}, bf16[208,384]{1,0:T(8,128)(2,1)}, u32[]{:S(2)}, u32[]{:S(2)}) collective-permute-start(bf16[208,384]{1,0:T(8,128)(2,1)} %copy-done.34), channel_id=1, source_target_pairs={{0,7},{1,0},{2,1},{3,2},{4,3},{5,4},{6,5},{7,6},{8,15},{9,8},{10,9... | collective-permute-start | bytes 479240 | tf_op jit(solution)/shard_map/ppermute | solution.py:63
  177.3 38.4 %copy-start.2 = (bf16[768,1536]{1,0:T(8,128)(2,1)S(1)}, bf16[768,1536]{1,0:T(8,128)(2,1)}, u32[]{:S(2)}) copy-start(bf16[768,1536]{1,0:T(8,128)(2,1)} %two_ref.3) | copy-start | bytes 7077892
  192.1 25.6 %copy-start.14 = (bf16[32,16,192]{2,1,0:T(8,128)(2,1)}, bf16[32,16,192]{2,1,0:T(8,128)(2,1)S(1)}, u32[]{:S(2)}) copy-start(bf16[32,16,192]{2,1,0:T(8,128)(2,1)S(1)} %all_to_all.41) | copy-start | bytes 589828
  192.1 23.5 %copy-start.18 = (bf16[192,768]{1,0:T(8,128)(2,1)S(1)}, bf16[192,768]{1,0:T(8,128)(2,1)}, u32[]{:S(2)}) copy-start(bf16[192,768]{1,0:T(8,128)(2,1)} %copy-done.17) | copy-start | bytes 884740
  217.7 4.6 %collective-permute-start.16 = (bf16[16,96,768]{2,1,0:T(8,128)(2,1)S(1)}, bf16[16,96,768]{2,1,0:T(8,128)(2,1)S(1)}, u32[]{:S(2)}, u32[]{:S(2)}) collective-permute-start(bf16[16,96,768]{2,1,0:T(8,128)(2,1)S(1)} %get-tuple-element.78), channel_id=1, source_target_pairs={{0,8},{8,0},{1,9},{9,1},{2,10},{10,2},{3,11},{11,3},{4,12},{12,4},... | collective-permute-start | bytes 7077896 | tf_op jit(solution)/shard_map/ppermute | solution.py:622
  223.2 1.4 copy-start
  224.6 41.0 %all-to-all-start.7 = ((bf16[16,96,768]{2,1,0:T(8,128)(2,1)}), bf16[16,96,768]{2,1,0:T(8,128)(2,1)S(1)}, u32[]{:S(2)}, u32[]{:S(2)}) async-start(bf16[16,96,768]{2,1,0:T(8,128)(2,1)} %copy-done), calls=%async_computation.7 | async-start | bytes 4718592 | tf_op jit(solution)/shard_map/all_to_all | solution.py:31
  (19 other events, 16.7 us)
where the time goes:
time: 270 us; the launch traced here: 267 us
  waiting for transfers between devices  91.1 us (34%)
  starting transfers between devices  58.6 us (22%)
  blocking collectives  52.9 us (20%)
  local copies, waits for them, and re-layouts  37.6 us (14%)
  Pallas kernels  17.4 us (6%)
  matrix products  5.31 us (2%)
    all_to_all x3, blocking collectives, exchange(): return lax.all_to_all(values, axis, 0, 0, tiled=True)  52.9 us
    all_to_all x5, waiting for transfers between devices, exchange(): return lax.all_to_all(values, axis, 0, 0, tiled=True)  52.3 us
    unnamed x94, local copies, waits for them, and re-layouts  29.2 us
    all_to_all x5, starting transfers between devices, exchange(): return lax.all_to_all(values, axis, 0, 0, tiled=True)  28.6 us
    ppermute x7, waiting for transfers between devices, scatter_ring(): lax.ppermute(pieces[k], 'mp', turn(count, k))  18.9 us
    pallas_call x11, Pallas kernels, call(): pl.pallas_call(kernel if skip else body, out_shape=[jax.ShapeDtypeStruct(...  17.4 us
    ppermute x7, starting transfers between devices, scatter_ring(): lax.ppermute(pieces[k], 'mp', turn(count, k))  16.5 us
    ppermute x3, waiting for transfers between devices, gather_ring(): back = lax.ppermute(back, 'mp', turn(count, 1))  11.5 us
  transfers between devices with their start and end apart: 22, of which 17 were waited for; matrix products, arithmetic and copies ran while one was open for 7% of the time, Pallas kernels for 0%

commit v1 on v0

--- a/solution.py
+++ b/solution.py
@@ -35,23 +35,38 @@
     return lax.dynamic_index_in_dim(values, index, axis, keepdims=False)
 
 
-def call(body, outs, *args, scalars=(), scratch=(), anchors=(), limit=16):
+def call(body, outs, *args, scalars=(), scratch=(), anchors=(), far=(), limit=16):
     count = len(scalars)
     skip = len(anchors)
+    vmem = pl.BlockSpec(memory_space=pltpu.VMEM)
+    away = pl.BlockSpec(memory_space=pl.ANY)
 
     def kernel(*refs):
         body(*refs[skip:])
 
     return pl.pallas_call(
         kernel if skip else body,
-        out_shape=[jax.ShapeDtypeStruct(shape, kind) for shape, kind in outs],
-        in_specs=[pl.BlockSpec(memory_space=pl.ANY)] * skip
+        out_shape=[jax.ShapeDtypeStruct(out[0], out[1]) for out in outs],
+        in_specs=[away] * skip
         + [pl.BlockSpec(memory_space=pltpu.SMEM)] * count
-        + [pl.BlockSpec(memory_space=pltpu.VMEM)] * len(args),
-        out_specs=[pl.BlockSpec(memory_space=pltpu.VMEM)] * len(outs),
-        scratch_shapes=[pltpu.VMEM(shape, kind) for shape, kind in scratch],
+        + [away if index in far else vmem for index in range(len(args))],
+        out_specs=[vmem if len(out) == 2 else away for out in outs],
+        scratch_shapes=[
+            pltpu.VMEM(*part) if isinstance(part, tuple) else pltpu.SemaphoreType.DMA((part,))
+            for part in scratch
+        ],
         compiler_params=pltpu.CompilerParams(vmem_limit_bytes=limit * 1024 * 1024),
     )(*anchors, *[jnp.reshape(s, (1,)).astype(i32) for s in scalars], *args)
+
+
+def fetch(sources, targets, semaphores):
+    copies = [
+        pltpu.make_async_copy(source, target, semaphores.at[index])
+        for index, (source, target) in enumerate(zip(sources, targets))
+    ]
+    for copy in copies:
+        copy.start()
+    return copies
 
 
 def turn(count, step):
@@ -104,17 +119,23 @@
     )
 
 
-def tile_forward(x_ref, one_ref, two_ref, norm_ref, hidden_ref, slope_ref, out_ref):
+def tile_forward(
+    far_x, far_one, far_two, norm_ref, hidden_ref, slope_ref, out_ref, x_ref, one_ref, two_ref, sems
+):
+    copies = fetch((far_x, far_one, far_two), (x_ref, one_ref, two_ref), sems)
+    copies[0].wait()
     x = x_ref[...].astype(f32)
     centred = x - jnp.mean(x, -1, keepdims=True)
     normed = centred * lax.rsqrt(jnp.mean(centred * centred, -1, keepdims=True) + eps)
     normed = normed.astype(bf16)
     norm_ref[...] = normed
+    copies[1].wait()
     pre = jnp.dot(normed, one_ref[...], preferred_element_type=f32)
     bell = 0.5 * (1.0 + lax.erf(pre * 0.7071067811865476))
     hidden = (pre * bell).astype(bf16)
     hidden_ref[...] = hidden
     slope_ref[...] = bell + pre * jnp.exp(-0.5 * pre * pre) * 0.3989422804014327
+    copies[2].wait()
     partial = jnp.dot(hidden, two_ref[...], preferred_element_type=f32).astype(bf16)
     count = out_ref.shape[0]
     block = partial.shape[1] // count
@@ -157,18 +178,20 @@
 ):
     pieces = rest[:9]
     (
-        norm_ref,
+        far_norm,
+        far_heads,
+        far_attention,
         stat_ref,
-        query_ref,
-        key_ref,
-        value_ref,
         scale_ref,
-        attention_ref,
         mass_ref,
         attended_ref,
         pooled_ref,
         reports_ref,
         slide_ref,
+        norm_ref,
+        heads_ref,
+        attention_ref,
+        sems,
     ) = rest[9:]
     count, owners, block = reports_ref.shape
 
@@ -187,8 +210,10 @@
     centred = slide - mean
     inverse = lax.rsqrt(jnp.mean(centred * centred, 0, keepdims=True) + eps)
     stat_ref[...] = jnp.concatenate([mean, inverse], 0)
-    norm_ref[...] = (centred * inverse).astype(bf16)
-    normed = norm_ref[...]
+    normed = (centred * inverse).astype(bf16)
+    norm_ref[...] = normed
+    copies = [pltpu.make_async_copy(norm_ref, far_norm, sems.at[0])]
+    copies[0].start()
     all_query = jnp.dot(query_weights_ref[...], normed, preferred_element_type=f32)
     all_keys = jnp.dot(key_weights_ref[...], normed, preferred_element_type=f32)
     all_values = jnp.dot(value_weights_ref[...], normed, preferred_element_type=f32)
@@ -203,14 +228,20 @@
         key_scale = lax.rsqrt(jnp.mean(keys * keys, 0, keepdims=True) + eps)
         query_unit = query * query_scale
         key_unit = keys * key_scale
-        query_ref[h] = query_unit
-        key_ref[h] = key_unit
-        value_ref[h] = values
+        heads_ref[h, 0] = query_unit
+        heads_ref[h, 1] = key_unit
+        heads_ref[h, 2] = values
+        copies.append(pltpu.make_async_copy(heads_ref.at[h], far_heads.at[h], sems.at[1 + 2 * h]))
+        copies[-1].start()
         scale_ref[h] = jnp.concatenate([query_scale, key_scale], 0)
         scores = contract(query_unit.astype(bf16), key_unit.astype(bf16), 0, 0)
         weights = jnp.exp(scores * (score_scale / HEAD)) * valid
         weights = weights * (1.0 / jnp.sum(weights, 1, keepdims=True))
         attention_ref[h] = weights
+        copies.append(
+            pltpu.make_async_copy(attention_ref.at[h], far_attention.at[h], sems.at[2 + 2 * h])
+        )
+        copies[-1].start()
         weights_low = weights.astype(bf16)
         mass_ref[h : h + 1, :] = jnp.dot(valid_low, weights_low, preferred_element_type=f32)
         attended.append(contract(values.astype(bf16), weights_low, 1, 1))
@@ -224,6 +255,8 @@
     slide_sum = contract(valid_low, low, 1, 1)
     pooled = (part + slide_sum * (1.0 / count)) / jnp.sum(valid)
     pooled_ref[...] = jnp.broadcast_to(pooled[None], pooled_ref.shape)
+    for copy in copies:
+        copy.wait()
 
 
 def logits_row(parts_ref, reports_ref, unit_ref, report_ref, row_ref):
@@ -253,23 +286,44 @@
     unit_ref,
     report_ref,
     valid_ref,
-    out_weights_ref,
-    query_weights_ref,
-    key_weights_ref,
-    value_weights_ref,
-    norm_ref,
-    query_ref,
-    key_ref,
-    value_ref,
     scale_ref,
-    attention_ref,
     mass_ref,
+    far_out_weights,
+    far_heads,
+    far_attention,
+    far_query_weights,
+    far_key_weights,
+    far_value_weights,
+    far_norm,
     loss_ref,
     grad_ref,
     up_ref,
     grads_ref,
-    *outs,
+    *rest,
 ):
+    outs, fetched, sems = rest[:-8], rest[-8:-1], rest[-1]
+    (
+        out_weights_ref,
+        heads_ref,
+        attention_ref,
+        query_weights_ref,
+        key_weights_ref,
+        value_weights_ref,
+        norm_ref,
+    ) = fetched
+    copies = fetch(
+        (
+            far_out_weights,
+            far_heads,
+            far_attention,
+            far_query_weights,
+            far_key_weights,
+            far_value_weights,
+            far_norm,
+        ),
+        fetched,
+        sems,
+    )
     owners = report_ref.shape[0]
     valid = valid_ref[...]
     logits = logits_ref[...]
@@ -300,20 +354,23 @@
     grad = grad_pooled / jnp.sum(valid)
     grad_ref[...] = grad
     low = grad.astype(bf16)
+    copies[0].wait()
     out_weights = out_weights_ref[...]
     up_ref[...] = contract(low, out_weights, 1, 1)
     up = jnp.sum(out_weights.astype(f32) * low.astype(f32), 1, keepdims=True)
-    heads = query_ref.shape[0]
+    heads = heads_ref.shape[0]
     inner = heads * HEAD
+    copies[1].wait()
+    copies[2].wait()
     for h in range(heads):
         up_head = up[h * HEAD : (h + 1) * HEAD]
-        values = value_ref[h]
+        values = heads_ref[h, 2]
         weights = attention_ref[h]
         pull = jnp.sum(up_head * values, 0, keepdims=True)
         pull_mean = jnp.sum(weights * pull, 1, keepdims=True)
         grad_scores = (weights * (pull - pull_mean) * (score_scale / HEAD)).astype(bf16)
-        query_unit = query_ref[h]
-        key_unit = key_ref[h]
+        query_unit = heads_ref[h, 0]
+        key_unit = heads_ref[h, 1]
         grad_query = contract(key_unit.astype(bf16), grad_scores, 1, 1) * valid
         grad_key = jnp.dot(query_unit.astype(bf16), grad_scores, preferred_element_type=f32)
         grad_query = scale_ref[h, 0:1] * (
@@ -329,6 +386,8 @@
     grad_query = grads_ref[0:inner, :]
     grad_key = grads_ref[inner : 2 * inner, :]
     grad_value = grads_ref[2 * inner : 3 * inner, :]
+    for copy in copies[3:]:
+        copy.wait()
     count = len(outs)
     block = norm_ref.shape[0] // count
     first = jnp.zeros_like(valid)
@@ -352,6 +411,21 @@
         outs[k][block : block + EXTRA, :] = stats
 
 
+def wide_grads(which, norm_ref, grads_ref, *rest):
+    got, out_ref = rest[:-1], rest[-1]
+    chips, share, columns = out_ref.shape
+    rows = [
+        norm_ref[pl.ds(pl.multiple_of((CORES * chip + which[0]) * share, 16), share), :]
+        for chip in range(chips)
+    ]
+    values = contract(jnp.concatenate(rows, 0), grads_ref[0:columns, :], 1, 1)
+    for chip in range(chips):
+        part = values[chip * share : (chip + 1) * share]
+        if got:
+            part = part + got[0][chip].astype(f32)
+        out_ref[chip] = part.astype(bf16)
+
+
 def slot_grads(own_ref, valid_ref, stat_ref, chunk_ref, select_ref, extra_ref, *rest):
     refs, out_ref = rest[:-1], rest[-1]
     total = refs[0][...].astype(f32)
@@ -389,11 +463,23 @@
     both_layers(other[0], norm_ref, hidden_ref, grad_ref, hidden_grad_ref, out_ref.shape, store)
 
 
-def own_grads(own, norm_ref, hidden_ref, grad_ref, hidden_grad_ref, got_ref, out_ref):
+def own_grads(
+    own, norm_ref, hidden_ref, grad_ref, hidden_grad_ref, got_ref, far_out, out_ref, sems
+):
+    copies = []
+
     def store(rows, values):
         out_ref[rows] = (values + got_ref[rows].astype(f32)).astype(bf16)
+        chip = rows[0]
+        if rows[1].start:
+            copies.append(
+                pltpu.make_async_copy(out_ref.at[chip], far_out.at[chip], sems.at[chip])
+            )
+            copies[-1].start()
 
     both_layers(own[0], norm_ref, hidden_ref, grad_ref, hidden_grad_ref, out_ref.shape, store)
+    for copy in copies:
+        copy.wait()
 
 
 def both_layers(which, norm_ref, hidden_ref, grad_ref, hidden_grad_ref, shape, store):
@@ -457,6 +543,13 @@
         tile_features,
         w_one,
         w_two,
+        far=(0, 1, 2),
+        scratch=[
+            (tile_features.shape, bf16),
+            (w_one.shape, bf16),
+            (w_two.shape, bf16),
+            3,
+        ],
         limit=24,
     )
     partial = exchange(partial, "mp")
@@ -501,12 +594,10 @@
 
     (
         slide_norm,
+        by_head,
+        attention,
         stat,
-        query,
-        keys,
-        values,
         scales,
-        attention,
         mass,
         attended_sum,
         pooled,
@@ -514,13 +605,11 @@
     ) = call(
         slide_forward,
         [
-            ((width, length), bf16),
+            ((width, length), bf16, "far"),
+            ((heads, 3, HEAD, length), f32, "far"),
+            ((heads, length, length), f32, "far"),
             ((2, length), f32),
-            ((heads, HEAD, length), f32),
-            ((heads, HEAD, length), f32),
-            ((heads, HEAD, length), f32),
             ((heads, 2, length), f32),
-            ((heads, length, length), f32),
             ((heads, length), f32),
             ((1, inner), f32),
             ((parts, 1, width), f32),
@@ -533,7 +622,13 @@
         w_out,
         *pieces,
         scalars=(here,),
-        scratch=[((width, length), bf16)],
+        scratch=[
+            ((width, length), bf16),
+            ((width, length), bf16),
+            ((heads, 3, HEAD, length), f32),
+            ((heads, length, length), f32),
+            1 + 2 * heads,
+        ],
         limit=28,
     )
     pooled = exchange(pooled, "mp")
@@ -553,29 +648,45 @@
         unit,
         report_unit,
         valid,
+        scales,
+        mass,
         w_out,
+        by_head,
+        attention,
         w_query,
         w_key,
         w_value,
         slide_norm,
-        query,
-        keys,
-        values,
-        scales,
-        attention,
-        mass,
         scalars=(here, owner),
-        limit=24,
+        far=tuple(range(7, 14)),
+        scratch=[
+            (w_out.shape, bf16),
+            (by_head.shape, f32),
+            (attention.shape, f32),
+            (w_query.shape, bf16),
+            (w_key.shape, bf16),
+            (w_value.shape, bf16),
+            (slide_norm.shape, bf16),
+            7,
+        ],
+        limit=28,
     )
     pieces = scatter_ring(pieces, parts)
 
-    norm_own, norm_other = halves(slide_norm)
     wide = (chips, share, 2 * inner)
-    wide_other = contract(norm_other, grads[: 2 * inner], 1, 1).astype(bf16).reshape(wide)
-    wide_got = lax.ppermute(wide_other, "core", [(0, 1), (1, 0)])
-    wide_own = contract(norm_own, grads[: 2 * inner], 1, 1).reshape(wide)
-    wide_sent = (wide_own + wide_got.astype(f32)).astype(bf16)
-    grad_wide = jnp.sum(exchange(wide_sent, "chip").astype(f32), 0)
+    (wide_sent,) = call(
+        wide_grads,
+        [(wide, bf16)],
+        slide_norm,
+        grads,
+        scalars=(1 - core,),
+        anchors=(pieces[1],),
+    )
+    wide_got = lax.ppermute(wide_sent, "core", [(0, 1), (1, 0)])
+    (wide_both,) = call(
+        wide_grads, [(wide, bf16)], slide_norm, grads, wide_got, scalars=(core,)
+    )
+    grad_wide = jnp.sum(exchange(wide_both, "chip").astype(f32), 0)
     value_rows = contract(mass.astype(bf16), slide_norm, 1, 1)
     extra = jnp.concatenate(
         [
@@ -622,13 +733,14 @@
     got = lax.ppermute(sent, "core", [(0, 1), (1, 0)])
     (both,) = call(
         own_grads,
-        [(size, bf16)],
+        [(size, bf16, "far")],
         tile_own,
         hidden,
         grad_embedding,
         grad_hidden,
         got,
         scalars=(core,),
+        scratch=[(size, bf16), chips],
         limit=24,
     )
     grad_one, grad_two = call(

time: 270 us -> 282 us (1.044)
  blocking collectives: 52.9 us -> 66.9 us
  Pallas kernels: 17.4 us -> 28.3 us
  starting transfers between devices: 58.6 us -> 49.4 us
  waiting for transfers between devices: 91.1 us -> 95.5 us
  matrix products: 5.31 us -> 1.48 us
  local copies, waits for them, and re-layouts: 37.6 us -> 34 us
    all_to_all x3 -> x4, blocking collectives: 52.9 us -> 66.9 us  [exchange(): return lax.all_to_all(values, axis, 0, 0, tiled=True)]
    ppermute x7, waiting for transfers between devices: 18.9 us -> 29.8 us  [scatter_ring(): lax.ppermute(pieces[k], 'mp', turn(count, k))]
    pallas_call x11 -> x13, Pallas kernels: 17.4 us -> 28.3 us  [call(): pl.pallas_call(kernel if skip else body, out_shape=[jax.ShapeDtypeStruct(...]
    all_to_all x5 -> x4, waiting for transfers between devices: 52.3 us -> 45.8 us  [exchange(): return lax.all_to_all(values, axis, 0, 0, tiled=True)]
    ppermute x7, starting transfers between devices: 16.5 us -> 10.3 us  [scatter_ring(): lax.ppermute(pieces[k], 'mp', turn(count, k))]
    dot_general x4 -> x2, matrix products: 5.12 us -> 1.28 us  [contract(): lax.dot_general(left, right, (((left_dim,), (right_dim,)), ((), ())), pre...]
    all_to_all x5 -> x4, starting transfers between devices: 28.6 us -> 25.7 us  [exchange(): return lax.all_to_all(values, axis, 0, 0, tiled=True)]
    unnamed x94 -> x86, local copies, waits for them, and re-layouts: 29.2 us -> 26.5 us
  transfers between devices with their start and end apart: 22 -> 21, of which waited for: 17 -> 15; matrix products, arithmetic and copies ran while one was open for 7% -> 7% of each run, Pallas kernels for 0% -> 0%
where the time goes in v1:
time: 282 us; the launch traced here: 279 us
  waiting for transfers between devices  95.5 us (34%)
  blocking collectives  66.9 us (24%)
  starting transfers between devices  49.4 us (18%)
  local copies, waits for them, and re-layouts  34 us (12%)
  Pallas kernels  28.3 us (10%)
    all_to_all x4, blocking collectives, exchange(): return lax.all_to_all(values, axis, 0, 0, tiled=True)  66.9 us
    all_to_all x4, waiting for transfers between devices, exchange(): return lax.all_to_all(values, axis, 0, 0, tiled=True)  45.8 us
    ppermute x7, waiting for transfers between devices, scatter_ring(): lax.ppermute(pieces[k], 'mp', turn(count, k))  29.8 us
    pallas_call x13, Pallas kernels, call(): pl.pallas_call(kernel if skip else body, out_shape=[jax.ShapeDtypeStruct(...  28.3 us
    unnamed x86, local copies, waits for them, and re-layouts  26.5 us
    all_to_all x4, starting transfers between devices, exchange(): return lax.all_to_all(values, axis, 0, 0, tiled=True)  25.7 us
    ppermute x3, waiting for transfers between devices, gather_ring(): back = lax.ppermute(back, 'mp', turn(count, 1))  11.5 us
    ppermute x7, starting transfers between devices, scatter_ring(): lax.ppermute(pieces[k], 'mp', turn(count, k))  10.3 us
  transfers between devices with their start and end apart: 21, of which 15 were waited for; matrix products, arithmetic and copies ran while one was open for 7% of the time, Pallas kernels for 0%

profile of v1, /device:TPU:8, one launch (start us, length us, event | category | flops | bytes accessed | tf_op | source)
XLA Modules:
  0.0 279.3 jit_solution(5063537216317029817)
XLA Ops:
  0.6 1.7 copy-done.1
  2.3 1.7 copy-done.12
  5.0 3.4 %shard_map.153 = (bf16[192,1536]{1,0:T(8,128)(2,1)S(1)}, bf16[192,768]{1,0:T(8,128)(2,1)S(1)}, f32[192,768]{1,0:T(8,128)S(1)}, bf16[8,288,128]{2,1,0:T(8,128)(2,1)}) custom-call(bf16[192,1536]{1,0:T(8,128)(2,1)S(1)} %copy-done.13, bf16[1536,768]{1,0:T(8,128)(2,1)S(1)} %copy-done.12, bf16[768,1536]{1,0:T(8,128)(2,1)S(1)} %copy-done.1), custom_call_target="tpu_custom_call" | custom-call | tf_op jit(solution)/shard_map/pallas_call | solution.py:47
  9.2 8.5 %all-to-all-start = ((bf16[8,288,128]{2,1,0:T(8,128)(2,1)}), bf16[8,288,128]{2,1,0:T(8,128)(2,1)S(1)}, u32[]{:S(2)}, u32[]{:S(2)}) async-start(bf16[8,288,128]{2,1,0:T(8,128)(2,1)} %get-tuple-element.44), calls=%async_computation | async-start | bytes 1179648 | tf_op jit(solution)/shard_map/all_to_all | solution.py:31
  18.3 1.2 copy.42
  21.5 1.2 constant_dynamic-slice_fusion.3
  22.9 13.6 %all-to-all-done.refs_9_ = bf16[8,288,128]{2,1,0:T(8,128)(2,1)S(1)} async-done(((bf16[8,288,128]{2,1,0:T(8,128)(2,1)}), bf16[8,288,128]{2,1,0:T(8,128)(2,1)S(1)}, u32[]{:S(2)}, u32[]{:S(2)}) %all-to-all-start) | async-done | bytes 589856 | tf_op jit(solution)/shard_map/all_to_all | solution.py:31
  36.9 14.9 %all_to_all.40 = bf16[32,16,256]{2,1,0:T(8,128)(2,1)S(1)} all-to-all(bf16[32,16,256]{2,1,0:T(8,128)(2,1)S(1)} %bitcast.57), channel_id=1, replica_groups=mesh['chip'=16,'core'=2,'mp'=8] {'chip','core'}, dimensions={0} | all-to-all | bytes 524288 | tf_op jit(solution)/shard_map/all_to_all | solution.py:31
  52.8 2.7 collective-permute-start.1
  55.5 4.5 %collective-permute-done.rest_1_ = bf16[208,384]{1,0:T(8,128)(2,1)S(1)} collective-permute-done((bf16[208,384]{1,0:T(8,128)(2,1)S(1)}, bf16[208,384]{1,0:T(8,128)(2,1)S(1)}, u32[]{:S(2)}, u32[]{:S(2)}) %collective-permute-start) | collective-permute-done | bytes 159776 | tf_op jit(solution)/shard_map/ppermute | solution.py:86
  60.0 3.2 %collective-permute-start.3 = (bf16[208,384]{1,0:T(8,128)(2,1)S(1)}, bf16[208,384]{1,0:T(8,128)(2,1)S(1)}, u32[]{:S(2)}, u32[]{:S(2)}) collective-permute-start(bf16[208,384]{1,0:T(8,128)(2,1)S(1)} %collective-permute-done.1.rest_2_), channel_id=1, source_target_pairs={{0,7},{1,0},{2,1},{3,2},{4,3},{5,4},{6,5},{7,6},{8,15},{9,8},{10,9... | collective-permute-start | bytes 479240 | tf_op jit(solution)/shard_map/ppermute | solution.py:87
  63.2 3.8 %collective-permute-done.2.rest_3_ = bf16[208,384]{1,0:T(8,128)(2,1)S(1)} collective-permute-done((bf16[208,384]{1,0:T(8,128)(2,1)S(1)}, bf16[208,384]{1,0:T(8,128)(2,1)S(1)}, u32[]{:S(2)}, u32[]{:S(2)}) %collective-permute-start.2) | collective-permute-done | bytes 159776 | tf_op jit(solution)/shard_map/ppermute | solution.py:86
  67.0 3.2 %collective-permute-start.5 = (bf16[208,384]{1,0:T(8,128)(2,1)S(1)}, bf16[208,384]{1,0:T(8,128)(2,1)S(1)}, u32[]{:S(2)}, u32[]{:S(2)}) collective-permute-start(bf16[208,384]{1,0:T(8,128)(2,1)S(1)} %collective-permute-done.3.rest_4_), channel_id=1, source_target_pairs={{0,7},{1,0},{2,1},{3,2},{4,3},{5,4},{6,5},{7,6},{8,15},{9,8},{10,9... | collective-permute-start | bytes 479240 | tf_op jit(solution)/shard_map/ppermute | solution.py:87
  70.2 3.2 %collective-permute-done.4.rest_5_ = bf16[208,384]{1,0:T(8,128)(2,1)S(1)} collective-permute-done((bf16[208,384]{1,0:T(8,128)(2,1)S(1)}, bf16[208,384]{1,0:T(8,128)(2,1)S(1)}, u32[]{:S(2)}, u32[]{:S(2)}) %collective-permute-start.4) | collective-permute-done | bytes 159776 | tf_op jit(solution)/shard_map/ppermute | solution.py:86
  73.6 3.5 %collective-permute-start.7 = (bf16[96,384]{1,0:T(8,128)(2,1)S(1)}, bf16[96,384]{1,0:T(8,128)(2,1)S(1)}, u32[]{:S(2)}, u32[]{:S(2)}) collective-permute-start(bf16[96,384]{1,0:T(8,128)(2,1)S(1)} %slice.51), channel_id=1, source_target_pairs={{0,7},{1,0},{2,1},{3,2},{4,3},{5,4},{6,5},{7,6},{8,15},{9,8},{10,9... | collective-permute-start | bytes 221192 | tf_op jit(solution)/shard_map/ppermute | solution.py:91
  77.1 2.0 collective-permute-done.7.rest_8_
  79.3 5.6 %shard_map.156 = (bf16[1536,384]{1,0:T(8,128)(2,1)S(1)}, f32[2,3,96,384]{3,2,1,0:T(8,128)S(1)}, f32[2,384,384]{2,1,0:T(8,128)S(1)}, f32[2,384]{1,0:T(2,128)S(1)}...) custom-call(s32[1]{0:T(128)} %bitcast.here, ...), custom_call_target="tpu_custom_call" | custom-call | tf_op jit(solution)/shard_map/pallas_call | solution.py:47
  86.8 12.8 %all_to_all.41.parts_ref = f32[8,1,1536]{2,1,0:T(1,128)S(1)} all-to-all(f32[8,1,1536]{2,1,0:T(1,128)S(1)} %get-tuple-element.47), channel_id=1, replica_groups=mesh['chip'=16,'core'=2,'mp'=8] {'mp'}, dimensions={0} | all-to-all | bytes 98304 | tf_op jit(solution)/shard_map/all_to_all | solution.py:31
  101.3 4.9 %all-to-all-start.3 = ((f32[32,1,128]{2,1,0:T(1,128)}), f32[32,1,128]{2,1,0:T(1,128)S(1)}, u32[]{:S(2)}, u32[]{:S(2)}) async-start(f32[32,1,128]{2,1,0:T(1,128)} %get-tuple-element.49), calls=%async_computation.3 | async-start | bytes 32768 | tf_op jit(solution)/shard_map/all_to_all | solution.py:31
  106.2 2.2 copy.49.far_query_weights
  108.5 2.2 copy.50.far_key_weights
  110.7 2.2 copy.51.far_value_weights
  117.5 1.3 copy-done.19
  118.8 1.2 copy-done.23
  120.9 4.4 %shard_map.158 = (f32[1,1]{1,0:T(1,128)}, f32[1,1536]{1,0:T(1,128)S(1)}, f32[1,192]{1,0:T(1,128)S(1)}, bf16[576,384]{1,0:T(8,128)(2,1)S(1)}, bf16[208,384]{1,0:T...) custom-call(s32[1]{0:T(128)} %bitcast.here, ...), custom_call_target="tpu_custom_call" | custom-call | tf_op jit(solution)/shard_map/pallas_call | solution.py:47
  125.9 6.8 %collective-permute-done.8.refs_0_.refs_8_ = bf16[208,384]{1,0:T(8,128)(2,1)S(1)} collective-permute-done((bf16[208,384]{1,0:T(8,128)(2,1)S(1)}, bf16[208,384]{1,0:T(8,128)(2,1)S(1)}, u32[]{:S(2)}, u32[]{:S(2)}) %collective-permute-start.8) | collective-permute-done | bytes 159776 | tf_op jit(solution)/shard_map/ppermute | solution.py:78
  132.7 1.4 shard_map.159
  135.7 1.6 collective-permute-done.9.rest_0_
  138.3 1.6 shard_map.160
  140.8 7.4 %all-to-all-start.4 = ((bf16[16,48,384]{2,1,0:T(8,128)(2,1)}), bf16[16,48,384]{2,1,0:T(8,128)(2,1)}, u32[]{:S(2)}, u32[]{:S(2)}) async-start(bf16[16,48,384]{2,1,0:T(8,128)(2,1)} %copy-done.11), calls=%async_computation.4 | async-start | bytes 1179648 | tf_op jit(solution)/shard_map/all_to_all | solution.py:31
  149.1 4.5 %collective-permute-start.12 = (bf16[208,384]{1,0:T(8,128)(2,1)}, bf16[208,384]{1,0:T(8,128)(2,1)}, u32[]{:S(2)}, u32[]{:S(2)}) collective-permute-start(bf16[208,384]{1,0:T(8,128)(2,1)} %copy-done.35), channel_id=1, source_target_pairs={{0,4},{1,5},{2,6},{3,7},{4,0},{5,1},{6,2},{7,3},{8,12},{9,13},{10,... | collective-permute-start | bytes 479240 | tf_op jit(solution)/shard_map/ppermute | solution.py:78
  153.7 1.4 collective-permute-start.13
  155.0 3.0 %collective-permute-start.14 = (bf16[208,384]{1,0:T(8,128)(2,1)}, bf16[208,384]{1,0:T(8,128)(2,1)}, u32[]{:S(2)}, u32[]{:S(2)}) collective-permute-start(bf16[208,384]{1,0:T(8,128)(2,1)} %copy-done.33), channel_id=1, source_target_pairs={{0,6},{1,7},{2,0},{3,1},{4,2},{5,3},{6,4},{7,5},{8,14},{9,15},{10,... | collective-permute-start | bytes 479240 | tf_op jit(solution)/shard_map/ppermute | solution.py:78
  158.1 5.0 %collective-permute-done.10.refs_9_ = bf16[208,384]{1,0:T(8,128)(2,1)S(1)} collective-permute-done((bf16[208,384]{1,0:T(8,128)(2,1)}, bf16[208,384]{1,0:T(8,128)(2,1)S(1)}, u32[]{:S(2)}, u32[]{:S(2)}) %collective-permute-start.10) | collective-permute-done | bytes 159776 | tf_op jit(solution)/shard_map/ppermute | solution.py:78
  163.5 1.2 convert_reduce_fusion.refs_0_
  164.7 6.3 %collective-permute-done.11.refs_10_ = bf16[208,384]{1,0:T(8,128)(2,1)S(1)} collective-permute-done((bf16[208,384]{1,0:T(8,128)(2,1)}, bf16[208,384]{1,0:T(8,128)(2,1)S(1)}, u32[]{:S(2)}, u32[]{:S(2)}) %collective-permute-start.11) | collective-permute-done | bytes 159776 | tf_op jit(solution)/shard_map/ppermute | solution.py:78
  171.0 1.5 collective-permute-done.13.refs_12_
  172.5 7.6 %collective-permute-done.14.refs_13_ = bf16[208,384]{1,0:T(8,128)(2,1)} collective-permute-done((bf16[208,384]{1,0:T(8,128)(2,1)}, bf16[208,384]{1,0:T(8,128)(2,1)}, u32[]{:S(2)}, u32[]{:S(2)}) %collective-permute-start.14) | collective-permute-done | bytes 159776 | tf_op jit(solution)/shard_map/ppermute | solution.py:78
  180.1 2.6 collective-permute-done.15.refs_14_
  182.7 1.9 shard_map.161
  184.6 14.6 %all_to_all.42 = bf16[32,16,192]{2,1,0:T(8,128)(2,1)S(1)} all-to-all(bf16[32,16,192]{2,1,0:T(8,128)(2,1)S(1)} %bitcast.60), channel_id=1, replica_groups=mesh['chip'=16,'core'=2,'mp'=8] {'chip','core'}, dimensions={0} | all-to-all | bytes 393216 | tf_op jit(solution)/shard_map/all_to_all | solution.py:31
  199.6 24.5 %all_to_all.43.parts_ref = bf16[8,288,128]{2,1,0:T(8,128)(2,1)S(1)} all-to-all(bf16[8,288,128]{2,1,0:T(8,128)(2,1)S(1)} %shard_map.162), channel_id=1, replica_groups=mesh['chip'=16,'core'=2,'mp'=8] {'mp'}, dimensions={0} | all-to-all | bytes 1179648 | tf_op jit(solution)/shard_map/all_to_all | solution.py:31
  224.1 2.1 shard_map.163
  226.3 4.5 %collective-permute-done.16.got_ref = bf16[16,96,768]{2,1,0:T(8,128)(2,1)S(1)} collective-permute-done((bf16[16,96,768]{2,1,0:T(8,128)(2,1)S(1)}, bf16[16,96,768]{2,1,0:T(8,128)(2,1)S(1)}, u32[]{:S(2)}, u32[]{:S(2)}) %collective-permute-start.16) | collective-permute-done | bytes 2359328 | tf_op jit(solution)/shard_map/ppermute | solution.py:733
  230.8 5.0 %shard_map.164 = bf16[16,96,768]{2,1,0:T(8,128)(2,1)S(1)} custom-call(s32[1]{0:T(128)} %bitcast.19.which.own, bf16[768,192]{1,0:T(8,128)(2,1)S(1)} %bitcast.52, bf16[192,768]{1,0:T(8,128)(2,1)S(1)} %copy-done.21, bf16[1536,192]{1,0:T(8,128)(2,1)S(1)} %get-tuple-element.72.grad_ref, bf16[768,192]{1,0:T(8,128)(2,1)S(1)} %get-tuple-element.73.hidden_grad_ref, ...), custom_call_target="tpu_custom_call" | custom-call | tf_op jit(solution)/shard_map/pallas_call | solution.py:47
  235.9 1.4 copy-done
  237.3 4.9 %all-to-all-start.7 = ((bf16[16,96,768]{2,1,0:T(8,128)(2,1)}), bf16[16,96,768]{2,1,0:T(8,128)(2,1)S(1)}, u32[]{:S(2)}, u32[]{:S(2)}) async-start(bf16[16,96,768]{2,1,0:T(8,128)(2,1)} %copy-done), calls=%async_computation.7 | async-start | bytes 4718592 | tf_op jit(solution)/shard_map/all_to_all | solution.py:31
  246.1 32.2 %all-to-all-done.7.values_ref = bf16[16,96,768]{2,1,0:T(8,128)(2,1)S(1)} async-done(((bf16[16,96,768]{2,1,0:T(8,128)(2,1)}), bf16[16,96,768]{2,1,0:T(8,128)(2,1)S(1)}, u32[]{:S(2)}, u32[]{:S(2)}) %all-to-all-start.7) | async-done | bytes 2359328 | tf_op jit(solution)/shard_map/all_to_all | solution.py:31
  (153 shorter events, 26.1 us)
Async XLA Ops:
  0.6 1.7 copy-start.1
  2.3 1.7 copy-start.12
  5.0 12.6 %copy-start.14 = (bf16[192,1536]{1,0:T(8,128)(2,1)S(1)}, bf16[192,1536]{1,0:T(8,128)(2,1)}, u32[]{:S(2)}) copy-start(bf16[192,1536]{1,0:T(8,128)(2,1)} %far_x.1) | copy-start | bytes 1769476
  9.2 27.4 %all-to-all-start = ((bf16[8,288,128]{2,1,0:T(8,128)(2,1)}), bf16[8,288,128]{2,1,0:T(8,128)(2,1)S(1)}, u32[]{:S(2)}, u32[]{:S(2)}) async-start(bf16[8,288,128]{2,1,0:T(8,128)(2,1)} %get-tuple-element.44), calls=%async_computation | async-start | bytes 1179648 | tf_op jit(solution)/shard_map/all_to_all | solution.py:31
  17.7 2.3 copy-start.39
  17.7 2.5 copy-start.38
  36.5 42.7 %copy-start.6 = (bf16[192,1536]{1,0:T(8,128)(2,1)S(1)}, bf16[192,1536]{1,0:T(8,128)(2,1)}, u32[]{:S(2)}) copy-start(bf16[192,1536]{1,0:T(8,128)(2,1)} %far_out_weights.1) | copy-start | bytes 1769476
  36.5 42.7 %copy-start.8 = (bf16[1536,192]{0,1:T(8,128)(2,1)S(1)}, bf16[1536,192]{0,1:T(8,128)(2,1)}, u32[]{:S(2)}) copy-start(bf16[1536,192]{0,1:T(8,128)(2,1)} %param.16) | copy-start | bytes 1769476
  36.6 42.7 %copy-start.9 = (bf16[1536,192]{0,1:T(8,128)(2,1)S(1)}, bf16[1536,192]{0,1:T(8,128)(2,1)}, u32[]{:S(2)}) copy-start(bf16[1536,192]{0,1:T(8,128)(2,1)} %param.17) | copy-start | bytes 1769476
  36.6 42.7 %copy-start.10 = (bf16[1536,192]{0,1:T(8,128)(2,1)S(1)}, bf16[1536,192]{0,1:T(8,128)(2,1)}, u32[]{:S(2)}) copy-start(bf16[1536,192]{0,1:T(8,128)(2,1)} %param.18) | copy-start | bytes 1769476
  52.2 32.6 %copy-start.24 = (bf16[208,384]{1,0:T(8,128)(2,1)}, bf16[208,384]{1,0:T(8,128)(2,1)S(1)}, u32[]{:S(2)}) copy-start(bf16[208,384]{1,0:T(8,128)(2,1)S(1)} %get-tuple-element.46.rest_0_.refs_4_) | copy-start | bytes 479236
  52.2 7.8 %collective-permute-start = (bf16[208,384]{1,0:T(8,128)(2,1)S(1)}, bf16[208,384]{1,0:T(8,128)(2,1)S(1)}, u32[]{:S(2)}, u32[]{:S(2)}) collective-permute-start(bf16[208,384]{1,0:T(8,128)(2,1)S(1)} %get-tuple-element.46.rest_0_.refs_4_), channel_id=1, source_target_pairs={{0,1},{1,2},{2,3},{3,4},{4,5},{5,6},{6,7},{7,0},{8,9},{9,10},{10,1... | collective-permute-start | bytes 479240 | tf_op jit(solution)/shard_map/ppermute | solution.py:86
  52.8 7.2 %collective-permute-start.1 = (bf16[208,384]{1,0:T(8,128)(2,1)S(1)}, bf16[208,384]{1,0:T(8,128)(2,1)S(1)}, u32[]{:S(2)}, u32[]{:S(2)}) collective-permute-start(bf16[208,384]{1,0:T(8,128)(2,1)S(1)} %get-tuple-element.46.rest_0_.refs_4_), channel_id=1, source_target_pairs={{0,7},{1,0},{2,1},{3,2},{4,3},{5,4},{6,5},{7,6},{8,15},{9,8},{10,9... | collective-permute-start | bytes 479240 | tf_op jit(solution)/shard_map/ppermute | solution.py:87
  60.0 7.0 %collective-permute-start.2 = (bf16[208,384]{1,0:T(8,128)(2,1)S(1)}, bf16[208,384]{1,0:T(8,128)(2,1)S(1)}, u32[]{:S(2)}, u32[]{:S(2)}) collective-permute-start(bf16[208,384]{1,0:T(8,128)(2,1)S(1)} %collective-permute-done.rest_1_), channel_id=1, source_target_pairs={{0,1},{1,2},{2,3},{3,4},{4,5},{5,6},{6,7},{7,0},{8,9},{9,10},{10,1... | collective-permute-start | bytes 479240 | tf_op jit(solution)/shard_map/ppermute | solution.py:86
  60.0 7.0 %collective-permute-start.3 = (bf16[208,384]{1,0:T(8,128)(2,1)S(1)}, bf16[208,384]{1,0:T(8,128)(2,1)S(1)}, u32[]{:S(2)}, u32[]{:S(2)}) collective-permute-start(bf16[208,384]{1,0:T(8,128)(2,1)S(1)} %collective-permute-done.1.rest_2_), channel_id=1, source_target_pairs={{0,7},{1,0},{2,1},{3,2},{4,3},{5,4},{6,5},{7,6},{8,15},{9,8},{10,9... | collective-permute-start | bytes 479240 | tf_op jit(solution)/shard_map/ppermute | solution.py:87
  67.0 6.5 %collective-permute-start.4 = (bf16[208,384]{1,0:T(8,128)(2,1)S(1)}, bf16[208,384]{1,0:T(8,128)(2,1)S(1)}, u32[]{:S(2)}, u32[]{:S(2)}) collective-permute-start(bf16[208,384]{1,0:T(8,128)(2,1)S(1)} %collective-permute-done.2.rest_3_), channel_id=1, source_target_pairs={{0,1},{1,2},{2,3},{3,4},{4,5},{5,6},{6,7},{7,0},{8,9},{9,10},{10,1... | collective-permute-start | bytes 479240 | tf_op jit(solution)/shard_map/ppermute | solution.py:86
  67.0 6.6 %collective-permute-start.5 = (bf16[208,384]{1,0:T(8,128)(2,1)S(1)}, bf16[208,384]{1,0:T(8,128)(2,1)S(1)}, u32[]{:S(2)}, u32[]{:S(2)}) collective-permute-start(bf16[208,384]{1,0:T(8,128)(2,1)S(1)} %collective-permute-done.3.rest_4_), channel_id=1, source_target_pairs={{0,7},{1,0},{2,1},{3,2},{4,3},{5,4},{6,5},{7,6},{8,15},{9,8},{10,9... | collective-permute-start | bytes 479240 | tf_op jit(solution)/shard_map/ppermute | solution.py:87
  73.5 5.8 %collective-permute-start.6 = (bf16[112,384]{1,0:T(8,128)(2,1)S(1)}, bf16[112,384]{1,0:T(8,128)(2,1)S(1)}, u32[]{:S(2)}, u32[]{:S(2)}) collective-permute-start(bf16[112,384]{1,0:T(8,128)(2,1)S(1)} %slice.50), channel_id=1, source_target_pairs={{0,1},{1,2},{2,3},{3,4},{4,5},{5,6},{6,7},{7,0},{8,9},{9,10},{10,1... | collective-permute-start | bytes 258056 | tf_op jit(solution)/shard_map/ppermute | solution.py:90
  73.6 5.5 %collective-permute-start.7 = (bf16[96,384]{1,0:T(8,128)(2,1)S(1)}, bf16[96,384]{1,0:T(8,128)(2,1)S(1)}, u32[]{:S(2)}, u32[]{:S(2)}) collective-permute-start(bf16[96,384]{1,0:T(8,128)(2,1)S(1)} %slice.51), channel_id=1, source_target_pairs={{0,7},{1,0},{2,1},{3,2},{4,3},{5,4},{6,5},{7,6},{8,15},{9,8},{10,9... | collective-permute-start | bytes 221192 | tf_op jit(solution)/shard_map/ppermute | solution.py:91
  86.8 26.1 %copy-start.40 = (s32[32]{0:T(128)S(1)}, s32[32]{0:T(128)}, u32[]{:S(2)}) copy-start(s32[32]{0:T(128)} %param.12) | copy-start | bytes 388
  101.3 11.7 %all-to-all-start.3 = ((f32[32,1,128]{2,1,0:T(1,128)}), f32[32,1,128]{2,1,0:T(1,128)S(1)}, u32[]{:S(2)}, u32[]{:S(2)}) async-start(f32[32,1,128]{2,1,0:T(1,128)} %get-tuple-element.49), calls=%async_computation.3 | async-start | bytes 32768 | tf_op jit(solution)/shard_map/all_to_all | solution.py:31
  117.5 1.3 copy-start.19
  125.2 8.9 %copy-start.30 = (bf16[208,384]{1,0:T(8,128)(2,1)}, bf16[208,384]{1,0:T(8,128)(2,1)S(1)}, u32[]{:S(2)}) copy-start(bf16[208,384]{1,0:T(8,128)(2,1)S(1)} %get-tuple-element.65.refs_7_) | copy-start | bytes 479236
  125.2 8.9 %copy-start.32 = (bf16[208,384]{1,0:T(8,128)(2,1)}, bf16[208,384]{1,0:T(8,128)(2,1)S(1)}, u32[]{:S(2)}) copy-start(bf16[208,384]{1,0:T(8,128)(2,1)S(1)} %get-tuple-element.71) | copy-start | bytes 479236
  125.2 8.9 %copy-start.33 = (bf16[208,384]{1,0:T(8,128)(2,1)}, bf16[208,384]{1,0:T(8,128)(2,1)S(1)}, u32[]{:S(2)}) copy-start(bf16[208,384]{1,0:T(8,128)(2,1)S(1)} %get-tuple-element.70) | copy-start | bytes 479236
  125.2 8.9 %copy-start.34 = (bf16[208,384]{1,0:T(8,128)(2,1)}, bf16[208,384]{1,0:T(8,128)(2,1)S(1)}, u32[]{:S(2)}) copy-start(bf16[208,384]{1,0:T(8,128)(2,1)S(1)} %get-tuple-element.69) | copy-start | bytes 479236
  125.3 8.9 %copy-start.35 = (bf16[208,384]{1,0:T(8,128)(2,1)}, bf16[208,384]{1,0:T(8,128)(2,1)S(1)}, u32[]{:S(2)}) copy-start(bf16[208,384]{1,0:T(8,128)(2,1)S(1)} %get-tuple-element.68) | copy-start | bytes 479236
  125.3 8.9 %copy-start.36 = (bf16[208,384]{1,0:T(8,128)(2,1)}, bf16[208,384]{1,0:T(8,128)(2,1)S(1)}, u32[]{:S(2)}) copy-start(bf16[208,384]{1,0:T(8,128)(2,1)S(1)} %get-tuple-element.67) | copy-start | bytes 479236
  125.3 8.9 %copy-start.37 = (bf16[208,384]{1,0:T(8,128)(2,1)}, bf16[208,384]{1,0:T(8,128)(2,1)S(1)}, u32[]{:S(2)}) copy-start(bf16[208,384]{1,0:T(8,128)(2,1)S(1)} %get-tuple-element.66) | copy-start | bytes 479236
  125.3 7.5 %collective-permute-start.8 = (bf16[208,384]{1,0:T(8,128)(2,1)S(1)}, bf16[208,384]{1,0:T(8,128)(2,1)S(1)}, u32[]{:S(2)}, u32[]{:S(2)}) collective-permute-start(bf16[208,384]{1,0:T(8,128)(2,1)S(1)} %get-tuple-element.60), channel_id=1, source_target_pairs={{0,1},{1,2},{2,3},{3,4},{4,5},{5,6},{6,7},{7,0},{8,9},{9,10},{10,1... | collective-permute-start | bytes 479240 | tf_op jit(solution)/shard_map/ppermute | solution.py:78
  132.7 1.4 copy-start.26
  135.0 2.3 collective-permute-start.9
  140.8 41.9 %copy-start.25 = (bf16[208,384]{1,0:T(8,128)(2,1)S(1)}, bf16[208,384]{1,0:T(8,128)(2,1)}, u32[]{:S(2)}) copy-start(bf16[208,384]{1,0:T(8,128)(2,1)} %copy-done.24) | copy-start | bytes 479236
  140.8 41.9 %copy-start.27 = (bf16[208,384]{1,0:T(8,128)(2,1)S(1)}, bf16[208,384]{1,0:T(8,128)(2,1)}, u32[]{:S(2)}) copy-start(bf16[208,384]{1,0:T(8,128)(2,1)} %copy-done.26) | copy-start | bytes 479236
  140.8 42.0 %copy-start.31 = (bf16[208,384]{1,0:T(8,128)(2,1)S(1)}, bf16[208,384]{1,0:T(8,128)(2,1)}, u32[]{:S(2)}) copy-start(bf16[208,384]{1,0:T(8,128)(2,1)} %copy-done.30) | copy-start | bytes 479236
  140.8 22.8 %all-to-all-start.4 = ((bf16[16,48,384]{2,1,0:T(8,128)(2,1)}), bf16[16,48,384]{2,1,0:T(8,128)(2,1)}, u32[]{:S(2)}, u32[]{:S(2)}) async-start(bf16[16,48,384]{2,1,0:T(8,128)(2,1)} %copy-done.11), calls=%async_computation.4 | async-start | bytes 1179648 | tf_op jit(solution)/shard_map/all_to_all | solution.py:31
  148.3 14.8 %collective-permute-start.10 = (bf16[208,384]{1,0:T(8,128)(2,1)}, bf16[208,384]{1,0:T(8,128)(2,1)S(1)}, u32[]{:S(2)}, u32[]{:S(2)}) collective-permute-start(bf16[208,384]{1,0:T(8,128)(2,1)} %copy-done.37), channel_id=1, source_target_pairs={{0,2},{1,3},{2,4},{3,5},{4,6},{5,7},{6,0},{7,1},{8,10},{9,11},{10,... | collective-permute-start | bytes 479240 | tf_op jit(solution)/shard_map/ppermute | solution.py:78
  148.4 22.6 %collective-permute-start.11 = (bf16[208,384]{1,0:T(8,128)(2,1)}, bf16[208,384]{1,0:T(8,128)(2,1)S(1)}, u32[]{:S(2)}, u32[]{:S(2)}) collective-permute-start(bf16[208,384]{1,0:T(8,128)(2,1)} %copy-done.36), channel_id=1, source_target_pairs={{0,3},{1,4},{2,5},{3,6},{4,7},{5,0},{6,1},{7,2},{8,11},{9,12},{10,... | collective-permute-start | bytes 479240 | tf_op jit(solution)/shard_map/ppermute | solution.py:78
  149.1 21.9 %collective-permute-start.12 = (bf16[208,384]{1,0:T(8,128)(2,1)}, bf16[208,384]{1,0:T(8,128)(2,1)}, u32[]{:S(2)}, u32[]{:S(2)}) collective-permute-start(bf16[208,384]{1,0:T(8,128)(2,1)} %copy-done.35), channel_id=1, source_target_pairs={{0,4},{1,5},{2,6},{3,7},{4,0},{5,1},{6,2},{7,3},{8,12},{9,13},{10,... | collective-permute-start | bytes 479240 | tf_op jit(solution)/shard_map/ppermute | solution.py:78
  153.7 18.9 %collective-permute-start.13 = (bf16[208,384]{1,0:T(8,128)(2,1)}, bf16[208,384]{1,0:T(8,128)(2,1)}, u32[]{:S(2)}, u32[]{:S(2)}) collective-permute-start(bf16[208,384]{1,0:T(8,128)(2,1)} %copy-done.34), channel_id=1, source_target_pairs={{0,5},{1,6},{2,7},{3,0},{4,1},{5,2},{6,3},{7,4},{8,13},{9,14},{10,... | collective-permute-start | bytes 479240 | tf_op jit(solution)/shard_map/ppermute | solution.py:78
  155.0 25.1 %collective-permute-start.14 = (bf16[208,384]{1,0:T(8,128)(2,1)}, bf16[208,384]{1,0:T(8,128)(2,1)}, u32[]{:S(2)}, u32[]{:S(2)}) collective-permute-start(bf16[208,384]{1,0:T(8,128)(2,1)} %copy-done.33), channel_id=1, source_target_pairs={{0,6},{1,7},{2,0},{3,1},{4,2},{5,3},{6,4},{7,5},{8,14},{9,15},{10,... | collective-permute-start | bytes 479240 | tf_op jit(solution)/shard_map/ppermute | solution.py:78
  163.1 19.6 %collective-permute-start.15 = (bf16[208,384]{1,0:T(8,128)(2,1)}, bf16[208,384]{1,0:T(8,128)(2,1)}, u32[]{:S(2)}, u32[]{:S(2)}) collective-permute-start(bf16[208,384]{1,0:T(8,128)(2,1)} %copy-done.32), channel_id=1, source_target_pairs={{0,7},{1,0},{2,1},{3,2},{4,3},{5,4},{6,5},{7,6},{8,15},{9,8},{10,9... | collective-permute-start | bytes 479240 | tf_op jit(solution)/shard_map/ppermute | solution.py:78
  182.7 41.4 %copy-start.2 = (bf16[768,1536]{1,0:T(8,128)(2,1)S(1)}, bf16[768,1536]{1,0:T(8,128)(2,1)}, u32[]{:S(2)}) copy-start(bf16[768,1536]{1,0:T(8,128)(2,1)} %two_ref.1) | copy-start | bytes 7077892
  182.7 41.4 %copy-start.21 = (bf16[192,768]{1,0:T(8,128)(2,1)S(1)}, bf16[192,768]{1,0:T(8,128)(2,1)}, u32[]{:S(2)}) copy-start(bf16[192,768]{1,0:T(8,128)(2,1)} %copy-done.20) | copy-start | bytes 884740
  199.2 27.0 %copy-start.17 = (bf16[32,16,192]{2,1,0:T(8,128)(2,1)}, bf16[32,16,192]{2,1,0:T(8,128)(2,1)S(1)}, u32[]{:S(2)}) copy-start(bf16[32,16,192]{2,1,0:T(8,128)(2,1)S(1)} %all_to_all.42) | copy-start | bytes 589828
  226.2 4.6 %collective-permute-start.16 = (bf16[16,96,768]{2,1,0:T(8,128)(2,1)S(1)}, bf16[16,96,768]{2,1,0:T(8,128)(2,1)S(1)}, u32[]{:S(2)}, u32[]{:S(2)}) collective-permute-start(bf16[16,96,768]{2,1,0:T(8,128)(2,1)S(1)} %get-tuple-element.74), channel_id=1, source_target_pairs={{0,8},{8,0},{1,9},{9,1},{2,10},{10,2},{3,11},{11,3},{4,12},{12,4},... | collective-permute-start | bytes 7077896 | tf_op jit(solution)/shard_map/ppermute | solution.py:733
  235.8 1.4 copy-start
  237.3 41.0 %all-to-all-start.7 = ((bf16[16,96,768]{2,1,0:T(8,128)(2,1)}), bf16[16,96,768]{2,1,0:T(8,128)(2,1)S(1)}, u32[]{:S(2)}, u32[]{:S(2)}) async-start(bf16[16,96,768]{2,1,0:T(8,128)(2,1)} %copy-done), calls=%async_computation.7 | async-start | bytes 4718592 | tf_op jit(solution)/shard_map/all_to_all | solution.py:31
  (14 other events, 13.7 us)

commit v2 on v1

--- a/solution.py
+++ b/solution.py
@@ -1,3 +1,5 @@
+import math
+
 import jax
 import jax.numpy as jnp
 from jax import lax
@@ -39,7 +41,7 @@
     count = len(scalars)
     skip = len(anchors)
     vmem = pl.BlockSpec(memory_space=pltpu.VMEM)
-    away = pl.BlockSpec(memory_space=pl.ANY)
+    away = pl.BlockSpec(memory_space=pltpu.HBM)
 
     def kernel(*refs):
         body(*refs[skip:])
@@ -47,7 +49,7 @@
     return pl.pallas_call(
         kernel if skip else body,
         out_shape=[jax.ShapeDtypeStruct(out[0], out[1]) for out in outs],
-        in_specs=[away] * skip
+        in_specs=[pl.BlockSpec(memory_space=pl.ANY)] * skip
         + [pl.BlockSpec(memory_space=pltpu.SMEM)] * count
         + [away if index in far else vmem for index in range(len(args))],
         out_specs=[vmem if len(out) == 2 else away for out in outs],
@@ -71,12 +73,6 @@
 
 def turn(count, step):
     return [(index, (index + step) % count) for index in range(count)]
-
-
-def scatter_ring(pieces, count):
-    return [pieces[0]] + [
-        lax.ppermute(pieces[k], "mp", turn(count, k)) for k in range(1, count)
-    ]
 
 
 def gather_ring(piece, count):
@@ -279,7 +275,6 @@
 
 
 def slide_backward(
-    here,
     owner,
     logits_ref,
     pair_ref,
@@ -299,9 +294,10 @@
     grad_ref,
     up_ref,
     grads_ref,
+    out_ref,
     *rest,
 ):
-    outs, fetched, sems = rest[:-8], rest[-8:-1], rest[-1]
+    fetched, sems = rest[:-1], rest[-1]
     (
         out_weights_ref,
         heads_ref,
@@ -388,17 +384,16 @@
     grad_value = grads_ref[2 * inner : 3 * inner, :]
     for copy in copies[3:]:
         copy.wait()
-    count = len(outs)
+    count = out_ref.shape[0]
     block = norm_ref.shape[0] // count
     first = jnp.zeros_like(valid)
     second = jnp.zeros_like(valid)
     for k in range(count):
-        start = pl.multiple_of(lax.rem(here[0] + k, count) * block, 16)
-        rows = pl.ds(start, block)
+        rows = slice(k * block, (k + 1) * block)
         part = jnp.dot(query_weights_ref[rows, :], grad_query, preferred_element_type=f32)
         part = part + jnp.dot(key_weights_ref[rows, :], grad_key, preferred_element_type=f32)
         part = part + jnp.dot(value_weights_ref[rows, :], grad_value, preferred_element_type=f32)
-        outs[k][0:block, :] = part.astype(bf16)
+        out_ref[k, 0:block, :] = part.astype(bf16)
         first = first + jnp.sum(part, 0, keepdims=True)
         second = second + jnp.sum(part * norm_ref[rows, :].astype(f32), 0, keepdims=True)
     width = norm_ref.shape[0]
@@ -408,29 +403,52 @@
         [high, stats - high, jnp.zeros((EXTRA - 4, stats.shape[1]), f32)], 0
     ).astype(bf16)
     for k in range(count):
-        outs[k][block : block + EXTRA, :] = stats
-
-
-def wide_grads(which, norm_ref, grads_ref, *rest):
-    got, out_ref = rest[:-1], rest[-1]
+        out_ref[k, block : block + EXTRA, :] = stats
+
+
+def wide_other(which, norm_ref, grads_ref, out_ref):
     chips, share, columns = out_ref.shape
     rows = [
         norm_ref[pl.ds(pl.multiple_of((CORES * chip + which[0]) * share, 16), share), :]
         for chip in range(chips)
     ]
+    values = contract(jnp.concatenate(rows, 0), grads_ref[0:columns, :], 1, 1).astype(bf16)
+    for chip in range(chips):
+        out_ref[chip] = values[chip * share : (chip + 1) * share]
+
+
+def wide_own(which, column, norm_ref, grads_ref, got_ref, *outs):
+    side = len(outs)
+    lines, share, columns = outs[0].shape
+    chips = [
+        line * side + lax.rem(column[0] + k, side) for k in range(side) for line in range(lines)
+    ]
+    rows = [
+        norm_ref[pl.ds(pl.multiple_of((CORES * chip + which[0]) * share, 16), share), :]
+        for chip in chips
+    ]
     values = contract(jnp.concatenate(rows, 0), grads_ref[0:columns, :], 1, 1)
-    for chip in range(chips):
-        part = values[chip * share : (chip + 1) * share]
-        if got:
-            part = part + got[0][chip].astype(f32)
-        out_ref[chip] = part.astype(bf16)
-
-
-def slot_grads(own_ref, valid_ref, stat_ref, chunk_ref, select_ref, extra_ref, *rest):
-    refs, out_ref = rest[:-1], rest[-1]
-    total = refs[0][...].astype(f32)
-    for ref in refs[1:]:
-        total = total + ref[...].astype(f32)
+    for index, chip in enumerate(chips):
+        part = values[index * share : (index + 1) * share] + got_ref[chip].astype(f32)
+        outs[index // lines][index % lines] = part.astype(bf16)
+
+
+def wide_line(line, *refs):
+    side = len(refs) // 2
+    for k in range(side):
+        row = lax.rem(line[0] + k, side)
+        total = refs[0][row].astype(f32)
+        for ref in refs[1:side]:
+            total = total + ref[row].astype(f32)
+        refs[side + k][...] = total.astype(bf16)
+
+
+def slot_grads(
+    own_ref, valid_ref, stat_ref, chunk_ref, select_ref, extra_ref, parts_ref, out_ref
+):
+    total = parts_ref[0].astype(f32)
+    for j in range(1, parts_ref.shape[0]):
+        total = total + parts_ref[j].astype(f32)
     block = chunk_ref.shape[0] - EXTRA
     first = total[block : block + 1] + total[block + 2 : block + 3]
     second = total[block + 1 : block + 2] + total[block + 3 : block + 4]
@@ -550,7 +568,7 @@
             (w_two.shape, bf16),
             3,
         ],
-        limit=24,
+        limit=62,
     )
     partial = exchange(partial, "mp")
 
@@ -629,7 +647,7 @@
             ((heads, length, length), f32),
             1 + 2 * heads,
         ],
-        limit=28,
+        limit=60,
     )
     pooled = exchange(pooled, "mp")
     unit, report_unit, row = call(
@@ -639,10 +657,10 @@
         all_reports,
     )
     logits = exchange(row, DP).reshape(owners, 128)
-    loss, grad, up, grads, *pieces = call(
+    loss, grad, up, grads, sending = call(
         slide_backward,
         [((1, 1), f32), ((1, width), f32), ((1, inner), f32), ((3 * inner, length), bf16)]
-        + [((block + EXTRA, length), bf16)] * parts,
+        + [((parts, block + EXTRA, length), bf16)],
         logits,
         slide_pair[:, None],
         unit,
@@ -657,7 +675,7 @@
         w_key,
         w_value,
         slide_norm,
-        scalars=(here, owner),
+        scalars=(owner,),
         far=tuple(range(7, 14)),
         scratch=[
             (w_out.shape, bf16),
@@ -669,24 +687,43 @@
             (slide_norm.shape, bf16),
             7,
         ],
-        limit=28,
-    )
-    pieces = scatter_ring(pieces, parts)
-
-    wide = (chips, share, 2 * inner)
+        limit=60,
+    )
+    received = exchange(sending, "mp")
+
+    lines = math.isqrt(chips)
+    side = chips // lines
+    chip = lax.axis_index("chip")
     (wide_sent,) = call(
-        wide_grads,
-        [(wide, bf16)],
+        wide_other,
+        [((chips, share, 2 * inner), bf16)],
         slide_norm,
         grads,
         scalars=(1 - core,),
-        anchors=(pieces[1],),
     )
     wide_got = lax.ppermute(wide_sent, "core", [(0, 1), (1, 0)])
-    (wide_both,) = call(
-        wide_grads, [(wide, bf16)], slide_norm, grads, wide_got, scalars=(core,)
-    )
-    grad_wide = jnp.sum(exchange(wide_both, "chip").astype(f32), 0)
+    along = call(
+        wide_own,
+        [((lines, share, 2 * inner), bf16)] * side,
+        slide_norm,
+        grads,
+        wide_got,
+        scalars=(core, chip % side),
+    )
+    along = [along[0]] + [
+        lax.ppermute(
+            along[k], "chip", [(c, c // side * side + (c + k) % side) for c in range(chips)]
+        )
+        for k in range(1, side)
+    ]
+    across = call(
+        wide_line, [((share, 2 * inner), bf16)] * lines, *along, scalars=(chip // side,)
+    )
+    across = [across[0]] + [
+        lax.ppermute(across[k], "chip", [(c, (c + k * side) % chips) for c in range(chips)])
+        for k in range(1, lines)
+    ]
+    grad_wide = sum(part.astype(f32) for part in across)
     value_rows = contract(mass.astype(bf16), slide_norm, 1, 1)
     extra = jnp.concatenate(
         [
@@ -712,8 +749,7 @@
         chunk,
         select,
         extra,
-        *pieces,
-        anchors=(grad_wide,),
+        received,
     )
     back = exchange(going.reshape(owners, ROWS, block), DP).reshape(slots, block)
     (spreading,) = call(tile_grads, [((parts,) + packed, bf16)], back, dispatch)
@@ -728,6 +764,7 @@
         hidden,
         exchange(spreading, "mp"),
         scalars=(1 - core,),
+        anchors=(grad_wide,),
         limit=24,
     )
     got = lax.ppermute(sent, "core", [(0, 1), (1, 0)])
@@ -741,7 +778,7 @@
         got,
         scalars=(core,),
         scratch=[(size, bf16), chips],
-        limit=24,
+        limit=60,
     )
     grad_one, grad_two = call(
         last_sums, [((share, units), f32), ((share, units), f32)], exchange(both, "chip")

time: 282 us -> 266 us (0.943)
  blocking collectives: 66.9 us -> 40.8 us
  waiting for transfers between devices: 95.5 us -> 106 us
  Pallas kernels: 28.3 us -> 31.6 us
  local copies, waits for them, and re-layouts: 34 us -> 30.8 us
    all_to_all x4 -> x5, waiting for transfers between devices: 45.8 us -> 75.7 us  [exchange(): return lax.all_to_all(values, axis, 0, 0, tiled=True)]
    all_to_all x4 -> x3, blocking collectives: 66.9 us -> 40.8 us  [exchange(): return lax.all_to_all(values, axis, 0, 0, tiled=True)]
    ppermute x7 -> x6, waiting for transfers between devices: 29.8 us -> 10.3 us  [the longest x3 7.48 us: per_device(): lax.ppermute(along[k], 'chip', [(c, c // side * side + (c + k) % side) fo...]
    unnamed x86 -> x104, local copies, waits for them, and re-layouts: 26.5 us -> 19.5 us
    pallas_call x13 -> x14, Pallas kernels: 28.3 us -> 31.6 us  [call(): pl.pallas_call(kernel if skip else body, out_shape=[jax.ShapeDtypeStruct(...]
    ppermute x7 -> x6, starting transfers between devices: 10.3 us -> 7.95 us  [the longest x3 4.1 us: per_device(): lax.ppermute(across[k], 'chip', [(c, (c + k * side) % chips) for c in ran...]
    all_to_all x4 -> x5, starting transfers between devices: 25.7 us -> 28 us  [exchange(): return lax.all_to_all(values, axis, 0, 0, tiled=True)]
  transfers between devices with their start and end apart: 21 -> 21, of which waited for: 15 -> 14; matrix products, arithmetic and copies ran while one was open for 7% -> 7% of each run, Pallas kernels for 0% -> 1%
where the time goes in v2:
time: 266 us; the launch traced here: 263 us
  waiting for transfers between devices  106 us (40%)
  starting transfers between devices  49.8 us (19%)
  blocking collectives  40.8 us (15%)
  Pallas kernels  31.6 us (12%)
  local copies, waits for them, and re-layouts  30.8 us (12%)
    all_to_all x5, waiting for transfers between devices, exchange(): return lax.all_to_all(values, axis, 0, 0, tiled=True)  75.7 us
    all_to_all x3, blocking collectives, exchange(): return lax.all_to_all(values, axis, 0, 0, tiled=True)  40.8 us
    pallas_call x14, Pallas kernels, call(): pl.pallas_call(kernel if skip else body, out_shape=[jax.ShapeDtypeStruct(...  31.6 us
    all_to_all x5, starting transfers between devices, exchange(): return lax.all_to_all(values, axis, 0, 0, tiled=True)  28 us
    unnamed x104, local copies, waits for them, and re-layouts  19.5 us
    ppermute x3, waiting for transfers between devices, gather_ring(): back = lax.ppermute(back, 'mp', turn(count, 1))  11.5 us
    ppermute x3, starting transfers between devices, gather_ring(): ahead = lax.ppermute(ahead, 'mp', turn(count, count - 1))  9.12 us
    ppermute x3, waiting for transfers between devices, per_device(): lax.ppermute(along[k], 'chip', [(c, c // side * side + (c + k) % side) fo...  7.48 us
  transfers between devices with their start and end apart: 21, of which 14 were waited for; matrix products, arithmetic and copies ran while one was open for 7% of the time, Pallas kernels for 1%

profile of v2, /device:TPU:8, one launch (start us, length us, event | category | flops | bytes accessed | tf_op | source)
XLA Modules:
  0.0 263.2 jit_solution(16963810808048310807)
XLA Ops:
  0.6 4.5 %shard_map.153 = (bf16[192,1536]{1,0:T(8,128)(2,1)}, bf16[192,768]{1,0:T(8,128)(2,1)}, f32[192,768]{1,0:T(8,128)}, bf16[8,288,128]{2,1,0:T(8,128)(2,1)}) custom-call(bf16[192,1536]{1,0:T(8,128)(2,1)} %far_x.1, bf16[1536,768]{1,0:T(8,128)(2,1)} %far_one.1, bf16[768,1536]{1,0:T(8,128)(2,1)} %refs_2_.1), custom_call_target="tpu_custom_call" | custom-call | tf_op jit(solution)/shard_map/pallas_call | solution.py:49
  5.2 8.6 %all-to-all-start = ((bf16[8,288,128]{2,1,0:T(8,128)(2,1)}), bf16[8,288,128]{2,1,0:T(8,128)(2,1)S(1)}, u32[]{:S(2)}, u32[]{:S(2)}) async-start(bf16[8,288,128]{2,1,0:T(8,128)(2,1)} %get-tuple-element.45), calls=%async_computation | async-start | bytes 1179648 | tf_op jit(solution)/shard_map/all_to_all | solution.py:33
  14.4 2.2 copy.42
  18.8 1.2 constant_dynamic-slice_fusion.3
  20.3 12.4 %all-to-all-done.refs_9_ = bf16[8,288,128]{2,1,0:T(8,128)(2,1)S(1)} async-done(((bf16[8,288,128]{2,1,0:T(8,128)(2,1)}), bf16[8,288,128]{2,1,0:T(8,128)(2,1)S(1)}, u32[]{:S(2)}, u32[]{:S(2)}) %all-to-all-start) | async-done | bytes 589856 | tf_op jit(solution)/shard_map/all_to_all | solution.py:33
  33.0 14.8 %all_to_all.40 = bf16[32,16,256]{2,1,0:T(8,128)(2,1)S(1)} all-to-all(bf16[32,16,256]{2,1,0:T(8,128)(2,1)S(1)} %bitcast.56), channel_id=1, replica_groups=mesh['chip'=16,'core'=2,'mp'=8] {'chip','core'}, dimensions={0} | all-to-all | bytes 524288 | tf_op jit(solution)/shard_map/all_to_all | solution.py:33
  48.8 2.7 %collective-permute-start.1 = (bf16[208,384]{1,0:T(8,128)(2,1)S(1)}, bf16[208,384]{1,0:T(8,128)(2,1)S(1)}, u32[]{:S(2)}, u32[]{:S(2)}) collective-permute-start(bf16[208,384]{1,0:T(8,128)(2,1)S(1)} %get-tuple-element.47.rest_0_.chunk_ref), channel_id=1, source_target_pairs={{0,7},{1,0},{2,1},{3,2},{4,3},{5,4},{6,5},{7,6},{8,15},{9,8},{10,9... | collective-permute-start | bytes 479240 | tf_op jit(solution)/shard_map/ppermute | solution.py:83
  51.5 4.5 %collective-permute-done.rest_1_ = bf16[208,384]{1,0:T(8,128)(2,1)S(1)} collective-permute-done((bf16[208,384]{1,0:T(8,128)(2,1)S(1)}, bf16[208,384]{1,0:T(8,128)(2,1)S(1)}, u32[]{:S(2)}, u32[]{:S(2)}) %collective-permute-start) | collective-permute-done | bytes 159776 | tf_op jit(solution)/shard_map/ppermute | solution.py:82
  56.0 3.2 %collective-permute-start.3 = (bf16[208,384]{1,0:T(8,128)(2,1)S(1)}, bf16[208,384]{1,0:T(8,128)(2,1)S(1)}, u32[]{:S(2)}, u32[]{:S(2)}) collective-permute-start(bf16[208,384]{1,0:T(8,128)(2,1)S(1)} %collective-permute-done.1.rest_2_), channel_id=1, source_target_pairs={{0,7},{1,0},{2,1},{3,2},{4,3},{5,4},{6,5},{7,6},{8,15},{9,8},{10,9... | collective-permute-start | bytes 479240 | tf_op jit(solution)/shard_map/ppermute | solution.py:83
  59.3 3.7 %collective-permute-done.2.rest_3_ = bf16[208,384]{1,0:T(8,128)(2,1)S(1)} collective-permute-done((bf16[208,384]{1,0:T(8,128)(2,1)S(1)}, bf16[208,384]{1,0:T(8,128)(2,1)S(1)}, u32[]{:S(2)}, u32[]{:S(2)}) %collective-permute-start.2) | collective-permute-done | bytes 159776 | tf_op jit(solution)/shard_map/ppermute | solution.py:82
  63.0 3.2 %collective-permute-start.5 = (bf16[208,384]{1,0:T(8,128)(2,1)S(1)}, bf16[208,384]{1,0:T(8,128)(2,1)S(1)}, u32[]{:S(2)}, u32[]{:S(2)}) collective-permute-start(bf16[208,384]{1,0:T(8,128)(2,1)S(1)} %collective-permute-done.3.rest_4_), channel_id=1, source_target_pairs={{0,7},{1,0},{2,1},{3,2},{4,3},{5,4},{6,5},{7,6},{8,15},{9,8},{10,9... | collective-permute-start | bytes 479240 | tf_op jit(solution)/shard_map/ppermute | solution.py:83
  66.3 3.2 %collective-permute-done.4.rest_5_ = bf16[208,384]{1,0:T(8,128)(2,1)S(1)} collective-permute-done((bf16[208,384]{1,0:T(8,128)(2,1)S(1)}, bf16[208,384]{1,0:T(8,128)(2,1)S(1)}, u32[]{:S(2)}, u32[]{:S(2)}) %collective-permute-start.4) | collective-permute-done | bytes 159776 | tf_op jit(solution)/shard_map/ppermute | solution.py:82
  69.7 3.5 %collective-permute-start.7 = (bf16[96,384]{1,0:T(8,128)(2,1)S(1)}, bf16[96,384]{1,0:T(8,128)(2,1)S(1)}, u32[]{:S(2)}, u32[]{:S(2)}) collective-permute-start(bf16[96,384]{1,0:T(8,128)(2,1)S(1)} %slice.51), channel_id=1, source_target_pairs={{0,7},{1,0},{2,1},{3,2},{4,3},{5,4},{6,5},{7,6},{8,15},{9,8},{10,9... | collective-permute-start | bytes 221192 | tf_op jit(solution)/shard_map/ppermute | solution.py:87
  73.1 2.0 collective-permute-done.7.rest_8_
  75.9 7.1 %shard_map.156 = (bf16[1536,384]{1,0:T(8,128)(2,1)}, f32[2,3,96,384]{3,2,1,0:T(8,128)}, f32[2,384,384]{2,1,0:T(8,128)}, f32[2,384]{1,0:T(2,128)}, f32[2,2,384]{2...) custom-call(s32[1]{0:T(128)} %bitcast.1.here, ...), custom_call_target="tpu_custom_call" | custom-call | tf_op jit(solution)/shard_map/pallas_call | solution.py:49
  83.0 12.9 %all_to_all.41.parts_ref = f32[8,1,1536]{2,1,0:T(1,128)S(1)} all-to-all(f32[8,1,1536]{2,1,0:T(1,128)} %get-tuple-element.48), channel_id=1, replica_groups=mesh['chip'=16,'core'=2,'mp'=8] {'mp'}, dimensions={0} | all-to-all | bytes 98304 | tf_op jit(solution)/shard_map/all_to_all | solution.py:33
  96.8 1.0 shard_map.157
  99.1 4.9 %all-to-all-start.3 = ((f32[32,1,128]{2,1,0:T(1,128)}), f32[32,1,128]{2,1,0:T(1,128)S(1)}, u32[]{:S(2)}, u32[]{:S(2)}) async-start(f32[32,1,128]{2,1,0:T(1,128)} %get-tuple-element.50), calls=%async_computation.3 | async-start | bytes 32768 | tf_op jit(solution)/shard_map/all_to_all | solution.py:33
  104.0 1.2 copy.49.far_query_weights
  105.2 1.2 copy.50.far_key_weights
  106.3 1.2 copy.51.far_value_weights
  108.3 1.8 all-to-all-done.3
  110.7 6.3 %shard_map.158 = (f32[1,1]{1,0:T(1,128)}, f32[1,1536]{1,0:T(1,128)}, f32[1,192]{1,0:T(1,128)}, bf16[576,384]{1,0:T(8,128)(2,1)}, bf16[8,208,384]{2,1,0:T(8,128)(2,1)}) custom-call(s32[1]{0:T(128)} %bitcast.owner, f32[32,128]{1,0:T(8,128)} %bitcast.66, s32[32,1]{1,0:T(8,128)} %copy.48.pair_ref, f32[2,1536]{1,0:T(2,128)} %copy-done.26, f32[32,1536]{1,0:T(8,128)} %copy-done.20, ...), custom_call_target="tpu_custom_call" | custom-call | tf_op jit(solution)/shard_map/pallas_call | solution.py:49
  117.0 3.7 %all-to-all-start.4 = ((bf16[8,208,384]{2,1,0:T(8,128)(2,1)}), bf16[8,208,384]{2,1,0:T(8,128)(2,1)S(1)}, u32[]{:S(2)}, u32[]{:S(2)}) async-start(bf16[8,208,384]{2,1,0:T(8,128)(2,1)} %get-tuple-element.73), calls=%async_computation.4 | async-start | bytes 2555904 | tf_op jit(solution)/shard_map/all_to_all | solution.py:33
  124.4 30.3 %all-to-all-done.4.parts_ref = bf16[8,208,384]{2,1,0:T(8,128)(2,1)S(1)} async-done(((bf16[8,208,384]{2,1,0:T(8,128)(2,1)}), bf16[8,208,384]{2,1,0:T(8,128)(2,1)S(1)}, u32[]{:S(2)}, u32[]{:S(2)}) %all-to-all-start.4) | async-done | bytes 1277984 | tf_op jit(solution)/shard_map/all_to_all | solution.py:33
  156.1 13.1 %all_to_all.42 = bf16[32,16,192]{2,1,0:T(8,128)(2,1)S(1)} all-to-all(bf16[32,16,192]{2,1,0:T(8,128)(2,1)S(1)} %bitcast.59), channel_id=1, replica_groups=mesh['chip'=16,'core'=2,'mp'=8] {'chip','core'}, dimensions={0} | all-to-all | bytes 393216 | tf_op jit(solution)/shard_map/all_to_all | solution.py:33
  169.2 1.1 shard_map.163
  171.0 4.2 %all-to-all-start.6 = ((bf16[8,288,128]{2,1,0:T(8,128)(2,1)}), bf16[8,288,128]{2,1,0:T(8,128)(2,1)}, u32[]{:S(2)}, u32[]{:S(2)}) async-start(bf16[8,288,128]{2,1,0:T(8,128)(2,1)} %shard_map.163), calls=%async_computation.6 | async-start | bytes 1179648 | tf_op jit(solution)/shard_map/all_to_all | solution.py:33
  176.4 1.6 collective-permute-done.8.got_ref
  178.9 1.0 copy-done.8
  179.9 1.1 copy-done.17
  180.9 1.3 shard_map.160
  183.6 2.1 collective-permute-start.10
  185.8 1.0 collective-permute-start.11
  186.7 6.9 %collective-permute-done.9.refs_1_ = bf16[4,48,384]{2,1,0:T(8,128)(2,1)S(1)} collective-permute-done((bf16[4,48,384]{2,1,0:T(8,128)(2,1)}, bf16[4,48,384]{2,1,0:T(8,128)(2,1)S(1)}, u32[]{:S(2)}, u32[]{:S(2)}) %collective-permute-start.9) | collective-permute-done | bytes 147488 | tf_op jit(solution)/shard_map/ppermute | solution.py:714
  195.2 1.5 collective-permute-start.14
  197.5 1.8 collective-permute-start.12
  199.3 2.8 %collective-permute-done.13 = bf16[48,384]{1,0:T(8,128)(2,1)S(1)} collective-permute-done((bf16[48,384]{1,0:T(8,128)(2,1)S(1)}, bf16[48,384]{1,0:T(8,128)(2,1)S(1)}, u32[]{:S(2)}, u32[]{:S(2)}) %collective-permute-start.13) | collective-permute-done | bytes 36896 | tf_op jit(solution)/shard_map/ppermute | solution.py:723
  202.2 1.1 copy-done.3
  203.3 1.0 copy-done.5
  204.3 1.0 copy-done.10
  205.3 3.2 %shard_map.164 = (bf16[1536,192]{1,0:T(8,128)(2,1)S(1)}, bf16[768,192]{1,0:T(8,128)(2,1)S(1)}, bf16[16,96,768]{2,1,0:T(8,128)(2,1)S(1)}) custom-call(f32[48,384]{1,0:T(8,128)S(1)} %convert_add_fusion.refs_0_, s32[1]{0:T(128)} %bitcast.22.which.refs_1_, bf16[768,1536]{1,0:T(8,128)(2,1)S(1)} %copy-done.1, f32[768,192]{1,0:T(8,128)S(1)} %bitcast.50, ...), custom_call_target="tpu_custom_call" | custom-call | tf_op jit(solution)/shard_map/pallas_call | solution.py:49
  210.1 4.5 %collective-permute-done.15.got_ref = bf16[16,96,768]{2,1,0:T(8,128)(2,1)S(1)} collective-permute-done((bf16[16,96,768]{2,1,0:T(8,128)(2,1)S(1)}, bf16[16,96,768]{2,1,0:T(8,128)(2,1)S(1)}, u32[]{:S(2)}, u32[]{:S(2)}) %collective-permute-start.15) | collective-permute-done | bytes 2359328 | tf_op jit(solution)/shard_map/ppermute | solution.py:770
  214.7 1.5 copy-done.28
  216.1 4.4 %shard_map.165 = bf16[16,96,768]{2,1,0:T(8,128)(2,1)} custom-call(s32[1]{0:T(128)} %bitcast.19.which.own, bf16[768,192]{1,0:T(8,128)(2,1)} %bitcast.54, bf16[192,768]{1,0:T(8,128)(2,1)} %get-tuple-element.59.refs_5_.hidden_ref, bf16[1536,192]{1,0:T(8,128)(2,1)} %copy-done.13, bf16[768,192]{1,0:T(8,128)(2,1)} %copy-done.19, bf16[16,96,768]{2,1,0:T(8,128)(2,1)} %copy-done.28), custom_call_target="tpu_custom_call" | custom-call | tf_op jit(solution)/shard_map/pallas_call | solution.py:49
  220.5 6.6 %all-to-all-start.7 = ((bf16[16,96,768]{2,1,0:T(8,128)(2,1)}), bf16[16,96,768]{2,1,0:T(8,128)(2,1)S(1)}, u32[]{:S(2)}, u32[]{:S(2)}) async-start(bf16[16,96,768]{2,1,0:T(8,128)(2,1)} %shard_map.165), calls=%async_computation.7 | async-start | bytes 4718592 | tf_op jit(solution)/shard_map/all_to_all | solution.py:33
  230.9 31.3 %all-to-all-done.7.values_ref = bf16[16,96,768]{2,1,0:T(8,128)(2,1)S(1)} async-done(((bf16[16,96,768]{2,1,0:T(8,128)(2,1)}), bf16[16,96,768]{2,1,0:T(8,128)(2,1)S(1)}, u32[]{:S(2)}, u32[]{:S(2)}) %all-to-all-start.7) | async-done | bytes 2359328 | tf_op jit(solution)/shard_map/all_to_all | solution.py:33
  262.2 1.0 shard_map.166
  (171 shorter events, 25.7 us)
Async XLA Ops:
  5.2 8.6 %copy-start.32 = (bf16[192,1536]{1,0:T(8,128)(2,1)S(1)}, bf16[192,1536]{1,0:T(8,128)(2,1)}, u32[]{:S(2)}) copy-start(bf16[192,1536]{1,0:T(8,128)(2,1)} %far_x.1) | copy-start | bytes 1769476
  5.2 27.5 %all-to-all-start = ((bf16[8,288,128]{2,1,0:T(8,128)(2,1)}), bf16[8,288,128]{2,1,0:T(8,128)(2,1)S(1)}, u32[]{:S(2)}, u32[]{:S(2)}) async-start(bf16[8,288,128]{2,1,0:T(8,128)(2,1)} %get-tuple-element.45), calls=%async_computation | async-start | bytes 1179648 | tf_op jit(solution)/shard_map/all_to_all | solution.py:33
  13.8 2.9 %copy-start.33 = (f32[192,768]{1,0:T(8,128)S(1)}, f32[192,768]{1,0:T(8,128)}, u32[]{:S(2)}) copy-start(f32[192,768]{1,0:T(8,128)} %get-tuple-element.44) | copy-start | bytes 1769476
  16.9 15.7 %copy-start.2 = (f32[192,768]{0,1:T(8,128)}, f32[192,768]{0,1:T(8,128)S(1)}, u32[]{:S(2)}) copy-start(f32[192,768]{0,1:T(8,128)S(1)} %copy.43) | copy-start | bytes 1769476
  20.0 13.0 %copy-start.4 = (bf16[16,1,48,192]{3,2,1,0:T(8,128)(2,1)}, bf16[16,1,48,192]{3,2,1,0:T(8,128)(2,1)S(1)}, u32[]{:S(2)}) copy-start(bf16[16,1,48,192]{3,2,1,0:T(8,128)(2,1)S(1)} %get-tuple-element.79) | copy-start | bytes 884740
  20.0 13.0 %copy-start.6 = (bf16[16,1,48,192]{3,2,1,0:T(8,128)(2,1)}, bf16[16,1,48,192]{3,2,1,0:T(8,128)(2,1)S(1)}, u32[]{:S(2)}) copy-start(bf16[16,1,48,192]{3,2,1,0:T(8,128)(2,1)S(1)} %get-tuple-element.80) | copy-start | bytes 884740
  48.2 27.1 %copy-start.14 = (bf16[208,384]{1,0:T(8,128)(2,1)}, bf16[208,384]{1,0:T(8,128)(2,1)S(1)}, u32[]{:S(2)}) copy-start(bf16[208,384]{1,0:T(8,128)(2,1)S(1)} %get-tuple-element.47.rest_0_.chunk_ref) | copy-start | bytes 479236
  48.2 27.1 %copy-start.24 = (f32[1,384]{1,0:T(1,128)}, f32[1,384]{1,0:T(1,128)S(1)}, u32[]{:S(2)}) copy-start(f32[1,384]{1,0:T(1,128)S(1)} %get-tuple-element.46.valid_ref) | copy-start | bytes 4612
  48.2 7.8 %collective-permute-start = (bf16[208,384]{1,0:T(8,128)(2,1)S(1)}, bf16[208,384]{1,0:T(8,128)(2,1)S(1)}, u32[]{:S(2)}, u32[]{:S(2)}) collective-permute-start(bf16[208,384]{1,0:T(8,128)(2,1)S(1)} %get-tuple-element.47.rest_0_.chunk_ref), channel_id=1, source_target_pairs={{0,1},{1,2},{2,3},{3,4},{4,5},{5,6},{6,7},{7,0},{8,9},{9,10},{10,1... | collective-permute-start | bytes 479240 | tf_op jit(solution)/shard_map/ppermute | solution.py:82
  48.8 7.2 %collective-permute-start.1 = (bf16[208,384]{1,0:T(8,128)(2,1)S(1)}, bf16[208,384]{1,0:T(8,128)(2,1)S(1)}, u32[]{:S(2)}, u32[]{:S(2)}) collective-permute-start(bf16[208,384]{1,0:T(8,128)(2,1)S(1)} %get-tuple-element.47.rest_0_.chunk_ref), channel_id=1, source_target_pairs={{0,7},{1,0},{2,1},{3,2},{4,3},{5,4},{6,5},{7,6},{8,15},{9,8},{10,9... | collective-permute-start | bytes 479240 | tf_op jit(solution)/shard_map/ppermute | solution.py:83
  56.0 19.3 %copy-start.36 = (bf16[208,384]{1,0:T(8,128)(2,1)}, bf16[208,384]{1,0:T(8,128)(2,1)S(1)}, u32[]{:S(2)}) copy-start(bf16[208,384]{1,0:T(8,128)(2,1)S(1)} %collective-permute-done.rest_1_) | copy-start | bytes 479236
  56.0 7.0 %collective-permute-start.2 = (bf16[208,384]{1,0:T(8,128)(2,1)S(1)}, bf16[208,384]{1,0:T(8,128)(2,1)S(1)}, u32[]{:S(2)}, u32[]{:S(2)}) collective-permute-start(bf16[208,384]{1,0:T(8,128)(2,1)S(1)} %collective-permute-done.rest_1_), channel_id=1, source_target_pairs={{0,1},{1,2},{2,3},{3,4},{4,5},{5,6},{6,7},{7,0},{8,9},{9,10},{10,1... | collective-permute-start | bytes 479240 | tf_op jit(solution)/shard_map/ppermute | solution.py:82
  56.0 19.3 %copy-start.37 = (bf16[208,384]{1,0:T(8,128)(2,1)}, bf16[208,384]{1,0:T(8,128)(2,1)S(1)}, u32[]{:S(2)}) copy-start(bf16[208,384]{1,0:T(8,128)(2,1)S(1)} %collective-permute-done.1.rest_2_) | copy-start | bytes 479236
  56.0 7.0 %collective-permute-start.3 = (bf16[208,384]{1,0:T(8,128)(2,1)S(1)}, bf16[208,384]{1,0:T(8,128)(2,1)S(1)}, u32[]{:S(2)}, u32[]{:S(2)}) collective-permute-start(bf16[208,384]{1,0:T(8,128)(2,1)S(1)} %collective-permute-done.1.rest_2_), channel_id=1, source_target_pairs={{0,7},{1,0},{2,1},{3,2},{4,3},{5,4},{6,5},{7,6},{8,15},{9,8},{10,9... | collective-permute-start | bytes 479240 | tf_op jit(solution)/shard_map/ppermute | solution.py:83
  63.0 12.3 %copy-start.38 = (bf16[208,384]{1,0:T(8,128)(2,1)}, bf16[208,384]{1,0:T(8,128)(2,1)S(1)}, u32[]{:S(2)}) copy-start(bf16[208,384]{1,0:T(8,128)(2,1)S(1)} %collective-permute-done.2.rest_3_) | copy-start | bytes 479236
  63.0 6.5 %collective-permute-start.4 = (bf16[208,384]{1,0:T(8,128)(2,1)S(1)}, bf16[208,384]{1,0:T(8,128)(2,1)S(1)}, u32[]{:S(2)}, u32[]{:S(2)}) collective-permute-start(bf16[208,384]{1,0:T(8,128)(2,1)S(1)} %collective-permute-done.2.rest_3_), channel_id=1, source_target_pairs={{0,1},{1,2},{2,3},{3,4},{4,5},{5,6},{6,7},{7,0},{8,9},{9,10},{10,1... | collective-permute-start | bytes 479240 | tf_op jit(solution)/shard_map/ppermute | solution.py:82
  63.0 12.3 %copy-start.39 = (bf16[208,384]{1,0:T(8,128)(2,1)}, bf16[208,384]{1,0:T(8,128)(2,1)S(1)}, u32[]{:S(2)}) copy-start(bf16[208,384]{1,0:T(8,128)(2,1)S(1)} %collective-permute-done.3.rest_4_) | copy-start | bytes 479236
  63.0 6.6 %collective-permute-start.5 = (bf16[208,384]{1,0:T(8,128)(2,1)S(1)}, bf16[208,384]{1,0:T(8,128)(2,1)S(1)}, u32[]{:S(2)}, u32[]{:S(2)}) collective-permute-start(bf16[208,384]{1,0:T(8,128)(2,1)S(1)} %collective-permute-done.3.rest_4_), channel_id=1, source_target_pairs={{0,7},{1,0},{2,1},{3,2},{4,3},{5,4},{6,5},{7,6},{8,15},{9,8},{10,9... | collective-permute-start | bytes 479240 | tf_op jit(solution)/shard_map/ppermute | solution.py:83
  69.5 5.8 %copy-start.34 = (bf16[208,384]{1,0:T(8,128)(2,1)}, bf16[208,384]{1,0:T(8,128)(2,1)S(1)}, u32[]{:S(2)}) copy-start(bf16[208,384]{1,0:T(8,128)(2,1)S(1)} %collective-permute-done.4.rest_5_) | copy-start | bytes 479236
  69.5 5.8 %collective-permute-start.6 = (bf16[112,384]{1,0:T(8,128)(2,1)S(1)}, bf16[112,384]{1,0:T(8,128)(2,1)S(1)}, u32[]{:S(2)}, u32[]{:S(2)}) collective-permute-start(bf16[112,384]{1,0:T(8,128)(2,1)S(1)} %slice.50), channel_id=1, source_target_pairs={{0,1},{1,2},{2,3},{3,4},{4,5},{5,6},{6,7},{7,0},{8,9},{9,10},{10,1... | collective-permute-start | bytes 258056 | tf_op jit(solution)/shard_map/ppermute | solution.py:86
  69.6 5.7 %copy-start.35 = (bf16[208,384]{1,0:T(8,128)(2,1)}, bf16[208,384]{1,0:T(8,128)(2,1)S(1)}, u32[]{:S(2)}) copy-start(bf16[208,384]{1,0:T(8,128)(2,1)S(1)} %collective-permute-done.5.rest_6_) | copy-start | bytes 479236
  69.7 5.4 %collective-permute-start.7 = (bf16[96,384]{1,0:T(8,128)(2,1)S(1)}, bf16[96,384]{1,0:T(8,128)(2,1)S(1)}, u32[]{:S(2)}, u32[]{:S(2)}) collective-permute-start(bf16[96,384]{1,0:T(8,128)(2,1)S(1)} %slice.51), channel_id=1, source_target_pairs={{0,7},{1,0},{2,1},{3,2},{4,3},{5,4},{6,5},{7,6},{8,15},{9,8},{10,9... | collective-permute-start | bytes 221192 | tf_op jit(solution)/shard_map/ppermute | solution.py:87
  75.9 28.1 %copy-start.29 = (bf16[1536,192]{0,1:T(8,128)(2,1)S(1)}, bf16[1536,192]{0,1:T(8,128)(2,1)}, u32[]{:S(2)}) copy-start(bf16[1536,192]{0,1:T(8,128)(2,1)} %param.16) | copy-start | bytes 1769476
  75.9 29.2 %copy-start.30 = (bf16[1536,192]{0,1:T(8,128)(2,1)S(1)}, bf16[1536,192]{0,1:T(8,128)(2,1)}, u32[]{:S(2)}) copy-start(bf16[1536,192]{0,1:T(8,128)(2,1)} %param.17) | copy-start | bytes 1769476
  99.1 11.0 %all-to-all-start.3 = ((f32[32,1,128]{2,1,0:T(1,128)}), f32[32,1,128]{2,1,0:T(1,128)S(1)}, u32[]{:S(2)}, u32[]{:S(2)}) async-start(f32[32,1,128]{2,1,0:T(1,128)} %get-tuple-element.50), calls=%async_computation.3 | async-start | bytes 32768 | tf_op jit(solution)/shard_map/all_to_all | solution.py:33
  104.0 2.3 copy-start.31
  105.2 2.4 copy-start.47
  117.0 3.8 %copy-start = (bf16[1536,384]{1,0:T(8,128)(2,1)S(1)}, bf16[1536,384]{1,0:T(8,128)(2,1)}, u32[]{:S(2)}) copy-start(bf16[1536,384]{1,0:T(8,128)(2,1)} %get-tuple-element.57.far_norm.norm_ref) | copy-start | bytes 3538948
  117.0 3.8 %copy-start.43 = (f32[2,384]{1,0:T(2,128)S(1)}, f32[2,384]{1,0:T(2,128)}, u32[]{:S(2)}) copy-start(f32[2,384]{1,0:T(2,128)} %get-tuple-element.54.mass_ref) | copy-start | bytes 9220
  117.0 37.6 %all-to-all-start.4 = ((bf16[8,208,384]{2,1,0:T(8,128)(2,1)}), bf16[8,208,384]{2,1,0:T(8,128)(2,1)S(1)}, u32[]{:S(2)}, u32[]{:S(2)}) async-start(bf16[8,208,384]{2,1,0:T(8,128)(2,1)} %get-tuple-element.73), calls=%async_computation.4 | async-start | bytes 2555904 | tf_op jit(solution)/shard_map/all_to_all | solution.py:33
  120.8 1.8 copy-start.49
  120.8 33.9 %copy-start.15 = (bf16[208,384]{1,0:T(8,128)(2,1)S(1)}, bf16[208,384]{1,0:T(8,128)(2,1)}, u32[]{:S(2)}) copy-start(bf16[208,384]{1,0:T(8,128)(2,1)} %copy-done.14) | copy-start | bytes 479236
  120.8 33.9 %copy-start.25 = (f32[1,384]{1,0:T(1,128)S(1)}, f32[1,384]{1,0:T(1,128)}, u32[]{:S(2)}) copy-start(f32[1,384]{1,0:T(1,128)} %copy-done.24) | copy-start | bytes 4612
  120.8 33.9 %copy-start.27 = (f32[2,384]{1,0:T(2,128)S(1)}, f32[2,384]{1,0:T(2,128)}, u32[]{:S(2)}) copy-start(f32[2,384]{1,0:T(2,128)} %get-tuple-element.70.stat_ref) | copy-start | bytes 9220
  169.2 6.1 %copy-start.7 = (bf16[576,384]{1,0:T(8,128)(2,1)S(1)}, bf16[576,384]{1,0:T(8,128)(2,1)}, u32[]{:S(2)}) copy-start(bf16[576,384]{1,0:T(8,128)(2,1)} %get-tuple-element.60.grads_ref) | copy-start | bytes 1327108
  171.0 31.1 %all-to-all-start.6 = ((bf16[8,288,128]{2,1,0:T(8,128)(2,1)}), bf16[8,288,128]{2,1,0:T(8,128)(2,1)}, u32[]{:S(2)}, u32[]{:S(2)}) async-start(bf16[8,288,128]{2,1,0:T(8,128)(2,1)} %shard_map.163), calls=%async_computation.6 | async-start | bytes 1179648 | tf_op jit(solution)/shard_map/all_to_all | solution.py:33
  175.8 2.3 collective-permute-start.8
  180.9 21.2 %copy-start.1 = (bf16[768,1536]{1,0:T(8,128)(2,1)S(1)}, bf16[768,1536]{1,0:T(8,128)(2,1)}, u32[]{:S(2)}) copy-start(bf16[768,1536]{1,0:T(8,128)(2,1)} %refs_2_.1) | copy-start | bytes 7077892
  182.9 10.7 %collective-permute-start.9 = (bf16[4,48,384]{2,1,0:T(8,128)(2,1)}, bf16[4,48,384]{2,1,0:T(8,128)(2,1)S(1)}, u32[]{:S(2)}, u32[]{:S(2)}) collective-permute-start(bf16[4,48,384]{2,1,0:T(8,128)(2,1)} %get-tuple-element.62), channel_id=1, source_target_pairs={{0,16},{16,32},{32,48},{48,0},{64,80},{80,96},{96,112},{112,64},{1... | collective-permute-start | bytes 442376 | tf_op jit(solution)/shard_map/ppermute | solution.py:714
  183.6 9.9 %collective-permute-start.10 = (bf16[4,48,384]{2,1,0:T(8,128)(2,1)}, bf16[4,48,384]{2,1,0:T(8,128)(2,1)S(1)}, u32[]{:S(2)}, u32[]{:S(2)}) collective-permute-start(bf16[4,48,384]{2,1,0:T(8,128)(2,1)} %get-tuple-element.63), channel_id=1, source_target_pairs={{0,32},{16,48},{32,0},{48,16},{64,96},{80,112},{96,64},{112,80},{1... | collective-permute-start | bytes 442376 | tf_op jit(solution)/shard_map/ppermute | solution.py:714
  185.8 8.4 %collective-permute-start.11 = (bf16[4,48,384]{2,1,0:T(8,128)(2,1)}, bf16[4,48,384]{2,1,0:T(8,128)(2,1)S(1)}, u32[]{:S(2)}, u32[]{:S(2)}) collective-permute-start(bf16[4,48,384]{2,1,0:T(8,128)(2,1)} %get-tuple-element.64), channel_id=1, source_target_pairs={{0,48},{16,0},{32,16},{48,32},{64,112},{80,64},{96,80},{112,96},{1... | collective-permute-start | bytes 442376 | tf_op jit(solution)/shard_map/ppermute | solution.py:714
  195.2 4.1 %collective-permute-start.14 = (bf16[48,384]{1,0:T(8,128)(2,1)S(1)}, bf16[48,384]{1,0:T(8,128)(2,1)S(1)}, u32[]{:S(2)}, u32[]{:S(2)}) collective-permute-start(bf16[48,384]{1,0:T(8,128)(2,1)S(1)} %get-tuple-element.68), channel_id=1, source_target_pairs={{0,192},{16,208},{32,224},{48,240},{64,0},{80,16},{96,32},{112,48}... | collective-permute-start | bytes 110600 | tf_op jit(solution)/shard_map/ppermute | solution.py:723
  196.7 5.5 %collective-permute-start.13 = (bf16[48,384]{1,0:T(8,128)(2,1)S(1)}, bf16[48,384]{1,0:T(8,128)(2,1)S(1)}, u32[]{:S(2)}, u32[]{:S(2)}) collective-permute-start(bf16[48,384]{1,0:T(8,128)(2,1)S(1)} %get-tuple-element.67), channel_id=1, source_target_pairs={{0,128},{16,144},{32,160},{48,176},{64,192},{80,208},{96,224},{112... | collective-permute-start | bytes 110600 | tf_op jit(solution)/shard_map/ppermute | solution.py:723
  197.5 4.7 %collective-permute-start.12 = (bf16[48,384]{1,0:T(8,128)(2,1)S(1)}, bf16[48,384]{1,0:T(8,128)(2,1)S(1)}, u32[]{:S(2)}, u32[]{:S(2)}) collective-permute-start(bf16[48,384]{1,0:T(8,128)(2,1)S(1)} %get-tuple-element.66), channel_id=1, source_target_pairs={{0,64},{16,80},{32,96},{48,112},{64,128},{80,144},{96,160},{112,17... | collective-permute-start | bytes 110600 | tf_op jit(solution)/shard_map/ppermute | solution.py:723
  202.2 6.3 %copy-start.11 = (f32[48,384]{1,0:T(8,128)}, f32[48,384]{1,0:T(8,128)S(1)}, u32[]{:S(2)}) copy-start(f32[48,384]{1,0:T(8,128)S(1)} %convert_add_fusion.refs_0_) | copy-start | bytes 221188
  210.1 4.5 %collective-permute-start.15 = (bf16[16,96,768]{2,1,0:T(8,128)(2,1)S(1)}, bf16[16,96,768]{2,1,0:T(8,128)(2,1)S(1)}, u32[]{:S(2)}, u32[]{:S(2)}) collective-permute-start(bf16[16,96,768]{2,1,0:T(8,128)(2,1)S(1)} %get-tuple-element.76), channel_id=1, source_target_pairs={{0,8},{8,0},{1,9},{9,1},{2,10},{10,2},{3,11},{11,3},{4,12},{12,4},... | collective-permute-start | bytes 7077896 | tf_op jit(solution)/shard_map/ppermute | solution.py:770
  220.5 6.6 %copy-start.12 = (f32[48,384]{1,0:T(8,128)S(1)}, f32[48,384]{1,0:T(8,128)}, u32[]{:S(2)}) copy-start(f32[48,384]{1,0:T(8,128)} %copy-done.11) | copy-start | bytes 221188
  220.5 41.7 %all-to-all-start.7 = ((bf16[16,96,768]{2,1,0:T(8,128)(2,1)}), bf16[16,96,768]{2,1,0:T(8,128)(2,1)S(1)}, u32[]{:S(2)}, u32[]{:S(2)}) async-start(bf16[16,96,768]{2,1,0:T(8,128)(2,1)} %shard_map.165), calls=%async_computation.7 | async-start | bytes 4718592 | tf_op jit(solution)/shard_map/all_to_all | solution.py:33
  (23 other events, 19.4 us)

commit v3 on v2

--- a/solution.py
+++ b/solution.py
@@ -481,23 +481,11 @@
     both_layers(other[0], norm_ref, hidden_ref, grad_ref, hidden_grad_ref, out_ref.shape, store)
 
 
-def own_grads(
-    own, norm_ref, hidden_ref, grad_ref, hidden_grad_ref, got_ref, far_out, out_ref, sems
-):
-    copies = []
-
+def own_grads(own, norm_ref, hidden_ref, grad_ref, hidden_grad_ref, got_ref, out_ref):
     def store(rows, values):
         out_ref[rows] = (values + got_ref[rows].astype(f32)).astype(bf16)
-        chip = rows[0]
-        if rows[1].start:
-            copies.append(
-                pltpu.make_async_copy(out_ref.at[chip], far_out.at[chip], sems.at[chip])
-            )
-            copies[-1].start()
 
     both_layers(own[0], norm_ref, hidden_ref, grad_ref, hidden_grad_ref, out_ref.shape, store)
-    for copy in copies:
-        copy.wait()
 
 
 def both_layers(which, norm_ref, hidden_ref, grad_ref, hidden_grad_ref, shape, store):
@@ -750,6 +738,7 @@
         select,
         extra,
         received,
+        anchors=(across[0],),
     )
     back = exchange(going.reshape(owners, ROWS, block), DP).reshape(slots, block)
     (spreading,) = call(tile_grads, [((parts,) + packed, bf16)], back, dispatch)
@@ -764,21 +753,19 @@
         hidden,
         exchange(spreading, "mp"),
         scalars=(1 - core,),
-        anchors=(grad_wide,),
         limit=24,
     )
     got = lax.ppermute(sent, "core", [(0, 1), (1, 0)])
     (both,) = call(
         own_grads,
-        [(size, bf16, "far")],
+        [(size, bf16)],
         tile_own,
         hidden,
         grad_embedding,
         grad_hidden,
         got,
         scalars=(core,),
-        scratch=[(size, bf16), chips],
-        limit=60,
+        limit=24,
     )
     grad_one, grad_two = call(
         last_sums, [((share, units), f32), ((share, units), f32)], exchange(both, "chip")

time: 266 us -> 248 us (0.932)
  waiting for transfers between devices: 106 us -> 80 us
  blocking collectives: 40.8 us -> 64.3 us
  local copies, waits for them, and re-layouts: 30.8 us -> 21.4 us
  starting transfers between devices: 49.8 us -> 46.1 us
    all_to_all x5 -> x4, waiting for transfers between devices: 75.7 us -> 29.5 us  [exchange(): return lax.all_to_all(values, axis, 0, 0, tiled=True)]
    all_to_all x3 -> x4, blocking collectives: 40.8 us -> 64.3 us  [exchange(): return lax.all_to_all(values, axis, 0, 0, tiled=True)]
    ppermute x3, waiting for transfers between devices: 2.84 us -> 25.3 us  [per_device(): lax.ppermute(across[k], 'chip', [(c, (c + k * side) % chips) for c in ran...]
    unnamed x104 -> x92, local copies, waits for them, and re-layouts: 19.5 us -> 13.3 us
    all_to_all x5 -> x4, starting transfers between devices: 28 us -> 23 us  [exchange(): return lax.all_to_all(values, axis, 0, 0, tiled=True)]
  transfers between devices with their start and end apart: 21 -> 20, of which waited for: 14 -> 16; matrix products, arithmetic and copies ran while one was open for 7% -> 6% of each run, Pallas kernels for 1% -> 2%
where the time goes in v3:
time: 248 us; the launch traced here: 245 us
  waiting for transfers between devices  80 us (32%)
  blocking collectives  64.3 us (26%)
  starting transfers between devices  46.1 us (19%)
  Pallas kernels  29.4 us (12%)
  local copies, waits for them, and re-layouts  21.4 us (9%)
    all_to_all x4, blocking collectives, exchange(): return lax.all_to_all(values, axis, 0, 0, tiled=True)  64.3 us
    all_to_all x4, waiting for transfers between devices, exchange(): return lax.all_to_all(values, axis, 0, 0, tiled=True)  29.5 us
    pallas_call x14, Pallas kernels, call(): pl.pallas_call(kernel if skip else body, out_shape=[jax.ShapeDtypeStruct(...  29.4 us
    ppermute x3, waiting for transfers between devices, per_device(): lax.ppermute(across[k], 'chip', [(c, (c + k * side) % chips) for c in ran...  25.3 us
    all_to_all x4, starting transfers between devices, exchange(): return lax.all_to_all(values, axis, 0, 0, tiled=True)  23 us
    unnamed x92, local copies, waits for them, and re-layouts  13.3 us
    ppermute x3, waiting for transfers between devices, gather_ring(): back = lax.ppermute(back, 'mp', turn(count, 1))  11.5 us
    ppermute x3, starting transfers between devices, gather_ring(): ahead = lax.ppermute(ahead, 'mp', turn(count, count - 1))  9.12 us
  transfers between devices with their start and end apart: 20, of which 16 were waited for; matrix products, arithmetic and copies ran while one was open for 6% of the time, Pallas kernels for 2%

profile of v3, /device:TPU:8, one launch (start us, length us, event | category | flops | bytes accessed | tf_op | source)
XLA Modules:
  0.0 245.3 jit_solution(16316359308294956335)
XLA Ops:
  0.6 4.5 %shard_map.153 = (bf16[192,1536]{1,0:T(8,128)(2,1)}, bf16[192,768]{1,0:T(8,128)(2,1)}, f32[192,768]{1,0:T(8,128)}, bf16[8,288,128]{2,1,0:T(8,128)(2,1)}) custom-call(bf16[192,1536]{1,0:T(8,128)(2,1)} %far_x.1, bf16[1536,768]{1,0:T(8,128)(2,1)} %far_one.1, bf16[768,1536]{1,0:T(8,128)(2,1)} %two_ref.1), custom_call_target="tpu_custom_call" | custom-call | tf_op jit(solution)/shard_map/pallas_call | solution.py:49
  5.2 8.6 %all-to-all-start = ((bf16[8,288,128]{2,1,0:T(8,128)(2,1)}), bf16[8,288,128]{2,1,0:T(8,128)(2,1)S(1)}, u32[]{:S(2)}, u32[]{:S(2)}) async-start(bf16[8,288,128]{2,1,0:T(8,128)(2,1)} %get-tuple-element.45), calls=%async_computation | async-start | bytes 1179648 | tf_op jit(solution)/shard_map/all_to_all | solution.py:33
  14.4 1.2 copy.42
  17.8 1.2 constant_dynamic-slice_fusion.3
  19.2 13.5 %all-to-all-done.refs_9_ = bf16[8,288,128]{2,1,0:T(8,128)(2,1)S(1)} async-done(((bf16[8,288,128]{2,1,0:T(8,128)(2,1)}), bf16[8,288,128]{2,1,0:T(8,128)(2,1)S(1)}, u32[]{:S(2)}, u32[]{:S(2)}) %all-to-all-start) | async-done | bytes 589856 | tf_op jit(solution)/shard_map/all_to_all | solution.py:33
  33.0 14.8 %all_to_all.40 = bf16[32,16,256]{2,1,0:T(8,128)(2,1)S(1)} all-to-all(bf16[32,16,256]{2,1,0:T(8,128)(2,1)S(1)} %bitcast.56), channel_id=1, replica_groups=mesh['chip'=16,'core'=2,'mp'=8] {'chip','core'}, dimensions={0} | all-to-all | bytes 524288 | tf_op jit(solution)/shard_map/all_to_all | solution.py:33
  48.8 2.7 %collective-permute-start.1 = (bf16[208,384]{1,0:T(8,128)(2,1)S(1)}, bf16[208,384]{1,0:T(8,128)(2,1)S(1)}, u32[]{:S(2)}, u32[]{:S(2)}) collective-permute-start(bf16[208,384]{1,0:T(8,128)(2,1)S(1)} %get-tuple-element.47.rest_0_.refs_4_), channel_id=1, source_target_pairs={{0,7},{1,0},{2,1},{3,2},{4,3},{5,4},{6,5},{7,6},{8,15},{9,8},{10,9... | collective-permute-start | bytes 479240 | tf_op jit(solution)/shard_map/ppermute | solution.py:83
  51.5 4.5 %collective-permute-done.rest_1_ = bf16[208,384]{1,0:T(8,128)(2,1)S(1)} collective-permute-done((bf16[208,384]{1,0:T(8,128)(2,1)S(1)}, bf16[208,384]{1,0:T(8,128)(2,1)S(1)}, u32[]{:S(2)}, u32[]{:S(2)}) %collective-permute-start) | collective-permute-done | bytes 159776 | tf_op jit(solution)/shard_map/ppermute | solution.py:82
  56.0 3.2 %collective-permute-start.3 = (bf16[208,384]{1,0:T(8,128)(2,1)S(1)}, bf16[208,384]{1,0:T(8,128)(2,1)S(1)}, u32[]{:S(2)}, u32[]{:S(2)}) collective-permute-start(bf16[208,384]{1,0:T(8,128)(2,1)S(1)} %collective-permute-done.1.rest_2_), channel_id=1, source_target_pairs={{0,7},{1,0},{2,1},{3,2},{4,3},{5,4},{6,5},{7,6},{8,15},{9,8},{10,9... | collective-permute-start | bytes 479240 | tf_op jit(solution)/shard_map/ppermute | solution.py:83
  59.2 3.7 %collective-permute-done.2.rest_3_ = bf16[208,384]{1,0:T(8,128)(2,1)S(1)} collective-permute-done((bf16[208,384]{1,0:T(8,128)(2,1)S(1)}, bf16[208,384]{1,0:T(8,128)(2,1)S(1)}, u32[]{:S(2)}, u32[]{:S(2)}) %collective-permute-start.2) | collective-permute-done | bytes 159776 | tf_op jit(solution)/shard_map/ppermute | solution.py:82
  63.0 3.2 %collective-permute-start.5 = (bf16[208,384]{1,0:T(8,128)(2,1)S(1)}, bf16[208,384]{1,0:T(8,128)(2,1)S(1)}, u32[]{:S(2)}, u32[]{:S(2)}) collective-permute-start(bf16[208,384]{1,0:T(8,128)(2,1)S(1)} %collective-permute-done.3.rest_4_), channel_id=1, source_target_pairs={{0,7},{1,0},{2,1},{3,2},{4,3},{5,4},{6,5},{7,6},{8,15},{9,8},{10,9... | collective-permute-start | bytes 479240 | tf_op jit(solution)/shard_map/ppermute | solution.py:83
  66.2 3.2 %collective-permute-done.4.rest_5_ = bf16[208,384]{1,0:T(8,128)(2,1)S(1)} collective-permute-done((bf16[208,384]{1,0:T(8,128)(2,1)S(1)}, bf16[208,384]{1,0:T(8,128)(2,1)S(1)}, u32[]{:S(2)}, u32[]{:S(2)}) %collective-permute-start.4) | collective-permute-done | bytes 159776 | tf_op jit(solution)/shard_map/ppermute | solution.py:82
  69.6 3.5 %collective-permute-start.7 = (bf16[96,384]{1,0:T(8,128)(2,1)S(1)}, bf16[96,384]{1,0:T(8,128)(2,1)S(1)}, u32[]{:S(2)}, u32[]{:S(2)}) collective-permute-start(bf16[96,384]{1,0:T(8,128)(2,1)S(1)} %slice.51), channel_id=1, source_target_pairs={{0,7},{1,0},{2,1},{3,2},{4,3},{5,4},{6,5},{7,6},{8,15},{9,8},{10,9... | collective-permute-start | bytes 221192 | tf_op jit(solution)/shard_map/ppermute | solution.py:87
  73.1 2.0 collective-permute-done.7.rest_8_
  75.9 7.0 %shard_map.156 = (bf16[1536,384]{1,0:T(8,128)(2,1)}, f32[2,3,96,384]{3,2,1,0:T(8,128)}, f32[2,384,384]{2,1,0:T(8,128)}, f32[2,384]{1,0:T(2,128)}, f32[2,2,384]{2...) custom-call(s32[1]{0:T(128)} %bitcast.1.here, ...), custom_call_target="tpu_custom_call" | custom-call | tf_op jit(solution)/shard_map/pallas_call | solution.py:49
  82.9 12.9 %all_to_all.41.parts_ref = f32[8,1,1536]{2,1,0:T(1,128)S(1)} all-to-all(f32[8,1,1536]{2,1,0:T(1,128)} %get-tuple-element.48), channel_id=1, replica_groups=mesh['chip'=16,'core'=2,'mp'=8] {'mp'}, dimensions={0} | all-to-all | bytes 98304 | tf_op jit(solution)/shard_map/all_to_all | solution.py:33
  96.8 1.0 shard_map.157
  99.1 4.9 %all-to-all-start.3 = ((f32[32,1,128]{2,1,0:T(1,128)}), f32[32,1,128]{2,1,0:T(1,128)S(1)}, u32[]{:S(2)}, u32[]{:S(2)}) async-start(f32[32,1,128]{2,1,0:T(1,128)} %get-tuple-element.50), calls=%async_computation.3 | async-start | bytes 32768 | tf_op jit(solution)/shard_map/all_to_all | solution.py:33
  104.0 1.2 copy.49.far_query_weights
  105.1 2.2 copy.50.far_key_weights
  107.4 1.2 copy.51.far_value_weights
  110.7 6.3 %shard_map.158 = (f32[1,1]{1,0:T(1,128)}, f32[1,1536]{1,0:T(1,128)}, f32[1,192]{1,0:T(1,128)}, bf16[576,384]{1,0:T(8,128)(2,1)}, bf16[8,208,384]{2,1,0:T(8,128)(2,1)}) custom-call(s32[1]{0:T(128)} %bitcast.owner, f32[32,128]{1,0:T(8,128)} %bitcast.66, s32[32,1]{1,0:T(8,128)} %copy.48.pair_ref, f32[2,1536]{1,0:T(2,128)} %copy-done.15, f32[32,1536]{1,0:T(8,128)} %copy-done.9, ...), custom_call_target="tpu_custom_call" | custom-call | tf_op jit(solution)/shard_map/pallas_call | solution.py:49
  117.0 4.4 %all-to-all-start.4 = ((bf16[8,208,384]{2,1,0:T(8,128)(2,1)}), bf16[8,208,384]{2,1,0:T(8,128)(2,1)}, u32[]{:S(2)}, u32[]{:S(2)}) async-start(bf16[8,208,384]{2,1,0:T(8,128)(2,1)} %get-tuple-element.70), calls=%async_computation.4 | async-start | bytes 2555904 | tf_op jit(solution)/shard_map/all_to_all | solution.py:33
  121.4 1.0 copy-done.3
  122.4 1.4 shard_map.159
  125.0 1.2 collective-permute-done.8.got_ref
  126.2 1.0 copy-done.4
  127.2 2.3 shard_map.160
  130.9 2.7 %collective-permute-start.10 = (bf16[4,48,384]{2,1,0:T(8,128)(2,1)}, bf16[4,48,384]{2,1,0:T(8,128)(2,1)S(1)}, u32[]{:S(2)}, u32[]{:S(2)}) collective-permute-start(bf16[4,48,384]{2,1,0:T(8,128)(2,1)} %get-tuple-element.63), channel_id=1, source_target_pairs={{0,32},{16,48},{32,0},{48,16},{64,96},{80,112},{96,64},{112,80},{1... | collective-permute-start | bytes 442376 | tf_op jit(solution)/shard_map/ppermute | solution.py:702
  133.6 1.5 collective-permute-start.11
  135.3 2.8 %collective-permute-done.9.refs_1_ = bf16[4,48,384]{2,1,0:T(8,128)(2,1)S(1)} collective-permute-done((bf16[4,48,384]{2,1,0:T(8,128)(2,1)}, bf16[4,48,384]{2,1,0:T(8,128)(2,1)S(1)}, u32[]{:S(2)}, u32[]{:S(2)}) %collective-permute-start.9) | collective-permute-done | bytes 147488 | tf_op jit(solution)/shard_map/ppermute | solution.py:702
  138.1 2.7 %collective-permute-done.10.refs_2_ = bf16[4,48,384]{2,1,0:T(8,128)(2,1)S(1)} collective-permute-done((bf16[4,48,384]{2,1,0:T(8,128)(2,1)}, bf16[4,48,384]{2,1,0:T(8,128)(2,1)S(1)}, u32[]{:S(2)}, u32[]{:S(2)}) %collective-permute-start.10) | collective-permute-done | bytes 147488 | tf_op jit(solution)/shard_map/ppermute | solution.py:702
  141.2 0.9 copy-done.11
  142.2 13.1 %all-to-all-done.4.refs_7_ = bf16[8,208,384]{2,1,0:T(8,128)(2,1)} async-done(((bf16[8,208,384]{2,1,0:T(8,128)(2,1)}), bf16[8,208,384]{2,1,0:T(8,128)(2,1)}, u32[]{:S(2)}, u32[]{:S(2)}) %all-to-all-start.4) | async-done | bytes 1277984 | tf_op jit(solution)/shard_map/all_to_all | solution.py:33
  155.4 1.8 shard_map.162
  157.2 14.3 %all_to_all.42 = bf16[32,16,192]{2,1,0:T(8,128)(2,1)S(1)} all-to-all(bf16[32,16,192]{2,1,0:T(8,128)(2,1)S(1)} %bitcast.59), channel_id=1, replica_groups=mesh['chip'=16,'core'=2,'mp'=8] {'chip','core'}, dimensions={0} | all-to-all | bytes 393216 | tf_op jit(solution)/shard_map/all_to_all | solution.py:33
  171.9 22.3 %all_to_all.43.parts_ref = bf16[8,288,128]{2,1,0:T(8,128)(2,1)S(1)} all-to-all(bf16[8,288,128]{2,1,0:T(8,128)(2,1)S(1)} %shard_map.163), channel_id=1, replica_groups=mesh['chip'=16,'core'=2,'mp'=8] {'mp'}, dimensions={0} | all-to-all | bytes 1179648 | tf_op jit(solution)/shard_map/all_to_all | solution.py:33
  194.2 2.1 shard_map.164
  196.4 4.5 %collective-permute-done.12.got_ref = bf16[16,96,768]{2,1,0:T(8,128)(2,1)S(1)} collective-permute-done((bf16[16,96,768]{2,1,0:T(8,128)(2,1)S(1)}, bf16[16,96,768]{2,1,0:T(8,128)(2,1)S(1)}, u32[]{:S(2)}, u32[]{:S(2)}) %collective-permute-start.12) | collective-permute-done | bytes 2359328 | tf_op jit(solution)/shard_map/ppermute | solution.py:758
  201.7 1.4 copy-done.1
  203.1 5.1 %all-to-all-start.7 = ((bf16[16,96,768]{2,1,0:T(8,128)(2,1)}), bf16[16,96,768]{2,1,0:T(8,128)(2,1)S(1)}, u32[]{:S(2)}, u32[]{:S(2)}) async-start(bf16[16,96,768]{2,1,0:T(8,128)(2,1)} %copy-done.1), calls=%async_computation.7 | async-start | bytes 4718592 | tf_op jit(solution)/shard_map/all_to_all | solution.py:33
  208.5 2.7 %collective-permute-start.14 = (bf16[48,384]{1,0:T(8,128)(2,1)S(1)}, bf16[48,384]{1,0:T(8,128)(2,1)S(1)}, u32[]{:S(2)}, u32[]{:S(2)}) collective-permute-start(bf16[48,384]{1,0:T(8,128)(2,1)S(1)} %copy-done.20), channel_id=1, source_target_pairs={{0,128},{16,144},{32,160},{48,176},{64,192},{80,208},{96,224},{112... | collective-permute-start | bytes 110600 | tf_op jit(solution)/shard_map/ppermute | solution.py:711
  211.2 1.8 collective-permute-start.13
  213.0 11.1 %collective-permute-done.15 = bf16[48,384]{1,0:T(8,128)(2,1)S(1)} collective-permute-done((bf16[48,384]{1,0:T(8,128)(2,1)S(1)}, bf16[48,384]{1,0:T(8,128)(2,1)S(1)}, u32[]{:S(2)}, u32[]{:S(2)}) %collective-permute-start.15) | collective-permute-done | bytes 36896 | tf_op jit(solution)/shard_map/ppermute | solution.py:711
  224.1 14.2 %collective-permute-done.14 = bf16[48,384]{1,0:T(8,128)(2,1)S(1)} collective-permute-done((bf16[48,384]{1,0:T(8,128)(2,1)S(1)}, bf16[48,384]{1,0:T(8,128)(2,1)S(1)}, u32[]{:S(2)}, u32[]{:S(2)}) %collective-permute-start.14) | collective-permute-done | bytes 36896 | tf_op jit(solution)/shard_map/ppermute | solution.py:711
  239.0 0.9 slice.54
  242.2 2.1 all-to-all-done.7.values_ref
  244.3 1.0 shard_map.166
  (158 shorter events, 17.2 us)
Async XLA Ops:
  5.2 8.6 %copy-start.25 = (bf16[192,1536]{1,0:T(8,128)(2,1)S(1)}, bf16[192,1536]{1,0:T(8,128)(2,1)}, u32[]{:S(2)}) copy-start(bf16[192,1536]{1,0:T(8,128)(2,1)} %far_x.1) | copy-start | bytes 1769476
  5.2 9.3 %copy-start.27 = (bf16[192,1536]{1,0:T(8,128)(2,1)S(1)}, bf16[192,1536]{1,0:T(8,128)(2,1)}, u32[]{:S(2)}) copy-start(bf16[192,1536]{1,0:T(8,128)(2,1)} %get-tuple-element.43) | copy-start | bytes 1769476
  5.2 27.5 %all-to-all-start = ((bf16[8,288,128]{2,1,0:T(8,128)(2,1)}), bf16[8,288,128]{2,1,0:T(8,128)(2,1)S(1)}, u32[]{:S(2)}, u32[]{:S(2)}) async-start(bf16[8,288,128]{2,1,0:T(8,128)(2,1)} %get-tuple-element.45), calls=%async_computation | async-start | bytes 1179648 | tf_op jit(solution)/shard_map/all_to_all | solution.py:33
  48.2 27.5 %copy-start.7 = (bf16[208,384]{1,0:T(8,128)(2,1)}, bf16[208,384]{1,0:T(8,128)(2,1)S(1)}, u32[]{:S(2)}) copy-start(bf16[208,384]{1,0:T(8,128)(2,1)S(1)} %get-tuple-element.47.rest_0_.refs_4_) | copy-start | bytes 479236
  48.2 27.5 %copy-start.13 = (f32[1,384]{1,0:T(1,128)}, f32[1,384]{1,0:T(1,128)S(1)}, u32[]{:S(2)}) copy-start(f32[1,384]{1,0:T(1,128)S(1)} %get-tuple-element.46.valid_ref.refs_2_) | copy-start | bytes 4612
  48.2 7.8 %collective-permute-start = (bf16[208,384]{1,0:T(8,128)(2,1)S(1)}, bf16[208,384]{1,0:T(8,128)(2,1)S(1)}, u32[]{:S(2)}, u32[]{:S(2)}) collective-permute-start(bf16[208,384]{1,0:T(8,128)(2,1)S(1)} %get-tuple-element.47.rest_0_.refs_4_), channel_id=1, source_target_pairs={{0,1},{1,2},{2,3},{3,4},{4,5},{5,6},{6,7},{7,0},{8,9},{9,10},{10,1... | collective-permute-start | bytes 479240 | tf_op jit(solution)/shard_map/ppermute | solution.py:82
  48.8 7.2 %collective-permute-start.1 = (bf16[208,384]{1,0:T(8,128)(2,1)S(1)}, bf16[208,384]{1,0:T(8,128)(2,1)S(1)}, u32[]{:S(2)}, u32[]{:S(2)}) collective-permute-start(bf16[208,384]{1,0:T(8,128)(2,1)S(1)} %get-tuple-element.47.rest_0_.refs_4_), channel_id=1, source_target_pairs={{0,7},{1,0},{2,1},{3,2},{4,3},{5,4},{6,5},{7,6},{8,15},{9,8},{10,9... | collective-permute-start | bytes 479240 | tf_op jit(solution)/shard_map/ppermute | solution.py:83
  56.0 19.7 %copy-start.30 = (bf16[208,384]{1,0:T(8,128)(2,1)}, bf16[208,384]{1,0:T(8,128)(2,1)S(1)}, u32[]{:S(2)}) copy-start(bf16[208,384]{1,0:T(8,128)(2,1)S(1)} %collective-permute-done.rest_1_) | copy-start | bytes 479236
  56.0 7.0 %collective-permute-start.2 = (bf16[208,384]{1,0:T(8,128)(2,1)S(1)}, bf16[208,384]{1,0:T(8,128)(2,1)S(1)}, u32[]{:S(2)}, u32[]{:S(2)}) collective-permute-start(bf16[208,384]{1,0:T(8,128)(2,1)S(1)} %collective-permute-done.rest_1_), channel_id=1, source_target_pairs={{0,1},{1,2},{2,3},{3,4},{4,5},{5,6},{6,7},{7,0},{8,9},{9,10},{10,1... | collective-permute-start | bytes 479240 | tf_op jit(solution)/shard_map/ppermute | solution.py:82
  56.0 19.7 %copy-start.31 = (bf16[208,384]{1,0:T(8,128)(2,1)}, bf16[208,384]{1,0:T(8,128)(2,1)S(1)}, u32[]{:S(2)}) copy-start(bf16[208,384]{1,0:T(8,128)(2,1)S(1)} %collective-permute-done.1.rest_2_) | copy-start | bytes 479236
  56.0 7.0 %collective-permute-start.3 = (bf16[208,384]{1,0:T(8,128)(2,1)S(1)}, bf16[208,384]{1,0:T(8,128)(2,1)S(1)}, u32[]{:S(2)}, u32[]{:S(2)}) collective-permute-start(bf16[208,384]{1,0:T(8,128)(2,1)S(1)} %collective-permute-done.1.rest_2_), channel_id=1, source_target_pairs={{0,7},{1,0},{2,1},{3,2},{4,3},{5,4},{6,5},{7,6},{8,15},{9,8},{10,9... | collective-permute-start | bytes 479240 | tf_op jit(solution)/shard_map/ppermute | solution.py:83
  63.0 12.7 %copy-start.32 = (bf16[208,384]{1,0:T(8,128)(2,1)}, bf16[208,384]{1,0:T(8,128)(2,1)S(1)}, u32[]{:S(2)}) copy-start(bf16[208,384]{1,0:T(8,128)(2,1)S(1)} %collective-permute-done.2.rest_3_) | copy-start | bytes 479236
  63.0 6.5 %collective-permute-start.4 = (bf16[208,384]{1,0:T(8,128)(2,1)S(1)}, bf16[208,384]{1,0:T(8,128)(2,1)S(1)}, u32[]{:S(2)}, u32[]{:S(2)}) collective-permute-start(bf16[208,384]{1,0:T(8,128)(2,1)S(1)} %collective-permute-done.2.rest_3_), channel_id=1, source_target_pairs={{0,1},{1,2},{2,3},{3,4},{4,5},{5,6},{6,7},{7,0},{8,9},{9,10},{10,1... | collective-permute-start | bytes 479240 | tf_op jit(solution)/shard_map/ppermute | solution.py:82
  63.0 12.3 %copy-start.33 = (bf16[208,384]{1,0:T(8,128)(2,1)}, bf16[208,384]{1,0:T(8,128)(2,1)S(1)}, u32[]{:S(2)}) copy-start(bf16[208,384]{1,0:T(8,128)(2,1)S(1)} %collective-permute-done.3.rest_4_) | copy-start | bytes 479236
  63.0 6.6 %collective-permute-start.5 = (bf16[208,384]{1,0:T(8,128)(2,1)S(1)}, bf16[208,384]{1,0:T(8,128)(2,1)S(1)}, u32[]{:S(2)}, u32[]{:S(2)}) collective-permute-start(bf16[208,384]{1,0:T(8,128)(2,1)S(1)} %collective-permute-done.3.rest_4_), channel_id=1, source_target_pairs={{0,7},{1,0},{2,1},{3,2},{4,3},{5,4},{6,5},{7,6},{8,15},{9,8},{10,9... | collective-permute-start | bytes 479240 | tf_op jit(solution)/shard_map/ppermute | solution.py:83
  69.5 6.2 %copy-start.28 = (bf16[208,384]{1,0:T(8,128)(2,1)}, bf16[208,384]{1,0:T(8,128)(2,1)S(1)}, u32[]{:S(2)}) copy-start(bf16[208,384]{1,0:T(8,128)(2,1)S(1)} %collective-permute-done.4.rest_5_) | copy-start | bytes 479236
  69.5 5.8 %collective-permute-start.6 = (bf16[112,384]{1,0:T(8,128)(2,1)S(1)}, bf16[112,384]{1,0:T(8,128)(2,1)S(1)}, u32[]{:S(2)}, u32[]{:S(2)}) collective-permute-start(bf16[112,384]{1,0:T(8,128)(2,1)S(1)} %slice.50), channel_id=1, source_target_pairs={{0,1},{1,2},{2,3},{3,4},{4,5},{5,6},{6,7},{7,0},{8,9},{9,10},{10,1... | collective-permute-start | bytes 258056 | tf_op jit(solution)/shard_map/ppermute | solution.py:86
  69.6 6.1 %copy-start.29 = (bf16[208,384]{1,0:T(8,128)(2,1)}, bf16[208,384]{1,0:T(8,128)(2,1)S(1)}, u32[]{:S(2)}) copy-start(bf16[208,384]{1,0:T(8,128)(2,1)S(1)} %collective-permute-done.5.rest_6_) | copy-start | bytes 479236
  69.6 5.4 %collective-permute-start.7 = (bf16[96,384]{1,0:T(8,128)(2,1)S(1)}, bf16[96,384]{1,0:T(8,128)(2,1)S(1)}, u32[]{:S(2)}, u32[]{:S(2)}) collective-permute-start(bf16[96,384]{1,0:T(8,128)(2,1)S(1)} %slice.51), channel_id=1, source_target_pairs={{0,7},{1,0},{2,1},{3,2},{4,3},{5,4},{6,5},{7,6},{8,15},{9,8},{10,9... | collective-permute-start | bytes 221192 | tf_op jit(solution)/shard_map/ppermute | solution.py:87
  75.9 28.1 %copy-start.23 = (bf16[1536,192]{0,1:T(8,128)(2,1)S(1)}, bf16[1536,192]{0,1:T(8,128)(2,1)}, u32[]{:S(2)}) copy-start(bf16[1536,192]{0,1:T(8,128)(2,1)} %param.16) | copy-start | bytes 1769476
  99.1 11.0 %all-to-all-start.3 = ((f32[32,1,128]{2,1,0:T(1,128)}), f32[32,1,128]{2,1,0:T(1,128)S(1)}, u32[]{:S(2)}, u32[]{:S(2)}) async-start(f32[32,1,128]{2,1,0:T(1,128)} %get-tuple-element.50), calls=%async_computation.3 | async-start | bytes 32768 | tf_op jit(solution)/shard_map/all_to_all | solution.py:33
  104.0 3.4 %copy-start.24 = (bf16[1536,192]{0,1:T(8,128)(2,1)S(1)}, bf16[1536,192]{0,1:T(8,128)(2,1)}, u32[]{:S(2)}) copy-start(bf16[1536,192]{0,1:T(8,128)(2,1)} %param.18) | copy-start | bytes 1769476
  105.1 3.5 %copy-start.41 = (s32[32]{0:T(128)S(1)}, s32[32]{0:T(128)}, u32[]{:S(2)}) copy-start(s32[32]{0:T(128)} %param.12) | copy-start | bytes 388
  117.0 4.5 %copy-start = (bf16[1536,384]{1,0:T(8,128)(2,1)S(1)}, bf16[1536,384]{1,0:T(8,128)(2,1)}, u32[]{:S(2)}) copy-start(bf16[1536,384]{1,0:T(8,128)(2,1)} %get-tuple-element.57.far_norm.norm_ref) | copy-start | bytes 3538948
  117.0 38.4 %all-to-all-start.4 = ((bf16[8,208,384]{2,1,0:T(8,128)(2,1)}), bf16[8,208,384]{2,1,0:T(8,128)(2,1)}, u32[]{:S(2)}, u32[]{:S(2)}) async-start(bf16[8,208,384]{2,1,0:T(8,128)(2,1)} %get-tuple-element.70), calls=%async_computation.4 | async-start | bytes 2555904 | tf_op jit(solution)/shard_map/all_to_all | solution.py:33
  121.4 2.4 copy-start.37
  122.4 2.4 copy-start.43
  123.8 2.3 collective-permute-start.8
  127.2 28.2 %copy-start.14 = (f32[1,384]{1,0:T(1,128)S(1)}, f32[1,384]{1,0:T(1,128)}, u32[]{:S(2)}) copy-start(f32[1,384]{1,0:T(1,128)} %copy-done.13) | copy-start | bytes 4612
  127.2 28.2 %copy-start.16 = (f32[2,384]{1,0:T(2,128)S(1)}, f32[2,384]{1,0:T(2,128)}, u32[]{:S(2)}) copy-start(f32[2,384]{1,0:T(2,128)} %get-tuple-element.67.refs_3_) | copy-start | bytes 9220
  130.2 25.2 %copy-start.8 = (bf16[208,384]{1,0:T(8,128)(2,1)S(1)}, bf16[208,384]{1,0:T(8,128)(2,1)}, u32[]{:S(2)}) copy-start(bf16[208,384]{1,0:T(8,128)(2,1)} %copy-done.7) | copy-start | bytes 479236
  130.2 7.9 %collective-permute-start.9 = (bf16[4,48,384]{2,1,0:T(8,128)(2,1)}, bf16[4,48,384]{2,1,0:T(8,128)(2,1)S(1)}, u32[]{:S(2)}, u32[]{:S(2)}) collective-permute-start(bf16[4,48,384]{2,1,0:T(8,128)(2,1)} %get-tuple-element.62), channel_id=1, source_target_pairs={{0,16},{16,32},{32,48},{48,0},{64,80},{80,96},{96,112},{112,64},{1... | collective-permute-start | bytes 442376 | tf_op jit(solution)/shard_map/ppermute | solution.py:702
  130.9 9.9 %collective-permute-start.10 = (bf16[4,48,384]{2,1,0:T(8,128)(2,1)}, bf16[4,48,384]{2,1,0:T(8,128)(2,1)S(1)}, u32[]{:S(2)}, u32[]{:S(2)}) collective-permute-start(bf16[4,48,384]{2,1,0:T(8,128)(2,1)} %get-tuple-element.63), channel_id=1, source_target_pairs={{0,32},{16,48},{32,0},{48,16},{64,96},{80,112},{96,64},{112,80},{1... | collective-permute-start | bytes 442376 | tf_op jit(solution)/shard_map/ppermute | solution.py:702
  133.6 7.7 %collective-permute-start.11 = (bf16[4,48,384]{2,1,0:T(8,128)(2,1)}, bf16[4,48,384]{2,1,0:T(8,128)(2,1)S(1)}, u32[]{:S(2)}, u32[]{:S(2)}) collective-permute-start(bf16[4,48,384]{2,1,0:T(8,128)(2,1)} %get-tuple-element.64), channel_id=1, source_target_pairs={{0,48},{16,0},{32,16},{48,32},{64,112},{80,64},{96,80},{112,96},{1... | collective-permute-start | bytes 442376 | tf_op jit(solution)/shard_map/ppermute | solution.py:702
  142.2 29.3 %copy-start.17 = (bf16[48,384]{1,0:T(8,128)(2,1)}, bf16[48,384]{1,0:T(8,128)(2,1)S(1)}, u32[]{:S(2)}) copy-start(bf16[48,384]{1,0:T(8,128)(2,1)S(1)} %get-tuple-element.76) | copy-start | bytes 110596
  142.2 29.3 %copy-start.19 = (bf16[48,384]{1,0:T(8,128)(2,1)}, bf16[48,384]{1,0:T(8,128)(2,1)S(1)}, u32[]{:S(2)}) copy-start(bf16[48,384]{1,0:T(8,128)(2,1)S(1)} %get-tuple-element.77) | copy-start | bytes 110596
  142.2 29.3 %copy-start.21 = (bf16[48,384]{1,0:T(8,128)(2,1)}, bf16[48,384]{1,0:T(8,128)(2,1)S(1)}, u32[]{:S(2)}) copy-start(bf16[48,384]{1,0:T(8,128)(2,1)S(1)} %get-tuple-element.78) | copy-start | bytes 110596
  157.2 36.9 %copy-start.2 = (bf16[768,1536]{1,0:T(8,128)(2,1)S(1)}, bf16[768,1536]{1,0:T(8,128)(2,1)}, u32[]{:S(2)}) copy-start(bf16[768,1536]{1,0:T(8,128)(2,1)} %two_ref.1) | copy-start | bytes 7077892
  171.5 24.7 %copy-start.5 = (bf16[32,16,192]{2,1,0:T(8,128)(2,1)}, bf16[32,16,192]{2,1,0:T(8,128)(2,1)S(1)}, u32[]{:S(2)}) copy-start(bf16[32,16,192]{2,1,0:T(8,128)(2,1)S(1)} %all_to_all.42) | copy-start | bytes 589828
  171.6 22.6 %copy-start.6 = (bf16[192,768]{1,0:T(8,128)(2,1)S(1)}, bf16[192,768]{1,0:T(8,128)(2,1)}, u32[]{:S(2)}) copy-start(bf16[192,768]{1,0:T(8,128)(2,1)} %get-tuple-element.59.hidden_ref) | copy-start | bytes 884740
  196.3 4.6 %collective-permute-start.12 = (bf16[16,96,768]{2,1,0:T(8,128)(2,1)S(1)}, bf16[16,96,768]{2,1,0:T(8,128)(2,1)S(1)}, u32[]{:S(2)}, u32[]{:S(2)}) collective-permute-start(bf16[16,96,768]{2,1,0:T(8,128)(2,1)S(1)} %get-tuple-element.73), channel_id=1, source_target_pairs={{0,8},{8,0},{1,9},{9,1},{2,10},{10,2},{3,11},{11,3},{4,12},{12,4},... | collective-permute-start | bytes 7077896 | tf_op jit(solution)/shard_map/ppermute | solution.py:758
  203.1 5.1 %copy-start.22 = (bf16[48,384]{1,0:T(8,128)(2,1)S(1)}, bf16[48,384]{1,0:T(8,128)(2,1)}, u32[]{:S(2)}) copy-start(bf16[48,384]{1,0:T(8,128)(2,1)} %copy-done.21) | copy-start | bytes 110596
  203.1 5.4 %copy-start.20 = (bf16[48,384]{1,0:T(8,128)(2,1)S(1)}, bf16[48,384]{1,0:T(8,128)(2,1)}, u32[]{:S(2)}) copy-start(bf16[48,384]{1,0:T(8,128)(2,1)} %copy-done.19) | copy-start | bytes 110596
  203.1 8.1 %copy-start.18 = (bf16[48,384]{1,0:T(8,128)(2,1)S(1)}, bf16[48,384]{1,0:T(8,128)(2,1)}, u32[]{:S(2)}) copy-start(bf16[48,384]{1,0:T(8,128)(2,1)} %copy-done.17) | copy-start | bytes 110596
  203.1 41.2 %all-to-all-start.7 = ((bf16[16,96,768]{2,1,0:T(8,128)(2,1)}), bf16[16,96,768]{2,1,0:T(8,128)(2,1)S(1)}, u32[]{:S(2)}, u32[]{:S(2)}) async-start(bf16[16,96,768]{2,1,0:T(8,128)(2,1)} %copy-done.1), calls=%async_computation.7 | async-start | bytes 4718592 | tf_op jit(solution)/shard_map/all_to_all | solution.py:33
  208.2 15.9 %collective-permute-start.15 = (bf16[48,384]{1,0:T(8,128)(2,1)S(1)}, bf16[48,384]{1,0:T(8,128)(2,1)S(1)}, u32[]{:S(2)}, u32[]{:S(2)}) collective-permute-start(bf16[48,384]{1,0:T(8,128)(2,1)S(1)} %copy-done.22), channel_id=1, source_target_pairs={{0,192},{16,208},{32,224},{48,240},{64,0},{80,16},{96,32},{112,48}... | collective-permute-start | bytes 110600 | tf_op jit(solution)/shard_map/ppermute | solution.py:711
  208.5 29.8 %collective-permute-start.14 = (bf16[48,384]{1,0:T(8,128)(2,1)S(1)}, bf16[48,384]{1,0:T(8,128)(2,1)S(1)}, u32[]{:S(2)}, u32[]{:S(2)}) collective-permute-start(bf16[48,384]{1,0:T(8,128)(2,1)S(1)} %copy-done.20), channel_id=1, source_target_pairs={{0,128},{16,144},{32,160},{48,176},{64,192},{80,208},{96,224},{112... | collective-permute-start | bytes 110600 | tf_op jit(solution)/shard_map/ppermute | solution.py:711
  211.2 27.1 %collective-permute-start.13 = (bf16[48,384]{1,0:T(8,128)(2,1)S(1)}, bf16[48,384]{1,0:T(8,128)(2,1)S(1)}, u32[]{:S(2)}, u32[]{:S(2)}) collective-permute-start(bf16[48,384]{1,0:T(8,128)(2,1)S(1)} %copy-done.18), channel_id=1, source_target_pairs={{0,64},{16,80},{32,96},{48,112},{64,128},{80,144},{96,160},{112,17... | collective-permute-start | bytes 110600 | tf_op jit(solution)/shard_map/ppermute | solution.py:711
  (16 other events, 16.4 us)

commit v4 on v3

--- a/solution.py
+++ b/solution.py
@@ -20,7 +20,7 @@
 f32 = jnp.float32
 bf16 = jnp.bfloat16
 i32 = jnp.int32
-DP = ("chip", "core")
+DP = ("line", "column", "core")
 
 
 def contract(left, right, left_dim, right_dim, **kw):
@@ -481,11 +481,36 @@
     both_layers(other[0], norm_ref, hidden_ref, grad_ref, hidden_grad_ref, out_ref.shape, store)
 
 
-def own_grads(own, norm_ref, hidden_ref, grad_ref, hidden_grad_ref, got_ref, out_ref):
+def own_grads(own, column, norm_ref, hidden_ref, grad_ref, hidden_grad_ref, got_ref, *rest):
+    outs, line_ref, one_ref = rest[:-2], rest[-2], rest[-1]
+    side = len(outs)
+
     def store(rows, values):
-        out_ref[rows] = (values + got_ref[rows].astype(f32)).astype(bf16)
-
-    both_layers(own[0], norm_ref, hidden_ref, grad_ref, hidden_grad_ref, out_ref.shape, store)
+        values = (values + got_ref[rows].astype(f32)).astype(bf16)
+        line, place = divmod(rows[0], side)
+        if rows[1].start:
+            line_ref[line, place] = values
+        else:
+            one_ref[place, line] = values
+
+    both_layers(own[0], norm_ref, hidden_ref, grad_ref, hidden_grad_ref, got_ref.shape, store)
+    for k in range(side):
+        outs[k][...] = one_ref[lax.rem(column[0] + k, side)]
+
+
+def half_way(column, *refs):
+    side = (len(refs) - 2) // 2
+    lines_ref, out_ref = refs[side], refs[side + 1]
+    total = refs[0][...].astype(f32)
+    for ref in refs[1:side]:
+        total = total + ref[...].astype(f32)
+    out_ref[...] = total.astype(bf16)
+    for k in range(side):
+        place = lax.rem(column[0] + k, side)
+        total = lines_ref[0, place].astype(f32)
+        for line in range(1, lines_ref.shape[0]):
+            total = total + lines_ref[line, place].astype(f32)
+        refs[side + 2 + k][...] = total.astype(bf16)
 
 
 def both_layers(which, norm_ref, hidden_ref, grad_ref, hidden_grad_ref, shape, store):
@@ -502,19 +527,26 @@
         store((chip, slice(share, 2 * share)), two[start : start + share])
 
 
-def last_sums(values_ref, one_ref, two_ref):
-    share = one_ref.shape[0]
-    total = values_ref[0].astype(f32)
-    for chip in range(1, values_ref.shape[0]):
-        total = total + values_ref[chip].astype(f32)
-    one_ref[...] = total[:share]
-    two_ref[...] = total[share:]
+def last_sums(lines_ref, *refs):
+    one_ref, two_ref = refs[-2:]
+    total = lines_ref[0].astype(f32)
+    for line in range(1, lines_ref.shape[0]):
+        total = total + lines_ref[line].astype(f32)
+    one_ref[...] = total
+    total = refs[0][...].astype(f32)
+    for ref in refs[1:-2]:
+        total = total + ref[...].astype(f32)
+    two_ref[...] = total
 
 
 def per_device(
     tile_features, tile_slide, slide_pair, reports, w_one, w_two, w_query, w_key, w_value, w_out
 ):
-    chips = lax.axis_size("chip")
+    lines = lax.axis_size("line")
+    side = lax.axis_size("column")
+    line = lax.axis_index("line")
+    column = lax.axis_index("column")
+    chips = lines * side
     owners = chips * CORES
     parts = lax.axis_size("mp")
     core = lax.axis_index("core")
@@ -679,9 +711,6 @@
     )
     received = exchange(sending, "mp")
 
-    lines = math.isqrt(chips)
-    side = chips // lines
-    chip = lax.axis_index("chip")
     (wide_sent,) = call(
         wide_other,
         [((chips, share, 2 * inner), bf16)],
@@ -696,21 +725,18 @@
         slide_norm,
         grads,
         wide_got,
-        scalars=(core, chip % side),
-    )
-    along = [along[0]] + [
-        lax.ppermute(
-            along[k], "chip", [(c, c // side * side + (c + k) % side) for c in range(chips)]
-        )
-        for k in range(1, side)
-    ]
+        scalars=(core, column),
+    )
+    def shift(values, axis):
+        return [values[0]] + [
+            lax.ppermute(values[k], axis, turn(len(values), k)) for k in range(1, len(values))
+        ]
+
+    along = shift(along, "column")
     across = call(
-        wide_line, [((share, 2 * inner), bf16)] * lines, *along, scalars=(chip // side,)
-    )
-    across = [across[0]] + [
-        lax.ppermute(across[k], "chip", [(c, (c + k * side) % chips) for c in range(chips)])
-        for k in range(1, lines)
-    ]
+        wide_line, [((share, 2 * inner), bf16)] * lines, *along, scalars=(line,)
+    )
+    across = shift(across, "line")
     grad_wide = sum(part.astype(f32) for part in across)
     value_rows = contract(mass.astype(bf16), slide_norm, 1, 1)
     extra = jnp.concatenate(
@@ -738,7 +764,7 @@
         select,
         extra,
         received,
-        anchors=(across[0],),
+        anchors=(grad_wide,),
     )
     back = exchange(going.reshape(owners, ROWS, block), DP).reshape(slots, block)
     (spreading,) = call(tile_grads, [((parts,) + packed, bf16)], back, dispatch)
@@ -756,19 +782,30 @@
         limit=24,
     )
     got = lax.ppermute(sent, "core", [(0, 1), (1, 0)])
-    (both,) = call(
+    *along, across = call(
         own_grads,
-        [(size, bf16)],
+        [((lines, share, units), bf16)] * side + [((lines, side, share, units), bf16)],
         tile_own,
         hidden,
         grad_embedding,
         grad_hidden,
         got,
-        scalars=(core,),
+        scalars=(core, column),
+        scratch=[((side, lines, share, units), bf16)],
         limit=24,
     )
+    across, *along = call(
+        half_way,
+        [((lines, share, units), bf16)] + [((share, units), bf16)] * side,
+        *shift(along, "column"),
+        exchange(across, "line"),
+        scalars=(column,),
+    )
     grad_one, grad_two = call(
-        last_sums, [((share, units), f32), ((share, units), f32)], exchange(both, "chip")
+        last_sums,
+        [((share, units), f32)] * 2,
+        exchange(across, "line"),
+        *shift(along, "column"),
     )
     grad_two = grad_two.T
 
@@ -796,8 +833,10 @@
 
 def solution(mesh):
     owners, parts = mesh.devices.shape
+    side = math.isqrt(owners // CORES)
     split = Mesh(
-        mesh.devices.reshape(owners // CORES, CORES, parts), ("chip", "core", "mp")
+        mesh.devices.reshape(owners // CORES // side, side, CORES, parts),
+        ("line", "column", "core", "mp"),
     )
     return jax.shard_map(
         per_device,

time: 248 us -> 241 us (0.972)
  waiting for transfers between devices: 80 us -> 65.3 us
  starting transfers between devices: 46.1 us -> 57.8 us
  local copies, waits for them, and re-layouts: 21.4 us -> 18.6 us
    ppermute x6 -> x12, waiting for transfers between devices: 31.2 us -> 23 us  [shift(): lax.ppermute(values[k], axis, turn(len(values), k))]
    ppermute x6 -> x12, starting transfers between devices: 9.68 us -> 16.8 us  [shift(): lax.ppermute(values[k], axis, turn(len(values), k))]
    all_to_all x4 -> x5, waiting for transfers between devices: 29.5 us -> 22.7 us  [exchange(): return lax.all_to_all(values, axis, 0, 0, tiled=True)]
    all_to_all x4 -> x5, starting transfers between devices: 23 us -> 27.6 us  [exchange(): return lax.all_to_all(values, axis, 0, 0, tiled=True)]
    unnamed x92 -> x74, local copies, waits for them, and re-layouts: 13.3 us -> 11.4 us
    pallas_call x14 -> x15, Pallas kernels: 29.4 us -> 30.3 us  [call(): pl.pallas_call(kernel if skip else body, out_shape=[jax.ShapeDtypeStruct(...]
  transfers between devices with their start and end apart: 20 -> 27, of which waited for: 16 -> 19; matrix products, arithmetic and copies ran while one was open for 6% -> 6% of each run, Pallas kernels for 2% -> 1%
where the time goes in v4:
time: 241 us; the launch traced here: 240 us
  waiting for transfers between devices  65.3 us (27%)
  blocking collectives  64.3 us (27%)
  starting transfers between devices  57.8 us (24%)
  Pallas kernels  30.3 us (13%)
  local copies, waits for them, and re-layouts  18.6 us (8%)
    all_to_all x4, blocking collectives, exchange(): return lax.all_to_all(values, axis, 0, 0, tiled=True)  64.3 us
    pallas_call x15, Pallas kernels, call(): pl.pallas_call(kernel if skip else body, out_shape=[jax.ShapeDtypeStruct(...  30.3 us
    all_to_all x5, starting transfers between devices, exchange(): return lax.all_to_all(values, axis, 0, 0, tiled=True)  27.6 us
    ppermute x12, waiting for transfers between devices, shift(): lax.ppermute(values[k], axis, turn(len(values), k))  23 us
    all_to_all x5, waiting for transfers between devices, exchange(): return lax.all_to_all(values, axis, 0, 0, tiled=True)  22.7 us
    ppermute x12, starting transfers between devices, shift(): lax.ppermute(values[k], axis, turn(len(values), k))  16.8 us
    ppermute x3, waiting for transfers between devices, gather_ring(): back = lax.ppermute(back, 'mp', turn(count, 1))  11.5 us
    unnamed x74, local copies, waits for them, and re-layouts  11.4 us
  transfers between devices with their start and end apart: 27, of which 19 were waited for; matrix products, arithmetic and copies ran while one was open for 6% of the time, Pallas kernels for 1%

profile of v4, /device:TPU:8, one launch (start us, length us, event | category | flops | bytes accessed | tf_op | source)
XLA Modules:
  0.0 240.3 jit_solution(8725816649004113227)
XLA Ops:
  0.6 4.5 %shard_map.153 = (bf16[192,1536]{1,0:T(8,128)(2,1)}, bf16[192,768]{1,0:T(8,128)(2,1)}, f32[192,768]{1,0:T(8,128)}, bf16[8,288,128]{2,1,0:T(8,128)(2,1)}) custom-call(bf16[192,1536]{1,0:T(8,128)(2,1)} %far_x.1, bf16[1536,768]{1,0:T(8,128)(2,1)} %far_one.1, bf16[768,1536]{1,0:T(8,128)(2,1)} %two_ref.1), custom_call_target="tpu_custom_call" | custom-call | tf_op jit(solution)/shard_map/pallas_call | solution.py:49
  5.2 8.6 %all-to-all-start = ((bf16[8,288,128]{2,1,0:T(8,128)(2,1)}), bf16[8,288,128]{2,1,0:T(8,128)(2,1)S(1)}, u32[]{:S(2)}, u32[]{:S(2)}) async-start(bf16[8,288,128]{2,1,0:T(8,128)(2,1)} %get-tuple-element.55), calls=%async_computation | async-start | bytes 1179648 | tf_op jit(solution)/shard_map/all_to_all | solution.py:33
  14.4 1.2 copy.42
  17.8 1.2 constant_dynamic-slice_fusion.3
  19.2 13.5 %all-to-all-done.refs_9_ = bf16[8,288,128]{2,1,0:T(8,128)(2,1)S(1)} async-done(((bf16[8,288,128]{2,1,0:T(8,128)(2,1)}), bf16[8,288,128]{2,1,0:T(8,128)(2,1)S(1)}, u32[]{:S(2)}, u32[]{:S(2)}) %all-to-all-start) | async-done | bytes 589856 | tf_op jit(solution)/shard_map/all_to_all | solution.py:33
  33.0 14.8 %all_to_all.45 = bf16[32,16,256]{2,1,0:T(8,128)(2,1)S(1)} all-to-all(bf16[32,16,256]{2,1,0:T(8,128)(2,1)S(1)} %bitcast.56), channel_id=1, replica_groups=mesh['line'=4,'column'=4,'core'=2,'mp'=8] {'line','column','core'}, dimensions={0} | all-to-all | bytes 524288 | tf_op jit(solution)/shard_map/all_to_all | solution.py:33
  48.8 2.7 %collective-permute-start.1 = (bf16[208,384]{1,0:T(8,128)(2,1)S(1)}, bf16[208,384]{1,0:T(8,128)(2,1)S(1)}, u32[]{:S(2)}, u32[]{:S(2)}) collective-permute-start(bf16[208,384]{1,0:T(8,128)(2,1)S(1)} %get-tuple-element.57.rest_0_.refs_4_), channel_id=1, source_target_pairs={{0,7},{1,0},{2,1},{3,2},{4,3},{5,4},{6,5},{7,6},{8,15},{9,8},{10,9... | collective-permute-start | bytes 479240 | tf_op jit(solution)/shard_map/ppermute | solution.py:83
  51.5 4.5 %collective-permute-done.rest_1_ = bf16[208,384]{1,0:T(8,128)(2,1)S(1)} collective-permute-done((bf16[208,384]{1,0:T(8,128)(2,1)S(1)}, bf16[208,384]{1,0:T(8,128)(2,1)S(1)}, u32[]{:S(2)}, u32[]{:S(2)}) %collective-permute-start) | collective-permute-done | bytes 159776 | tf_op jit(solution)/shard_map/ppermute | solution.py:82
  56.0 3.2 %collective-permute-start.3 = (bf16[208,384]{1,0:T(8,128)(2,1)S(1)}, bf16[208,384]{1,0:T(8,128)(2,1)S(1)}, u32[]{:S(2)}, u32[]{:S(2)}) collective-permute-start(bf16[208,384]{1,0:T(8,128)(2,1)S(1)} %collective-permute-done.1.rest_2_), channel_id=1, source_target_pairs={{0,7},{1,0},{2,1},{3,2},{4,3},{5,4},{6,5},{7,6},{8,15},{9,8},{10,9... | collective-permute-start | bytes 479240 | tf_op jit(solution)/shard_map/ppermute | solution.py:83
  59.2 3.7 %collective-permute-done.2.rest_3_ = bf16[208,384]{1,0:T(8,128)(2,1)S(1)} collective-permute-done((bf16[208,384]{1,0:T(8,128)(2,1)S(1)}, bf16[208,384]{1,0:T(8,128)(2,1)S(1)}, u32[]{:S(2)}, u32[]{:S(2)}) %collective-permute-start.2) | collective-permute-done | bytes 159776 | tf_op jit(solution)/shard_map/ppermute | solution.py:82
  63.0 3.2 %collective-permute-start.5 = (bf16[208,384]{1,0:T(8,128)(2,1)S(1)}, bf16[208,384]{1,0:T(8,128)(2,1)S(1)}, u32[]{:S(2)}, u32[]{:S(2)}) collective-permute-start(bf16[208,384]{1,0:T(8,128)(2,1)S(1)} %collective-permute-done.3.rest_4_), channel_id=1, source_target_pairs={{0,7},{1,0},{2,1},{3,2},{4,3},{5,4},{6,5},{7,6},{8,15},{9,8},{10,9... | collective-permute-start | bytes 479240 | tf_op jit(solution)/shard_map/ppermute | solution.py:83
  66.2 3.2 %collective-permute-done.4.rest_5_ = bf16[208,384]{1,0:T(8,128)(2,1)S(1)} collective-permute-done((bf16[208,384]{1,0:T(8,128)(2,1)S(1)}, bf16[208,384]{1,0:T(8,128)(2,1)S(1)}, u32[]{:S(2)}, u32[]{:S(2)}) %collective-permute-start.4) | collective-permute-done | bytes 159776 | tf_op jit(solution)/shard_map/ppermute | solution.py:82
  69.6 3.5 %collective-permute-start.7 = (bf16[96,384]{1,0:T(8,128)(2,1)S(1)}, bf16[96,384]{1,0:T(8,128)(2,1)S(1)}, u32[]{:S(2)}, u32[]{:S(2)}) collective-permute-start(bf16[96,384]{1,0:T(8,128)(2,1)S(1)} %slice.51), channel_id=1, source_target_pairs={{0,7},{1,0},{2,1},{3,2},{4,3},{5,4},{6,5},{7,6},{8,15},{9,8},{10,9... | collective-permute-start | bytes 221192 | tf_op jit(solution)/shard_map/ppermute | solution.py:87
  73.1 2.0 collective-permute-done.7.rest_8_
  75.9 7.0 %shard_map.156 = (bf16[1536,384]{1,0:T(8,128)(2,1)}, f32[2,3,96,384]{3,2,1,0:T(8,128)}, f32[2,384,384]{2,1,0:T(8,128)}, f32[2,384]{1,0:T(2,128)}, f32[2,2,384]{2...) custom-call(s32[1]{0:T(128)} %bitcast.1.here, ...), custom_call_target="tpu_custom_call" | custom-call | tf_op jit(solution)/shard_map/pallas_call | solution.py:49
  82.9 12.9 %all_to_all.46.parts_ref = f32[8,1,1536]{2,1,0:T(1,128)S(1)} all-to-all(f32[8,1,1536]{2,1,0:T(1,128)} %get-tuple-element.58), channel_id=1, replica_groups=mesh['line'=4,'column'=4,'core'=2,'mp'=8] {'mp'}, dimensions={0} | all-to-all | bytes 98304 | tf_op jit(solution)/shard_map/all_to_all | solution.py:33
  96.7 1.0 shard_map.157
  99.1 4.9 %all-to-all-start.3 = ((f32[32,1,128]{2,1,0:T(1,128)}), f32[32,1,128]{2,1,0:T(1,128)S(1)}, u32[]{:S(2)}, u32[]{:S(2)}) async-start(f32[32,1,128]{2,1,0:T(1,128)} %get-tuple-element.60), calls=%async_computation.3 | async-start | bytes 32768 | tf_op jit(solution)/shard_map/all_to_all | solution.py:33
  104.0 1.2 copy.49.far_query_weights
  105.1 2.2 copy.50.far_key_weights
  107.4 1.3 copy.51.far_value_weights
  110.6 6.3 %shard_map.158 = (f32[1,1]{1,0:T(1,128)}, f32[1,1536]{1,0:T(1,128)}, f32[1,192]{1,0:T(1,128)}, bf16[576,384]{1,0:T(8,128)(2,1)}, bf16[8,208,384]{2,1,0:T(8,128)(2,1)}) custom-call(s32[1]{0:T(128)} %bitcast.owner, f32[32,128]{1,0:T(8,128)} %bitcast.66, s32[32,1]{1,0:T(8,128)} %copy.48.pair_ref, f32[2,1536]{1,0:T(2,128)} %copy-done.12, f32[32,1536]{1,0:T(8,128)} %copy-done.8, ...), custom_call_target="tpu_custom_call" | custom-call | tf_op jit(solution)/shard_map/pallas_call | solution.py:49
  117.0 4.4 %all-to-all-start.4 = ((bf16[8,208,384]{2,1,0:T(8,128)(2,1)}), bf16[8,208,384]{2,1,0:T(8,128)(2,1)}, u32[]{:S(2)}, u32[]{:S(2)}) async-start(bf16[8,208,384]{2,1,0:T(8,128)(2,1)} %get-tuple-element.83), calls=%async_computation.4 | async-start | bytes 2555904 | tf_op jit(solution)/shard_map/all_to_all | solution.py:33
  122.4 1.4 shard_map.159
  124.8 1.4 collective-permute-done.8.got_ref
  127.2 1.6 shard_map.160
  129.6 2.7 %collective-permute-start.10 = (bf16[4,48,384]{2,1,0:T(8,128)(2,1)S(1)}, bf16[4,48,384]{2,1,0:T(8,128)(2,1)S(1)}, u32[]{:S(2)}, u32[]{:S(2)}) collective-permute-start(bf16[4,48,384]{2,1,0:T(8,128)(2,1)S(1)} %get-tuple-element.73), channel_id=1, source_target_pairs={{0,32},{16,48},{32,0},{48,16},{1,33},{17,49},{33,1},{49,17},{2,34}... | collective-permute-start | bytes 442376 | tf_op jit(solution)/shard_map/ppermute | solution.py:732
  132.3 1.5 collective-permute-start.11
  133.8 2.7 %collective-permute-done.9.refs_1_ = bf16[4,48,384]{2,1,0:T(8,128)(2,1)S(1)} collective-permute-done((bf16[4,48,384]{2,1,0:T(8,128)(2,1)S(1)}, bf16[4,48,384]{2,1,0:T(8,128)(2,1)S(1)}, u32[]{:S(2)}, u32[]{:S(2)}) %collective-permute-start.9) | collective-permute-done | bytes 147488 | tf_op jit(solution)/shard_map/ppermute | solution.py:732
  136.6 2.8 %collective-permute-done.10.refs_2_ = bf16[4,48,384]{2,1,0:T(8,128)(2,1)S(1)} collective-permute-done((bf16[4,48,384]{2,1,0:T(8,128)(2,1)S(1)}, bf16[4,48,384]{2,1,0:T(8,128)(2,1)S(1)}, u32[]{:S(2)}, u32[]{:S(2)}) %collective-permute-start.10) | collective-permute-done | bytes 147488 | tf_op jit(solution)/shard_map/ppermute | solution.py:732
  139.8 1.5 collective-permute-start.14
  141.3 1.1 collective-permute-start.13
  142.4 1.8 collective-permute-start.12
  144.7 2.1 collective-permute-done.13
  146.8 8.6 %all-to-all-done.4.refs_7_ = bf16[8,208,384]{2,1,0:T(8,128)(2,1)} async-done(((bf16[8,208,384]{2,1,0:T(8,128)(2,1)}), bf16[8,208,384]{2,1,0:T(8,128)(2,1)}, u32[]{:S(2)}, u32[]{:S(2)}) %all-to-all-start.4) | async-done | bytes 1277984 | tf_op jit(solution)/shard_map/all_to_all | solution.py:33
  155.4 1.8 shard_map.162
  157.2 14.3 %all_to_all.47 = bf16[32,16,192]{2,1,0:T(8,128)(2,1)S(1)} all-to-all(bf16[32,16,192]{2,1,0:T(8,128)(2,1)S(1)} %bitcast.59), channel_id=1, replica_groups=mesh['line'=4,'column'=4,'core'=2,'mp'=8] {'line','column','core'}, dimensions={0} | all-to-all | bytes 393216 | tf_op jit(solution)/shard_map/all_to_all | solution.py:33
  171.9 22.3 %all_to_all.48.parts_ref = bf16[8,288,128]{2,1,0:T(8,128)(2,1)S(1)} all-to-all(bf16[8,288,128]{2,1,0:T(8,128)(2,1)S(1)} %shard_map.163), channel_id=1, replica_groups=mesh['line'=4,'column'=4,'core'=2,'mp'=8] {'mp'}, dimensions={0} | all-to-all | bytes 1179648 | tf_op jit(solution)/shard_map/all_to_all | solution.py:33
  194.2 2.1 shard_map.164
  196.4 4.5 %collective-permute-done.15.got_ref = bf16[16,96,768]{2,1,0:T(8,128)(2,1)S(1)} collective-permute-done((bf16[16,96,768]{2,1,0:T(8,128)(2,1)S(1)}, bf16[16,96,768]{2,1,0:T(8,128)(2,1)S(1)}, u32[]{:S(2)}, u32[]{:S(2)}) %collective-permute-start.15) | collective-permute-done | bytes 2359328 | tf_op jit(solution)/shard_map/ppermute | solution.py:784
  200.9 1.7 shard_map.165
  203.7 4.9 %all-to-all-start.7 = ((bf16[4,4,48,768]{3,2,1,0:T(8,128)(2,1)}), bf16[4,4,48,768]{3,2,1,0:T(8,128)(2,1)S(1)}, u32[]{:S(2)}, u32[]{:S(2)}) async-start(bf16[4,4,48,768]{3,2,1,0:T(8,128)(2,1)} %copy-done.5), calls=%async_computation.7 | async-start | bytes 2359296 | tf_op jit(solution)/shard_map/all_to_all | solution.py:33
  209.3 2.1 collective-permute-start.17
  213.4 11.7 %collective-permute-done.16.refs_1_ = bf16[4,48,768]{2,1,0:T(8,128)(2,1)S(1)} collective-permute-done((bf16[4,48,768]{2,1,0:T(8,128)(2,1)}, bf16[4,48,768]{2,1,0:T(8,128)(2,1)S(1)}, u32[]{:S(2)}, u32[]{:S(2)}) %collective-permute-start.16) | collective-permute-done | bytes 294944 | tf_op jit(solution)/shard_map/ppermute | solution.py:732
  226.6 4.8 %all-to-all-start.8 = ((bf16[4,48,768]{2,1,0:T(8,128)(2,1)}), bf16[4,48,768]{2,1,0:T(8,128)(2,1)S(1)}, u32[]{:S(2)}, u32[]{:S(2)}) async-start(bf16[4,48,768]{2,1,0:T(8,128)(2,1)} %get-tuple-element.92), calls=%async_computation.8 | async-start | bytes 589824 | tf_op jit(solution)/shard_map/all_to_all | solution.py:33
  231.8 3.4 %collective-permute-start.20 = (bf16[48,768]{1,0:T(8,128)(2,1)S(1)}, bf16[48,768]{1,0:T(8,128)(2,1)S(1)}, u32[]{:S(2)}, u32[]{:S(2)}) collective-permute-start(bf16[48,768]{1,0:T(8,128)(2,1)S(1)} %get-tuple-element.95), channel_id=1, source_target_pairs={{0,32},{16,48},{32,0},{48,16},{1,33},{17,49},{33,1},{49,17},{2,34}... | collective-permute-start | bytes 221192 | tf_op jit(solution)/shard_map/ppermute | solution.py:732
  237.2 1.1 collective-permute-done.20.refs_2_
  238.3 1.2 collective-permute-done.21.refs_3_
  (155 shorter events, 23.1 us)
Async XLA Ops:
  5.2 8.6 %copy-start.16 = (bf16[192,1536]{1,0:T(8,128)(2,1)S(1)}, bf16[192,1536]{1,0:T(8,128)(2,1)}, u32[]{:S(2)}) copy-start(bf16[192,1536]{1,0:T(8,128)(2,1)} %far_x.1) | copy-start | bytes 1769476
  5.2 9.3 %copy-start.18 = (bf16[192,1536]{1,0:T(8,128)(2,1)S(1)}, bf16[192,1536]{1,0:T(8,128)(2,1)}, u32[]{:S(2)}) copy-start(bf16[192,1536]{1,0:T(8,128)(2,1)} %get-tuple-element.53) | copy-start | bytes 1769476
  5.2 27.5 %all-to-all-start = ((bf16[8,288,128]{2,1,0:T(8,128)(2,1)}), bf16[8,288,128]{2,1,0:T(8,128)(2,1)S(1)}, u32[]{:S(2)}, u32[]{:S(2)}) async-start(bf16[8,288,128]{2,1,0:T(8,128)(2,1)} %get-tuple-element.55), calls=%async_computation | async-start | bytes 1179648 | tf_op jit(solution)/shard_map/all_to_all | solution.py:33
  13.8 1.8 copy-start.17
  48.2 27.1 %copy-start.6 = (bf16[208,384]{1,0:T(8,128)(2,1)}, bf16[208,384]{1,0:T(8,128)(2,1)S(1)}, u32[]{:S(2)}) copy-start(bf16[208,384]{1,0:T(8,128)(2,1)S(1)} %get-tuple-element.57.rest_0_.refs_4_) | copy-start | bytes 479236
  48.2 27.1 %copy-start.10 = (f32[1,384]{1,0:T(1,128)}, f32[1,384]{1,0:T(1,128)S(1)}, u32[]{:S(2)}) copy-start(f32[1,384]{1,0:T(1,128)S(1)} %get-tuple-element.56.valid_ref.refs_2_) | copy-start | bytes 4612
  48.2 7.8 %collective-permute-start = (bf16[208,384]{1,0:T(8,128)(2,1)S(1)}, bf16[208,384]{1,0:T(8,128)(2,1)S(1)}, u32[]{:S(2)}, u32[]{:S(2)}) collective-permute-start(bf16[208,384]{1,0:T(8,128)(2,1)S(1)} %get-tuple-element.57.rest_0_.refs_4_), channel_id=1, source_target_pairs={{0,1},{1,2},{2,3},{3,4},{4,5},{5,6},{6,7},{7,0},{8,9},{9,10},{10,1... | collective-permute-start | bytes 479240 | tf_op jit(solution)/shard_map/ppermute | solution.py:82
  48.8 7.2 %collective-permute-start.1 = (bf16[208,384]{1,0:T(8,128)(2,1)S(1)}, bf16[208,384]{1,0:T(8,128)(2,1)S(1)}, u32[]{:S(2)}, u32[]{:S(2)}) collective-permute-start(bf16[208,384]{1,0:T(8,128)(2,1)S(1)} %get-tuple-element.57.rest_0_.refs_4_), channel_id=1, source_target_pairs={{0,7},{1,0},{2,1},{3,2},{4,3},{5,4},{6,5},{7,6},{8,15},{9,8},{10,9... | collective-permute-start | bytes 479240 | tf_op jit(solution)/shard_map/ppermute | solution.py:83
  56.0 19.3 %copy-start.21 = (bf16[208,384]{1,0:T(8,128)(2,1)}, bf16[208,384]{1,0:T(8,128)(2,1)S(1)}, u32[]{:S(2)}) copy-start(bf16[208,384]{1,0:T(8,128)(2,1)S(1)} %collective-permute-done.rest_1_) | copy-start | bytes 479236
  56.0 7.0 %collective-permute-start.2 = (bf16[208,384]{1,0:T(8,128)(2,1)S(1)}, bf16[208,384]{1,0:T(8,128)(2,1)S(1)}, u32[]{:S(2)}, u32[]{:S(2)}) collective-permute-start(bf16[208,384]{1,0:T(8,128)(2,1)S(1)} %collective-permute-done.rest_1_), channel_id=1, source_target_pairs={{0,1},{1,2},{2,3},{3,4},{4,5},{5,6},{6,7},{7,0},{8,9},{9,10},{10,1... | collective-permute-start | bytes 479240 | tf_op jit(solution)/shard_map/ppermute | solution.py:82
  56.0 19.3 %copy-start.22 = (bf16[208,384]{1,0:T(8,128)(2,1)}, bf16[208,384]{1,0:T(8,128)(2,1)S(1)}, u32[]{:S(2)}) copy-start(bf16[208,384]{1,0:T(8,128)(2,1)S(1)} %collective-permute-done.1.rest_2_) | copy-start | bytes 479236
  56.0 7.0 %collective-permute-start.3 = (bf16[208,384]{1,0:T(8,128)(2,1)S(1)}, bf16[208,384]{1,0:T(8,128)(2,1)S(1)}, u32[]{:S(2)}, u32[]{:S(2)}) collective-permute-start(bf16[208,384]{1,0:T(8,128)(2,1)S(1)} %collective-permute-done.1.rest_2_), channel_id=1, source_target_pairs={{0,7},{1,0},{2,1},{3,2},{4,3},{5,4},{6,5},{7,6},{8,15},{9,8},{10,9... | collective-permute-start | bytes 479240 | tf_op jit(solution)/shard_map/ppermute | solution.py:83
  63.0 12.3 %copy-start.23 = (bf16[208,384]{1,0:T(8,128)(2,1)}, bf16[208,384]{1,0:T(8,128)(2,1)S(1)}, u32[]{:S(2)}) copy-start(bf16[208,384]{1,0:T(8,128)(2,1)S(1)} %collective-permute-done.2.rest_3_) | copy-start | bytes 479236
  63.0 6.5 %collective-permute-start.4 = (bf16[208,384]{1,0:T(8,128)(2,1)S(1)}, bf16[208,384]{1,0:T(8,128)(2,1)S(1)}, u32[]{:S(2)}, u32[]{:S(2)}) collective-permute-start(bf16[208,384]{1,0:T(8,128)(2,1)S(1)} %collective-permute-done.2.rest_3_), channel_id=1, source_target_pairs={{0,1},{1,2},{2,3},{3,4},{4,5},{5,6},{6,7},{7,0},{8,9},{9,10},{10,1... | collective-permute-start | bytes 479240 | tf_op jit(solution)/shard_map/ppermute | solution.py:82
  63.0 12.3 %copy-start.24 = (bf16[208,384]{1,0:T(8,128)(2,1)}, bf16[208,384]{1,0:T(8,128)(2,1)S(1)}, u32[]{:S(2)}) copy-start(bf16[208,384]{1,0:T(8,128)(2,1)S(1)} %collective-permute-done.3.rest_4_) | copy-start | bytes 479236
  63.0 6.6 %collective-permute-start.5 = (bf16[208,384]{1,0:T(8,128)(2,1)S(1)}, bf16[208,384]{1,0:T(8,128)(2,1)S(1)}, u32[]{:S(2)}, u32[]{:S(2)}) collective-permute-start(bf16[208,384]{1,0:T(8,128)(2,1)S(1)} %collective-permute-done.3.rest_4_), channel_id=1, source_target_pairs={{0,7},{1,0},{2,1},{3,2},{4,3},{5,4},{6,5},{7,6},{8,15},{9,8},{10,9... | collective-permute-start | bytes 479240 | tf_op jit(solution)/shard_map/ppermute | solution.py:83
  69.5 5.8 %copy-start.19 = (bf16[208,384]{1,0:T(8,128)(2,1)}, bf16[208,384]{1,0:T(8,128)(2,1)S(1)}, u32[]{:S(2)}) copy-start(bf16[208,384]{1,0:T(8,128)(2,1)S(1)} %collective-permute-done.4.rest_5_) | copy-start | bytes 479236
  69.5 5.8 %collective-permute-start.6 = (bf16[112,384]{1,0:T(8,128)(2,1)S(1)}, bf16[112,384]{1,0:T(8,128)(2,1)S(1)}, u32[]{:S(2)}, u32[]{:S(2)}) collective-permute-start(bf16[112,384]{1,0:T(8,128)(2,1)S(1)} %slice.50), channel_id=1, source_target_pairs={{0,1},{1,2},{2,3},{3,4},{4,5},{5,6},{6,7},{7,0},{8,9},{9,10},{10,1... | collective-permute-start | bytes 258056 | tf_op jit(solution)/shard_map/ppermute | solution.py:86
  69.6 5.7 %copy-start.20 = (bf16[208,384]{1,0:T(8,128)(2,1)}, bf16[208,384]{1,0:T(8,128)(2,1)S(1)}, u32[]{:S(2)}) copy-start(bf16[208,384]{1,0:T(8,128)(2,1)S(1)} %collective-permute-done.5.rest_6_) | copy-start | bytes 479236
  69.6 5.4 %collective-permute-start.7 = (bf16[96,384]{1,0:T(8,128)(2,1)S(1)}, bf16[96,384]{1,0:T(8,128)(2,1)S(1)}, u32[]{:S(2)}, u32[]{:S(2)}) collective-permute-start(bf16[96,384]{1,0:T(8,128)(2,1)S(1)} %slice.51), channel_id=1, source_target_pairs={{0,7},{1,0},{2,1},{3,2},{4,3},{5,4},{6,5},{7,6},{8,15},{9,8},{10,9... | collective-permute-start | bytes 221192 | tf_op jit(solution)/shard_map/ppermute | solution.py:87
  75.9 28.0 %copy-start.14 = (bf16[1536,192]{0,1:T(8,128)(2,1)S(1)}, bf16[1536,192]{0,1:T(8,128)(2,1)}, u32[]{:S(2)}) copy-start(bf16[1536,192]{0,1:T(8,128)(2,1)} %param.16) | copy-start | bytes 1769476
  99.1 11.0 %all-to-all-start.3 = ((f32[32,1,128]{2,1,0:T(1,128)}), f32[32,1,128]{2,1,0:T(1,128)S(1)}, u32[]{:S(2)}, u32[]{:S(2)}) async-start(f32[32,1,128]{2,1,0:T(1,128)} %get-tuple-element.60), calls=%async_computation.3 | async-start | bytes 32768 | tf_op jit(solution)/shard_map/all_to_all | solution.py:33
  103.9 3.4 %copy-start.15 = (bf16[1536,192]{0,1:T(8,128)(2,1)S(1)}, bf16[1536,192]{0,1:T(8,128)(2,1)}, u32[]{:S(2)}) copy-start(bf16[1536,192]{0,1:T(8,128)(2,1)} %param.18) | copy-start | bytes 1769476
  105.1 3.5 %copy-start.32 = (s32[32]{0:T(128)S(1)}, s32[32]{0:T(128)}, u32[]{:S(2)}) copy-start(s32[32]{0:T(128)} %param.12) | copy-start | bytes 388
  117.0 4.4 %copy-start = (bf16[1536,384]{1,0:T(8,128)(2,1)S(1)}, bf16[1536,384]{1,0:T(8,128)(2,1)}, u32[]{:S(2)}) copy-start(bf16[1536,384]{1,0:T(8,128)(2,1)} %get-tuple-element.67.far_norm.norm_ref) | copy-start | bytes 3538948
  117.0 38.4 %all-to-all-start.4 = ((bf16[8,208,384]{2,1,0:T(8,128)(2,1)}), bf16[8,208,384]{2,1,0:T(8,128)(2,1)}, u32[]{:S(2)}, u32[]{:S(2)}) async-start(bf16[8,208,384]{2,1,0:T(8,128)(2,1)} %get-tuple-element.83), calls=%async_computation.4 | async-start | bytes 2555904 | tf_op jit(solution)/shard_map/all_to_all | solution.py:33
  121.4 2.4 %copy-start.28 = (f32[2,384]{1,0:T(2,128)S(1)}, f32[2,384]{1,0:T(2,128)}, u32[]{:S(2)}) copy-start(f32[2,384]{1,0:T(2,128)} %get-tuple-element.64.mass_ref) | copy-start | bytes 9220
  123.8 2.3 collective-permute-start.8
  128.8 26.6 %copy-start.7 = (bf16[208,384]{1,0:T(8,128)(2,1)S(1)}, bf16[208,384]{1,0:T(8,128)(2,1)}, u32[]{:S(2)}) copy-start(bf16[208,384]{1,0:T(8,128)(2,1)} %copy-done.6) | copy-start | bytes 479236
  128.8 26.6 %copy-start.11 = (f32[1,384]{1,0:T(1,128)S(1)}, f32[1,384]{1,0:T(1,128)}, u32[]{:S(2)}) copy-start(f32[1,384]{1,0:T(1,128)} %copy-done.10) | copy-start | bytes 4612
  128.8 26.6 %copy-start.13 = (f32[2,384]{1,0:T(2,128)S(1)}, f32[2,384]{1,0:T(2,128)}, u32[]{:S(2)}) copy-start(f32[2,384]{1,0:T(2,128)} %get-tuple-element.80.refs_3_) | copy-start | bytes 9220
  128.8 7.8 %collective-permute-start.9 = (bf16[4,48,384]{2,1,0:T(8,128)(2,1)S(1)}, bf16[4,48,384]{2,1,0:T(8,128)(2,1)S(1)}, u32[]{:S(2)}, u32[]{:S(2)}) collective-permute-start(bf16[4,48,384]{2,1,0:T(8,128)(2,1)S(1)} %get-tuple-element.72), channel_id=1, source_target_pairs={{0,16},{16,32},{32,48},{48,0},{1,17},{17,33},{33,49},{49,1},{2,18}... | collective-permute-start | bytes 442376 | tf_op jit(solution)/shard_map/ppermute | solution.py:732
  129.6 9.7 %collective-permute-start.10 = (bf16[4,48,384]{2,1,0:T(8,128)(2,1)S(1)}, bf16[4,48,384]{2,1,0:T(8,128)(2,1)S(1)}, u32[]{:S(2)}, u32[]{:S(2)}) collective-permute-start(bf16[4,48,384]{2,1,0:T(8,128)(2,1)S(1)} %get-tuple-element.73), channel_id=1, source_target_pairs={{0,32},{16,48},{32,0},{48,16},{1,33},{17,49},{33,1},{49,17},{2,34}... | collective-permute-start | bytes 442376 | tf_op jit(solution)/shard_map/ppermute | solution.py:732
  132.3 7.4 %collective-permute-start.11 = (bf16[4,48,384]{2,1,0:T(8,128)(2,1)S(1)}, bf16[4,48,384]{2,1,0:T(8,128)(2,1)S(1)}, u32[]{:S(2)}, u32[]{:S(2)}) collective-permute-start(bf16[4,48,384]{2,1,0:T(8,128)(2,1)S(1)} %get-tuple-element.74), channel_id=1, source_target_pairs={{0,48},{16,0},{32,16},{48,32},{1,49},{17,1},{33,17},{49,33},{2,50}... | collective-permute-start | bytes 442376 | tf_op jit(solution)/shard_map/ppermute | solution.py:732
  139.8 4.9 %collective-permute-start.14 = (bf16[48,384]{1,0:T(8,128)(2,1)S(1)}, bf16[48,384]{1,0:T(8,128)(2,1)S(1)}, u32[]{:S(2)}, u32[]{:S(2)}) collective-permute-start(bf16[48,384]{1,0:T(8,128)(2,1)S(1)} %get-tuple-element.78), channel_id=1, source_target_pairs={{0,192},{64,0},{128,64},{192,128},{1,193},{65,1},{129,65},{193,129... | collective-permute-start | bytes 110600 | tf_op jit(solution)/shard_map/ppermute | solution.py:732
  141.3 5.5 %collective-permute-start.13 = (bf16[48,384]{1,0:T(8,128)(2,1)S(1)}, bf16[48,384]{1,0:T(8,128)(2,1)S(1)}, u32[]{:S(2)}, u32[]{:S(2)}) collective-permute-start(bf16[48,384]{1,0:T(8,128)(2,1)S(1)} %get-tuple-element.77), channel_id=1, source_target_pairs={{0,128},{64,192},{128,0},{192,64},{1,129},{65,193},{129,1},{193,65... | collective-permute-start | bytes 110600 | tf_op jit(solution)/shard_map/ppermute | solution.py:732
  142.4 4.3 %collective-permute-start.12 = (bf16[48,384]{1,0:T(8,128)(2,1)S(1)}, bf16[48,384]{1,0:T(8,128)(2,1)S(1)}, u32[]{:S(2)}, u32[]{:S(2)}) collective-permute-start(bf16[48,384]{1,0:T(8,128)(2,1)S(1)} %get-tuple-element.76), channel_id=1, source_target_pairs={{0,64},{64,128},{128,192},{192,0},{1,65},{65,129},{129,193},{193,1... | collective-permute-start | bytes 110600 | tf_op jit(solution)/shard_map/ppermute | solution.py:732
  157.2 36.9 %copy-start.1 = (bf16[768,1536]{1,0:T(8,128)(2,1)S(1)}, bf16[768,1536]{1,0:T(8,128)(2,1)}, u32[]{:S(2)}) copy-start(bf16[768,1536]{1,0:T(8,128)(2,1)} %two_ref.1) | copy-start | bytes 7077892
  171.6 22.6 %copy-start.4 = (bf16[192,768]{1,0:T(8,128)(2,1)S(1)}, bf16[192,768]{1,0:T(8,128)(2,1)}, u32[]{:S(2)}) copy-start(bf16[192,768]{1,0:T(8,128)(2,1)} %get-tuple-element.69.hidden_ref) | copy-start | bytes 884740
  196.3 4.6 %collective-permute-start.15 = (bf16[16,96,768]{2,1,0:T(8,128)(2,1)S(1)}, bf16[16,96,768]{2,1,0:T(8,128)(2,1)S(1)}, u32[]{:S(2)}, u32[]{:S(2)}) collective-permute-start(bf16[16,96,768]{2,1,0:T(8,128)(2,1)S(1)} %get-tuple-element.86), channel_id=1, source_target_pairs={{0,8},{8,0},{1,9},{9,1},{2,10},{10,2},{3,11},{11,3},{4,12},{12,4},... | collective-permute-start | bytes 7077896 | tf_op jit(solution)/shard_map/ppermute | solution.py:784
  203.7 22.0 %all-to-all-start.7 = ((bf16[4,4,48,768]{3,2,1,0:T(8,128)(2,1)}), bf16[4,4,48,768]{3,2,1,0:T(8,128)(2,1)S(1)}, u32[]{:S(2)}, u32[]{:S(2)}) async-start(bf16[4,4,48,768]{3,2,1,0:T(8,128)(2,1)} %copy-done.5), calls=%async_computation.7 | async-start | bytes 2359296 | tf_op jit(solution)/shard_map/all_to_all | solution.py:33
  208.6 16.5 %collective-permute-start.16 = (bf16[4,48,768]{2,1,0:T(8,128)(2,1)}, bf16[4,48,768]{2,1,0:T(8,128)(2,1)S(1)}, u32[]{:S(2)}, u32[]{:S(2)}) collective-permute-start(bf16[4,48,768]{2,1,0:T(8,128)(2,1)} %get-tuple-element.88), channel_id=1, source_target_pairs={{0,16},{16,32},{32,48},{48,0},{1,17},{17,33},{33,49},{49,1},{2,18}... | collective-permute-start | bytes 884744 | tf_op jit(solution)/shard_map/ppermute | solution.py:732
  209.3 15.8 %collective-permute-start.17 = (bf16[4,48,768]{2,1,0:T(8,128)(2,1)}, bf16[4,48,768]{2,1,0:T(8,128)(2,1)S(1)}, u32[]{:S(2)}, u32[]{:S(2)}) collective-permute-start(bf16[4,48,768]{2,1,0:T(8,128)(2,1)} %get-tuple-element.89), channel_id=1, source_target_pairs={{0,32},{16,48},{32,0},{48,16},{1,33},{17,49},{33,1},{49,17},{2,34}... | collective-permute-start | bytes 884744 | tf_op jit(solution)/shard_map/ppermute | solution.py:732
  211.4 14.2 %collective-permute-start.18 = (bf16[4,48,768]{2,1,0:T(8,128)(2,1)S(1)}, bf16[4,48,768]{2,1,0:T(8,128)(2,1)S(1)}, u32[]{:S(2)}, u32[]{:S(2)}) collective-permute-start(bf16[4,48,768]{2,1,0:T(8,128)(2,1)S(1)} %get-tuple-element.90), channel_id=1, source_target_pairs={{0,48},{16,0},{32,16},{48,32},{1,49},{17,1},{33,17},{49,33},{2,50}... | collective-permute-start | bytes 884744 | tf_op jit(solution)/shard_map/ppermute | solution.py:732
  226.6 12.9 %all-to-all-start.8 = ((bf16[4,48,768]{2,1,0:T(8,128)(2,1)}), bf16[4,48,768]{2,1,0:T(8,128)(2,1)S(1)}, u32[]{:S(2)}, u32[]{:S(2)}) async-start(bf16[4,48,768]{2,1,0:T(8,128)(2,1)} %get-tuple-element.92), calls=%async_computation.8 | async-start | bytes 589824 | tf_op jit(solution)/shard_map/all_to_all | solution.py:33
  231.4 5.8 %collective-permute-start.19 = (bf16[48,768]{1,0:T(8,128)(2,1)S(1)}, bf16[48,768]{1,0:T(8,128)(2,1)S(1)}, u32[]{:S(2)}, u32[]{:S(2)}) collective-permute-start(bf16[48,768]{1,0:T(8,128)(2,1)S(1)} %get-tuple-element.94), channel_id=1, source_target_pairs={{0,16},{16,32},{32,48},{48,0},{1,17},{17,33},{33,49},{49,1},{2,18}... | collective-permute-start | bytes 221192 | tf_op jit(solution)/shard_map/ppermute | solution.py:732
  231.8 6.5 %collective-permute-start.20 = (bf16[48,768]{1,0:T(8,128)(2,1)S(1)}, bf16[48,768]{1,0:T(8,128)(2,1)S(1)}, u32[]{:S(2)}, u32[]{:S(2)}) collective-permute-start(bf16[48,768]{1,0:T(8,128)(2,1)S(1)} %get-tuple-element.95), channel_id=1, source_target_pairs={{0,32},{16,48},{32,0},{48,16},{1,33},{17,49},{33,1},{49,17},{2,34}... | collective-permute-start | bytes 221192 | tf_op jit(solution)/shard_map/ppermute | solution.py:732
  235.2 4.4 %collective-permute-start.21 = (bf16[48,768]{1,0:T(8,128)(2,1)S(1)}, bf16[48,768]{1,0:T(8,128)(2,1)S(1)}, u32[]{:S(2)}, u32[]{:S(2)}) collective-permute-start(bf16[48,768]{1,0:T(8,128)(2,1)S(1)} %get-tuple-element.96), channel_id=1, source_target_pairs={{0,48},{16,0},{32,16},{48,32},{1,49},{17,1},{33,17},{49,33},{2,50}... | collective-permute-start | bytes 221192 | tf_op jit(solution)/shard_map/ppermute | solution.py:732
  (14 other events, 10.9 us)

commit v5 on v4

--- a/solution.py
+++ b/solution.py
@@ -255,11 +255,9 @@
         copy.wait()
 
 
-def logits_row(parts_ref, reports_ref, unit_ref, report_ref, row_ref):
+def unit_vectors(parts_ref, reports_ref, report_ref):
     pooled = jnp.sum(parts_ref[...], 0)
     inverse = lax.rsqrt(jnp.sum(pooled * pooled, -1, keepdims=True) + eps)
-    unit = pooled * inverse
-    unit_ref[...] = jnp.concatenate([unit, jnp.broadcast_to(inverse, unit.shape)], 0)
     count, owners, block = reports_ref.shape
     squares = jnp.zeros((owners, 1), f32)
     for j in range(count):
@@ -267,7 +265,11 @@
         report_ref[:, j * block : (j + 1) * block] = reports
         squares = squares + jnp.sum(reports * reports, -1, keepdims=True)
     report = report_ref[...] * lax.rsqrt(squares + eps)
-    report_ref[...] = report
+    return pooled * inverse, inverse, report
+
+
+def logits_row(parts_ref, reports_ref, row_ref, report_ref):
+    unit, inverse, report = unit_vectors(parts_ref, reports_ref, report_ref)
     row = contract(unit, report, 1, 1, precision=exact) / contrast_divisor_factor
     pad = row_ref.shape[2] - row.shape[1]
     row = jnp.concatenate([row, jnp.zeros((1, pad), f32)], 1)
@@ -278,8 +280,8 @@
     owner,
     logits_ref,
     pair_ref,
-    unit_ref,
-    report_ref,
+    parts_ref,
+    reports_ref,
     valid_ref,
     scale_ref,
     mass_ref,
@@ -297,7 +299,7 @@
     out_ref,
     *rest,
 ):
-    fetched, sems = rest[:-1], rest[-1]
+    fetched, report_ref, sems = rest[:-2], rest[-2], rest[-1]
     (
         out_weights_ref,
         heads_ref,
@@ -320,7 +322,8 @@
         fetched,
         sems,
     )
-    owners = report_ref.shape[0]
+    unit, inverse, report = unit_vectors(parts_ref, reports_ref, report_ref)
+    owners = report.shape[0]
     valid = valid_ref[...]
     logits = logits_ref[...]
     shape = logits.shape
@@ -341,11 +344,9 @@
     )
     grad_row = jnp.sum(jnp.where(rows == owner[0], grad_logits, 0.0), 0, keepdims=True)
     grad_unit = (
-        jnp.dot(grad_row[:, :owners], report_ref[...], precision=exact, preferred_element_type=f32)
+        jnp.dot(grad_row[:, :owners], report, precision=exact, preferred_element_type=f32)
         / contrast_divisor_factor
     )
-    unit = unit_ref[0:1]
-    inverse = unit_ref[1:2]
     grad_pooled = (grad_unit - unit * jnp.sum(unit * grad_unit, -1, keepdims=True)) * inverse
     grad = grad_pooled / jnp.sum(valid)
     grad_ref[...] = grad
@@ -465,66 +466,73 @@
     out_ref[...] = jnp.broadcast_to(piece[None], out_ref.shape)
 
 
-def other_grads(
-    other, two_ref, slope_ref, norm_ref, hidden_ref, parts_ref, grad_ref, hidden_grad_ref, out_ref
-):
+def rows_of(which, ref, chips, share):
+    rows = [
+        ref[pl.ds(pl.multiple_of((CORES * chip + which) * share, 16), share), :]
+        for chip in range(chips)
+    ]
+    return jnp.concatenate(rows, 0)
+
+
+def other_two(other, hidden_ref, parts_ref, grad_ref, out_ref):
     count = parts_ref.shape[0]
     rows = grad_ref.shape[0] // count
     for j in range(count):
         grad_ref[j * rows : (j + 1) * rows, :] = unpack(parts_ref[j])
+    chips, share = out_ref.shape[:2]
+    rows = rows_of(other[0], grad_ref, chips, share)
+    two = jnp.dot(rows, hidden_ref[...], preferred_element_type=f32).astype(bf16)
+    for chip in range(chips):
+        out_ref[chip] = two[chip * share : (chip + 1) * share]
+
+
+def other_one(two_ref, slope_ref, norm_ref, grad_ref, hidden_grad_ref, out_ref):
     grad_hidden = jnp.dot(two_ref[...], grad_ref[...], preferred_element_type=f32)
     hidden_grad_ref[...] = (grad_hidden * slope_ref[...]).astype(bf16)
-
-    def store(rows, values):
-        out_ref[rows] = values.astype(bf16)
-
-    both_layers(other[0], norm_ref, hidden_ref, grad_ref, hidden_grad_ref, out_ref.shape, store)
-
-
-def own_grads(own, column, norm_ref, hidden_ref, grad_ref, hidden_grad_ref, got_ref, *rest):
-    outs, line_ref, one_ref = rest[:-2], rest[-2], rest[-1]
+    one = contract(norm_ref[...], hidden_grad_ref[...], 1, 1).astype(bf16)
+    chips, share = out_ref.shape[:2]
+    for chip in range(chips):
+        out_ref[chip] = one[chip * share : (chip + 1) * share]
+
+
+def own_two(own, hidden_ref, grad_ref, got_ref, out_ref):
+    chips, share = got_ref.shape[:2]
+    side = out_ref.shape[1]
+    rows = rows_of(own[0], grad_ref, chips, share)
+    two = jnp.dot(rows, hidden_ref[...], preferred_element_type=f32)
+    for chip in range(chips):
+        part = two[chip * share : (chip + 1) * share] + got_ref[chip].astype(f32)
+        out_ref[chip // side, chip % side] = part.astype(bf16)
+
+
+def own_one(column, norm_ref, hidden_grad_ref, got_ref, *rest):
+    outs, one_ref = rest[:-1], rest[-1]
+    chips, share = got_ref.shape[:2]
     side = len(outs)
-
-    def store(rows, values):
-        values = (values + got_ref[rows].astype(f32)).astype(bf16)
-        line, place = divmod(rows[0], side)
-        if rows[1].start:
-            line_ref[line, place] = values
-        else:
-            one_ref[place, line] = values
-
-    both_layers(own[0], norm_ref, hidden_ref, grad_ref, hidden_grad_ref, got_ref.shape, store)
+    one = contract(norm_ref[...], hidden_grad_ref[...], 1, 1)
+    for chip in range(chips):
+        part = one[chip * share : (chip + 1) * share] + got_ref[chip].astype(f32)
+        one_ref[chip % side, chip // side] = part.astype(bf16)
     for k in range(side):
         outs[k][...] = one_ref[lax.rem(column[0] + k, side)]
 
 
-def half_way(column, *refs):
-    side = (len(refs) - 2) // 2
-    lines_ref, out_ref = refs[side], refs[side + 1]
+def half_way_one(*refs):
+    out_ref = refs[-1]
     total = refs[0][...].astype(f32)
-    for ref in refs[1:side]:
+    for ref in refs[1:-1]:
         total = total + ref[...].astype(f32)
     out_ref[...] = total.astype(bf16)
+
+
+def half_way_two(column, lines_ref, *outs):
+    side = len(outs)
     for k in range(side):
         place = lax.rem(column[0] + k, side)
         total = lines_ref[0, place].astype(f32)
         for line in range(1, lines_ref.shape[0]):
             total = total + lines_ref[line, place].astype(f32)
-        refs[side + 2 + k][...] = total.astype(bf16)
-
-
-def both_layers(which, norm_ref, hidden_ref, grad_ref, hidden_grad_ref, shape, store):
-    chips, share = shape[0], shape[1] // 2
-    rows = [
-        grad_ref[pl.ds(pl.multiple_of((CORES * chip + which) * share, 16), share), :]
-        for chip in range(chips)
-    ]
-    two = jnp.dot(jnp.concatenate(rows, 0), hidden_ref[...], preferred_element_type=f32)
-    one = contract(norm_ref[...], hidden_grad_ref[...], 1, 1)
-    for chip in range(chips):
-        start = chip * share
-        store((chip, slice(0, share)), one[start : start + share])
-        store((chip, slice(share, 2 * share)), two[start : start + share])
+        outs[k][...] = total.astype(bf16)
 
 
 def last_sums(lines_ref, *refs):
@@ -670,11 +678,12 @@
         limit=60,
     )
     pooled = exchange(pooled, "mp")
-    unit, report_unit, row = call(
+    (row,) = call(
         logits_row,
-        [((2, width), f32), ((owners, width), f32), ((owners, 1, 128), f32)],
+        [((owners, 1, 128), f32)],
         pooled,
         all_reports,
+        scratch=[((owners, width), f32)],
     )
     logits = exchange(row, DP).reshape(owners, 128)
     loss, grad, up, grads, sending = call(
@@ -683,8 +692,8 @@
         + [((parts, block + EXTRA, length), bf16)],
         logits,
         slide_pair[:, None],
-        unit,
-        report_unit,
+        pooled,
+        all_reports,
         valid,
         scales,
         mass,
@@ -705,6 +714,7 @@
             (w_key.shape, bf16),
             (w_value.shape, bf16),
             (slide_norm.shape, bf16),
+            ((owners, width), f32),
             7,
         ],
         limit=60,
@@ -769,43 +779,54 @@
     back = exchange(going.reshape(owners, ROWS, block), DP).reshape(slots, block)
     (spreading,) = call(tile_grads, [((parts,) + packed, bf16)], back, dispatch)
 
-    size = (chips, 2 * share, units)
-    grad_embedding, grad_hidden, sent = call(
-        other_grads,
-        [((width, tiles), bf16), ((units, tiles), bf16), (size, bf16)],
+    size = (chips, share, units)
+    swap = [(0, 1), (1, 0)]
+    grad_embedding, two_sent = call(
+        other_two,
+        [((width, tiles), bf16), (size, bf16)],
+        hidden,
+        exchange(spreading, "mp"),
+        scalars=(1 - core,),
+    )
+    two_got = lax.ppermute(two_sent, "core", swap)
+    grad_hidden, one_sent = call(
+        other_one,
+        [((units, tiles), bf16), (size, bf16)],
         w_two,
         slope,
         tile_other,
-        hidden,
-        exchange(spreading, "mp"),
-        scalars=(1 - core,),
-        limit=24,
-    )
-    got = lax.ppermute(sent, "core", [(0, 1), (1, 0)])
-    *along, across = call(
-        own_grads,
-        [((lines, share, units), bf16)] * side + [((lines, side, share, units), bf16)],
-        tile_own,
+        grad_embedding,
+    )
+    one_got = lax.ppermute(one_sent, "core", swap)
+    (across,) = call(
+        own_two,
+        [((lines, side, share, units), bf16)],
         hidden,
         grad_embedding,
+        two_got,
+        scalars=(core,),
+    )
+    across = exchange(across, "line")
+    along = call(
+        own_one,
+        [((lines, share, units), bf16)] * side,
+        tile_own,
         grad_hidden,
-        got,
-        scalars=(core, column),
+        one_got,
+        scalars=(column,),
         scratch=[((side, lines, share, units), bf16)],
-        limit=24,
-    )
-    across, *along = call(
-        half_way,
-        [((lines, share, units), bf16)] + [((share, units), bf16)] * side,
-        *shift(along, "column"),
-        exchange(across, "line"),
-        scalars=(column,),
+    )
+    (one_lines,) = call(
+        half_way_one, [((lines, share, units), bf16)], *shift(along, "column")
+    )
+    two_columns = call(
+        half_way_two, [((share, units), bf16)] * side, across, scalars=(column,)
     )
     grad_one, grad_two = call(
         last_sums,
         [((share, units), f32)] * 2,
-        exchange(across, "line"),
-        *shift(along, "column"),
+        exchange(one_lines, "line"),
+        *shift(two_columns, "column"),
     )
     grad_two = grad_two.T
 

time: 241 us -> 239 us (level)
  Pallas kernels: 30.3 us -> 34.1 us
    ppermute x1 -> x2, waiting for transfers between devices: 4.46 us -> 0.01 us  [the longest x1 0.01 us: per_device(): two_got = lax.ppermute(two_sent, 'core', swap)]
    pallas_call x15 -> x18, Pallas kernels: 30.3 us -> 34.1 us  [call(): pl.pallas_call(kernel if skip else body, out_shape=[jax.ShapeDtypeStruct(...]
    unnamed x74 -> x76, local copies, waits for them, and re-layouts: 11.4 us -> 9.47 us
  transfers between devices with their start and end apart: 27 -> 28, of which waited for: 19 -> 17; matrix products, arithmetic and copies ran while one was open for 6% -> 6% of each run, Pallas kernels for 1% -> 5%
where the time goes in v5:
time: 239 us; the launch traced here: 238 us
  waiting for transfers between devices  63.2 us (26%)
  blocking collectives  63.2 us (26%)
  starting transfers between devices  56.6 us (24%)
  Pallas kernels  34.1 us (14%)
  local copies, waits for them, and re-layouts  16.7 us (7%)
    all_to_all x4, blocking collectives, exchange(): return lax.all_to_all(values, axis, 0, 0, tiled=True)  63.2 us
    pallas_call x18, Pallas kernels, call(): pl.pallas_call(kernel if skip else body, out_shape=[jax.ShapeDtypeStruct(...  34.1 us
    all_to_all x5, starting transfers between devices, exchange(): return lax.all_to_all(values, axis, 0, 0, tiled=True)  27.7 us
    ppermute x12, waiting for transfers between devices, shift(): lax.ppermute(values[k], axis, turn(len(values), k))  24.4 us
    all_to_all x5, waiting for transfers between devices, exchange(): return lax.all_to_all(values, axis, 0, 0, tiled=True)  23.8 us
    ppermute x12, starting transfers between devices, shift(): lax.ppermute(values[k], axis, turn(len(values), k))  15.6 us
    ppermute x3, waiting for transfers between devices, gather_ring(): back = lax.ppermute(back, 'mp', turn(count, 1))  11.4 us
    unnamed x76, local copies, waits for them, and re-layouts  9.47 us
  transfers between devices with their start and end apart: 28, of which 17 were waited for; matrix products, arithmetic and copies ran while one was open for 6% of the time, Pallas kernels for 5%

profile of v5, /device:TPU:8, one launch (start us, length us, event | category | flops | bytes accessed | tf_op | source)
XLA Modules:
  0.0 237.9 jit_solution(11934597724177584224)
XLA Ops:
  0.6 4.5 %shard_map.153 = (bf16[192,1536]{1,0:T(8,128)(2,1)}, bf16[192,768]{1,0:T(8,128)(2,1)}, f32[192,768]{1,0:T(8,128)}, bf16[8,288,128]{2,1,0:T(8,128)(2,1)}) custom-call(bf16[192,1536]{1,0:T(8,128)(2,1)} %far_x.1, bf16[1536,768]{1,0:T(8,128)(2,1)} %far_one.1, bf16[768,1536]{1,0:T(8,128)(2,1)} %two_ref.1), custom_call_target="tpu_custom_call" | custom-call | tf_op jit(solution)/shard_map/pallas_call | solution.py:49
  5.2 8.6 %all-to-all-start = ((bf16[8,288,128]{2,1,0:T(8,128)(2,1)}), bf16[8,288,128]{2,1,0:T(8,128)(2,1)S(1)}, u32[]{:S(2)}, u32[]{:S(2)}) async-start(bf16[8,288,128]{2,1,0:T(8,128)(2,1)} %get-tuple-element.51), calls=%async_computation | async-start | bytes 1179648 | tf_op jit(solution)/shard_map/all_to_all | solution.py:33
  14.4 1.2 copy.42
  17.8 1.2 constant_dynamic-slice_fusion.3
  19.2 13.5 %all-to-all-done.refs_9_ = bf16[8,288,128]{2,1,0:T(8,128)(2,1)S(1)} async-done(((bf16[8,288,128]{2,1,0:T(8,128)(2,1)}), bf16[8,288,128]{2,1,0:T(8,128)(2,1)S(1)}, u32[]{:S(2)}, u32[]{:S(2)}) %all-to-all-start) | async-done | bytes 589856 | tf_op jit(solution)/shard_map/all_to_all | solution.py:33
  33.0 14.8 %all_to_all.45 = bf16[32,16,256]{2,1,0:T(8,128)(2,1)S(1)} all-to-all(bf16[32,16,256]{2,1,0:T(8,128)(2,1)S(1)} %bitcast.56), channel_id=1, replica_groups=mesh['line'=4,'column'=4,'core'=2,'mp'=8] {'line','column','core'}, dimensions={0} | all-to-all | bytes 524288 | tf_op jit(solution)/shard_map/all_to_all | solution.py:33
  48.8 2.7 %collective-permute-start.1 = (bf16[208,384]{1,0:T(8,128)(2,1)S(1)}, bf16[208,384]{1,0:T(8,128)(2,1)S(1)}, u32[]{:S(2)}, u32[]{:S(2)}) collective-permute-start(bf16[208,384]{1,0:T(8,128)(2,1)S(1)} %get-tuple-element.53.rest_0_.refs_4_), channel_id=1, source_target_pairs={{0,7},{1,0},{2,1},{3,2},{4,3},{5,4},{6,5},{7,6},{8,15},{9,8},{10,9... | collective-permute-start | bytes 479240 | tf_op jit(solution)/shard_map/ppermute | solution.py:83
  51.5 4.5 %collective-permute-done.rest_1_ = bf16[208,384]{1,0:T(8,128)(2,1)S(1)} collective-permute-done((bf16[208,384]{1,0:T(8,128)(2,1)S(1)}, bf16[208,384]{1,0:T(8,128)(2,1)S(1)}, u32[]{:S(2)}, u32[]{:S(2)}) %collective-permute-start) | collective-permute-done | bytes 159776 | tf_op jit(solution)/shard_map/ppermute | solution.py:82
  56.0 3.2 %collective-permute-start.3 = (bf16[208,384]{1,0:T(8,128)(2,1)S(1)}, bf16[208,384]{1,0:T(8,128)(2,1)S(1)}, u32[]{:S(2)}, u32[]{:S(2)}) collective-permute-start(bf16[208,384]{1,0:T(8,128)(2,1)S(1)} %collective-permute-done.1.rest_2_), channel_id=1, source_target_pairs={{0,7},{1,0},{2,1},{3,2},{4,3},{5,4},{6,5},{7,6},{8,15},{9,8},{10,9... | collective-permute-start | bytes 479240 | tf_op jit(solution)/shard_map/ppermute | solution.py:83
  59.2 3.7 %collective-permute-done.2.rest_3_ = bf16[208,384]{1,0:T(8,128)(2,1)S(1)} collective-permute-done((bf16[208,384]{1,0:T(8,128)(2,1)S(1)}, bf16[208,384]{1,0:T(8,128)(2,1)S(1)}, u32[]{:S(2)}, u32[]{:S(2)}) %collective-permute-start.2) | collective-permute-done | bytes 159776 | tf_op jit(solution)/shard_map/ppermute | solution.py:82
  63.7 2.7 %collective-permute-start.5 = (bf16[208,384]{1,0:T(8,128)(2,1)S(1)}, bf16[208,384]{1,0:T(8,128)(2,1)S(1)}, u32[]{:S(2)}, u32[]{:S(2)}) collective-permute-start(bf16[208,384]{1,0:T(8,128)(2,1)S(1)} %collective-permute-done.3.rest_4_), channel_id=1, source_target_pairs={{0,7},{1,0},{2,1},{3,2},{4,3},{5,4},{6,5},{7,6},{8,15},{9,8},{10,9... | collective-permute-start | bytes 479240 | tf_op jit(solution)/shard_map/ppermute | solution.py:83
  66.3 3.2 %collective-permute-done.4.rest_5_ = bf16[208,384]{1,0:T(8,128)(2,1)S(1)} collective-permute-done((bf16[208,384]{1,0:T(8,128)(2,1)S(1)}, bf16[208,384]{1,0:T(8,128)(2,1)S(1)}, u32[]{:S(2)}, u32[]{:S(2)}) %collective-permute-start.4) | collective-permute-done | bytes 159776 | tf_op jit(solution)/shard_map/ppermute | solution.py:82
  69.6 3.5 %collective-permute-start.7 = (bf16[96,384]{1,0:T(8,128)(2,1)S(1)}, bf16[96,384]{1,0:T(8,128)(2,1)S(1)}, u32[]{:S(2)}, u32[]{:S(2)}) collective-permute-start(bf16[96,384]{1,0:T(8,128)(2,1)S(1)} %slice.51), channel_id=1, source_target_pairs={{0,7},{1,0},{2,1},{3,2},{4,3},{5,4},{6,5},{7,6},{8,15},{9,8},{10,9... | collective-permute-start | bytes 221192 | tf_op jit(solution)/shard_map/ppermute | solution.py:87
  73.1 2.0 collective-permute-done.7.rest_8_
  75.9 7.1 %shard_map.156 = (bf16[1536,384]{1,0:T(8,128)(2,1)}, f32[2,3,96,384]{3,2,1,0:T(8,128)}, f32[2,384,384]{2,1,0:T(8,128)}, f32[2,384]{1,0:T(2,128)}, f32[2,2,384]{2...) custom-call(s32[1]{0:T(128)} %bitcast.1.here, ...), custom_call_target="tpu_custom_call" | custom-call | tf_op jit(solution)/shard_map/pallas_call | solution.py:49
  83.0 12.9 %all_to_all.46.parts_ref = f32[8,1,1536]{2,1,0:T(1,128)S(1)} all-to-all(f32[8,1,1536]{2,1,0:T(1,128)} %get-tuple-element.54), channel_id=1, replica_groups=mesh['line'=4,'column'=4,'core'=2,'mp'=8] {'mp'}, dimensions={0} | all-to-all | bytes 98304 | tf_op jit(solution)/shard_map/all_to_all | solution.py:33
  96.8 1.0 shard_map.157
  97.8 4.9 %all-to-all-start.3 = ((f32[32,1,128]{2,1,0:T(1,128)}), f32[32,1,128]{2,1,0:T(1,128)S(1)}, u32[]{:S(2)}, u32[]{:S(2)}) async-start(f32[32,1,128]{2,1,0:T(1,128)} %shard_map.157), calls=%async_computation.3 | async-start | bytes 32768 | tf_op jit(solution)/shard_map/all_to_all | solution.py:33
  102.7 1.2 copy.49.far_query_weights
  103.9 1.2 copy.50.far_key_weights
  105.1 1.3 copy.51.far_value_weights
  107.0 1.8 all-to-all-done.3
  109.4 6.3 %shard_map.158 = (f32[1,1]{1,0:T(1,128)}, f32[1,1536]{1,0:T(1,128)}, f32[1,192]{1,0:T(1,128)}, bf16[576,384]{1,0:T(8,128)(2,1)}, bf16[8,208,384]{2,1,0:T(8,128)(2,1)}) custom-call(s32[1]{0:T(128)} %bitcast.owner, f32[32,128]{1,0:T(8,128)} %bitcast.66, s32[32,1]{1,0:T(8,128)} %copy.48.pair_ref, f32[8,1,1536]{2,1,0:T(1,128)} %copy-done.8, ...), custom_call_target="tpu_custom_call" | custom-call | tf_op jit(solution)/shard_map/pallas_call | solution.py:49
  115.7 4.4 %all-to-all-start.4 = ((bf16[8,208,384]{2,1,0:T(8,128)(2,1)}), bf16[8,208,384]{2,1,0:T(8,128)(2,1)}, u32[]{:S(2)}, u32[]{:S(2)}) async-start(bf16[8,208,384]{2,1,0:T(8,128)(2,1)} %get-tuple-element.76), calls=%async_computation.4 | async-start | bytes 2555904 | tf_op jit(solution)/shard_map/all_to_all | solution.py:33
  120.2 1.0 copy-done.2
  121.2 1.4 shard_map.159
  123.5 1.4 collective-permute-done.8.got_ref
  124.9 1.0 copy-done.3
  125.9 1.6 shard_map.160
  128.2 2.0 collective-permute-start.10
  130.3 1.2 collective-permute-start.11
  131.5 6.4 %collective-permute-done.9.refs_1_ = bf16[4,48,384]{2,1,0:T(8,128)(2,1)S(1)} collective-permute-done((bf16[4,48,384]{2,1,0:T(8,128)(2,1)S(1)}, bf16[4,48,384]{2,1,0:T(8,128)(2,1)S(1)}, u32[]{:S(2)}, u32[]{:S(2)}) %collective-permute-start.9) | collective-permute-done | bytes 147488 | tf_op jit(solution)/shard_map/ppermute | solution.py:742
  138.6 1.5 collective-permute-start.14
  140.7 2.0 collective-permute-start.12
  143.1 2.5 %collective-permute-done.13 = bf16[48,384]{1,0:T(8,128)(2,1)S(1)} collective-permute-done((bf16[48,384]{1,0:T(8,128)(2,1)S(1)}, bf16[48,384]{1,0:T(8,128)(2,1)S(1)}, u32[]{:S(2)}, u32[]{:S(2)}) %collective-permute-start.13) | collective-permute-done | bytes 36896 | tf_op jit(solution)/shard_map/ppermute | solution.py:742
  145.6 8.6 %all-to-all-done.4.refs_7_ = bf16[8,208,384]{2,1,0:T(8,128)(2,1)} async-done(((bf16[8,208,384]{2,1,0:T(8,128)(2,1)}), bf16[8,208,384]{2,1,0:T(8,128)(2,1)}, u32[]{:S(2)}, u32[]{:S(2)}) %all-to-all-start.4) | async-done | bytes 1277984 | tf_op jit(solution)/shard_map/all_to_all | solution.py:33
  154.1 1.8 shard_map.162
  156.0 13.1 %all_to_all.47 = bf16[32,16,192]{2,1,0:T(8,128)(2,1)S(1)} all-to-all(bf16[32,16,192]{2,1,0:T(8,128)(2,1)S(1)} %bitcast.59), channel_id=1, replica_groups=mesh['line'=4,'column'=4,'core'=2,'mp'=8] {'line','column','core'}, dimensions={0} | all-to-all | bytes 393216 | tf_op jit(solution)/shard_map/all_to_all | solution.py:33
  169.5 22.4 %all_to_all.48.parts_ref = bf16[8,288,128]{2,1,0:T(8,128)(2,1)S(1)} all-to-all(bf16[8,288,128]{2,1,0:T(8,128)(2,1)S(1)} %shard_map.163), channel_id=1, replica_groups=mesh['line'=4,'column'=4,'core'=2,'mp'=8] {'mp'}, dimensions={0} | all-to-all | bytes 1179648 | tf_op jit(solution)/shard_map/all_to_all | solution.py:33
  192.6 2.7 %shard_map.165 = (bf16[768,192]{1,0:T(8,128)(2,1)S(1)}, bf16[16,48,768]{2,1,0:T(8,128)(2,1)}) custom-call(bf16[768,1536]{1,0:T(8,128)(2,1)S(1)} %copy-done.1, f32[768,192]{1,0:T(8,128)S(1)} %bitcast.50, bf16[768,192]{1,0:T(8,128)(2,1)S(1)} %bitcast.52, bf16[1536,192]{1,0:T(8,128)(2,1)S(1)} %get-tuple-element.77.grad_ref), custom_call_target="tpu_custom_call" | custom-call | tf_op jit(solution)/shard_map/pallas_call | solution.py:49
  196.5 1.5 shard_map.168
  198.0 5.0 %all-to-all-start.8 = ((bf16[4,4,48,768]{3,2,1,0:T(8,128)(2,1)}), bf16[4,4,48,768]{3,2,1,0:T(8,128)(2,1)S(1)}, u32[]{:S(2)}, u32[]{:S(2)}) async-start(bf16[4,4,48,768]{3,2,1,0:T(8,128)(2,1)} %shard_map.168), calls=%async_computation.8 | async-start | bytes 2359296 | tf_op jit(solution)/shard_map/all_to_all | solution.py:33
  203.1 2.8 %shard_map.166 = (bf16[4,48,768]{2,1,0:T(8,128)(2,1)S(1)}, bf16[4,48,768]{2,1,0:T(8,128)(2,1)}, bf16[4,48,768]{2,1,0:T(8,128)(2,1)}, bf16[4,48,768]{2,1,0:T(8,128)(2,1)}) custom-call(s32[1]{0:T(128)} %bitcast.19.column, bf16[768,192]{1,0:T(8,128)(2,1)S(1)} %bitcast.54, bf16[768,192]{1,0:T(8,128)(2,1)S(1)} %copy-done.10, ...), custom_call_target="tpu_custom_call" | custom-call | tf_op jit(solution)/shard_map/pallas_call | solution.py:49
  206.6 2.1 collective-permute-start.17
  210.7 11.6 %collective-permute-done.16.refs_1_ = bf16[4,48,768]{2,1,0:T(8,128)(2,1)S(1)} collective-permute-done((bf16[4,48,768]{2,1,0:T(8,128)(2,1)}, bf16[4,48,768]{2,1,0:T(8,128)(2,1)S(1)}, u32[]{:S(2)}, u32[]{:S(2)}) %collective-permute-start.16) | collective-permute-done | bytes 294944 | tf_op jit(solution)/shard_map/ppermute | solution.py:742
  223.8 4.8 %all-to-all-start.7 = ((bf16[4,48,768]{2,1,0:T(8,128)(2,1)}), bf16[4,48,768]{2,1,0:T(8,128)(2,1)S(1)}, u32[]{:S(2)}, u32[]{:S(2)}) async-start(bf16[4,48,768]{2,1,0:T(8,128)(2,1)} %shard_map.167), calls=%async_computation.7 | async-start | bytes 589824 | tf_op jit(solution)/shard_map/all_to_all | solution.py:33
  229.2 3.6 %collective-permute-start.21 = (bf16[48,768]{1,0:T(8,128)(2,1)S(1)}, bf16[48,768]{1,0:T(8,128)(2,1)S(1)}, u32[]{:S(2)}, u32[]{:S(2)}) collective-permute-start(bf16[48,768]{1,0:T(8,128)(2,1)S(1)} %get-tuple-element.87), channel_id=1, source_target_pairs={{0,32},{16,48},{32,0},{48,16},{1,33},{17,49},{33,1},{49,17},{2,34}... | collective-permute-start | bytes 221192 | tf_op jit(solution)/shard_map/ppermute | solution.py:742
  235.9 1.2 collective-permute-done.22.refs_3_
  (162 shorter events, 22.4 us)
Async XLA Ops:
  5.2 8.6 %copy-start.17 = (bf16[192,1536]{1,0:T(8,128)(2,1)S(1)}, bf16[192,1536]{1,0:T(8,128)(2,1)}, u32[]{:S(2)}) copy-start(bf16[192,1536]{1,0:T(8,128)(2,1)} %far_x.1) | copy-start | bytes 1769476
  5.2 9.3 %copy-start.19 = (bf16[192,1536]{1,0:T(8,128)(2,1)S(1)}, bf16[192,1536]{1,0:T(8,128)(2,1)}, u32[]{:S(2)}) copy-start(bf16[192,1536]{1,0:T(8,128)(2,1)} %get-tuple-element.49) | copy-start | bytes 1769476
  5.2 27.5 %all-to-all-start = ((bf16[8,288,128]{2,1,0:T(8,128)(2,1)}), bf16[8,288,128]{2,1,0:T(8,128)(2,1)S(1)}, u32[]{:S(2)}, u32[]{:S(2)}) async-start(bf16[8,288,128]{2,1,0:T(8,128)(2,1)} %get-tuple-element.51), calls=%async_computation | async-start | bytes 1179648 | tf_op jit(solution)/shard_map/all_to_all | solution.py:33
  48.2 27.1 %copy-start.5 = (bf16[208,384]{1,0:T(8,128)(2,1)}, bf16[208,384]{1,0:T(8,128)(2,1)S(1)}, u32[]{:S(2)}) copy-start(bf16[208,384]{1,0:T(8,128)(2,1)S(1)} %get-tuple-element.53.rest_0_.refs_4_) | copy-start | bytes 479236
  48.2 27.1 %copy-start.11 = (f32[1,384]{1,0:T(1,128)}, f32[1,384]{1,0:T(1,128)S(1)}, u32[]{:S(2)}) copy-start(f32[1,384]{1,0:T(1,128)S(1)} %get-tuple-element.52.valid_ref.refs_2_) | copy-start | bytes 4612
  48.2 7.8 %collective-permute-start = (bf16[208,384]{1,0:T(8,128)(2,1)S(1)}, bf16[208,384]{1,0:T(8,128)(2,1)S(1)}, u32[]{:S(2)}, u32[]{:S(2)}) collective-permute-start(bf16[208,384]{1,0:T(8,128)(2,1)S(1)} %get-tuple-element.53.rest_0_.refs_4_), channel_id=1, source_target_pairs={{0,1},{1,2},{2,3},{3,4},{4,5},{5,6},{6,7},{7,0},{8,9},{9,10},{10,1... | collective-permute-start | bytes 479240 | tf_op jit(solution)/shard_map/ppermute | solution.py:82
  48.8 7.2 %collective-permute-start.1 = (bf16[208,384]{1,0:T(8,128)(2,1)S(1)}, bf16[208,384]{1,0:T(8,128)(2,1)S(1)}, u32[]{:S(2)}, u32[]{:S(2)}) collective-permute-start(bf16[208,384]{1,0:T(8,128)(2,1)S(1)} %get-tuple-element.53.rest_0_.refs_4_), channel_id=1, source_target_pairs={{0,7},{1,0},{2,1},{3,2},{4,3},{5,4},{6,5},{7,6},{8,15},{9,8},{10,9... | collective-permute-start | bytes 479240 | tf_op jit(solution)/shard_map/ppermute | solution.py:83
  56.0 3.2 %copy-start.22 = (bf16[208,384]{1,0:T(8,128)(2,1)}, bf16[208,384]{1,0:T(8,128)(2,1)S(1)}, u32[]{:S(2)}) copy-start(bf16[208,384]{1,0:T(8,128)(2,1)S(1)} %collective-permute-done.rest_1_) | copy-start | bytes 479236
  56.0 7.0 %collective-permute-start.2 = (bf16[208,384]{1,0:T(8,128)(2,1)S(1)}, bf16[208,384]{1,0:T(8,128)(2,1)S(1)}, u32[]{:S(2)}, u32[]{:S(2)}) collective-permute-start(bf16[208,384]{1,0:T(8,128)(2,1)S(1)} %collective-permute-done.rest_1_), channel_id=1, source_target_pairs={{0,1},{1,2},{2,3},{3,4},{4,5},{5,6},{6,7},{7,0},{8,9},{9,10},{10,1... | collective-permute-start | bytes 479240 | tf_op jit(solution)/shard_map/ppermute | solution.py:82
  56.0 7.0 %copy-start.23 = (bf16[208,384]{1,0:T(8,128)(2,1)}, bf16[208,384]{1,0:T(8,128)(2,1)S(1)}, u32[]{:S(2)}) copy-start(bf16[208,384]{1,0:T(8,128)(2,1)S(1)} %collective-permute-done.1.rest_2_) | copy-start | bytes 479236
  56.0 7.0 %collective-permute-start.3 = (bf16[208,384]{1,0:T(8,128)(2,1)S(1)}, bf16[208,384]{1,0:T(8,128)(2,1)S(1)}, u32[]{:S(2)}, u32[]{:S(2)}) collective-permute-start(bf16[208,384]{1,0:T(8,128)(2,1)S(1)} %collective-permute-done.1.rest_2_), channel_id=1, source_target_pairs={{0,7},{1,0},{2,1},{3,2},{4,3},{5,4},{6,5},{7,6},{8,15},{9,8},{10,9... | collective-permute-start | bytes 479240 | tf_op jit(solution)/shard_map/ppermute | solution.py:83
  63.0 6.5 %collective-permute-start.4 = (bf16[208,384]{1,0:T(8,128)(2,1)S(1)}, bf16[208,384]{1,0:T(8,128)(2,1)S(1)}, u32[]{:S(2)}, u32[]{:S(2)}) collective-permute-start(bf16[208,384]{1,0:T(8,128)(2,1)S(1)} %collective-permute-done.2.rest_3_), channel_id=1, source_target_pairs={{0,1},{1,2},{2,3},{3,4},{4,5},{5,6},{6,7},{7,0},{8,9},{9,10},{10,1... | collective-permute-start | bytes 479240 | tf_op jit(solution)/shard_map/ppermute | solution.py:82
  63.7 11.6 %copy-start.25 = (bf16[208,384]{1,0:T(8,128)(2,1)}, bf16[208,384]{1,0:T(8,128)(2,1)S(1)}, u32[]{:S(2)}) copy-start(bf16[208,384]{1,0:T(8,128)(2,1)S(1)} %collective-permute-done.3.rest_4_) | copy-start | bytes 479236
  63.7 5.9 %collective-permute-start.5 = (bf16[208,384]{1,0:T(8,128)(2,1)S(1)}, bf16[208,384]{1,0:T(8,128)(2,1)S(1)}, u32[]{:S(2)}, u32[]{:S(2)}) collective-permute-start(bf16[208,384]{1,0:T(8,128)(2,1)S(1)} %collective-permute-done.3.rest_4_), channel_id=1, source_target_pairs={{0,7},{1,0},{2,1},{3,2},{4,3},{5,4},{6,5},{7,6},{8,15},{9,8},{10,9... | collective-permute-start | bytes 479240 | tf_op jit(solution)/shard_map/ppermute | solution.py:83
  69.5 5.8 %copy-start.20 = (bf16[208,384]{1,0:T(8,128)(2,1)}, bf16[208,384]{1,0:T(8,128)(2,1)S(1)}, u32[]{:S(2)}) copy-start(bf16[208,384]{1,0:T(8,128)(2,1)S(1)} %collective-permute-done.4.rest_5_) | copy-start | bytes 479236
  69.5 5.8 %collective-permute-start.6 = (bf16[112,384]{1,0:T(8,128)(2,1)S(1)}, bf16[112,384]{1,0:T(8,128)(2,1)S(1)}, u32[]{:S(2)}, u32[]{:S(2)}) collective-permute-start(bf16[112,384]{1,0:T(8,128)(2,1)S(1)} %slice.50), channel_id=1, source_target_pairs={{0,1},{1,2},{2,3},{3,4},{4,5},{5,6},{6,7},{7,0},{8,9},{9,10},{10,1... | collective-permute-start | bytes 258056 | tf_op jit(solution)/shard_map/ppermute | solution.py:86
  69.6 5.7 %copy-start.21 = (bf16[208,384]{1,0:T(8,128)(2,1)}, bf16[208,384]{1,0:T(8,128)(2,1)S(1)}, u32[]{:S(2)}) copy-start(bf16[208,384]{1,0:T(8,128)(2,1)S(1)} %collective-permute-done.5.rest_6_) | copy-start | bytes 479236
  69.6 5.4 %collective-permute-start.7 = (bf16[96,384]{1,0:T(8,128)(2,1)S(1)}, bf16[96,384]{1,0:T(8,128)(2,1)S(1)}, u32[]{:S(2)}, u32[]{:S(2)}) collective-permute-start(bf16[96,384]{1,0:T(8,128)(2,1)S(1)} %slice.51), channel_id=1, source_target_pairs={{0,7},{1,0},{2,1},{3,2},{4,3},{5,4},{6,5},{7,6},{8,15},{9,8},{10,9... | collective-permute-start | bytes 221192 | tf_op jit(solution)/shard_map/ppermute | solution.py:87
  75.9 26.8 %copy-start.14 = (bf16[1536,192]{0,1:T(8,128)(2,1)S(1)}, bf16[1536,192]{0,1:T(8,128)(2,1)}, u32[]{:S(2)}) copy-start(bf16[1536,192]{0,1:T(8,128)(2,1)} %param.16) | copy-start | bytes 1769476
  75.9 28.0 %copy-start.15 = (bf16[1536,192]{0,1:T(8,128)(2,1)S(1)}, bf16[1536,192]{0,1:T(8,128)(2,1)}, u32[]{:S(2)}) copy-start(bf16[1536,192]{0,1:T(8,128)(2,1)} %param.17) | copy-start | bytes 1769476
  95.9 9.2 %copy-start.8 = (f32[8,1,1536]{2,1,0:T(1,128)}, f32[8,1,1536]{2,1,0:T(1,128)S(1)}, u32[]{:S(2)}) copy-start(f32[8,1,1536]{2,1,0:T(1,128)S(1)} %all_to_all.46.parts_ref) | copy-start | bytes 147460
  97.8 11.0 %all-to-all-start.3 = ((f32[32,1,128]{2,1,0:T(1,128)}), f32[32,1,128]{2,1,0:T(1,128)S(1)}, u32[]{:S(2)}, u32[]{:S(2)}) async-start(f32[32,1,128]{2,1,0:T(1,128)} %shard_map.157), calls=%async_computation.3 | async-start | bytes 32768 | tf_op jit(solution)/shard_map/all_to_all | solution.py:33
  103.9 2.4 %copy-start.33 = (s32[32]{0:T(128)S(1)}, s32[32]{0:T(128)}, u32[]{:S(2)}) copy-start(s32[32]{0:T(128)} %param.12) | copy-start | bytes 388
  115.7 4.4 %copy-start = (bf16[1536,384]{1,0:T(8,128)(2,1)S(1)}, bf16[1536,384]{1,0:T(8,128)(2,1)}, u32[]{:S(2)}) copy-start(bf16[1536,384]{1,0:T(8,128)(2,1)} %get-tuple-element.60.far_norm.norm_ref) | copy-start | bytes 3538948
  115.7 38.4 %all-to-all-start.4 = ((bf16[8,208,384]{2,1,0:T(8,128)(2,1)}), bf16[8,208,384]{2,1,0:T(8,128)(2,1)}, u32[]{:S(2)}, u32[]{:S(2)}) async-start(bf16[8,208,384]{2,1,0:T(8,128)(2,1)} %get-tuple-element.76), calls=%async_computation.4 | async-start | bytes 2555904 | tf_op jit(solution)/shard_map/all_to_all | solution.py:33
  122.6 2.3 collective-permute-start.8
  127.5 26.6 %copy-start.6 = (bf16[208,384]{1,0:T(8,128)(2,1)S(1)}, bf16[208,384]{1,0:T(8,128)(2,1)}, u32[]{:S(2)}) copy-start(bf16[208,384]{1,0:T(8,128)(2,1)} %copy-done.5) | copy-start | bytes 479236
  127.5 26.6 %copy-start.12 = (f32[1,384]{1,0:T(1,128)S(1)}, f32[1,384]{1,0:T(1,128)}, u32[]{:S(2)}) copy-start(f32[1,384]{1,0:T(1,128)} %copy-done.11) | copy-start | bytes 4612
  127.5 26.6 %copy-start.13 = (f32[2,384]{1,0:T(2,128)S(1)}, f32[2,384]{1,0:T(2,128)}, u32[]{:S(2)}) copy-start(f32[2,384]{1,0:T(2,128)} %get-tuple-element.73.refs_3_) | copy-start | bytes 9220
  127.5 10.3 %collective-permute-start.9 = (bf16[4,48,384]{2,1,0:T(8,128)(2,1)S(1)}, bf16[4,48,384]{2,1,0:T(8,128)(2,1)S(1)}, u32[]{:S(2)}, u32[]{:S(2)}) collective-permute-start(bf16[4,48,384]{2,1,0:T(8,128)(2,1)S(1)} %get-tuple-element.65), channel_id=1, source_target_pairs={{0,16},{16,32},{32,48},{48,0},{1,17},{17,33},{33,49},{49,1},{2,18}... | collective-permute-start | bytes 442376 | tf_op jit(solution)/shard_map/ppermute | solution.py:742
  128.2 9.7 %collective-permute-start.10 = (bf16[4,48,384]{2,1,0:T(8,128)(2,1)S(1)}, bf16[4,48,384]{2,1,0:T(8,128)(2,1)S(1)}, u32[]{:S(2)}, u32[]{:S(2)}) collective-permute-start(bf16[4,48,384]{2,1,0:T(8,128)(2,1)S(1)} %get-tuple-element.66), channel_id=1, source_target_pairs={{0,32},{16,48},{32,0},{48,16},{1,33},{17,49},{33,1},{49,17},{2,34}... | collective-permute-start | bytes 442376 | tf_op jit(solution)/shard_map/ppermute | solution.py:742
  130.3 8.2 %collective-permute-start.11 = (bf16[4,48,384]{2,1,0:T(8,128)(2,1)S(1)}, bf16[4,48,384]{2,1,0:T(8,128)(2,1)S(1)}, u32[]{:S(2)}, u32[]{:S(2)}) collective-permute-start(bf16[4,48,384]{2,1,0:T(8,128)(2,1)S(1)} %get-tuple-element.67), channel_id=1, source_target_pairs={{0,48},{16,0},{32,16},{48,32},{1,49},{17,1},{33,17},{49,33},{2,50}... | collective-permute-start | bytes 442376 | tf_op jit(solution)/shard_map/ppermute | solution.py:742
  138.6 4.5 %collective-permute-start.14 = (bf16[48,384]{1,0:T(8,128)(2,1)S(1)}, bf16[48,384]{1,0:T(8,128)(2,1)S(1)}, u32[]{:S(2)}, u32[]{:S(2)}) collective-permute-start(bf16[48,384]{1,0:T(8,128)(2,1)S(1)} %get-tuple-element.71), channel_id=1, source_target_pairs={{0,192},{64,0},{128,64},{192,128},{1,193},{65,1},{129,65},{193,129... | collective-permute-start | bytes 110600 | tf_op jit(solution)/shard_map/ppermute | solution.py:742
  140.1 5.5 %collective-permute-start.13 = (bf16[48,384]{1,0:T(8,128)(2,1)S(1)}, bf16[48,384]{1,0:T(8,128)(2,1)S(1)}, u32[]{:S(2)}, u32[]{:S(2)}) collective-permute-start(bf16[48,384]{1,0:T(8,128)(2,1)S(1)} %get-tuple-element.70), channel_id=1, source_target_pairs={{0,128},{64,192},{128,0},{192,64},{1,129},{65,193},{129,1},{193,65... | collective-permute-start | bytes 110600 | tf_op jit(solution)/shard_map/ppermute | solution.py:742
  140.7 4.9 %collective-permute-start.12 = (bf16[48,384]{1,0:T(8,128)(2,1)S(1)}, bf16[48,384]{1,0:T(8,128)(2,1)S(1)}, u32[]{:S(2)}, u32[]{:S(2)}) collective-permute-start(bf16[48,384]{1,0:T(8,128)(2,1)S(1)} %get-tuple-element.69), channel_id=1, source_target_pairs={{0,64},{64,128},{128,192},{192,0},{1,65},{65,129},{129,193},{193,1... | collective-permute-start | bytes 110600 | tf_op jit(solution)/shard_map/ppermute | solution.py:742
  169.1 22.7 %copy-start.4 = (bf16[192,768]{1,0:T(8,128)(2,1)S(1)}, bf16[192,768]{1,0:T(8,128)(2,1)}, u32[]{:S(2)}) copy-start(bf16[192,768]{1,0:T(8,128)(2,1)} %get-tuple-element.62.hidden_ref) | copy-start | bytes 884740
  169.1 23.5 %copy-start.1 = (bf16[768,1536]{1,0:T(8,128)(2,1)S(1)}, bf16[768,1536]{1,0:T(8,128)(2,1)}, u32[]{:S(2)}) copy-start(bf16[768,1536]{1,0:T(8,128)(2,1)} %two_ref.1) | copy-start | bytes 7077892
  192.4 4.1 %collective-permute-start.19 = (bf16[16,48,768]{2,1,0:T(8,128)(2,1)S(1)}, bf16[16,48,768]{2,1,0:T(8,128)(2,1)S(1)}, u32[]{:S(2)}, u32[]{:S(2)}) collective-permute-start(bf16[16,48,768]{2,1,0:T(8,128)(2,1)S(1)} %get-tuple-element.84), channel_id=1, source_target_pairs={{0,8},{8,0},{1,9},{9,1},{2,10},{10,2},{3,11},{11,3},{4,12},{12,4},... | collective-permute-start | bytes 3538952 | tf_op jit(solution)/shard_map/ppermute | solution.py:791
  196.1 7.0 %collective-permute-start.15 = (bf16[16,48,768]{2,1,0:T(8,128)(2,1)}, bf16[16,48,768]{2,1,0:T(8,128)(2,1)}, u32[]{:S(2)}, u32[]{:S(2)}) collective-permute-start(bf16[16,48,768]{2,1,0:T(8,128)(2,1)} %get-tuple-element.79), channel_id=1, source_target_pairs={{0,8},{8,0},{1,9},{9,1},{2,10},{10,2},{3,11},{11,3},{4,12},{12,4},... | collective-permute-start | bytes 3538952 | tf_op jit(solution)/shard_map/ppermute | solution.py:800
  198.0 5.0 %copy-start.10 = (bf16[768,192]{1,0:T(8,128)(2,1)S(1)}, bf16[768,192]{1,0:T(8,128)(2,1)}, u32[]{:S(2)}) copy-start(bf16[768,192]{1,0:T(8,128)(2,1)} %copy-done.9) | copy-start | bytes 884740
  198.0 25.7 %all-to-all-start.8 = ((bf16[4,4,48,768]{3,2,1,0:T(8,128)(2,1)}), bf16[4,4,48,768]{3,2,1,0:T(8,128)(2,1)S(1)}, u32[]{:S(2)}, u32[]{:S(2)}) async-start(bf16[4,4,48,768]{3,2,1,0:T(8,128)(2,1)} %shard_map.168), calls=%async_computation.8 | async-start | bytes 2359296 | tf_op jit(solution)/shard_map/all_to_all | solution.py:33
  205.9 16.4 %collective-permute-start.16 = (bf16[4,48,768]{2,1,0:T(8,128)(2,1)}, bf16[4,48,768]{2,1,0:T(8,128)(2,1)S(1)}, u32[]{:S(2)}, u32[]{:S(2)}) collective-permute-start(bf16[4,48,768]{2,1,0:T(8,128)(2,1)} %get-tuple-element.81), channel_id=1, source_target_pairs={{0,16},{16,32},{32,48},{48,0},{1,17},{17,33},{33,49},{49,1},{2,18}... | collective-permute-start | bytes 884744 | tf_op jit(solution)/shard_map/ppermute | solution.py:742
  206.6 15.7 %collective-permute-start.17 = (bf16[4,48,768]{2,1,0:T(8,128)(2,1)}, bf16[4,48,768]{2,1,0:T(8,128)(2,1)S(1)}, u32[]{:S(2)}, u32[]{:S(2)}) collective-permute-start(bf16[4,48,768]{2,1,0:T(8,128)(2,1)} %get-tuple-element.82), channel_id=1, source_target_pairs={{0,32},{16,48},{32,0},{48,16},{1,33},{17,49},{33,1},{49,17},{2,34}... | collective-permute-start | bytes 884744 | tf_op jit(solution)/shard_map/ppermute | solution.py:742
  208.7 14.2 %collective-permute-start.18 = (bf16[4,48,768]{2,1,0:T(8,128)(2,1)}, bf16[4,48,768]{2,1,0:T(8,128)(2,1)S(1)}, u32[]{:S(2)}, u32[]{:S(2)}) collective-permute-start(bf16[4,48,768]{2,1,0:T(8,128)(2,1)} %get-tuple-element.83), channel_id=1, source_target_pairs={{0,48},{16,0},{32,16},{48,32},{1,49},{17,1},{33,17},{49,33},{2,50}... | collective-permute-start | bytes 884744 | tf_op jit(solution)/shard_map/ppermute | solution.py:742
  223.8 10.7 %all-to-all-start.7 = ((bf16[4,48,768]{2,1,0:T(8,128)(2,1)}), bf16[4,48,768]{2,1,0:T(8,128)(2,1)S(1)}, u32[]{:S(2)}, u32[]{:S(2)}) async-start(bf16[4,48,768]{2,1,0:T(8,128)(2,1)} %shard_map.167), calls=%async_computation.7 | async-start | bytes 589824 | tf_op jit(solution)/shard_map/all_to_all | solution.py:33
  228.7 6.4 %collective-permute-start.20 = (bf16[48,768]{1,0:T(8,128)(2,1)S(1)}, bf16[48,768]{1,0:T(8,128)(2,1)S(1)}, u32[]{:S(2)}, u32[]{:S(2)}) collective-permute-start(bf16[48,768]{1,0:T(8,128)(2,1)S(1)} %get-tuple-element.86), channel_id=1, source_target_pairs={{0,16},{16,32},{32,48},{48,0},{1,17},{17,33},{33,49},{49,1},{2,18}... | collective-permute-start | bytes 221192 | tf_op jit(solution)/shard_map/ppermute | solution.py:742
  229.2 6.7 %collective-permute-start.21 = (bf16[48,768]{1,0:T(8,128)(2,1)S(1)}, bf16[48,768]{1,0:T(8,128)(2,1)S(1)}, u32[]{:S(2)}, u32[]{:S(2)}) collective-permute-start(bf16[48,768]{1,0:T(8,128)(2,1)S(1)} %get-tuple-element.87), channel_id=1, source_target_pairs={{0,32},{16,48},{32,0},{48,16},{1,33},{17,49},{33,1},{49,17},{2,34}... | collective-permute-start | bytes 221192 | tf_op jit(solution)/shard_map/ppermute | solution.py:742
  232.8 4.4 %collective-permute-start.22 = (bf16[48,768]{1,0:T(8,128)(2,1)S(1)}, bf16[48,768]{1,0:T(8,128)(2,1)S(1)}, u32[]{:S(2)}, u32[]{:S(2)}) collective-permute-start(bf16[48,768]{1,0:T(8,128)(2,1)S(1)} %get-tuple-element.88), channel_id=1, source_target_pairs={{0,48},{16,0},{32,16},{48,32},{1,49},{17,1},{33,17},{49,33},{2,50}... | collective-permute-start | bytes 221192 | tf_op jit(solution)/shard_map/ppermute | solution.py:742
  (16 other events, 15.5 us)

commit v6 on v5

--- a/solution.py
+++ b/solution.py
@@ -166,10 +166,10 @@
 def slide_forward(
     here,
     valid_ref,
-    query_weights_ref,
-    key_weights_ref,
-    value_weights_ref,
-    out_weights_ref,
+    far_query_weights,
+    far_key_weights,
+    far_value_weights,
+    far_out_weights,
     *rest,
 ):
     pieces = rest[:9]
@@ -187,8 +187,18 @@
         norm_ref,
         heads_ref,
         attention_ref,
+        query_weights_ref,
+        key_weights_ref,
+        value_weights_ref,
+        out_weights_ref,
+        weight_sems,
         sems,
     ) = rest[9:]
+    fetched = fetch(
+        (far_query_weights, far_key_weights, far_value_weights, far_out_weights),
+        (query_weights_ref, key_weights_ref, value_weights_ref, out_weights_ref),
+        weight_sems,
+    )
     count, owners, block = reports_ref.shape
 
     def store(index, piece):
@@ -210,6 +220,8 @@
     norm_ref[...] = normed
     copies = [pltpu.make_async_copy(norm_ref, far_norm, sems.at[0])]
     copies[0].start()
+    for copy in fetched:
+        copy.wait()
     all_query = jnp.dot(query_weights_ref[...], normed, preferred_element_type=f32)
     all_keys = jnp.dot(key_weights_ref[...], normed, preferred_element_type=f32)
     all_values = jnp.dot(value_weights_ref[...], normed, preferred_element_type=f32)
@@ -296,10 +308,10 @@
     grad_ref,
     up_ref,
     grads_ref,
-    out_ref,
+    far_out,
     *rest,
 ):
-    fetched, report_ref, sems = rest[:-2], rest[-2], rest[-1]
+    fetched, report_ref, out_ref, sems, out_sems = rest[:-4], *rest[-4:]
     (
         out_weights_ref,
         heads_ref,
@@ -387,6 +399,7 @@
         copy.wait()
     count = out_ref.shape[0]
     block = norm_ref.shape[0] // count
+    sending = []
     first = jnp.zeros_like(valid)
     second = jnp.zeros_like(valid)
     for k in range(count):
@@ -395,6 +408,12 @@
         part = part + jnp.dot(key_weights_ref[rows, :], grad_key, preferred_element_type=f32)
         part = part + jnp.dot(value_weights_ref[rows, :], grad_value, preferred_element_type=f32)
         out_ref[k, 0:block, :] = part.astype(bf16)
+        sending.append(
+            pltpu.make_async_copy(
+                out_ref.at[k, pl.ds(0, block)], far_out.at[k, pl.ds(0, block)], out_sems.at[k]
+            )
+        )
+        sending[-1].start()
         first = first + jnp.sum(part, 0, keepdims=True)
         second = second + jnp.sum(part * norm_ref[rows, :].astype(f32), 0, keepdims=True)
     width = norm_ref.shape[0]
@@ -405,6 +424,13 @@
     ).astype(bf16)
     for k in range(count):
         out_ref[k, block : block + EXTRA, :] = stats
+        tail = pl.ds(block, EXTRA)
+        sending.append(
+            pltpu.make_async_copy(out_ref.at[k, tail], far_out.at[k, tail], out_sems.at[count + k])
+        )
+        sending[-1].start()
+    for copy in sending:
+        copy.wait()
 
 
 def wide_other(which, norm_ref, grads_ref, out_ref):
@@ -486,46 +512,46 @@
         out_ref[chip] = two[chip * share : (chip + 1) * share]
 
 
-def other_one(two_ref, slope_ref, norm_ref, grad_ref, hidden_grad_ref, out_ref):
+def both_one(
+    two_ref, slope_ref, other_norm_ref, own_norm_ref, grad_ref, out_ref, own_ref, hidden_grad_ref
+):
     grad_hidden = jnp.dot(two_ref[...], grad_ref[...], preferred_element_type=f32)
     hidden_grad_ref[...] = (grad_hidden * slope_ref[...]).astype(bf16)
-    one = contract(norm_ref[...], hidden_grad_ref[...], 1, 1).astype(bf16)
     chips, share = out_ref.shape[:2]
-    for chip in range(chips):
-        out_ref[chip] = one[chip * share : (chip + 1) * share]
-
-
-def own_two(own, hidden_ref, grad_ref, got_ref, out_ref):
+    for norm_ref, target_ref in ((other_norm_ref, out_ref), (own_norm_ref, own_ref)):
+        one = contract(norm_ref[...], hidden_grad_ref[...], 1, 1).astype(bf16)
+        for chip in range(chips):
+            target_ref[chip] = one[chip * share : (chip + 1) * share]
+
+
+def own_two(own, column, hidden_ref, grad_ref, got_ref, *rest):
+    outs, two_ref = rest[:-1], rest[-1]
     chips, share = got_ref.shape[:2]
-    side = out_ref.shape[1]
+    side = len(outs)
     rows = rows_of(own[0], grad_ref, chips, share)
     two = jnp.dot(rows, hidden_ref[...], preferred_element_type=f32)
     for chip in range(chips):
         part = two[chip * share : (chip + 1) * share] + got_ref[chip].astype(f32)
+        two_ref[chip % side, chip // side] = part.astype(bf16)
+    for k in range(side):
+        outs[k][...] = two_ref[lax.rem(column[0] + k, side)]
+
+
+def own_one(own_ref, got_ref, out_ref):
+    side = out_ref.shape[1]
+    for chip in range(got_ref.shape[0]):
+        part = own_ref[chip].astype(f32) + got_ref[chip].astype(f32)
         out_ref[chip // side, chip % side] = part.astype(bf16)
 
 
-def own_one(column, norm_ref, hidden_grad_ref, got_ref, *rest):
-    outs, one_ref = rest[:-1], rest[-1]
-    chips, share = got_ref.shape[:2]
-    side = len(outs)
-    one = contract(norm_ref[...], hidden_grad_ref[...], 1, 1)
-    for chip in range(chips):
-        part = one[chip * share : (chip + 1) * share] + got_ref[chip].astype(f32)
-        one_ref[chip % side, chip // side] = part.astype(bf16)
-    for k in range(side):
-        outs[k][...] = one_ref[lax.rem(column[0] + k, side)]
-
-
-def half_way_one(*refs):
-    out_ref = refs[-1]
+def add_up(*refs):
     total = refs[0][...].astype(f32)
     for ref in refs[1:-1]:
         total = total + ref[...].astype(f32)
-    out_ref[...] = total.astype(bf16)
-
-
-def half_way_two(column, lines_ref, *outs):
+    refs[-1][...] = total.astype(refs[-1].dtype)
+
+
+def add_lines(column, lines_ref, *outs):
     side = len(outs)
     for k in range(side):
         place = lax.rem(column[0] + k, side)
@@ -540,11 +566,11 @@
     total = lines_ref[0].astype(f32)
     for line in range(1, lines_ref.shape[0]):
         total = total + lines_ref[line].astype(f32)
-    one_ref[...] = total
+    two_ref[...] = total
     total = refs[0][...].astype(f32)
     for ref in refs[1:-2]:
         total = total + ref[...].astype(f32)
-    two_ref[...] = total
+    one_ref[...] = total
 
 
 def per_device(
@@ -668,11 +694,17 @@
         w_out,
         *pieces,
         scalars=(here,),
+        far=(1, 2, 3, 4),
         scratch=[
             ((width, length), bf16),
             ((width, length), bf16),
             ((heads, 3, HEAD, length), f32),
             ((heads, length, length), f32),
+            ((inner, width), bf16),
+            ((inner, width), bf16),
+            ((inner, width), bf16),
+            ((inner, width), bf16),
+            4,
             1 + 2 * heads,
         ],
         limit=60,
@@ -689,7 +721,7 @@
     loss, grad, up, grads, sending = call(
         slide_backward,
         [((1, 1), f32), ((1, width), f32), ((1, inner), f32), ((3 * inner, length), bf16)]
-        + [((parts, block + EXTRA, length), bf16)],
+        + [((parts, block + EXTRA, length), bf16, "far")],
         logits,
         slide_pair[:, None],
         pooled,
@@ -715,7 +747,9 @@
             (w_value.shape, bf16),
             (slide_norm.shape, bf16),
             ((owners, width), f32),
+            ((parts, block + EXTRA, length), bf16),
             7,
+            2 * parts,
         ],
         limit=60,
     )
@@ -789,44 +823,36 @@
         scalars=(1 - core,),
     )
     two_got = lax.ppermute(two_sent, "core", swap)
-    grad_hidden, one_sent = call(
-        other_one,
-        [((units, tiles), bf16), (size, bf16)],
+    one_sent, one_own = call(
+        both_one,
+        [(size, bf16), (size, bf16)],
         w_two,
         slope,
         tile_other,
+        tile_own,
         grad_embedding,
+        scratch=[((units, tiles), bf16)],
     )
     one_got = lax.ppermute(one_sent, "core", swap)
-    (across,) = call(
+    two_along = call(
         own_two,
-        [((lines, side, share, units), bf16)],
+        [((lines, share, units), bf16)] * side,
         hidden,
         grad_embedding,
         two_got,
-        scalars=(core,),
-    )
-    across = exchange(across, "line")
-    along = call(
-        own_one,
-        [((lines, share, units), bf16)] * side,
-        tile_own,
-        grad_hidden,
-        one_got,
-        scalars=(column,),
+        scalars=(core, column),
         scratch=[((side, lines, share, units), bf16)],
     )
-    (one_lines,) = call(
-        half_way_one, [((lines, share, units), bf16)], *shift(along, "column")
-    )
-    two_columns = call(
-        half_way_two, [((share, units), bf16)] * side, across, scalars=(column,)
-    )
+    two_along = shift(two_along, "column")
+    (one_across,) = call(own_one, [((lines, side, share, units), bf16)], one_own, one_got)
+    one_across = exchange(one_across, "line")
+    (two_across,) = call(add_up, [((lines, share, units), bf16)], *two_along)
+    one_along = call(add_lines, [((share, units), bf16)] * side, one_across, scalars=(column,))
     grad_one, grad_two = call(
         last_sums,
         [((share, units), f32)] * 2,
-        exchange(one_lines, "line"),
-        *shift(two_columns, "column"),
+        exchange(two_across, "line"),
+        *shift(one_along, "column"),
     )
     grad_two = grad_two.T
 

time: 239 us -> 242 us (1.013)
  waiting for transfers between devices: 63.2 us -> 66.1 us
    ppermute x1, waiting for transfers between devices: 0.01 us -> 3.02 us  [per_device(): one_got = lax.ppermute(one_sent, 'core', swap)]
    unnamed x76 -> x78, local copies, waits for them, and re-layouts: 9.47 us -> 8.71 us
  transfers between devices with their start and end apart: 28 -> 28, of which waited for: 17 -> 18; matrix products, arithmetic and copies ran while one was open for 6% -> 6% of each run, Pallas kernels for 5% -> 3%
where the time goes in v6:
time: 242 us; the launch traced here: 241 us
  waiting for transfers between devices  66.1 us (27%)
  blocking collectives  63.2 us (26%)
  starting transfers between devices  56.8 us (23%)
  Pallas kernels  34.9 us (14%)
  local copies, waits for them, and re-layouts  15.9 us (7%)
    all_to_all x4, blocking collectives, exchange(): return lax.all_to_all(values, axis, 0, 0, tiled=True)  63.2 us
    pallas_call x18, Pallas kernels, call(): pl.pallas_call(kernel if skip else body, out_shape=[jax.ShapeDtypeStruct(...  34.9 us
    all_to_all x5, starting transfers between devices, exchange(): return lax.all_to_all(values, axis, 0, 0, tiled=True)  27.7 us
    ppermute x12, waiting for transfers between devices, shift(): lax.ppermute(values[k], axis, turn(len(values), k))  24.5 us
    all_to_all x5, waiting for transfers between devices, exchange(): return lax.all_to_all(values, axis, 0, 0, tiled=True)  23.6 us
    ppermute x12, starting transfers between devices, shift(): lax.ppermute(values[k], axis, turn(len(values), k))  15.8 us
    ppermute x3, waiting for transfers between devices, gather_ring(): back = lax.ppermute(back, 'mp', turn(count, 1))  11.4 us
    unnamed x78, local copies, waits for them, and re-layouts  8.71 us
  transfers between devices with their start and end apart: 28, of which 18 were waited for; matrix products, arithmetic and copies ran while one was open for 6% of the time, Pallas kernels for 3%

profile of v6, /device:TPU:8, one launch (start us, length us, event | category | flops | bytes accessed | tf_op | source)
XLA Modules:
  0.0 240.9 jit_solution(2466501575681530272)
XLA Ops:
  0.6 4.5 %shard_map.153 = (bf16[192,1536]{1,0:T(8,128)(2,1)}, bf16[192,768]{1,0:T(8,128)(2,1)}, f32[192,768]{1,0:T(8,128)}, bf16[8,288,128]{2,1,0:T(8,128)(2,1)}) custom-call(bf16[192,1536]{1,0:T(8,128)(2,1)} %far_x.1, bf16[1536,768]{1,0:T(8,128)(2,1)} %far_one.1, bf16[768,1536]{1,0:T(8,128)(2,1)} %two_ref.1), custom_call_target="tpu_custom_call" | custom-call | tf_op jit(solution)/shard_map/pallas_call | solution.py:49
  5.2 8.6 %all-to-all-start = ((bf16[8,288,128]{2,1,0:T(8,128)(2,1)}), bf16[8,288,128]{2,1,0:T(8,128)(2,1)S(1)}, u32[]{:S(2)}, u32[]{:S(2)}) async-start(bf16[8,288,128]{2,1,0:T(8,128)(2,1)} %get-tuple-element.51), calls=%async_computation | async-start | bytes 1179648 | tf_op jit(solution)/shard_map/all_to_all | solution.py:33
  14.4 1.2 copy.42
  17.8 1.2 constant_dynamic-slice_fusion.3
  19.2 13.5 %all-to-all-done.refs_9_ = bf16[8,288,128]{2,1,0:T(8,128)(2,1)S(1)} async-done(((bf16[8,288,128]{2,1,0:T(8,128)(2,1)}), bf16[8,288,128]{2,1,0:T(8,128)(2,1)S(1)}, u32[]{:S(2)}, u32[]{:S(2)}) %all-to-all-start) | async-done | bytes 589856 | tf_op jit(solution)/shard_map/all_to_all | solution.py:33
  33.0 14.8 %all_to_all.45 = bf16[32,16,256]{2,1,0:T(8,128)(2,1)S(1)} all-to-all(bf16[32,16,256]{2,1,0:T(8,128)(2,1)S(1)} %bitcast.56), channel_id=1, replica_groups=mesh['line'=4,'column'=4,'core'=2,'mp'=8] {'line','column','core'}, dimensions={0} | all-to-all | bytes 524288 | tf_op jit(solution)/shard_map/all_to_all | solution.py:33
  48.8 2.7 %collective-permute-start.1 = (bf16[208,384]{1,0:T(8,128)(2,1)S(1)}, bf16[208,384]{1,0:T(8,128)(2,1)S(1)}, u32[]{:S(2)}, u32[]{:S(2)}) collective-permute-start(bf16[208,384]{1,0:T(8,128)(2,1)S(1)} %get-tuple-element.53.rest_0_.refs_4_), channel_id=1, source_target_pairs={{0,7},{1,0},{2,1},{3,2},{4,3},{5,4},{6,5},{7,6},{8,15},{9,8},{10,9... | collective-permute-start | bytes 479240 | tf_op jit(solution)/shard_map/ppermute | solution.py:83
  51.5 4.5 %collective-permute-done.rest_1_ = bf16[208,384]{1,0:T(8,128)(2,1)S(1)} collective-permute-done((bf16[208,384]{1,0:T(8,128)(2,1)S(1)}, bf16[208,384]{1,0:T(8,128)(2,1)S(1)}, u32[]{:S(2)}, u32[]{:S(2)}) %collective-permute-start) | collective-permute-done | bytes 159776 | tf_op jit(solution)/shard_map/ppermute | solution.py:82
  56.0 3.2 %collective-permute-start.3 = (bf16[208,384]{1,0:T(8,128)(2,1)S(1)}, bf16[208,384]{1,0:T(8,128)(2,1)S(1)}, u32[]{:S(2)}, u32[]{:S(2)}) collective-permute-start(bf16[208,384]{1,0:T(8,128)(2,1)S(1)} %collective-permute-done.1.rest_2_), channel_id=1, source_target_pairs={{0,7},{1,0},{2,1},{3,2},{4,3},{5,4},{6,5},{7,6},{8,15},{9,8},{10,9... | collective-permute-start | bytes 479240 | tf_op jit(solution)/shard_map/ppermute | solution.py:83
  59.3 3.7 %collective-permute-done.2.rest_3_ = bf16[208,384]{1,0:T(8,128)(2,1)S(1)} collective-permute-done((bf16[208,384]{1,0:T(8,128)(2,1)S(1)}, bf16[208,384]{1,0:T(8,128)(2,1)S(1)}, u32[]{:S(2)}, u32[]{:S(2)}) %collective-permute-start.2) | collective-permute-done | bytes 159776 | tf_op jit(solution)/shard_map/ppermute | solution.py:82
  63.7 2.7 %collective-permute-start.5 = (bf16[208,384]{1,0:T(8,128)(2,1)S(1)}, bf16[208,384]{1,0:T(8,128)(2,1)S(1)}, u32[]{:S(2)}, u32[]{:S(2)}) collective-permute-start(bf16[208,384]{1,0:T(8,128)(2,1)S(1)} %collective-permute-done.3.rest_4_), channel_id=1, source_target_pairs={{0,7},{1,0},{2,1},{3,2},{4,3},{5,4},{6,5},{7,6},{8,15},{9,8},{10,9... | collective-permute-start | bytes 479240 | tf_op jit(solution)/shard_map/ppermute | solution.py:83
  66.3 3.2 %collective-permute-done.4.rest_5_ = bf16[208,384]{1,0:T(8,128)(2,1)S(1)} collective-permute-done((bf16[208,384]{1,0:T(8,128)(2,1)S(1)}, bf16[208,384]{1,0:T(8,128)(2,1)S(1)}, u32[]{:S(2)}, u32[]{:S(2)}) %collective-permute-start.4) | collective-permute-done | bytes 159776 | tf_op jit(solution)/shard_map/ppermute | solution.py:82
  69.6 3.5 %collective-permute-start.7 = (bf16[96,384]{1,0:T(8,128)(2,1)S(1)}, bf16[96,384]{1,0:T(8,128)(2,1)S(1)}, u32[]{:S(2)}, u32[]{:S(2)}) collective-permute-start(bf16[96,384]{1,0:T(8,128)(2,1)S(1)} %slice.51), channel_id=1, source_target_pairs={{0,7},{1,0},{2,1},{3,2},{4,3},{5,4},{6,5},{7,6},{8,15},{9,8},{10,9... | collective-permute-start | bytes 221192 | tf_op jit(solution)/shard_map/ppermute | solution.py:87
  73.1 2.0 collective-permute-done.7.rest_8_
  75.9 6.6 %shard_map.156 = (bf16[1536,384]{1,0:T(8,128)(2,1)}, f32[2,3,96,384]{3,2,1,0:T(8,128)}, f32[2,384,384]{2,1,0:T(8,128)}, f32[2,384]{1,0:T(2,128)}, f32[2,2,384]{2...) custom-call(s32[1]{0:T(128)} %bitcast.1.here, ...), custom_call_target="tpu_custom_call" | custom-call | tf_op jit(solution)/shard_map/pallas_call | solution.py:49
  82.5 12.9 %all_to_all.46.parts_ref = f32[8,1,1536]{2,1,0:T(1,128)S(1)} all-to-all(f32[8,1,1536]{2,1,0:T(1,128)} %get-tuple-element.54), channel_id=1, replica_groups=mesh['line'=4,'column'=4,'core'=2,'mp'=8] {'mp'}, dimensions={0} | all-to-all | bytes 98304 | tf_op jit(solution)/shard_map/all_to_all | solution.py:33
  96.3 1.0 shard_map.157
  97.4 4.9 %all-to-all-start.3 = ((f32[32,1,128]{2,1,0:T(1,128)}), f32[32,1,128]{2,1,0:T(1,128)S(1)}, u32[]{:S(2)}, u32[]{:S(2)}) async-start(f32[32,1,128]{2,1,0:T(1,128)} %shard_map.157), calls=%async_computation.3 | async-start | bytes 32768 | tf_op jit(solution)/shard_map/all_to_all | solution.py:33
  102.2 1.2 copy.49.far_query_weights
  103.4 1.2 copy.50.far_key_weights
  104.6 1.3 copy.51.far_value_weights
  106.5 1.8 all-to-all-done.3
  108.9 6.8 %shard_map.158 = (f32[1,1]{1,0:T(1,128)}, f32[1,1536]{1,0:T(1,128)}, f32[1,192]{1,0:T(1,128)}, bf16[576,384]{1,0:T(8,128)(2,1)}, bf16[8,208,384]{2,1,0:T(8,128)(2,1)}) custom-call(s32[1]{0:T(128)} %bitcast.owner, f32[32,128]{1,0:T(8,128)} %bitcast.66, s32[32,1]{1,0:T(8,128)} %copy.48.pair_ref, f32[8,1,1536]{2,1,0:T(1,128)} %copy-done.11, ...), custom_call_target="tpu_custom_call" | custom-call | tf_op jit(solution)/shard_map/pallas_call | solution.py:49
  115.8 4.4 %all-to-all-start.4 = ((bf16[8,208,384]{2,1,0:T(8,128)(2,1)}), bf16[8,208,384]{2,1,0:T(8,128)(2,1)}, u32[]{:S(2)}, u32[]{:S(2)}) async-start(bf16[8,208,384]{2,1,0:T(8,128)(2,1)} %get-tuple-element.76), calls=%async_computation.4 | async-start | bytes 2555904 | tf_op jit(solution)/shard_map/all_to_all | solution.py:33
  121.2 1.4 shard_map.159
  123.6 1.4 collective-permute-done.8.got_ref
  126.0 1.6 shard_map.160
  128.3 2.1 collective-permute-start.10
  130.3 1.2 collective-permute-start.11
  131.6 6.4 %collective-permute-done.9.refs_1_ = bf16[4,48,384]{2,1,0:T(8,128)(2,1)S(1)} collective-permute-done((bf16[4,48,384]{2,1,0:T(8,128)(2,1)S(1)}, bf16[4,48,384]{2,1,0:T(8,128)(2,1)S(1)}, u32[]{:S(2)}, u32[]{:S(2)}) %collective-permute-start.9) | collective-permute-done | bytes 147488 | tf_op jit(solution)/shard_map/ppermute | solution.py:776
  138.6 1.7 collective-permute-start.14
  140.9 2.0 collective-permute-start.12
  143.3 2.5 %collective-permute-done.13 = bf16[48,384]{1,0:T(8,128)(2,1)S(1)} collective-permute-done((bf16[48,384]{1,0:T(8,128)(2,1)S(1)}, bf16[48,384]{1,0:T(8,128)(2,1)S(1)}, u32[]{:S(2)}, u32[]{:S(2)}) %collective-permute-start.13) | collective-permute-done | bytes 36896 | tf_op jit(solution)/shard_map/ppermute | solution.py:776
  145.8 8.4 %all-to-all-done.4.refs_7_ = bf16[8,208,384]{2,1,0:T(8,128)(2,1)} async-done(((bf16[8,208,384]{2,1,0:T(8,128)(2,1)}), bf16[8,208,384]{2,1,0:T(8,128)(2,1)}, u32[]{:S(2)}, u32[]{:S(2)}) %all-to-all-start.4) | async-done | bytes 1277984 | tf_op jit(solution)/shard_map/all_to_all | solution.py:33
  154.2 1.8 shard_map.162
  156.0 13.1 %all_to_all.47 = bf16[32,16,192]{2,1,0:T(8,128)(2,1)S(1)} all-to-all(bf16[32,16,192]{2,1,0:T(8,128)(2,1)S(1)} %bitcast.59), channel_id=1, replica_groups=mesh['line'=4,'column'=4,'core'=2,'mp'=8] {'line','column','core'}, dimensions={0} | all-to-all | bytes 393216 | tf_op jit(solution)/shard_map/all_to_all | solution.py:33
  169.5 22.4 %all_to_all.48.parts_ref = bf16[8,288,128]{2,1,0:T(8,128)(2,1)S(1)} all-to-all(bf16[8,288,128]{2,1,0:T(8,128)(2,1)S(1)} %shard_map.163), channel_id=1, replica_groups=mesh['line'=4,'column'=4,'core'=2,'mp'=8] {'mp'}, dimensions={0} | all-to-all | bytes 1179648 | tf_op jit(solution)/shard_map/all_to_all | solution.py:33
  191.9 1.6 shard_map.164
  193.5 2.6 %shard_map.167 = (bf16[16,48,768]{2,1,0:T(8,128)(2,1)S(1)}, bf16[16,48,768]{2,1,0:T(8,128)(2,1)S(1)}) custom-call(bf16[768,1536]{1,0:T(8,128)(2,1)S(1)} %copy-done.1, f32[768,192]{1,0:T(8,128)S(1)} %bitcast.50, bf16[768,192]{1,0:T(8,128)(2,1)S(1)} %bitcast.52, bf16[768,192]{1,0:T(8,128)(2,1)S(1)} %bitcast.54, bf16[1536,192]{1,0:T(8,128)(2,1)S(1)} %get-tuple-element.77.grad_ref), custom_call_target="tpu_custom_call" | custom-call | tf_op jit(solution)/shard_map/pallas_call | solution.py:49
  196.7 3.0 %collective-permute-done.19.got_ref = bf16[16,48,768]{2,1,0:T(8,128)(2,1)S(1)} collective-permute-done((bf16[16,48,768]{2,1,0:T(8,128)(2,1)S(1)}, bf16[16,48,768]{2,1,0:T(8,128)(2,1)S(1)}, u32[]{:S(2)}, u32[]{:S(2)}) %collective-permute-start.19) | collective-permute-done | bytes 1179680 | tf_op jit(solution)/shard_map/ppermute | solution.py:836
  199.7 1.3 shard_map.168
  201.0 5.0 %all-to-all-start.8 = ((bf16[4,4,48,768]{3,2,1,0:T(8,128)(2,1)}), bf16[4,4,48,768]{3,2,1,0:T(8,128)(2,1)S(1)}, u32[]{:S(2)}, u32[]{:S(2)}) async-start(bf16[4,4,48,768]{3,2,1,0:T(8,128)(2,1)} %shard_map.168), calls=%async_computation.8 | async-start | bytes 2359296 | tf_op jit(solution)/shard_map/all_to_all | solution.py:33
  206.1 2.8 %shard_map.165 = (bf16[4,48,768]{2,1,0:T(8,128)(2,1)S(1)}, bf16[4,48,768]{2,1,0:T(8,128)(2,1)}, bf16[4,48,768]{2,1,0:T(8,128)(2,1)}, bf16[4,48,768]{2,1,0:T(8,128)(2,1)}) custom-call(s32[1]{0:T(128)} %bitcast.19.which.own, s32[1]{0:T(128)} %bitcast.20.column, bf16[192,768]{1,0:T(8,128)(2,1)S(1)} %copy-done.7, bf16[1536,192]{1,0:T(8,128)(2,1)S(1)} %copy-done.3, ...), custom_call_target="tpu_custom_call" | custom-call | tf_op jit(solution)/shard_map/pallas_call | solution.py:49
  209.6 2.1 collective-permute-start.17
  213.7 11.7 %collective-permute-done.16.refs_1_ = bf16[4,48,768]{2,1,0:T(8,128)(2,1)S(1)} collective-permute-done((bf16[4,48,768]{2,1,0:T(8,128)(2,1)}, bf16[4,48,768]{2,1,0:T(8,128)(2,1)S(1)}, u32[]{:S(2)}, u32[]{:S(2)}) %collective-permute-start.16) | collective-permute-done | bytes 294944 | tf_op jit(solution)/shard_map/ppermute | solution.py:776
  226.8 4.8 %all-to-all-start.7 = ((bf16[4,48,768]{2,1,0:T(8,128)(2,1)}), bf16[4,48,768]{2,1,0:T(8,128)(2,1)S(1)}, u32[]{:S(2)}, u32[]{:S(2)}) async-start(bf16[4,48,768]{2,1,0:T(8,128)(2,1)} %shard_map.166), calls=%async_computation.7 | async-start | bytes 589824 | tf_op jit(solution)/shard_map/all_to_all | solution.py:33
  232.3 3.6 %collective-permute-start.21 = (bf16[48,768]{1,0:T(8,128)(2,1)S(1)}, bf16[48,768]{1,0:T(8,128)(2,1)S(1)}, u32[]{:S(2)}, u32[]{:S(2)}) collective-permute-start(bf16[48,768]{1,0:T(8,128)(2,1)S(1)} %get-tuple-element.87), channel_id=1, source_target_pairs={{0,32},{16,48},{32,0},{48,16},{1,33},{17,49},{33,1},{49,17},{2,34}... | collective-permute-start | bytes 221192 | tf_op jit(solution)/shard_map/ppermute | solution.py:776
  238.9 1.2 collective-permute-done.22.refs_3_
  (164 shorter events, 23.1 us)
Async XLA Ops:
  5.2 8.6 %copy-start.18 = (bf16[192,1536]{1,0:T(8,128)(2,1)S(1)}, bf16[192,1536]{1,0:T(8,128)(2,1)}, u32[]{:S(2)}) copy-start(bf16[192,1536]{1,0:T(8,128)(2,1)} %far_x.1) | copy-start | bytes 1769476
  5.2 9.3 %copy-start.20 = (bf16[192,1536]{1,0:T(8,128)(2,1)S(1)}, bf16[192,1536]{1,0:T(8,128)(2,1)}, u32[]{:S(2)}) copy-start(bf16[192,1536]{1,0:T(8,128)(2,1)} %get-tuple-element.49) | copy-start | bytes 1769476
  5.2 27.5 %all-to-all-start = ((bf16[8,288,128]{2,1,0:T(8,128)(2,1)}), bf16[8,288,128]{2,1,0:T(8,128)(2,1)S(1)}, u32[]{:S(2)}, u32[]{:S(2)}) async-start(bf16[8,288,128]{2,1,0:T(8,128)(2,1)} %get-tuple-element.51), calls=%async_computation | async-start | bytes 1179648 | tf_op jit(solution)/shard_map/all_to_all | solution.py:33
  48.2 27.1 %copy-start.8 = (bf16[208,384]{1,0:T(8,128)(2,1)}, bf16[208,384]{1,0:T(8,128)(2,1)S(1)}, u32[]{:S(2)}) copy-start(bf16[208,384]{1,0:T(8,128)(2,1)S(1)} %get-tuple-element.53.rest_0_.refs_4_) | copy-start | bytes 479236
  48.2 27.1 %copy-start.12 = (f32[1,384]{1,0:T(1,128)}, f32[1,384]{1,0:T(1,128)S(1)}, u32[]{:S(2)}) copy-start(f32[1,384]{1,0:T(1,128)S(1)} %get-tuple-element.52.valid_ref.refs_2_) | copy-start | bytes 4612
  48.2 7.8 %collective-permute-start = (bf16[208,384]{1,0:T(8,128)(2,1)S(1)}, bf16[208,384]{1,0:T(8,128)(2,1)S(1)}, u32[]{:S(2)}, u32[]{:S(2)}) collective-permute-start(bf16[208,384]{1,0:T(8,128)(2,1)S(1)} %get-tuple-element.53.rest_0_.refs_4_), channel_id=1, source_target_pairs={{0,1},{1,2},{2,3},{3,4},{4,5},{5,6},{6,7},{7,0},{8,9},{9,10},{10,1... | collective-permute-start | bytes 479240 | tf_op jit(solution)/shard_map/ppermute | solution.py:82
  48.8 7.2 %collective-permute-start.1 = (bf16[208,384]{1,0:T(8,128)(2,1)S(1)}, bf16[208,384]{1,0:T(8,128)(2,1)S(1)}, u32[]{:S(2)}, u32[]{:S(2)}) collective-permute-start(bf16[208,384]{1,0:T(8,128)(2,1)S(1)} %get-tuple-element.53.rest_0_.refs_4_), channel_id=1, source_target_pairs={{0,7},{1,0},{2,1},{3,2},{4,3},{5,4},{6,5},{7,6},{8,15},{9,8},{10,9... | collective-permute-start | bytes 479240 | tf_op jit(solution)/shard_map/ppermute | solution.py:83
  56.0 3.2 %copy-start.23 = (bf16[208,384]{1,0:T(8,128)(2,1)}, bf16[208,384]{1,0:T(8,128)(2,1)S(1)}, u32[]{:S(2)}) copy-start(bf16[208,384]{1,0:T(8,128)(2,1)S(1)} %collective-permute-done.rest_1_) | copy-start | bytes 479236
  56.0 7.0 %collective-permute-start.2 = (bf16[208,384]{1,0:T(8,128)(2,1)S(1)}, bf16[208,384]{1,0:T(8,128)(2,1)S(1)}, u32[]{:S(2)}, u32[]{:S(2)}) collective-permute-start(bf16[208,384]{1,0:T(8,128)(2,1)S(1)} %collective-permute-done.rest_1_), channel_id=1, source_target_pairs={{0,1},{1,2},{2,3},{3,4},{4,5},{5,6},{6,7},{7,0},{8,9},{9,10},{10,1... | collective-permute-start | bytes 479240 | tf_op jit(solution)/shard_map/ppermute | solution.py:82
  56.0 7.0 %copy-start.24 = (bf16[208,384]{1,0:T(8,128)(2,1)}, bf16[208,384]{1,0:T(8,128)(2,1)S(1)}, u32[]{:S(2)}) copy-start(bf16[208,384]{1,0:T(8,128)(2,1)S(1)} %collective-permute-done.1.rest_2_) | copy-start | bytes 479236
  56.0 7.0 %collective-permute-start.3 = (bf16[208,384]{1,0:T(8,128)(2,1)S(1)}, bf16[208,384]{1,0:T(8,128)(2,1)S(1)}, u32[]{:S(2)}, u32[]{:S(2)}) collective-permute-start(bf16[208,384]{1,0:T(8,128)(2,1)S(1)} %collective-permute-done.1.rest_2_), channel_id=1, source_target_pairs={{0,7},{1,0},{2,1},{3,2},{4,3},{5,4},{6,5},{7,6},{8,15},{9,8},{10,9... | collective-permute-start | bytes 479240 | tf_op jit(solution)/shard_map/ppermute | solution.py:83
  63.0 6.5 %collective-permute-start.4 = (bf16[208,384]{1,0:T(8,128)(2,1)S(1)}, bf16[208,384]{1,0:T(8,128)(2,1)S(1)}, u32[]{:S(2)}, u32[]{:S(2)}) collective-permute-start(bf16[208,384]{1,0:T(8,128)(2,1)S(1)} %collective-permute-done.2.rest_3_), channel_id=1, source_target_pairs={{0,1},{1,2},{2,3},{3,4},{4,5},{5,6},{6,7},{7,0},{8,9},{9,10},{10,1... | collective-permute-start | bytes 479240 | tf_op jit(solution)/shard_map/ppermute | solution.py:82
  63.7 11.6 %copy-start.26 = (bf16[208,384]{1,0:T(8,128)(2,1)}, bf16[208,384]{1,0:T(8,128)(2,1)S(1)}, u32[]{:S(2)}) copy-start(bf16[208,384]{1,0:T(8,128)(2,1)S(1)} %collective-permute-done.3.rest_4_) | copy-start | bytes 479236
  63.7 5.9 %collective-permute-start.5 = (bf16[208,384]{1,0:T(8,128)(2,1)S(1)}, bf16[208,384]{1,0:T(8,128)(2,1)S(1)}, u32[]{:S(2)}, u32[]{:S(2)}) collective-permute-start(bf16[208,384]{1,0:T(8,128)(2,1)S(1)} %collective-permute-done.3.rest_4_), channel_id=1, source_target_pairs={{0,7},{1,0},{2,1},{3,2},{4,3},{5,4},{6,5},{7,6},{8,15},{9,8},{10,9... | collective-permute-start | bytes 479240 | tf_op jit(solution)/shard_map/ppermute | solution.py:83
  69.5 5.8 %copy-start.21 = (bf16[208,384]{1,0:T(8,128)(2,1)}, bf16[208,384]{1,0:T(8,128)(2,1)S(1)}, u32[]{:S(2)}) copy-start(bf16[208,384]{1,0:T(8,128)(2,1)S(1)} %collective-permute-done.4.rest_5_) | copy-start | bytes 479236
  69.5 5.8 %collective-permute-start.6 = (bf16[112,384]{1,0:T(8,128)(2,1)S(1)}, bf16[112,384]{1,0:T(8,128)(2,1)S(1)}, u32[]{:S(2)}, u32[]{:S(2)}) collective-permute-start(bf16[112,384]{1,0:T(8,128)(2,1)S(1)} %slice.50), channel_id=1, source_target_pairs={{0,1},{1,2},{2,3},{3,4},{4,5},{5,6},{6,7},{7,0},{8,9},{9,10},{10,1... | collective-permute-start | bytes 258056 | tf_op jit(solution)/shard_map/ppermute | solution.py:86
  69.6 5.7 %copy-start.22 = (bf16[208,384]{1,0:T(8,128)(2,1)}, bf16[208,384]{1,0:T(8,128)(2,1)S(1)}, u32[]{:S(2)}) copy-start(bf16[208,384]{1,0:T(8,128)(2,1)S(1)} %collective-permute-done.5.rest_6_) | copy-start | bytes 479236
  69.6 5.4 %collective-permute-start.7 = (bf16[96,384]{1,0:T(8,128)(2,1)S(1)}, bf16[96,384]{1,0:T(8,128)(2,1)S(1)}, u32[]{:S(2)}, u32[]{:S(2)}) collective-permute-start(bf16[96,384]{1,0:T(8,128)(2,1)S(1)} %slice.51), channel_id=1, source_target_pairs={{0,7},{1,0},{2,1},{3,2},{4,3},{5,4},{6,5},{7,6},{8,15},{9,8},{10,9... | collective-permute-start | bytes 221192 | tf_op jit(solution)/shard_map/ppermute | solution.py:87
  75.9 26.3 %copy-start.15 = (bf16[1536,192]{0,1:T(8,128)(2,1)S(1)}, bf16[1536,192]{0,1:T(8,128)(2,1)}, u32[]{:S(2)}) copy-start(bf16[1536,192]{0,1:T(8,128)(2,1)} %param.16) | copy-start | bytes 1769476
  75.9 27.5 %copy-start.16 = (bf16[1536,192]{0,1:T(8,128)(2,1)S(1)}, bf16[1536,192]{0,1:T(8,128)(2,1)}, u32[]{:S(2)}) copy-start(bf16[1536,192]{0,1:T(8,128)(2,1)} %param.17) | copy-start | bytes 1769476
  95.4 9.2 %copy-start.11 = (f32[8,1,1536]{2,1,0:T(1,128)}, f32[8,1,1536]{2,1,0:T(1,128)S(1)}, u32[]{:S(2)}) copy-start(f32[8,1,1536]{2,1,0:T(1,128)S(1)} %all_to_all.46.parts_ref) | copy-start | bytes 147460
  97.4 11.0 %all-to-all-start.3 = ((f32[32,1,128]{2,1,0:T(1,128)}), f32[32,1,128]{2,1,0:T(1,128)S(1)}, u32[]{:S(2)}, u32[]{:S(2)}) async-start(f32[32,1,128]{2,1,0:T(1,128)} %shard_map.157), calls=%async_computation.3 | async-start | bytes 32768 | tf_op jit(solution)/shard_map/all_to_all | solution.py:33
  115.8 4.4 %copy-start = (bf16[1536,384]{1,0:T(8,128)(2,1)S(1)}, bf16[1536,384]{1,0:T(8,128)(2,1)}, u32[]{:S(2)}) copy-start(bf16[1536,384]{1,0:T(8,128)(2,1)} %get-tuple-element.60.far_norm.norm_ref) | copy-start | bytes 3538948
  115.8 38.4 %all-to-all-start.4 = ((bf16[8,208,384]{2,1,0:T(8,128)(2,1)}), bf16[8,208,384]{2,1,0:T(8,128)(2,1)}, u32[]{:S(2)}, u32[]{:S(2)}) async-start(bf16[8,208,384]{2,1,0:T(8,128)(2,1)} %get-tuple-element.76), calls=%async_computation.4 | async-start | bytes 2555904 | tf_op jit(solution)/shard_map/all_to_all | solution.py:33
  122.6 2.3 collective-permute-start.8
  127.6 26.6 %copy-start.9 = (bf16[208,384]{1,0:T(8,128)(2,1)S(1)}, bf16[208,384]{1,0:T(8,128)(2,1)}, u32[]{:S(2)}) copy-start(bf16[208,384]{1,0:T(8,128)(2,1)} %copy-done.8) | copy-start | bytes 479236
  127.6 26.6 %copy-start.13 = (f32[1,384]{1,0:T(1,128)S(1)}, f32[1,384]{1,0:T(1,128)}, u32[]{:S(2)}) copy-start(f32[1,384]{1,0:T(1,128)} %copy-done.12) | copy-start | bytes 4612
  127.6 26.6 %copy-start.14 = (f32[2,384]{1,0:T(2,128)S(1)}, f32[2,384]{1,0:T(2,128)}, u32[]{:S(2)}) copy-start(f32[2,384]{1,0:T(2,128)} %get-tuple-element.73.refs_3_) | copy-start | bytes 9220
  127.6 10.3 %collective-permute-start.9 = (bf16[4,48,384]{2,1,0:T(8,128)(2,1)S(1)}, bf16[4,48,384]{2,1,0:T(8,128)(2,1)S(1)}, u32[]{:S(2)}, u32[]{:S(2)}) collective-permute-start(bf16[4,48,384]{2,1,0:T(8,128)(2,1)S(1)} %get-tuple-element.65), channel_id=1, source_target_pairs={{0,16},{16,32},{32,48},{48,0},{1,17},{17,33},{33,49},{49,1},{2,18}... | collective-permute-start | bytes 442376 | tf_op jit(solution)/shard_map/ppermute | solution.py:776
  128.3 9.7 %collective-permute-start.10 = (bf16[4,48,384]{2,1,0:T(8,128)(2,1)S(1)}, bf16[4,48,384]{2,1,0:T(8,128)(2,1)S(1)}, u32[]{:S(2)}, u32[]{:S(2)}) collective-permute-start(bf16[4,48,384]{2,1,0:T(8,128)(2,1)S(1)} %get-tuple-element.66), channel_id=1, source_target_pairs={{0,32},{16,48},{32,0},{48,16},{1,33},{17,49},{33,1},{49,17},{2,34}... | collective-permute-start | bytes 442376 | tf_op jit(solution)/shard_map/ppermute | solution.py:776
  130.3 8.2 %collective-permute-start.11 = (bf16[4,48,384]{2,1,0:T(8,128)(2,1)S(1)}, bf16[4,48,384]{2,1,0:T(8,128)(2,1)S(1)}, u32[]{:S(2)}, u32[]{:S(2)}) collective-permute-start(bf16[4,48,384]{2,1,0:T(8,128)(2,1)S(1)} %get-tuple-element.67), channel_id=1, source_target_pairs={{0,48},{16,0},{32,16},{48,32},{1,49},{17,1},{33,17},{49,33},{2,50}... | collective-permute-start | bytes 442376 | tf_op jit(solution)/shard_map/ppermute | solution.py:776
  138.6 4.7 %collective-permute-start.14 = (bf16[48,384]{1,0:T(8,128)(2,1)S(1)}, bf16[48,384]{1,0:T(8,128)(2,1)S(1)}, u32[]{:S(2)}, u32[]{:S(2)}) collective-permute-start(bf16[48,384]{1,0:T(8,128)(2,1)S(1)} %get-tuple-element.71), channel_id=1, source_target_pairs={{0,192},{64,0},{128,64},{192,128},{1,193},{65,1},{129,65},{193,129... | collective-permute-start | bytes 110600 | tf_op jit(solution)/shard_map/ppermute | solution.py:776
  140.3 5.5 %collective-permute-start.13 = (bf16[48,384]{1,0:T(8,128)(2,1)S(1)}, bf16[48,384]{1,0:T(8,128)(2,1)S(1)}, u32[]{:S(2)}, u32[]{:S(2)}) collective-permute-start(bf16[48,384]{1,0:T(8,128)(2,1)S(1)} %get-tuple-element.70), channel_id=1, source_target_pairs={{0,128},{64,192},{128,0},{192,64},{1,129},{65,193},{129,1},{193,65... | collective-permute-start | bytes 110600 | tf_op jit(solution)/shard_map/ppermute | solution.py:776
  140.9 4.9 %collective-permute-start.12 = (bf16[48,384]{1,0:T(8,128)(2,1)S(1)}, bf16[48,384]{1,0:T(8,128)(2,1)S(1)}, u32[]{:S(2)}, u32[]{:S(2)}) collective-permute-start(bf16[48,384]{1,0:T(8,128)(2,1)S(1)} %get-tuple-element.69), channel_id=1, source_target_pairs={{0,64},{64,128},{128,192},{192,0},{1,65},{65,129},{129,193},{193,1... | collective-permute-start | bytes 110600 | tf_op jit(solution)/shard_map/ppermute | solution.py:776
  169.2 22.7 %copy-start.6 = (bf16[192,768]{1,0:T(8,128)(2,1)S(1)}, bf16[192,768]{1,0:T(8,128)(2,1)}, u32[]{:S(2)}) copy-start(bf16[192,768]{1,0:T(8,128)(2,1)} %get-tuple-element.62.hidden_ref) | copy-start | bytes 884740
  169.2 24.3 %copy-start.1 = (bf16[768,1536]{1,0:T(8,128)(2,1)S(1)}, bf16[768,1536]{1,0:T(8,128)(2,1)}, u32[]{:S(2)}) copy-start(bf16[768,1536]{1,0:T(8,128)(2,1)} %two_ref.1) | copy-start | bytes 7077892
  196.1 3.6 %collective-permute-start.19 = (bf16[16,48,768]{2,1,0:T(8,128)(2,1)S(1)}, bf16[16,48,768]{2,1,0:T(8,128)(2,1)S(1)}, u32[]{:S(2)}, u32[]{:S(2)}) collective-permute-start(bf16[16,48,768]{2,1,0:T(8,128)(2,1)S(1)} %get-tuple-element.84), channel_id=1, source_target_pairs={{0,8},{8,0},{1,9},{9,1},{2,10},{10,2},{3,11},{11,3},{4,12},{12,4},... | collective-permute-start | bytes 3538952 | tf_op jit(solution)/shard_map/ppermute | solution.py:836
  196.3 9.8 %collective-permute-start.15 = (bf16[16,48,768]{2,1,0:T(8,128)(2,1)}, bf16[16,48,768]{2,1,0:T(8,128)(2,1)}, u32[]{:S(2)}, u32[]{:S(2)}) collective-permute-start(bf16[16,48,768]{2,1,0:T(8,128)(2,1)} %get-tuple-element.78), channel_id=1, source_target_pairs={{0,8},{8,0},{1,9},{9,1},{2,10},{10,2},{3,11},{11,3},{4,12},{12,4},... | collective-permute-start | bytes 3538952 | tf_op jit(solution)/shard_map/ppermute | solution.py:825
  201.0 5.0 %copy-start.3 = (bf16[1536,192]{1,0:T(8,128)(2,1)S(1)}, bf16[1536,192]{1,0:T(8,128)(2,1)}, u32[]{:S(2)}) copy-start(bf16[1536,192]{1,0:T(8,128)(2,1)} %copy-done.2) | copy-start | bytes 1769476
  201.0 5.0 %copy-start.7 = (bf16[192,768]{1,0:T(8,128)(2,1)S(1)}, bf16[192,768]{1,0:T(8,128)(2,1)}, u32[]{:S(2)}) copy-start(bf16[192,768]{1,0:T(8,128)(2,1)} %get-tuple-element.62.hidden_ref) | copy-start | bytes 884740
  201.0 25.8 %all-to-all-start.8 = ((bf16[4,4,48,768]{3,2,1,0:T(8,128)(2,1)}), bf16[4,4,48,768]{3,2,1,0:T(8,128)(2,1)S(1)}, u32[]{:S(2)}, u32[]{:S(2)}) async-start(bf16[4,4,48,768]{3,2,1,0:T(8,128)(2,1)} %shard_map.168), calls=%async_computation.8 | async-start | bytes 2359296 | tf_op jit(solution)/shard_map/all_to_all | solution.py:33
  208.8 16.5 %collective-permute-start.16 = (bf16[4,48,768]{2,1,0:T(8,128)(2,1)}, bf16[4,48,768]{2,1,0:T(8,128)(2,1)S(1)}, u32[]{:S(2)}, u32[]{:S(2)}) collective-permute-start(bf16[4,48,768]{2,1,0:T(8,128)(2,1)} %get-tuple-element.80), channel_id=1, source_target_pairs={{0,16},{16,32},{32,48},{48,0},{1,17},{17,33},{33,49},{49,1},{2,18}... | collective-permute-start | bytes 884744 | tf_op jit(solution)/shard_map/ppermute | solution.py:776
  209.6 15.8 %collective-permute-start.17 = (bf16[4,48,768]{2,1,0:T(8,128)(2,1)}, bf16[4,48,768]{2,1,0:T(8,128)(2,1)S(1)}, u32[]{:S(2)}, u32[]{:S(2)}) collective-permute-start(bf16[4,48,768]{2,1,0:T(8,128)(2,1)} %get-tuple-element.81), channel_id=1, source_target_pairs={{0,32},{16,48},{32,0},{48,16},{1,33},{17,49},{33,1},{49,17},{2,34}... | collective-permute-start | bytes 884744 | tf_op jit(solution)/shard_map/ppermute | solution.py:776
  211.7 14.2 %collective-permute-start.18 = (bf16[4,48,768]{2,1,0:T(8,128)(2,1)}, bf16[4,48,768]{2,1,0:T(8,128)(2,1)S(1)}, u32[]{:S(2)}, u32[]{:S(2)}) collective-permute-start(bf16[4,48,768]{2,1,0:T(8,128)(2,1)} %get-tuple-element.82), channel_id=1, source_target_pairs={{0,48},{16,0},{32,16},{48,32},{1,49},{17,1},{33,17},{49,33},{2,50}... | collective-permute-start | bytes 884744 | tf_op jit(solution)/shard_map/ppermute | solution.py:776
  226.8 10.6 %all-to-all-start.7 = ((bf16[4,48,768]{2,1,0:T(8,128)(2,1)}), bf16[4,48,768]{2,1,0:T(8,128)(2,1)S(1)}, u32[]{:S(2)}, u32[]{:S(2)}) async-start(bf16[4,48,768]{2,1,0:T(8,128)(2,1)} %shard_map.166), calls=%async_computation.7 | async-start | bytes 589824 | tf_op jit(solution)/shard_map/all_to_all | solution.py:33
  231.8 6.3 %collective-permute-start.20 = (bf16[48,768]{1,0:T(8,128)(2,1)S(1)}, bf16[48,768]{1,0:T(8,128)(2,1)S(1)}, u32[]{:S(2)}, u32[]{:S(2)}) collective-permute-start(bf16[48,768]{1,0:T(8,128)(2,1)S(1)} %get-tuple-element.86), channel_id=1, source_target_pairs={{0,16},{16,32},{32,48},{48,0},{1,17},{17,33},{33,49},{49,1},{2,18}... | collective-permute-start | bytes 221192 | tf_op jit(solution)/shard_map/ppermute | solution.py:776
  232.3 6.7 %collective-permute-start.21 = (bf16[48,768]{1,0:T(8,128)(2,1)S(1)}, bf16[48,768]{1,0:T(8,128)(2,1)S(1)}, u32[]{:S(2)}, u32[]{:S(2)}) collective-permute-start(bf16[48,768]{1,0:T(8,128)(2,1)S(1)} %get-tuple-element.87), channel_id=1, source_target_pairs={{0,32},{16,48},{32,0},{48,16},{1,33},{17,49},{33,1},{49,17},{2,34}... | collective-permute-start | bytes 221192 | tf_op jit(solution)/shard_map/ppermute | solution.py:776
  235.8 4.4 %collective-permute-start.22 = (bf16[48,768]{1,0:T(8,128)(2,1)S(1)}, bf16[48,768]{1,0:T(8,128)(2,1)S(1)}, u32[]{:S(2)}, u32[]{:S(2)}) collective-permute-start(bf16[48,768]{1,0:T(8,128)(2,1)S(1)} %get-tuple-element.88), channel_id=1, source_target_pairs={{0,48},{16,0},{32,16},{48,32},{1,49},{17,1},{33,17},{49,33},{2,50}... | collective-permute-start | bytes 221192 | tf_op jit(solution)/shard_map/ppermute | solution.py:776
  (17 other events, 19.7 us)

commit v7 on v6

--- a/solution.py
+++ b/solution.py
@@ -308,10 +308,10 @@
     grad_ref,
     up_ref,
     grads_ref,
-    far_out,
+    out_ref,
     *rest,
 ):
-    fetched, report_ref, out_ref, sems, out_sems = rest[:-4], *rest[-4:]
+    fetched, report_ref, sems = rest[:-2], rest[-2], rest[-1]
     (
         out_weights_ref,
         heads_ref,
@@ -399,7 +399,6 @@
         copy.wait()
     count = out_ref.shape[0]
     block = norm_ref.shape[0] // count
-    sending = []
     first = jnp.zeros_like(valid)
     second = jnp.zeros_like(valid)
     for k in range(count):
@@ -408,12 +407,6 @@
         part = part + jnp.dot(key_weights_ref[rows, :], grad_key, preferred_element_type=f32)
         part = part + jnp.dot(value_weights_ref[rows, :], grad_value, preferred_element_type=f32)
         out_ref[k, 0:block, :] = part.astype(bf16)
-        sending.append(
-            pltpu.make_async_copy(
-                out_ref.at[k, pl.ds(0, block)], far_out.at[k, pl.ds(0, block)], out_sems.at[k]
-            )
-        )
-        sending[-1].start()
         first = first + jnp.sum(part, 0, keepdims=True)
         second = second + jnp.sum(part * norm_ref[rows, :].astype(f32), 0, keepdims=True)
     width = norm_ref.shape[0]
@@ -424,13 +417,6 @@
     ).astype(bf16)
     for k in range(count):
         out_ref[k, block : block + EXTRA, :] = stats
-        tail = pl.ds(block, EXTRA)
-        sending.append(
-            pltpu.make_async_copy(out_ref.at[k, tail], far_out.at[k, tail], out_sems.at[count + k])
-        )
-        sending[-1].start()
-    for copy in sending:
-        copy.wait()
 
 
 def wide_other(which, norm_ref, grads_ref, out_ref):
@@ -524,17 +510,20 @@
             target_ref[chip] = one[chip * share : (chip + 1) * share]
 
 
-def own_two(own, column, hidden_ref, grad_ref, got_ref, *rest):
-    outs, two_ref = rest[:-1], rest[-1]
-    chips, share = got_ref.shape[:2]
+def own_two(own, column, hidden_ref, grad_ref, got_ref, *outs):
     side = len(outs)
-    rows = rows_of(own[0], grad_ref, chips, share)
-    two = jnp.dot(rows, hidden_ref[...], preferred_element_type=f32)
-    for chip in range(chips):
-        part = two[chip * share : (chip + 1) * share] + got_ref[chip].astype(f32)
-        two_ref[chip % side, chip // side] = part.astype(bf16)
+    lines, share = outs[0].shape[:2]
     for k in range(side):
-        outs[k][...] = two_ref[lax.rem(column[0] + k, side)]
+        place = lax.rem(column[0] + k, side)
+        chips = [line * side + place for line in range(lines)]
+        rows = [
+            grad_ref[pl.ds(pl.multiple_of((CORES * chip + own[0]) * share, 16), share), :]
+            for chip in chips
+        ]
+        two = jnp.dot(jnp.concatenate(rows, 0), hidden_ref[...], preferred_element_type=f32)
+        for line, chip in enumerate(chips):
+            part = two[line * share : (line + 1) * share] + got_ref[chip].astype(f32)
+            outs[k][line] = part.astype(bf16)
 
 
 def own_one(own_ref, got_ref, out_ref):
@@ -721,7 +710,7 @@
     loss, grad, up, grads, sending = call(
         slide_backward,
         [((1, 1), f32), ((1, width), f32), ((1, inner), f32), ((3 * inner, length), bf16)]
-        + [((parts, block + EXTRA, length), bf16, "far")],
+        + [((parts, block + EXTRA, length), bf16)],
         logits,
         slide_pair[:, None],
         pooled,
@@ -747,9 +736,7 @@
             (w_value.shape, bf16),
             (slide_norm.shape, bf16),
             ((owners, width), f32),
-            ((parts, block + EXTRA, length), bf16),
             7,
-            2 * parts,
         ],
         limit=60,
     )
@@ -841,10 +828,15 @@
         grad_embedding,
         two_got,
         scalars=(core, column),
-        scratch=[((side, lines, share, units), bf16)],
+    )
+    (one_across,) = call(
+        own_one,
+        [((lines, side, share, units), bf16)],
+        one_own,
+        one_got,
+        anchors=(two_along[0],),
     )
     two_along = shift(two_along, "column")
-    (one_across,) = call(own_one, [((lines, side, share, units), bf16)], one_own, one_got)
     one_across = exchange(one_across, "line")
     (two_across,) = call(add_up, [((lines, share, units), bf16)], *two_along)
     one_along = call(add_lines, [((share, units), bf16)] * side, one_across, scalars=(column,))

time: 242 us -> 237 us (0.979)
  Pallas kernels: 34.9 us -> 31.6 us
    pallas_call x18, Pallas kernels: 34.9 us -> 31.6 us  [call(): pl.pallas_call(kernel if skip else body, out_shape=[jax.ShapeDtypeStruct(...]
    unnamed x78 -> x72, local copies, waits for them, and re-layouts: 8.71 us -> 8.73 us
where the time goes in v7:
time: 237 us; the launch traced here: 236 us
  waiting for transfers between devices  64.4 us (27%)
  blocking collectives  63.2 us (27%)
  starting transfers between devices  56.8 us (24%)
  Pallas kernels  31.6 us (13%)
  local copies, waits for them, and re-layouts  16 us (7%)
    all_to_all x4, blocking collectives, exchange(): return lax.all_to_all(values, axis, 0, 0, tiled=True)  63.2 us
    pallas_call x18, Pallas kernels, call(): pl.pallas_call(kernel if skip else body, out_shape=[jax.ShapeDtypeStruct(...  31.6 us
    all_to_all x5, starting transfers between devices, exchange(): return lax.all_to_all(values, axis, 0, 0, tiled=True)  27.6 us
    ppermute x12, waiting for transfers between devices, shift(): lax.ppermute(values[k], axis, turn(len(values), k))  24.5 us
    all_to_all x5, waiting for transfers between devices, exchange(): return lax.all_to_all(values, axis, 0, 0, tiled=True)  23.6 us
    ppermute x12, starting transfers between devices, shift(): lax.ppermute(values[k], axis, turn(len(values), k))  15.8 us
    ppermute x3, waiting for transfers between devices, gather_ring(): back = lax.ppermute(back, 'mp', turn(count, 1))  11.4 us
    unnamed x72, local copies, waits for them, and re-layouts  8.73 us
  transfers between devices with their start and end apart: 28, of which 18 were waited for; matrix products, arithmetic and copies ran while one was open for 6% of the time, Pallas kernels for 3%

profile of v7, /device:TPU:8, one launch (start us, length us, event | category | flops | bytes accessed | tf_op | source)
XLA Modules:
  0.0 236.1 jit_solution(1218832146550783295)
XLA Ops:
  0.6 4.5 %shard_map.153 = (bf16[192,1536]{1,0:T(8,128)(2,1)}, bf16[192,768]{1,0:T(8,128)(2,1)}, f32[192,768]{1,0:T(8,128)}, bf16[8,288,128]{2,1,0:T(8,128)(2,1)}) custom-call(bf16[192,1536]{1,0:T(8,128)(2,1)} %far_x.1, bf16[1536,768]{1,0:T(8,128)(2,1)} %far_one.1, bf16[768,1536]{1,0:T(8,128)(2,1)} %two_ref.1), custom_call_target="tpu_custom_call" | custom-call | tf_op jit(solution)/shard_map/pallas_call | solution.py:49
  5.2 8.6 %all-to-all-start = ((bf16[8,288,128]{2,1,0:T(8,128)(2,1)}), bf16[8,288,128]{2,1,0:T(8,128)(2,1)S(1)}, u32[]{:S(2)}, u32[]{:S(2)}) async-start(bf16[8,288,128]{2,1,0:T(8,128)(2,1)} %get-tuple-element.51), calls=%async_computation | async-start | bytes 1179648 | tf_op jit(solution)/shard_map/all_to_all | solution.py:33
  14.4 1.2 copy.42
  17.8 1.2 constant_dynamic-slice_fusion.3
  19.2 13.5 %all-to-all-done.refs_9_ = bf16[8,288,128]{2,1,0:T(8,128)(2,1)S(1)} async-done(((bf16[8,288,128]{2,1,0:T(8,128)(2,1)}), bf16[8,288,128]{2,1,0:T(8,128)(2,1)S(1)}, u32[]{:S(2)}, u32[]{:S(2)}) %all-to-all-start) | async-done | bytes 589856 | tf_op jit(solution)/shard_map/all_to_all | solution.py:33
  33.0 14.8 %all_to_all.45 = bf16[32,16,256]{2,1,0:T(8,128)(2,1)S(1)} all-to-all(bf16[32,16,256]{2,1,0:T(8,128)(2,1)S(1)} %bitcast.56), channel_id=1, replica_groups=mesh['line'=4,'column'=4,'core'=2,'mp'=8] {'line','column','core'}, dimensions={0} | all-to-all | bytes 524288 | tf_op jit(solution)/shard_map/all_to_all | solution.py:33
  48.8 2.7 %collective-permute-start.1 = (bf16[208,384]{1,0:T(8,128)(2,1)S(1)}, bf16[208,384]{1,0:T(8,128)(2,1)S(1)}, u32[]{:S(2)}, u32[]{:S(2)}) collective-permute-start(bf16[208,384]{1,0:T(8,128)(2,1)S(1)} %get-tuple-element.53.rest_0_.refs_4_), channel_id=1, source_target_pairs={{0,7},{1,0},{2,1},{3,2},{4,3},{5,4},{6,5},{7,6},{8,15},{9,8},{10,9... | collective-permute-start | bytes 479240 | tf_op jit(solution)/shard_map/ppermute | solution.py:83
  51.5 4.5 %collective-permute-done.rest_1_ = bf16[208,384]{1,0:T(8,128)(2,1)S(1)} collective-permute-done((bf16[208,384]{1,0:T(8,128)(2,1)S(1)}, bf16[208,384]{1,0:T(8,128)(2,1)S(1)}, u32[]{:S(2)}, u32[]{:S(2)}) %collective-permute-start) | collective-permute-done | bytes 159776 | tf_op jit(solution)/shard_map/ppermute | solution.py:82
  56.0 3.2 %collective-permute-start.3 = (bf16[208,384]{1,0:T(8,128)(2,1)S(1)}, bf16[208,384]{1,0:T(8,128)(2,1)S(1)}, u32[]{:S(2)}, u32[]{:S(2)}) collective-permute-start(bf16[208,384]{1,0:T(8,128)(2,1)S(1)} %collective-permute-done.1.rest_2_), channel_id=1, source_target_pairs={{0,7},{1,0},{2,1},{3,2},{4,3},{5,4},{6,5},{7,6},{8,15},{9,8},{10,9... | collective-permute-start | bytes 479240 | tf_op jit(solution)/shard_map/ppermute | solution.py:83
  59.3 3.7 %collective-permute-done.2.rest_3_ = bf16[208,384]{1,0:T(8,128)(2,1)S(1)} collective-permute-done((bf16[208,384]{1,0:T(8,128)(2,1)S(1)}, bf16[208,384]{1,0:T(8,128)(2,1)S(1)}, u32[]{:S(2)}, u32[]{:S(2)}) %collective-permute-start.2) | collective-permute-done | bytes 159776 | tf_op jit(solution)/shard_map/ppermute | solution.py:82
  63.7 2.7 %collective-permute-start.5 = (bf16[208,384]{1,0:T(8,128)(2,1)S(1)}, bf16[208,384]{1,0:T(8,128)(2,1)S(1)}, u32[]{:S(2)}, u32[]{:S(2)}) collective-permute-start(bf16[208,384]{1,0:T(8,128)(2,1)S(1)} %collective-permute-done.3.rest_4_), channel_id=1, source_target_pairs={{0,7},{1,0},{2,1},{3,2},{4,3},{5,4},{6,5},{7,6},{8,15},{9,8},{10,9... | collective-permute-start | bytes 479240 | tf_op jit(solution)/shard_map/ppermute | solution.py:83
  66.3 3.2 %collective-permute-done.4.rest_5_ = bf16[208,384]{1,0:T(8,128)(2,1)S(1)} collective-permute-done((bf16[208,384]{1,0:T(8,128)(2,1)S(1)}, bf16[208,384]{1,0:T(8,128)(2,1)S(1)}, u32[]{:S(2)}, u32[]{:S(2)}) %collective-permute-start.4) | collective-permute-done | bytes 159776 | tf_op jit(solution)/shard_map/ppermute | solution.py:82
  69.6 3.5 %collective-permute-start.7 = (bf16[96,384]{1,0:T(8,128)(2,1)S(1)}, bf16[96,384]{1,0:T(8,128)(2,1)S(1)}, u32[]{:S(2)}, u32[]{:S(2)}) collective-permute-start(bf16[96,384]{1,0:T(8,128)(2,1)S(1)} %slice.51), channel_id=1, source_target_pairs={{0,7},{1,0},{2,1},{3,2},{4,3},{5,4},{6,5},{7,6},{8,15},{9,8},{10,9... | collective-permute-start | bytes 221192 | tf_op jit(solution)/shard_map/ppermute | solution.py:87
  73.1 2.0 collective-permute-done.7.rest_8_
  75.9 6.6 %shard_map.156 = (bf16[1536,384]{1,0:T(8,128)(2,1)}, f32[2,3,96,384]{3,2,1,0:T(8,128)}, f32[2,384,384]{2,1,0:T(8,128)}, f32[2,384]{1,0:T(2,128)}, f32[2,2,384]{2...) custom-call(s32[1]{0:T(128)} %bitcast.1.here, ...), custom_call_target="tpu_custom_call" | custom-call | tf_op jit(solution)/shard_map/pallas_call | solution.py:49
  82.5 12.9 %all_to_all.46.parts_ref = f32[8,1,1536]{2,1,0:T(1,128)S(1)} all-to-all(f32[8,1,1536]{2,1,0:T(1,128)} %get-tuple-element.54), channel_id=1, replica_groups=mesh['line'=4,'column'=4,'core'=2,'mp'=8] {'mp'}, dimensions={0} | all-to-all | bytes 98304 | tf_op jit(solution)/shard_map/all_to_all | solution.py:33
  96.3 1.0 shard_map.157
  97.3 4.9 %all-to-all-start.3 = ((f32[32,1,128]{2,1,0:T(1,128)}), f32[32,1,128]{2,1,0:T(1,128)S(1)}, u32[]{:S(2)}, u32[]{:S(2)}) async-start(f32[32,1,128]{2,1,0:T(1,128)} %shard_map.157), calls=%async_computation.3 | async-start | bytes 32768 | tf_op jit(solution)/shard_map/all_to_all | solution.py:33
  102.2 1.2 copy.49.far_query_weights
  103.4 1.2 copy.50.far_key_weights
  104.6 1.3 copy.51.far_value_weights
  106.6 1.8 all-to-all-done.3
  108.9 6.3 %shard_map.158 = (f32[1,1]{1,0:T(1,128)}, f32[1,1536]{1,0:T(1,128)}, f32[1,192]{1,0:T(1,128)}, bf16[576,384]{1,0:T(8,128)(2,1)}, bf16[8,208,384]{2,1,0:T(8,128)(2,1)}) custom-call(s32[1]{0:T(128)} %bitcast.owner, f32[32,128]{1,0:T(8,128)} %bitcast.66, s32[32,1]{1,0:T(8,128)} %copy.48.pair_ref, f32[8,1,1536]{2,1,0:T(1,128)} %copy-done.8, ...), custom_call_target="tpu_custom_call" | custom-call | tf_op jit(solution)/shard_map/pallas_call | solution.py:49
  115.3 4.4 %all-to-all-start.4 = ((bf16[8,208,384]{2,1,0:T(8,128)(2,1)}), bf16[8,208,384]{2,1,0:T(8,128)(2,1)}, u32[]{:S(2)}, u32[]{:S(2)}) async-start(bf16[8,208,384]{2,1,0:T(8,128)(2,1)} %get-tuple-element.76), calls=%async_computation.4 | async-start | bytes 2555904 | tf_op jit(solution)/shard_map/all_to_all | solution.py:33
  120.7 1.4 shard_map.159
  123.1 1.4 collective-permute-done.8.got_ref
  124.4 1.0 copy-done.3
  125.5 1.6 shard_map.160
  127.7 2.1 collective-permute-start.10
  129.8 1.2 collective-permute-start.11
  131.1 6.3 %collective-permute-done.9.refs_1_ = bf16[4,48,384]{2,1,0:T(8,128)(2,1)S(1)} collective-permute-done((bf16[4,48,384]{2,1,0:T(8,128)(2,1)S(1)}, bf16[4,48,384]{2,1,0:T(8,128)(2,1)S(1)}, u32[]{:S(2)}, u32[]{:S(2)}) %collective-permute-start.9) | collective-permute-done | bytes 147488 | tf_op jit(solution)/shard_map/ppermute | solution.py:763
  138.1 1.7 collective-permute-start.14
  140.4 2.0 collective-permute-start.12
  142.8 2.5 %collective-permute-done.13 = bf16[48,384]{1,0:T(8,128)(2,1)S(1)} collective-permute-done((bf16[48,384]{1,0:T(8,128)(2,1)S(1)}, bf16[48,384]{1,0:T(8,128)(2,1)S(1)}, u32[]{:S(2)}, u32[]{:S(2)}) %collective-permute-start.13) | collective-permute-done | bytes 36896 | tf_op jit(solution)/shard_map/ppermute | solution.py:763
  145.3 8.3 %all-to-all-done.4.refs_7_ = bf16[8,208,384]{2,1,0:T(8,128)(2,1)} async-done(((bf16[8,208,384]{2,1,0:T(8,128)(2,1)}), bf16[8,208,384]{2,1,0:T(8,128)(2,1)}, u32[]{:S(2)}, u32[]{:S(2)}) %all-to-all-start.4) | async-done | bytes 1277984 | tf_op jit(solution)/shard_map/all_to_all | solution.py:33
  153.7 1.8 shard_map.162
  155.5 13.1 %all_to_all.47 = bf16[32,16,192]{2,1,0:T(8,128)(2,1)S(1)} all-to-all(bf16[32,16,192]{2,1,0:T(8,128)(2,1)S(1)} %bitcast.59), channel_id=1, replica_groups=mesh['line'=4,'column'=4,'core'=2,'mp'=8] {'line','column','core'}, dimensions={0} | all-to-all | bytes 393216 | tf_op jit(solution)/shard_map/all_to_all | solution.py:33
  169.0 22.4 %all_to_all.48.parts_ref = bf16[8,288,128]{2,1,0:T(8,128)(2,1)S(1)} all-to-all(bf16[8,288,128]{2,1,0:T(8,128)(2,1)S(1)} %shard_map.163), channel_id=1, replica_groups=mesh['line'=4,'column'=4,'core'=2,'mp'=8] {'mp'}, dimensions={0} | all-to-all | bytes 1179648 | tf_op jit(solution)/shard_map/all_to_all | solution.py:33
  192.2 2.6 %shard_map.167 = (bf16[16,48,768]{2,1,0:T(8,128)(2,1)S(1)}, bf16[16,48,768]{2,1,0:T(8,128)(2,1)S(1)}) custom-call(bf16[768,1536]{1,0:T(8,128)(2,1)S(1)} %copy-done.1, f32[768,192]{1,0:T(8,128)S(1)} %bitcast.50, bf16[768,192]{1,0:T(8,128)(2,1)S(1)} %bitcast.52, bf16[768,192]{1,0:T(8,128)(2,1)S(1)} %bitcast.54, bf16[1536,192]{1,0:T(8,128)(2,1)S(1)} %get-tuple-element.77.grad_ref), custom_call_target="tpu_custom_call" | custom-call | tf_op jit(solution)/shard_map/pallas_call | solution.py:49
  195.3 1.0 shard_map.165
  196.3 1.4 collective-permute-done.19.refs_2_
  197.8 1.3 shard_map.168
  199.0 4.9 %all-to-all-start.8 = ((bf16[4,4,48,768]{3,2,1,0:T(8,128)(2,1)}), bf16[4,4,48,768]{3,2,1,0:T(8,128)(2,1)S(1)}, u32[]{:S(2)}, u32[]{:S(2)}) async-start(bf16[4,4,48,768]{3,2,1,0:T(8,128)(2,1)} %shard_map.168), calls=%async_computation.8 | async-start | bytes 2359296 | tf_op jit(solution)/shard_map/all_to_all | solution.py:33
  204.7 2.1 collective-permute-start.17
  208.8 11.9 %collective-permute-done.16.refs_1_ = bf16[4,48,768]{2,1,0:T(8,128)(2,1)S(1)} collective-permute-done((bf16[4,48,768]{2,1,0:T(8,128)(2,1)}, bf16[4,48,768]{2,1,0:T(8,128)(2,1)S(1)}, u32[]{:S(2)}, u32[]{:S(2)}) %collective-permute-start.16) | collective-permute-done | bytes 294944 | tf_op jit(solution)/shard_map/ppermute | solution.py:763
  222.0 4.8 %all-to-all-start.7 = ((bf16[4,48,768]{2,1,0:T(8,128)(2,1)}), bf16[4,48,768]{2,1,0:T(8,128)(2,1)S(1)}, u32[]{:S(2)}, u32[]{:S(2)}) async-start(bf16[4,48,768]{2,1,0:T(8,128)(2,1)} %shard_map.166), calls=%async_computation.7 | async-start | bytes 589824 | tf_op jit(solution)/shard_map/all_to_all | solution.py:33
  227.4 3.6 %collective-permute-start.21 = (bf16[48,768]{1,0:T(8,128)(2,1)S(1)}, bf16[48,768]{1,0:T(8,128)(2,1)S(1)}, u32[]{:S(2)}, u32[]{:S(2)}) collective-permute-start(bf16[48,768]{1,0:T(8,128)(2,1)S(1)} %get-tuple-element.87), channel_id=1, source_target_pairs={{0,32},{16,48},{32,0},{48,16},{1,33},{17,49},{33,1},{49,17},{2,34}... | collective-permute-start | bytes 221192 | tf_op jit(solution)/shard_map/ppermute | solution.py:763
  234.1 1.2 collective-permute-done.22.refs_3_
  (158 shorter events, 22.5 us)
Async XLA Ops:
  5.2 8.6 %copy-start.15 = (bf16[192,1536]{1,0:T(8,128)(2,1)S(1)}, bf16[192,1536]{1,0:T(8,128)(2,1)}, u32[]{:S(2)}) copy-start(bf16[192,1536]{1,0:T(8,128)(2,1)} %far_x.1) | copy-start | bytes 1769476
  5.2 9.3 %copy-start.17 = (bf16[192,1536]{1,0:T(8,128)(2,1)S(1)}, bf16[192,1536]{1,0:T(8,128)(2,1)}, u32[]{:S(2)}) copy-start(bf16[192,1536]{1,0:T(8,128)(2,1)} %get-tuple-element.49) | copy-start | bytes 1769476
  5.2 27.5 %all-to-all-start = ((bf16[8,288,128]{2,1,0:T(8,128)(2,1)}), bf16[8,288,128]{2,1,0:T(8,128)(2,1)S(1)}, u32[]{:S(2)}, u32[]{:S(2)}) async-start(bf16[8,288,128]{2,1,0:T(8,128)(2,1)} %get-tuple-element.51), calls=%async_computation | async-start | bytes 1179648 | tf_op jit(solution)/shard_map/all_to_all | solution.py:33
  48.2 27.1 %copy-start.5 = (bf16[208,384]{1,0:T(8,128)(2,1)}, bf16[208,384]{1,0:T(8,128)(2,1)S(1)}, u32[]{:S(2)}) copy-start(bf16[208,384]{1,0:T(8,128)(2,1)S(1)} %get-tuple-element.53.rest_0_.refs_4_) | copy-start | bytes 479236
  48.2 27.1 %copy-start.9 = (f32[1,384]{1,0:T(1,128)}, f32[1,384]{1,0:T(1,128)S(1)}, u32[]{:S(2)}) copy-start(f32[1,384]{1,0:T(1,128)S(1)} %get-tuple-element.52.valid_ref.refs_2_) | copy-start | bytes 4612
  48.2 7.8 %collective-permute-start = (bf16[208,384]{1,0:T(8,128)(2,1)S(1)}, bf16[208,384]{1,0:T(8,128)(2,1)S(1)}, u32[]{:S(2)}, u32[]{:S(2)}) collective-permute-start(bf16[208,384]{1,0:T(8,128)(2,1)S(1)} %get-tuple-element.53.rest_0_.refs_4_), channel_id=1, source_target_pairs={{0,1},{1,2},{2,3},{3,4},{4,5},{5,6},{6,7},{7,0},{8,9},{9,10},{10,1... | collective-permute-start | bytes 479240 | tf_op jit(solution)/shard_map/ppermute | solution.py:82
  48.8 7.2 %collective-permute-start.1 = (bf16[208,384]{1,0:T(8,128)(2,1)S(1)}, bf16[208,384]{1,0:T(8,128)(2,1)S(1)}, u32[]{:S(2)}, u32[]{:S(2)}) collective-permute-start(bf16[208,384]{1,0:T(8,128)(2,1)S(1)} %get-tuple-element.53.rest_0_.refs_4_), channel_id=1, source_target_pairs={{0,7},{1,0},{2,1},{3,2},{4,3},{5,4},{6,5},{7,6},{8,15},{9,8},{10,9... | collective-permute-start | bytes 479240 | tf_op jit(solution)/shard_map/ppermute | solution.py:83
  56.0 3.2 %copy-start.20 = (bf16[208,384]{1,0:T(8,128)(2,1)}, bf16[208,384]{1,0:T(8,128)(2,1)S(1)}, u32[]{:S(2)}) copy-start(bf16[208,384]{1,0:T(8,128)(2,1)S(1)} %collective-permute-done.rest_1_) | copy-start | bytes 479236
  56.0 7.0 %collective-permute-start.2 = (bf16[208,384]{1,0:T(8,128)(2,1)S(1)}, bf16[208,384]{1,0:T(8,128)(2,1)S(1)}, u32[]{:S(2)}, u32[]{:S(2)}) collective-permute-start(bf16[208,384]{1,0:T(8,128)(2,1)S(1)} %collective-permute-done.rest_1_), channel_id=1, source_target_pairs={{0,1},{1,2},{2,3},{3,4},{4,5},{5,6},{6,7},{7,0},{8,9},{9,10},{10,1... | collective-permute-start | bytes 479240 | tf_op jit(solution)/shard_map/ppermute | solution.py:82
  56.0 7.0 %copy-start.21 = (bf16[208,384]{1,0:T(8,128)(2,1)}, bf16[208,384]{1,0:T(8,128)(2,1)S(1)}, u32[]{:S(2)}) copy-start(bf16[208,384]{1,0:T(8,128)(2,1)S(1)} %collective-permute-done.1.rest_2_) | copy-start | bytes 479236
  56.0 7.0 %collective-permute-start.3 = (bf16[208,384]{1,0:T(8,128)(2,1)S(1)}, bf16[208,384]{1,0:T(8,128)(2,1)S(1)}, u32[]{:S(2)}, u32[]{:S(2)}) collective-permute-start(bf16[208,384]{1,0:T(8,128)(2,1)S(1)} %collective-permute-done.1.rest_2_), channel_id=1, source_target_pairs={{0,7},{1,0},{2,1},{3,2},{4,3},{5,4},{6,5},{7,6},{8,15},{9,8},{10,9... | collective-permute-start | bytes 479240 | tf_op jit(solution)/shard_map/ppermute | solution.py:83
  63.0 6.5 %collective-permute-start.4 = (bf16[208,384]{1,0:T(8,128)(2,1)S(1)}, bf16[208,384]{1,0:T(8,128)(2,1)S(1)}, u32[]{:S(2)}, u32[]{:S(2)}) collective-permute-start(bf16[208,384]{1,0:T(8,128)(2,1)S(1)} %collective-permute-done.2.rest_3_), channel_id=1, source_target_pairs={{0,1},{1,2},{2,3},{3,4},{4,5},{5,6},{6,7},{7,0},{8,9},{9,10},{10,1... | collective-permute-start | bytes 479240 | tf_op jit(solution)/shard_map/ppermute | solution.py:82
  63.7 11.6 %copy-start.23 = (bf16[208,384]{1,0:T(8,128)(2,1)}, bf16[208,384]{1,0:T(8,128)(2,1)S(1)}, u32[]{:S(2)}) copy-start(bf16[208,384]{1,0:T(8,128)(2,1)S(1)} %collective-permute-done.3.rest_4_) | copy-start | bytes 479236
  63.7 5.9 %collective-permute-start.5 = (bf16[208,384]{1,0:T(8,128)(2,1)S(1)}, bf16[208,384]{1,0:T(8,128)(2,1)S(1)}, u32[]{:S(2)}, u32[]{:S(2)}) collective-permute-start(bf16[208,384]{1,0:T(8,128)(2,1)S(1)} %collective-permute-done.3.rest_4_), channel_id=1, source_target_pairs={{0,7},{1,0},{2,1},{3,2},{4,3},{5,4},{6,5},{7,6},{8,15},{9,8},{10,9... | collective-permute-start | bytes 479240 | tf_op jit(solution)/shard_map/ppermute | solution.py:83
  69.5 5.8 %copy-start.18 = (bf16[208,384]{1,0:T(8,128)(2,1)}, bf16[208,384]{1,0:T(8,128)(2,1)S(1)}, u32[]{:S(2)}) copy-start(bf16[208,384]{1,0:T(8,128)(2,1)S(1)} %collective-permute-done.4.rest_5_) | copy-start | bytes 479236
  69.5 5.8 %collective-permute-start.6 = (bf16[112,384]{1,0:T(8,128)(2,1)S(1)}, bf16[112,384]{1,0:T(8,128)(2,1)S(1)}, u32[]{:S(2)}, u32[]{:S(2)}) collective-permute-start(bf16[112,384]{1,0:T(8,128)(2,1)S(1)} %slice.50), channel_id=1, source_target_pairs={{0,1},{1,2},{2,3},{3,4},{4,5},{5,6},{6,7},{7,0},{8,9},{9,10},{10,1... | collective-permute-start | bytes 258056 | tf_op jit(solution)/shard_map/ppermute | solution.py:86
  69.6 5.7 %copy-start.19 = (bf16[208,384]{1,0:T(8,128)(2,1)}, bf16[208,384]{1,0:T(8,128)(2,1)S(1)}, u32[]{:S(2)}) copy-start(bf16[208,384]{1,0:T(8,128)(2,1)S(1)} %collective-permute-done.5.rest_6_) | copy-start | bytes 479236
  69.6 5.4 %collective-permute-start.7 = (bf16[96,384]{1,0:T(8,128)(2,1)S(1)}, bf16[96,384]{1,0:T(8,128)(2,1)S(1)}, u32[]{:S(2)}, u32[]{:S(2)}) collective-permute-start(bf16[96,384]{1,0:T(8,128)(2,1)S(1)} %slice.51), channel_id=1, source_target_pairs={{0,7},{1,0},{2,1},{3,2},{4,3},{5,4},{6,5},{7,6},{8,15},{9,8},{10,9... | collective-permute-start | bytes 221192 | tf_op jit(solution)/shard_map/ppermute | solution.py:87
  75.9 26.3 %copy-start.12 = (bf16[1536,192]{0,1:T(8,128)(2,1)S(1)}, bf16[1536,192]{0,1:T(8,128)(2,1)}, u32[]{:S(2)}) copy-start(bf16[1536,192]{0,1:T(8,128)(2,1)} %param.16) | copy-start | bytes 1769476
  75.9 27.5 %copy-start.13 = (bf16[1536,192]{0,1:T(8,128)(2,1)S(1)}, bf16[1536,192]{0,1:T(8,128)(2,1)}, u32[]{:S(2)}) copy-start(bf16[1536,192]{0,1:T(8,128)(2,1)} %param.17) | copy-start | bytes 1769476
  95.4 9.2 %copy-start.8 = (f32[8,1,1536]{2,1,0:T(1,128)}, f32[8,1,1536]{2,1,0:T(1,128)S(1)}, u32[]{:S(2)}) copy-start(f32[8,1,1536]{2,1,0:T(1,128)S(1)} %all_to_all.46.parts_ref) | copy-start | bytes 147460
  97.3 11.0 %all-to-all-start.3 = ((f32[32,1,128]{2,1,0:T(1,128)}), f32[32,1,128]{2,1,0:T(1,128)S(1)}, u32[]{:S(2)}, u32[]{:S(2)}) async-start(f32[32,1,128]{2,1,0:T(1,128)} %shard_map.157), calls=%async_computation.3 | async-start | bytes 32768 | tf_op jit(solution)/shard_map/all_to_all | solution.py:33
  103.4 2.4 %copy-start.31 = (s32[32]{0:T(128)S(1)}, s32[32]{0:T(128)}, u32[]{:S(2)}) copy-start(s32[32]{0:T(128)} %param.12) | copy-start | bytes 388
  115.3 4.4 %copy-start = (bf16[1536,384]{1,0:T(8,128)(2,1)S(1)}, bf16[1536,384]{1,0:T(8,128)(2,1)}, u32[]{:S(2)}) copy-start(bf16[1536,384]{1,0:T(8,128)(2,1)} %get-tuple-element.60.far_norm.norm_ref) | copy-start | bytes 3538948
  115.3 38.4 %all-to-all-start.4 = ((bf16[8,208,384]{2,1,0:T(8,128)(2,1)}), bf16[8,208,384]{2,1,0:T(8,128)(2,1)}, u32[]{:S(2)}, u32[]{:S(2)}) async-start(bf16[8,208,384]{2,1,0:T(8,128)(2,1)} %get-tuple-element.76), calls=%async_computation.4 | async-start | bytes 2555904 | tf_op jit(solution)/shard_map/all_to_all | solution.py:33
  119.7 2.4 %copy-start.27 = (f32[2,384]{1,0:T(2,128)S(1)}, f32[2,384]{1,0:T(2,128)}, u32[]{:S(2)}) copy-start(f32[2,384]{1,0:T(2,128)} %get-tuple-element.57.mass_ref) | copy-start | bytes 9220
  122.1 2.3 collective-permute-start.8
  127.1 26.6 %copy-start.6 = (bf16[208,384]{1,0:T(8,128)(2,1)S(1)}, bf16[208,384]{1,0:T(8,128)(2,1)}, u32[]{:S(2)}) copy-start(bf16[208,384]{1,0:T(8,128)(2,1)} %copy-done.5) | copy-start | bytes 479236
  127.1 26.6 %copy-start.10 = (f32[1,384]{1,0:T(1,128)S(1)}, f32[1,384]{1,0:T(1,128)}, u32[]{:S(2)}) copy-start(f32[1,384]{1,0:T(1,128)} %copy-done.9) | copy-start | bytes 4612
  127.1 26.6 %copy-start.11 = (f32[2,384]{1,0:T(2,128)S(1)}, f32[2,384]{1,0:T(2,128)}, u32[]{:S(2)}) copy-start(f32[2,384]{1,0:T(2,128)} %get-tuple-element.73.refs_3_) | copy-start | bytes 9220
  127.1 10.3 %collective-permute-start.9 = (bf16[4,48,384]{2,1,0:T(8,128)(2,1)S(1)}, bf16[4,48,384]{2,1,0:T(8,128)(2,1)S(1)}, u32[]{:S(2)}, u32[]{:S(2)}) collective-permute-start(bf16[4,48,384]{2,1,0:T(8,128)(2,1)S(1)} %get-tuple-element.65), channel_id=1, source_target_pairs={{0,16},{16,32},{32,48},{48,0},{1,17},{17,33},{33,49},{49,1},{2,18}... | collective-permute-start | bytes 442376 | tf_op jit(solution)/shard_map/ppermute | solution.py:763
  127.7 9.7 %collective-permute-start.10 = (bf16[4,48,384]{2,1,0:T(8,128)(2,1)S(1)}, bf16[4,48,384]{2,1,0:T(8,128)(2,1)S(1)}, u32[]{:S(2)}, u32[]{:S(2)}) collective-permute-start(bf16[4,48,384]{2,1,0:T(8,128)(2,1)S(1)} %get-tuple-element.66), channel_id=1, source_target_pairs={{0,32},{16,48},{32,0},{48,16},{1,33},{17,49},{33,1},{49,17},{2,34}... | collective-permute-start | bytes 442376 | tf_op jit(solution)/shard_map/ppermute | solution.py:763
  129.8 8.2 %collective-permute-start.11 = (bf16[4,48,384]{2,1,0:T(8,128)(2,1)S(1)}, bf16[4,48,384]{2,1,0:T(8,128)(2,1)S(1)}, u32[]{:S(2)}, u32[]{:S(2)}) collective-permute-start(bf16[4,48,384]{2,1,0:T(8,128)(2,1)S(1)} %get-tuple-element.67), channel_id=1, source_target_pairs={{0,48},{16,0},{32,16},{48,32},{1,49},{17,1},{33,17},{49,33},{2,50}... | collective-permute-start | bytes 442376 | tf_op jit(solution)/shard_map/ppermute | solution.py:763
  138.1 4.7 %collective-permute-start.14 = (bf16[48,384]{1,0:T(8,128)(2,1)S(1)}, bf16[48,384]{1,0:T(8,128)(2,1)S(1)}, u32[]{:S(2)}, u32[]{:S(2)}) collective-permute-start(bf16[48,384]{1,0:T(8,128)(2,1)S(1)} %get-tuple-element.71), channel_id=1, source_target_pairs={{0,192},{64,0},{128,64},{192,128},{1,193},{65,1},{129,65},{193,129... | collective-permute-start | bytes 110600 | tf_op jit(solution)/shard_map/ppermute | solution.py:763
  139.8 5.5 %collective-permute-start.13 = (bf16[48,384]{1,0:T(8,128)(2,1)S(1)}, bf16[48,384]{1,0:T(8,128)(2,1)S(1)}, u32[]{:S(2)}, u32[]{:S(2)}) collective-permute-start(bf16[48,384]{1,0:T(8,128)(2,1)S(1)} %get-tuple-element.70), channel_id=1, source_target_pairs={{0,128},{64,192},{128,0},{192,64},{1,129},{65,193},{129,1},{193,65... | collective-permute-start | bytes 110600 | tf_op jit(solution)/shard_map/ppermute | solution.py:763
  140.4 4.9 %collective-permute-start.12 = (bf16[48,384]{1,0:T(8,128)(2,1)S(1)}, bf16[48,384]{1,0:T(8,128)(2,1)S(1)}, u32[]{:S(2)}, u32[]{:S(2)}) collective-permute-start(bf16[48,384]{1,0:T(8,128)(2,1)S(1)} %get-tuple-element.69), channel_id=1, source_target_pairs={{0,64},{64,128},{128,192},{192,0},{1,65},{65,129},{129,193},{193,1... | collective-permute-start | bytes 110600 | tf_op jit(solution)/shard_map/ppermute | solution.py:763
  168.7 22.7 %copy-start.4 = (bf16[192,768]{1,0:T(8,128)(2,1)S(1)}, bf16[192,768]{1,0:T(8,128)(2,1)}, u32[]{:S(2)}) copy-start(bf16[192,768]{1,0:T(8,128)(2,1)} %get-tuple-element.62.hidden_ref) | copy-start | bytes 884740
  168.7 23.5 %copy-start.1 = (bf16[768,1536]{1,0:T(8,128)(2,1)S(1)}, bf16[768,1536]{1,0:T(8,128)(2,1)}, u32[]{:S(2)}) copy-start(bf16[768,1536]{1,0:T(8,128)(2,1)} %two_ref.1) | copy-start | bytes 7077892
  192.0 3.3 %collective-permute-start.15 = (bf16[16,48,768]{2,1,0:T(8,128)(2,1)S(1)}, bf16[16,48,768]{2,1,0:T(8,128)(2,1)S(1)}, u32[]{:S(2)}, u32[]{:S(2)}) collective-permute-start(bf16[16,48,768]{2,1,0:T(8,128)(2,1)S(1)} %get-tuple-element.78), channel_id=1, source_target_pairs={{0,8},{8,0},{1,9},{9,1},{2,10},{10,2},{3,11},{11,3},{4,12},{12,4},... | collective-permute-start | bytes 3538952 | tf_op jit(solution)/shard_map/ppermute | solution.py:812
  194.8 3.0 %collective-permute-start.19 = (bf16[16,48,768]{2,1,0:T(8,128)(2,1)S(1)}, bf16[16,48,768]{2,1,0:T(8,128)(2,1)S(1)}, u32[]{:S(2)}, u32[]{:S(2)}) collective-permute-start(bf16[16,48,768]{2,1,0:T(8,128)(2,1)S(1)} %get-tuple-element.84), channel_id=1, source_target_pairs={{0,8},{8,0},{1,9},{9,1},{2,10},{10,2},{3,11},{11,3},{4,12},{12,4},... | collective-permute-start | bytes 3538952 | tf_op jit(solution)/shard_map/ppermute | solution.py:823
  199.0 22.9 %all-to-all-start.8 = ((bf16[4,4,48,768]{3,2,1,0:T(8,128)(2,1)}), bf16[4,4,48,768]{3,2,1,0:T(8,128)(2,1)S(1)}, u32[]{:S(2)}, u32[]{:S(2)}) async-start(bf16[4,4,48,768]{3,2,1,0:T(8,128)(2,1)} %shard_map.168), calls=%async_computation.8 | async-start | bytes 2359296 | tf_op jit(solution)/shard_map/all_to_all | solution.py:33
  204.0 16.7 %collective-permute-start.16 = (bf16[4,48,768]{2,1,0:T(8,128)(2,1)}, bf16[4,48,768]{2,1,0:T(8,128)(2,1)S(1)}, u32[]{:S(2)}, u32[]{:S(2)}) collective-permute-start(bf16[4,48,768]{2,1,0:T(8,128)(2,1)} %get-tuple-element.80), channel_id=1, source_target_pairs={{0,16},{16,32},{32,48},{48,0},{1,17},{17,33},{33,49},{49,1},{2,18}... | collective-permute-start | bytes 884744 | tf_op jit(solution)/shard_map/ppermute | solution.py:763
  204.7 16.0 %collective-permute-start.17 = (bf16[4,48,768]{2,1,0:T(8,128)(2,1)S(1)}, bf16[4,48,768]{2,1,0:T(8,128)(2,1)S(1)}, u32[]{:S(2)}, u32[]{:S(2)}) collective-permute-start(bf16[4,48,768]{2,1,0:T(8,128)(2,1)S(1)} %get-tuple-element.81), channel_id=1, source_target_pairs={{0,32},{16,48},{32,0},{48,16},{1,33},{17,49},{33,1},{49,17},{2,34}... | collective-permute-start | bytes 884744 | tf_op jit(solution)/shard_map/ppermute | solution.py:763
  206.8 14.3 %collective-permute-start.18 = (bf16[4,48,768]{2,1,0:T(8,128)(2,1)S(1)}, bf16[4,48,768]{2,1,0:T(8,128)(2,1)S(1)}, u32[]{:S(2)}, u32[]{:S(2)}) collective-permute-start(bf16[4,48,768]{2,1,0:T(8,128)(2,1)S(1)} %get-tuple-element.82), channel_id=1, source_target_pairs={{0,48},{16,0},{32,16},{48,32},{1,49},{17,1},{33,17},{49,33},{2,50}... | collective-permute-start | bytes 884744 | tf_op jit(solution)/shard_map/ppermute | solution.py:763
  222.0 10.6 %all-to-all-start.7 = ((bf16[4,48,768]{2,1,0:T(8,128)(2,1)}), bf16[4,48,768]{2,1,0:T(8,128)(2,1)S(1)}, u32[]{:S(2)}, u32[]{:S(2)}) async-start(bf16[4,48,768]{2,1,0:T(8,128)(2,1)} %shard_map.166), calls=%async_computation.7 | async-start | bytes 589824 | tf_op jit(solution)/shard_map/all_to_all | solution.py:33
  226.9 6.4 %collective-permute-start.20 = (bf16[48,768]{1,0:T(8,128)(2,1)S(1)}, bf16[48,768]{1,0:T(8,128)(2,1)S(1)}, u32[]{:S(2)}, u32[]{:S(2)}) collective-permute-start(bf16[48,768]{1,0:T(8,128)(2,1)S(1)} %get-tuple-element.86), channel_id=1, source_target_pairs={{0,16},{16,32},{32,48},{48,0},{1,17},{17,33},{33,49},{49,1},{2,18}... | collective-permute-start | bytes 221192 | tf_op jit(solution)/shard_map/ppermute | solution.py:763
  227.4 6.7 %collective-permute-start.21 = (bf16[48,768]{1,0:T(8,128)(2,1)S(1)}, bf16[48,768]{1,0:T(8,128)(2,1)S(1)}, u32[]{:S(2)}, u32[]{:S(2)}) collective-permute-start(bf16[48,768]{1,0:T(8,128)(2,1)S(1)} %get-tuple-element.87), channel_id=1, source_target_pairs={{0,32},{16,48},{32,0},{48,16},{1,33},{17,49},{33,1},{49,17},{2,34}... | collective-permute-start | bytes 221192 | tf_op jit(solution)/shard_map/ppermute | solution.py:763
  231.0 4.4 %collective-permute-start.22 = (bf16[48,768]{1,0:T(8,128)(2,1)S(1)}, bf16[48,768]{1,0:T(8,128)(2,1)S(1)}, u32[]{:S(2)}, u32[]{:S(2)}) collective-permute-start(bf16[48,768]{1,0:T(8,128)(2,1)S(1)} %get-tuple-element.88), channel_id=1, source_target_pairs={{0,48},{16,0},{32,16},{48,32},{1,49},{17,1},{33,17},{49,33},{2,50}... | collective-permute-start | bytes 221192 | tf_op jit(solution)/shard_map/ppermute | solution.py:763
  (14 other events, 12.3 us)

commit v8 on v7

--- a/solution.py
+++ b/solution.py
@@ -510,27 +510,24 @@
             target_ref[chip] = one[chip * share : (chip + 1) * share]
 
 
-def own_two(own, column, hidden_ref, grad_ref, got_ref, *outs):
+def own_two(own, hidden_ref, grad_ref, got_ref, out_ref):
+    chips, share = got_ref.shape[:2]
+    side = out_ref.shape[1]
+    rows = rows_of(own[0], grad_ref, chips, share)
+    two = jnp.dot(rows, hidden_ref[...], preferred_element_type=f32)
+    for chip in range(chips):
+        part = two[chip * share : (chip + 1) * share] + got_ref[chip].astype(f32)
+        out_ref[chip // side, chip % side] = part.astype(bf16)
+
+
+def own_one(column, own_ref, got_ref, *outs):
     side = len(outs)
-    lines, share = outs[0].shape[:2]
     for k in range(side):
         place = lax.rem(column[0] + k, side)
-        chips = [line * side + place for line in range(lines)]
-        rows = [
-            grad_ref[pl.ds(pl.multiple_of((CORES * chip + own[0]) * share, 16), share), :]
-            for chip in chips
-        ]
-        two = jnp.dot(jnp.concatenate(rows, 0), hidden_ref[...], preferred_element_type=f32)
-        for line, chip in enumerate(chips):
-            part = two[line * share : (line + 1) * share] + got_ref[chip].astype(f32)
+        for line in range(outs[k].shape[0]):
+            chip = line * side + place
+            part = own_ref[chip].astype(f32) + got_ref[chip].astype(f32)
             outs[k][line] = part.astype(bf16)
-
-
-def own_one(own_ref, got_ref, out_ref):
-    side = out_ref.shape[1]
-    for chip in range(got_ref.shape[0]):
-        part = own_ref[chip].astype(f32) + got_ref[chip].astype(f32)
-        out_ref[chip // side, chip % side] = part.astype(bf16)
 
 
 def add_up(*refs):
@@ -555,11 +552,11 @@
     total = lines_ref[0].astype(f32)
     for line in range(1, lines_ref.shape[0]):
         total = total + lines_ref[line].astype(f32)
-    two_ref[...] = total
+    one_ref[...] = total
     total = refs[0][...].astype(f32)
     for ref in refs[1:-2]:
         total = total + ref[...].astype(f32)
-    one_ref[...] = total
+    two_ref[...] = total
 
 
 def per_device(
@@ -821,30 +818,31 @@
         scratch=[((units, tiles), bf16)],
     )
     one_got = lax.ppermute(one_sent, "core", swap)
-    two_along = call(
+    (two_across,) = call(
         own_two,
-        [((lines, share, units), bf16)] * side,
+        [((lines, side, share, units), bf16)],
         hidden,
         grad_embedding,
         two_got,
-        scalars=(core, column),
-    )
-    (one_across,) = call(
+        scalars=(core,),
+    )
+    two_across = exchange(two_across, "line")
+    one_along = call(
         own_one,
-        [((lines, side, share, units), bf16)],
+        [((lines, share, units), bf16)] * side,
         one_own,
         one_got,
-        anchors=(two_along[0],),
-    )
-    two_along = shift(two_along, "column")
-    one_across = exchange(one_across, "line")
-    (two_across,) = call(add_up, [((lines, share, units), bf16)], *two_along)
-    one_along = call(add_lines, [((share, units), bf16)] * side, one_across, scalars=(column,))
+        scalars=(column,),
+    )
+    (one_across,) = call(
+        add_up, [((lines, share, units), bf16)], *shift(one_along, "column")
+    )
+    two_along = call(add_lines, [((share, units), bf16)] * side, two_across, scalars=(column,))
     grad_one, grad_two = call(
         last_sums,
         [((share, units), f32)] * 2,
-        exchange(two_across, "line"),
-        *shift(one_along, "column"),
+        exchange(one_across, "line"),
+        *shift(two_along, "column"),
     )
     grad_two = grad_two.T
 

time: 237 us -> 240 us (1.013)
  waiting for transfers between devices: 64.4 us -> 60.3 us
    unnamed x72 -> x74, local copies, waits for them, and re-layouts: 8.73 us -> 10.2 us
  transfers between devices with their start and end apart: 28 -> 28, of which waited for: 18 -> 18; matrix products, arithmetic and copies ran while one was open for 6% -> 6% of each run, Pallas kernels for 3% -> 5%
where the time goes in v8:
time: 240 us; the launch traced here: 239 us
  blocking collectives  64.4 us (27%)
  waiting for transfers between devices  60.3 us (25%)
  starting transfers between devices  59 us (25%)
  Pallas kernels  34 us (14%)
  local copies, waits for them, and re-layouts  17.5 us (7%)
    all_to_all x4, blocking collectives, exchange(): return lax.all_to_all(values, axis, 0, 0, tiled=True)  64.4 us
    pallas_call x18, Pallas kernels, call(): pl.pallas_call(kernel if skip else body, out_shape=[jax.ShapeDtypeStruct(...  34 us
    all_to_all x5, starting transfers between devices, exchange(): return lax.all_to_all(values, axis, 0, 0, tiled=True)  27.7 us
    ppermute x12, waiting for transfers between devices, shift(): lax.ppermute(values[k], axis, turn(len(values), k))  22.8 us
    all_to_all x5, waiting for transfers between devices, exchange(): return lax.all_to_all(values, axis, 0, 0, tiled=True)  22.5 us
    ppermute x12, starting transfers between devices, shift(): lax.ppermute(values[k], axis, turn(len(values), k))  17.4 us
    ppermute x3, waiting for transfers between devices, gather_ring(): back = lax.ppermute(back, 'mp', turn(count, 1))  11.5 us
    unnamed x74, local copies, waits for them, and re-layouts  10.2 us
  transfers between devices with their start and end apart: 28, of which 18 were waited for; matrix products, arithmetic and copies ran while one was open for 6% of the time, Pallas kernels for 5%

profile of v8, /device:TPU:8, one launch (start us, length us, event | category | flops | bytes accessed | tf_op | source)
XLA Modules:
  0.0 239.2 jit_solution(4052370190582109983)
XLA Ops:
  0.6 4.5 %shard_map.153 = (bf16[192,1536]{1,0:T(8,128)(2,1)}, bf16[192,768]{1,0:T(8,128)(2,1)}, f32[192,768]{1,0:T(8,128)}, bf16[8,288,128]{2,1,0:T(8,128)(2,1)}) custom-call(bf16[192,1536]{1,0:T(8,128)(2,1)} %far_x.1, bf16[1536,768]{1,0:T(8,128)(2,1)} %far_one.1, bf16[768,1536]{1,0:T(8,128)(2,1)} %two_ref.1), custom_call_target="tpu_custom_call" | custom-call | tf_op jit(solution)/shard_map/pallas_call | solution.py:49
  5.2 8.6 %all-to-all-start = ((bf16[8,288,128]{2,1,0:T(8,128)(2,1)}), bf16[8,288,128]{2,1,0:T(8,128)(2,1)S(1)}, u32[]{:S(2)}, u32[]{:S(2)}) async-start(bf16[8,288,128]{2,1,0:T(8,128)(2,1)} %get-tuple-element.51), calls=%async_computation | async-start | bytes 1179648 | tf_op jit(solution)/shard_map/all_to_all | solution.py:33
  14.4 1.2 copy.42
  17.8 1.2 constant_dynamic-slice_fusion.3
  19.2 13.5 %all-to-all-done.refs_9_ = bf16[8,288,128]{2,1,0:T(8,128)(2,1)S(1)} async-done(((bf16[8,288,128]{2,1,0:T(8,128)(2,1)}), bf16[8,288,128]{2,1,0:T(8,128)(2,1)S(1)}, u32[]{:S(2)}, u32[]{:S(2)}) %all-to-all-start) | async-done | bytes 589856 | tf_op jit(solution)/shard_map/all_to_all | solution.py:33
  33.0 14.8 %all_to_all.45 = bf16[32,16,256]{2,1,0:T(8,128)(2,1)S(1)} all-to-all(bf16[32,16,256]{2,1,0:T(8,128)(2,1)S(1)} %bitcast.56), channel_id=1, replica_groups=mesh['line'=4,'column'=4,'core'=2,'mp'=8] {'line','column','core'}, dimensions={0} | all-to-all | bytes 524288 | tf_op jit(solution)/shard_map/all_to_all | solution.py:33
  48.8 2.7 %collective-permute-start.1 = (bf16[208,384]{1,0:T(8,128)(2,1)S(1)}, bf16[208,384]{1,0:T(8,128)(2,1)S(1)}, u32[]{:S(2)}, u32[]{:S(2)}) collective-permute-start(bf16[208,384]{1,0:T(8,128)(2,1)S(1)} %get-tuple-element.53.rest_0_.refs_4_), channel_id=1, source_target_pairs={{0,7},{1,0},{2,1},{3,2},{4,3},{5,4},{6,5},{7,6},{8,15},{9,8},{10,9... | collective-permute-start | bytes 479240 | tf_op jit(solution)/shard_map/ppermute | solution.py:83
  51.5 4.5 %collective-permute-done.rest_1_ = bf16[208,384]{1,0:T(8,128)(2,1)S(1)} collective-permute-done((bf16[208,384]{1,0:T(8,128)(2,1)S(1)}, bf16[208,384]{1,0:T(8,128)(2,1)S(1)}, u32[]{:S(2)}, u32[]{:S(2)}) %collective-permute-start) | collective-permute-done | bytes 159776 | tf_op jit(solution)/shard_map/ppermute | solution.py:82
  56.0 3.2 %collective-permute-start.3 = (bf16[208,384]{1,0:T(8,128)(2,1)S(1)}, bf16[208,384]{1,0:T(8,128)(2,1)S(1)}, u32[]{:S(2)}, u32[]{:S(2)}) collective-permute-start(bf16[208,384]{1,0:T(8,128)(2,1)S(1)} %collective-permute-done.1.rest_2_), channel_id=1, source_target_pairs={{0,7},{1,0},{2,1},{3,2},{4,3},{5,4},{6,5},{7,6},{8,15},{9,8},{10,9... | collective-permute-start | bytes 479240 | tf_op jit(solution)/shard_map/ppermute | solution.py:83
  59.2 3.7 %collective-permute-done.2.rest_3_ = bf16[208,384]{1,0:T(8,128)(2,1)S(1)} collective-permute-done((bf16[208,384]{1,0:T(8,128)(2,1)S(1)}, bf16[208,384]{1,0:T(8,128)(2,1)S(1)}, u32[]{:S(2)}, u32[]{:S(2)}) %collective-permute-start.2) | collective-permute-done | bytes 159776 | tf_op jit(solution)/shard_map/ppermute | solution.py:82
  63.0 3.2 %collective-permute-start.5 = (bf16[208,384]{1,0:T(8,128)(2,1)S(1)}, bf16[208,384]{1,0:T(8,128)(2,1)S(1)}, u32[]{:S(2)}, u32[]{:S(2)}) collective-permute-start(bf16[208,384]{1,0:T(8,128)(2,1)S(1)} %collective-permute-done.3.rest_4_), channel_id=1, source_target_pairs={{0,7},{1,0},{2,1},{3,2},{4,3},{5,4},{6,5},{7,6},{8,15},{9,8},{10,9... | collective-permute-start | bytes 479240 | tf_op jit(solution)/shard_map/ppermute | solution.py:83
  66.2 3.2 %collective-permute-done.4.rest_5_ = bf16[208,384]{1,0:T(8,128)(2,1)S(1)} collective-permute-done((bf16[208,384]{1,0:T(8,128)(2,1)S(1)}, bf16[208,384]{1,0:T(8,128)(2,1)S(1)}, u32[]{:S(2)}, u32[]{:S(2)}) %collective-permute-start.4) | collective-permute-done | bytes 159776 | tf_op jit(solution)/shard_map/ppermute | solution.py:82
  69.6 3.5 %collective-permute-start.7 = (bf16[96,384]{1,0:T(8,128)(2,1)S(1)}, bf16[96,384]{1,0:T(8,128)(2,1)S(1)}, u32[]{:S(2)}, u32[]{:S(2)}) collective-permute-start(bf16[96,384]{1,0:T(8,128)(2,1)S(1)} %slice.51), channel_id=1, source_target_pairs={{0,7},{1,0},{2,1},{3,2},{4,3},{5,4},{6,5},{7,6},{8,15},{9,8},{10,9... | collective-permute-start | bytes 221192 | tf_op jit(solution)/shard_map/ppermute | solution.py:87
  73.1 2.0 collective-permute-done.7.rest_8_
  75.9 6.5 %shard_map.156 = (bf16[1536,384]{1,0:T(8,128)(2,1)}, f32[2,3,96,384]{3,2,1,0:T(8,128)}, f32[2,384,384]{2,1,0:T(8,128)}, f32[2,384]{1,0:T(2,128)}, f32[2,2,384]{2...) custom-call(s32[1]{0:T(128)} %bitcast.1.here, ...), custom_call_target="tpu_custom_call" | custom-call | tf_op jit(solution)/shard_map/pallas_call | solution.py:49
  82.5 12.9 %all_to_all.46.parts_ref = f32[8,1,1536]{2,1,0:T(1,128)S(1)} all-to-all(f32[8,1,1536]{2,1,0:T(1,128)} %get-tuple-element.54), channel_id=1, replica_groups=mesh['line'=4,'column'=4,'core'=2,'mp'=8] {'mp'}, dimensions={0} | all-to-all | bytes 98304 | tf_op jit(solution)/shard_map/all_to_all | solution.py:33
  96.3 1.0 shard_map.157
  97.3 4.9 %all-to-all-start.3 = ((f32[32,1,128]{2,1,0:T(1,128)}), f32[32,1,128]{2,1,0:T(1,128)S(1)}, u32[]{:S(2)}, u32[]{:S(2)}) async-start(f32[32,1,128]{2,1,0:T(1,128)} %shard_map.157), calls=%async_computation.3 | async-start | bytes 32768 | tf_op jit(solution)/shard_map/all_to_all | solution.py:33
  102.2 1.2 copy.49.far_query_weights
  103.4 2.3 copy.50.far_key_weights
  105.7 1.3 copy.51.far_value_weights
  108.9 6.3 %shard_map.158 = (f32[1,1]{1,0:T(1,128)}, f32[1,1536]{1,0:T(1,128)}, f32[1,192]{1,0:T(1,128)}, bf16[576,384]{1,0:T(8,128)(2,1)}, bf16[8,208,384]{2,1,0:T(8,128)(2,1)}) custom-call(s32[1]{0:T(128)} %bitcast.owner, f32[32,128]{1,0:T(8,128)} %bitcast.66, s32[32,1]{1,0:T(8,128)} %copy.48.pair_ref, f32[8,1,1536]{2,1,0:T(1,128)} %copy-done.10, ...), custom_call_target="tpu_custom_call" | custom-call | tf_op jit(solution)/shard_map/pallas_call | solution.py:49
  115.3 4.4 %all-to-all-start.4 = ((bf16[8,208,384]{2,1,0:T(8,128)(2,1)}), bf16[8,208,384]{2,1,0:T(8,128)(2,1)}, u32[]{:S(2)}, u32[]{:S(2)}) async-start(bf16[8,208,384]{2,1,0:T(8,128)(2,1)} %get-tuple-element.76), calls=%async_computation.4 | async-start | bytes 2555904 | tf_op jit(solution)/shard_map/all_to_all | solution.py:33
  120.7 1.4 shard_map.159
  123.1 1.4 collective-permute-done.8.got_ref
  125.5 1.6 shard_map.160
  128.0 2.7 %collective-permute-start.10 = (bf16[4,48,384]{2,1,0:T(8,128)(2,1)S(1)}, bf16[4,48,384]{2,1,0:T(8,128)(2,1)S(1)}, u32[]{:S(2)}, u32[]{:S(2)}) collective-permute-start(bf16[4,48,384]{2,1,0:T(8,128)(2,1)S(1)} %get-tuple-element.66), channel_id=1, source_target_pairs={{0,32},{16,48},{32,0},{48,16},{1,33},{17,49},{33,1},{49,17},{2,34}... | collective-permute-start | bytes 442376 | tf_op jit(solution)/shard_map/ppermute | solution.py:760
  130.6 1.5 collective-permute-start.11
  132.2 2.6 %collective-permute-done.9.refs_1_ = bf16[4,48,384]{2,1,0:T(8,128)(2,1)S(1)} collective-permute-done((bf16[4,48,384]{2,1,0:T(8,128)(2,1)S(1)}, bf16[4,48,384]{2,1,0:T(8,128)(2,1)S(1)}, u32[]{:S(2)}, u32[]{:S(2)}) %collective-permute-start.9) | collective-permute-done | bytes 147488 | tf_op jit(solution)/shard_map/ppermute | solution.py:760
  134.8 2.8 %collective-permute-done.10.refs_2_ = bf16[4,48,384]{2,1,0:T(8,128)(2,1)S(1)} collective-permute-done((bf16[4,48,384]{2,1,0:T(8,128)(2,1)S(1)}, bf16[4,48,384]{2,1,0:T(8,128)(2,1)S(1)}, u32[]{:S(2)}, u32[]{:S(2)}) %collective-permute-start.10) | collective-permute-done | bytes 147488 | tf_op jit(solution)/shard_map/ppermute | solution.py:760
  138.1 1.7 collective-permute-start.14
  139.8 1.2 collective-permute-start.13
  141.0 1.8 collective-permute-start.12
  143.3 2.1 collective-permute-done.13
  145.3 8.3 %all-to-all-done.4.refs_7_ = bf16[8,208,384]{2,1,0:T(8,128)(2,1)} async-done(((bf16[8,208,384]{2,1,0:T(8,128)(2,1)}), bf16[8,208,384]{2,1,0:T(8,128)(2,1)}, u32[]{:S(2)}, u32[]{:S(2)}) %all-to-all-start.4) | async-done | bytes 1277984 | tf_op jit(solution)/shard_map/all_to_all | solution.py:33
  153.7 1.8 shard_map.162
  155.5 14.2 %all_to_all.47 = bf16[32,16,192]{2,1,0:T(8,128)(2,1)S(1)} all-to-all(bf16[32,16,192]{2,1,0:T(8,128)(2,1)S(1)} %bitcast.59), channel_id=1, replica_groups=mesh['line'=4,'column'=4,'core'=2,'mp'=8] {'line','column','core'}, dimensions={0} | all-to-all | bytes 393216 | tf_op jit(solution)/shard_map/all_to_all | solution.py:33
  170.1 22.4 %all_to_all.48.parts_ref = bf16[8,288,128]{2,1,0:T(8,128)(2,1)S(1)} all-to-all(bf16[8,288,128]{2,1,0:T(8,128)(2,1)S(1)} %shard_map.163), channel_id=1, replica_groups=mesh['line'=4,'column'=4,'core'=2,'mp'=8] {'mp'}, dimensions={0} | all-to-all | bytes 1179648 | tf_op jit(solution)/shard_map/all_to_all | solution.py:33
  193.2 3.6 %shard_map.165 = (bf16[16,48,768]{2,1,0:T(8,128)(2,1)}, bf16[16,48,768]{2,1,0:T(8,128)(2,1)S(1)}) custom-call(bf16[768,1536]{1,0:T(8,128)(2,1)S(1)} %copy-done.1, f32[768,192]{1,0:T(8,128)S(1)} %bitcast.50, bf16[768,192]{1,0:T(8,128)(2,1)S(1)} %bitcast.52, bf16[768,192]{1,0:T(8,128)(2,1)S(1)} %bitcast.54, bf16[1536,192]{1,0:T(8,128)(2,1)S(1)} %get-tuple-element.77.grad_ref), custom_call_target="tpu_custom_call" | custom-call | tf_op jit(solution)/shard_map/pallas_call | solution.py:49
  196.8 1.0 copy-done.5
  198.3 1.5 shard_map.168
  199.8 5.0 %all-to-all-start.8 = ((bf16[4,4,48,768]{3,2,1,0:T(8,128)(2,1)}), bf16[4,4,48,768]{3,2,1,0:T(8,128)(2,1)S(1)}, u32[]{:S(2)}, u32[]{:S(2)}) async-start(bf16[4,4,48,768]{3,2,1,0:T(8,128)(2,1)} %shard_map.168), calls=%async_computation.8 | async-start | bytes 2359296 | tf_op jit(solution)/shard_map/all_to_all | solution.py:33
  204.8 2.3 shard_map.166
  207.9 2.1 collective-permute-start.17
  212.0 11.6 %collective-permute-done.16.refs_1_ = bf16[4,48,768]{2,1,0:T(8,128)(2,1)S(1)} collective-permute-done((bf16[4,48,768]{2,1,0:T(8,128)(2,1)}, bf16[4,48,768]{2,1,0:T(8,128)(2,1)S(1)}, u32[]{:S(2)}, u32[]{:S(2)}) %collective-permute-start.16) | collective-permute-done | bytes 294944 | tf_op jit(solution)/shard_map/ppermute | solution.py:760
  225.0 4.8 %all-to-all-start.7 = ((bf16[4,48,768]{2,1,0:T(8,128)(2,1)}), bf16[4,48,768]{2,1,0:T(8,128)(2,1)S(1)}, u32[]{:S(2)}, u32[]{:S(2)}) async-start(bf16[4,48,768]{2,1,0:T(8,128)(2,1)} %shard_map.167), calls=%async_computation.7 | async-start | bytes 589824 | tf_op jit(solution)/shard_map/all_to_all | solution.py:33
  230.5 3.6 %collective-permute-start.21 = (bf16[48,768]{1,0:T(8,128)(2,1)S(1)}, bf16[48,768]{1,0:T(8,128)(2,1)S(1)}, u32[]{:S(2)}, u32[]{:S(2)}) collective-permute-start(bf16[48,768]{1,0:T(8,128)(2,1)S(1)} %get-tuple-element.87), channel_id=1, source_target_pairs={{0,32},{16,48},{32,0},{48,16},{1,33},{17,49},{33,1},{49,17},{2,34}... | collective-permute-start | bytes 221192 | tf_op jit(solution)/shard_map/ppermute | solution.py:760
  237.2 1.2 collective-permute-done.22.refs_3_
  (160 shorter events, 23.1 us)
Async XLA Ops:
  5.2 8.6 %copy-start.16 = (bf16[192,1536]{1,0:T(8,128)(2,1)S(1)}, bf16[192,1536]{1,0:T(8,128)(2,1)}, u32[]{:S(2)}) copy-start(bf16[192,1536]{1,0:T(8,128)(2,1)} %far_x.1) | copy-start | bytes 1769476
  5.2 9.3 %copy-start.18 = (bf16[192,1536]{1,0:T(8,128)(2,1)S(1)}, bf16[192,1536]{1,0:T(8,128)(2,1)}, u32[]{:S(2)}) copy-start(bf16[192,1536]{1,0:T(8,128)(2,1)} %get-tuple-element.49) | copy-start | bytes 1769476
  5.2 27.5 %all-to-all-start = ((bf16[8,288,128]{2,1,0:T(8,128)(2,1)}), bf16[8,288,128]{2,1,0:T(8,128)(2,1)S(1)}, u32[]{:S(2)}, u32[]{:S(2)}) async-start(bf16[8,288,128]{2,1,0:T(8,128)(2,1)} %get-tuple-element.51), calls=%async_computation | async-start | bytes 1179648 | tf_op jit(solution)/shard_map/all_to_all | solution.py:33
  48.2 27.5 %copy-start.7 = (bf16[208,384]{1,0:T(8,128)(2,1)}, bf16[208,384]{1,0:T(8,128)(2,1)S(1)}, u32[]{:S(2)}) copy-start(bf16[208,384]{1,0:T(8,128)(2,1)S(1)} %get-tuple-element.53.rest_0_.refs_4_) | copy-start | bytes 479236
  48.2 27.5 %copy-start.11 = (f32[1,384]{1,0:T(1,128)}, f32[1,384]{1,0:T(1,128)S(1)}, u32[]{:S(2)}) copy-start(f32[1,384]{1,0:T(1,128)S(1)} %get-tuple-element.52.valid_ref.refs_2_) | copy-start | bytes 4612
  48.2 7.8 %collective-permute-start = (bf16[208,384]{1,0:T(8,128)(2,1)S(1)}, bf16[208,384]{1,0:T(8,128)(2,1)S(1)}, u32[]{:S(2)}, u32[]{:S(2)}) collective-permute-start(bf16[208,384]{1,0:T(8,128)(2,1)S(1)} %get-tuple-element.53.rest_0_.refs_4_), channel_id=1, source_target_pairs={{0,1},{1,2},{2,3},{3,4},{4,5},{5,6},{6,7},{7,0},{8,9},{9,10},{10,1... | collective-permute-start | bytes 479240 | tf_op jit(solution)/shard_map/ppermute | solution.py:82
  48.8 7.2 %collective-permute-start.1 = (bf16[208,384]{1,0:T(8,128)(2,1)S(1)}, bf16[208,384]{1,0:T(8,128)(2,1)S(1)}, u32[]{:S(2)}, u32[]{:S(2)}) collective-permute-start(bf16[208,384]{1,0:T(8,128)(2,1)S(1)} %get-tuple-element.53.rest_0_.refs_4_), channel_id=1, source_target_pairs={{0,7},{1,0},{2,1},{3,2},{4,3},{5,4},{6,5},{7,6},{8,15},{9,8},{10,9... | collective-permute-start | bytes 479240 | tf_op jit(solution)/shard_map/ppermute | solution.py:83
  56.0 19.7 %copy-start.21 = (bf16[208,384]{1,0:T(8,128)(2,1)}, bf16[208,384]{1,0:T(8,128)(2,1)S(1)}, u32[]{:S(2)}) copy-start(bf16[208,384]{1,0:T(8,128)(2,1)S(1)} %collective-permute-done.rest_1_) | copy-start | bytes 479236
  56.0 7.0 %collective-permute-start.2 = (bf16[208,384]{1,0:T(8,128)(2,1)S(1)}, bf16[208,384]{1,0:T(8,128)(2,1)S(1)}, u32[]{:S(2)}, u32[]{:S(2)}) collective-permute-start(bf16[208,384]{1,0:T(8,128)(2,1)S(1)} %collective-permute-done.rest_1_), channel_id=1, source_target_pairs={{0,1},{1,2},{2,3},{3,4},{4,5},{5,6},{6,7},{7,0},{8,9},{9,10},{10,1... | collective-permute-start | bytes 479240 | tf_op jit(solution)/shard_map/ppermute | solution.py:82
  56.0 19.7 %copy-start.22 = (bf16[208,384]{1,0:T(8,128)(2,1)}, bf16[208,384]{1,0:T(8,128)(2,1)S(1)}, u32[]{:S(2)}) copy-start(bf16[208,384]{1,0:T(8,128)(2,1)S(1)} %collective-permute-done.1.rest_2_) | copy-start | bytes 479236
  56.0 7.0 %collective-permute-start.3 = (bf16[208,384]{1,0:T(8,128)(2,1)S(1)}, bf16[208,384]{1,0:T(8,128)(2,1)S(1)}, u32[]{:S(2)}, u32[]{:S(2)}) collective-permute-start(bf16[208,384]{1,0:T(8,128)(2,1)S(1)} %collective-permute-done.1.rest_2_), channel_id=1, source_target_pairs={{0,7},{1,0},{2,1},{3,2},{4,3},{5,4},{6,5},{7,6},{8,15},{9,8},{10,9... | collective-permute-start | bytes 479240 | tf_op jit(solution)/shard_map/ppermute | solution.py:83
  63.0 12.7 %copy-start.23 = (bf16[208,384]{1,0:T(8,128)(2,1)}, bf16[208,384]{1,0:T(8,128)(2,1)S(1)}, u32[]{:S(2)}) copy-start(bf16[208,384]{1,0:T(8,128)(2,1)S(1)} %collective-permute-done.2.rest_3_) | copy-start | bytes 479236
  63.0 6.5 %collective-permute-start.4 = (bf16[208,384]{1,0:T(8,128)(2,1)S(1)}, bf16[208,384]{1,0:T(8,128)(2,1)S(1)}, u32[]{:S(2)}, u32[]{:S(2)}) collective-permute-start(bf16[208,384]{1,0:T(8,128)(2,1)S(1)} %collective-permute-done.2.rest_3_), channel_id=1, source_target_pairs={{0,1},{1,2},{2,3},{3,4},{4,5},{5,6},{6,7},{7,0},{8,9},{9,10},{10,1... | collective-permute-start | bytes 479240 | tf_op jit(solution)/shard_map/ppermute | solution.py:82
  63.0 12.3 %copy-start.24 = (bf16[208,384]{1,0:T(8,128)(2,1)}, bf16[208,384]{1,0:T(8,128)(2,1)S(1)}, u32[]{:S(2)}) copy-start(bf16[208,384]{1,0:T(8,128)(2,1)S(1)} %collective-permute-done.3.rest_4_) | copy-start | bytes 479236
  63.0 6.6 %collective-permute-start.5 = (bf16[208,384]{1,0:T(8,128)(2,1)S(1)}, bf16[208,384]{1,0:T(8,128)(2,1)S(1)}, u32[]{:S(2)}, u32[]{:S(2)}) collective-permute-start(bf16[208,384]{1,0:T(8,128)(2,1)S(1)} %collective-permute-done.3.rest_4_), channel_id=1, source_target_pairs={{0,7},{1,0},{2,1},{3,2},{4,3},{5,4},{6,5},{7,6},{8,15},{9,8},{10,9... | collective-permute-start | bytes 479240 | tf_op jit(solution)/shard_map/ppermute | solution.py:83
  69.5 6.2 %copy-start.19 = (bf16[208,384]{1,0:T(8,128)(2,1)}, bf16[208,384]{1,0:T(8,128)(2,1)S(1)}, u32[]{:S(2)}) copy-start(bf16[208,384]{1,0:T(8,128)(2,1)S(1)} %collective-permute-done.4.rest_5_) | copy-start | bytes 479236
  69.5 5.8 %collective-permute-start.6 = (bf16[112,384]{1,0:T(8,128)(2,1)S(1)}, bf16[112,384]{1,0:T(8,128)(2,1)S(1)}, u32[]{:S(2)}, u32[]{:S(2)}) collective-permute-start(bf16[112,384]{1,0:T(8,128)(2,1)S(1)} %slice.50), channel_id=1, source_target_pairs={{0,1},{1,2},{2,3},{3,4},{4,5},{5,6},{6,7},{7,0},{8,9},{9,10},{10,1... | collective-permute-start | bytes 258056 | tf_op jit(solution)/shard_map/ppermute | solution.py:86
  69.6 6.1 %copy-start.20 = (bf16[208,384]{1,0:T(8,128)(2,1)}, bf16[208,384]{1,0:T(8,128)(2,1)S(1)}, u32[]{:S(2)}) copy-start(bf16[208,384]{1,0:T(8,128)(2,1)S(1)} %collective-permute-done.5.rest_6_) | copy-start | bytes 479236
  69.6 5.4 %collective-permute-start.7 = (bf16[96,384]{1,0:T(8,128)(2,1)S(1)}, bf16[96,384]{1,0:T(8,128)(2,1)S(1)}, u32[]{:S(2)}, u32[]{:S(2)}) collective-permute-start(bf16[96,384]{1,0:T(8,128)(2,1)S(1)} %slice.51), channel_id=1, source_target_pairs={{0,7},{1,0},{2,1},{3,2},{4,3},{5,4},{6,5},{7,6},{8,15},{9,8},{10,9... | collective-permute-start | bytes 221192 | tf_op jit(solution)/shard_map/ppermute | solution.py:87
  75.9 26.3 %copy-start.14 = (bf16[1536,192]{0,1:T(8,128)(2,1)S(1)}, bf16[1536,192]{0,1:T(8,128)(2,1)}, u32[]{:S(2)}) copy-start(bf16[1536,192]{0,1:T(8,128)(2,1)} %param.16) | copy-start | bytes 1769476
  95.4 10.3 %copy-start.10 = (f32[8,1,1536]{2,1,0:T(1,128)}, f32[8,1,1536]{2,1,0:T(1,128)S(1)}, u32[]{:S(2)}) copy-start(f32[8,1,1536]{2,1,0:T(1,128)S(1)} %all_to_all.46.parts_ref) | copy-start | bytes 147460
  97.3 11.0 %all-to-all-start.3 = ((f32[32,1,128]{2,1,0:T(1,128)}), f32[32,1,128]{2,1,0:T(1,128)S(1)}, u32[]{:S(2)}, u32[]{:S(2)}) async-start(f32[32,1,128]{2,1,0:T(1,128)} %shard_map.157), calls=%async_computation.3 | async-start | bytes 32768 | tf_op jit(solution)/shard_map/all_to_all | solution.py:33
  103.4 3.5 %copy-start.32 = (s32[32]{0:T(128)S(1)}, s32[32]{0:T(128)}, u32[]{:S(2)}) copy-start(s32[32]{0:T(128)} %param.12) | copy-start | bytes 388
  115.2 4.4 %copy-start = (bf16[1536,384]{1,0:T(8,128)(2,1)S(1)}, bf16[1536,384]{1,0:T(8,128)(2,1)}, u32[]{:S(2)}) copy-start(bf16[1536,384]{1,0:T(8,128)(2,1)} %get-tuple-element.60.far_norm.norm_ref) | copy-start | bytes 3538948
  115.3 38.4 %all-to-all-start.4 = ((bf16[8,208,384]{2,1,0:T(8,128)(2,1)}), bf16[8,208,384]{2,1,0:T(8,128)(2,1)}, u32[]{:S(2)}, u32[]{:S(2)}) async-start(bf16[8,208,384]{2,1,0:T(8,128)(2,1)} %get-tuple-element.76), calls=%async_computation.4 | async-start | bytes 2555904 | tf_op jit(solution)/shard_map/all_to_all | solution.py:33
  122.1 2.3 collective-permute-start.8
  127.1 26.6 %copy-start.8 = (bf16[208,384]{1,0:T(8,128)(2,1)S(1)}, bf16[208,384]{1,0:T(8,128)(2,1)}, u32[]{:S(2)}) copy-start(bf16[208,384]{1,0:T(8,128)(2,1)} %copy-done.7) | copy-start | bytes 479236
  127.1 26.6 %copy-start.12 = (f32[1,384]{1,0:T(1,128)S(1)}, f32[1,384]{1,0:T(1,128)}, u32[]{:S(2)}) copy-start(f32[1,384]{1,0:T(1,128)} %copy-done.11) | copy-start | bytes 4612
  127.1 26.6 %copy-start.13 = (f32[2,384]{1,0:T(2,128)S(1)}, f32[2,384]{1,0:T(2,128)}, u32[]{:S(2)}) copy-start(f32[2,384]{1,0:T(2,128)} %get-tuple-element.73.refs_3_) | copy-start | bytes 9220
  127.1 7.7 %collective-permute-start.9 = (bf16[4,48,384]{2,1,0:T(8,128)(2,1)S(1)}, bf16[4,48,384]{2,1,0:T(8,128)(2,1)S(1)}, u32[]{:S(2)}, u32[]{:S(2)}) collective-permute-start(bf16[4,48,384]{2,1,0:T(8,128)(2,1)S(1)} %get-tuple-element.65), channel_id=1, source_target_pairs={{0,16},{16,32},{32,48},{48,0},{1,17},{17,33},{33,49},{49,1},{2,18}... | collective-permute-start | bytes 442376 | tf_op jit(solution)/shard_map/ppermute | solution.py:760
  128.0 9.7 %collective-permute-start.10 = (bf16[4,48,384]{2,1,0:T(8,128)(2,1)S(1)}, bf16[4,48,384]{2,1,0:T(8,128)(2,1)S(1)}, u32[]{:S(2)}, u32[]{:S(2)}) collective-permute-start(bf16[4,48,384]{2,1,0:T(8,128)(2,1)S(1)} %get-tuple-element.66), channel_id=1, source_target_pairs={{0,32},{16,48},{32,0},{48,16},{1,33},{17,49},{33,1},{49,17},{2,34}... | collective-permute-start | bytes 442376 | tf_op jit(solution)/shard_map/ppermute | solution.py:760
  130.6 7.4 %collective-permute-start.11 = (bf16[4,48,384]{2,1,0:T(8,128)(2,1)S(1)}, bf16[4,48,384]{2,1,0:T(8,128)(2,1)S(1)}, u32[]{:S(2)}, u32[]{:S(2)}) collective-permute-start(bf16[4,48,384]{2,1,0:T(8,128)(2,1)S(1)} %get-tuple-element.67), channel_id=1, source_target_pairs={{0,48},{16,0},{32,16},{48,32},{1,49},{17,1},{33,17},{49,33},{2,50}... | collective-permute-start | bytes 442376 | tf_op jit(solution)/shard_map/ppermute | solution.py:760
  138.1 5.1 %collective-permute-start.14 = (bf16[48,384]{1,0:T(8,128)(2,1)S(1)}, bf16[48,384]{1,0:T(8,128)(2,1)S(1)}, u32[]{:S(2)}, u32[]{:S(2)}) collective-permute-start(bf16[48,384]{1,0:T(8,128)(2,1)S(1)} %get-tuple-element.71), channel_id=1, source_target_pairs={{0,192},{64,0},{128,64},{192,128},{1,193},{65,1},{129,65},{193,129... | collective-permute-start | bytes 110600 | tf_op jit(solution)/shard_map/ppermute | solution.py:760
  139.8 5.5 %collective-permute-start.13 = (bf16[48,384]{1,0:T(8,128)(2,1)S(1)}, bf16[48,384]{1,0:T(8,128)(2,1)S(1)}, u32[]{:S(2)}, u32[]{:S(2)}) collective-permute-start(bf16[48,384]{1,0:T(8,128)(2,1)S(1)} %get-tuple-element.70), channel_id=1, source_target_pairs={{0,128},{64,192},{128,0},{192,64},{1,129},{65,193},{129,1},{193,65... | collective-permute-start | bytes 110600 | tf_op jit(solution)/shard_map/ppermute | solution.py:760
  141.0 4.3 %collective-permute-start.12 = (bf16[48,384]{1,0:T(8,128)(2,1)S(1)}, bf16[48,384]{1,0:T(8,128)(2,1)S(1)}, u32[]{:S(2)}, u32[]{:S(2)}) collective-permute-start(bf16[48,384]{1,0:T(8,128)(2,1)S(1)} %get-tuple-element.69), channel_id=1, source_target_pairs={{0,64},{64,128},{128,192},{192,0},{1,65},{65,129},{129,193},{193,1... | collective-permute-start | bytes 110600 | tf_op jit(solution)/shard_map/ppermute | solution.py:760
  169.8 22.7 %copy-start.4 = (bf16[192,768]{1,0:T(8,128)(2,1)S(1)}, bf16[192,768]{1,0:T(8,128)(2,1)}, u32[]{:S(2)}) copy-start(bf16[192,768]{1,0:T(8,128)(2,1)} %get-tuple-element.62.hidden_ref) | copy-start | bytes 884740
  169.8 23.5 %copy-start.1 = (bf16[768,1536]{1,0:T(8,128)(2,1)S(1)}, bf16[768,1536]{1,0:T(8,128)(2,1)}, u32[]{:S(2)}) copy-start(bf16[768,1536]{1,0:T(8,128)(2,1)} %two_ref.1) | copy-start | bytes 7077892
  193.1 5.2 %collective-permute-start.19 = (bf16[16,48,768]{2,1,0:T(8,128)(2,1)S(1)}, bf16[16,48,768]{2,1,0:T(8,128)(2,1)S(1)}, u32[]{:S(2)}, u32[]{:S(2)}) collective-permute-start(bf16[16,48,768]{2,1,0:T(8,128)(2,1)S(1)} %get-tuple-element.84), channel_id=1, source_target_pairs={{0,8},{8,0},{1,9},{9,1},{2,10},{10,2},{3,11},{11,3},{4,12},{12,4},... | collective-permute-start | bytes 3538952 | tf_op jit(solution)/shard_map/ppermute | solution.py:809
  197.8 7.0 %collective-permute-start.15 = (bf16[16,48,768]{2,1,0:T(8,128)(2,1)}, bf16[16,48,768]{2,1,0:T(8,128)(2,1)}, u32[]{:S(2)}, u32[]{:S(2)}) collective-permute-start(bf16[16,48,768]{2,1,0:T(8,128)(2,1)} %get-tuple-element.79), channel_id=1, source_target_pairs={{0,8},{8,0},{1,9},{9,1},{2,10},{10,2},{3,11},{11,3},{4,12},{12,4},... | collective-permute-start | bytes 3538952 | tf_op jit(solution)/shard_map/ppermute | solution.py:820
  199.8 5.0 %copy-start.6 = (bf16[16,48,768]{2,1,0:T(8,128)(2,1)S(1)}, bf16[16,48,768]{2,1,0:T(8,128)(2,1)}, u32[]{:S(2)}) copy-start(bf16[16,48,768]{2,1,0:T(8,128)(2,1)} %copy-done.5) | copy-start | bytes 3538948
  199.8 25.3 %all-to-all-start.8 = ((bf16[4,4,48,768]{3,2,1,0:T(8,128)(2,1)}), bf16[4,4,48,768]{3,2,1,0:T(8,128)(2,1)S(1)}, u32[]{:S(2)}, u32[]{:S(2)}) async-start(bf16[4,4,48,768]{3,2,1,0:T(8,128)(2,1)} %shard_map.168), calls=%async_computation.8 | async-start | bytes 2359296 | tf_op jit(solution)/shard_map/all_to_all | solution.py:33
  207.1 16.4 %collective-permute-start.16 = (bf16[4,48,768]{2,1,0:T(8,128)(2,1)}, bf16[4,48,768]{2,1,0:T(8,128)(2,1)S(1)}, u32[]{:S(2)}, u32[]{:S(2)}) collective-permute-start(bf16[4,48,768]{2,1,0:T(8,128)(2,1)} %get-tuple-element.81), channel_id=1, source_target_pairs={{0,16},{16,32},{32,48},{48,0},{1,17},{17,33},{33,49},{49,1},{2,18}... | collective-permute-start | bytes 884744 | tf_op jit(solution)/shard_map/ppermute | solution.py:760
  207.9 15.7 %collective-permute-start.17 = (bf16[4,48,768]{2,1,0:T(8,128)(2,1)}, bf16[4,48,768]{2,1,0:T(8,128)(2,1)S(1)}, u32[]{:S(2)}, u32[]{:S(2)}) collective-permute-start(bf16[4,48,768]{2,1,0:T(8,128)(2,1)} %get-tuple-element.82), channel_id=1, source_target_pairs={{0,32},{16,48},{32,0},{48,16},{1,33},{17,49},{33,1},{49,17},{2,34}... | collective-permute-start | bytes 884744 | tf_op jit(solution)/shard_map/ppermute | solution.py:760
  210.0 14.2 %collective-permute-start.18 = (bf16[4,48,768]{2,1,0:T(8,128)(2,1)}, bf16[4,48,768]{2,1,0:T(8,128)(2,1)S(1)}, u32[]{:S(2)}, u32[]{:S(2)}) collective-permute-start(bf16[4,48,768]{2,1,0:T(8,128)(2,1)} %get-tuple-element.83), channel_id=1, source_target_pairs={{0,48},{16,0},{32,16},{48,32},{1,49},{17,1},{33,17},{49,33},{2,50}... | collective-permute-start | bytes 884744 | tf_op jit(solution)/shard_map/ppermute | solution.py:760
  225.0 10.7 %all-to-all-start.7 = ((bf16[4,48,768]{2,1,0:T(8,128)(2,1)}), bf16[4,48,768]{2,1,0:T(8,128)(2,1)S(1)}, u32[]{:S(2)}, u32[]{:S(2)}) async-start(bf16[4,48,768]{2,1,0:T(8,128)(2,1)} %shard_map.167), calls=%async_computation.7 | async-start | bytes 589824 | tf_op jit(solution)/shard_map/all_to_all | solution.py:33
  230.0 6.4 %collective-permute-start.20 = (bf16[48,768]{1,0:T(8,128)(2,1)S(1)}, bf16[48,768]{1,0:T(8,128)(2,1)S(1)}, u32[]{:S(2)}, u32[]{:S(2)}) collective-permute-start(bf16[48,768]{1,0:T(8,128)(2,1)S(1)} %get-tuple-element.86), channel_id=1, source_target_pairs={{0,16},{16,32},{32,48},{48,0},{1,17},{17,33},{33,49},{49,1},{2,18}... | collective-permute-start | bytes 221192 | tf_op jit(solution)/shard_map/ppermute | solution.py:760
  230.5 6.7 %collective-permute-start.21 = (bf16[48,768]{1,0:T(8,128)(2,1)S(1)}, bf16[48,768]{1,0:T(8,128)(2,1)S(1)}, u32[]{:S(2)}, u32[]{:S(2)}) collective-permute-start(bf16[48,768]{1,0:T(8,128)(2,1)S(1)} %get-tuple-element.87), channel_id=1, source_target_pairs={{0,32},{16,48},{32,0},{48,16},{1,33},{17,49},{33,1},{49,17},{2,34}... | collective-permute-start | bytes 221192 | tf_op jit(solution)/shard_map/ppermute | solution.py:760
  234.1 4.4 %collective-permute-start.22 = (bf16[48,768]{1,0:T(8,128)(2,1)S(1)}, bf16[48,768]{1,0:T(8,128)(2,1)S(1)}, u32[]{:S(2)}, u32[]{:S(2)}) collective-permute-start(bf16[48,768]{1,0:T(8,128)(2,1)S(1)} %get-tuple-element.88), channel_id=1, source_target_pairs={{0,48},{16,0},{32,16},{48,32},{1,49},{17,1},{33,17},{49,33},{2,50}... | collective-permute-start | bytes 221192 | tf_op jit(solution)/shard_map/ppermute | solution.py:760
  (15 other events, 16.2 us)

commit v9 on v7

--- a/solution.py
+++ b/solution.py
@@ -705,6 +705,7 @@
         pooled,
         all_reports,
         scratch=[((owners, width), f32)],
+        limit=60,
     )
     logits = exchange(row, DP).reshape(owners, 128)
     loss, grad, up, grads, sending = call(

time: 237 us -> 237 us (level)
    unnamed x72 -> x68, local copies, waits for them, and re-layouts: 8.73 us -> 7.06 us
where the time goes in v9:
time: 237 us; the launch traced here: 236 us
  waiting for transfers between devices  64.6 us (27%)
  blocking collectives  63.4 us (27%)
  starting transfers between devices  57.3 us (24%)
  Pallas kernels  32.5 us (14%)
  local copies, waits for them, and re-layouts  14.3 us (6%)
    all_to_all x4, blocking collectives, exchange(): return lax.all_to_all(values, axis, 0, 0, tiled=True)  63.4 us
    pallas_call x18, Pallas kernels, call(): pl.pallas_call(kernel if skip else body, out_shape=[jax.ShapeDtypeStruct(...  32.5 us
    all_to_all x5, starting transfers between devices, exchange(): return lax.all_to_all(values, axis, 0, 0, tiled=True)  27.6 us
    ppermute x12, waiting for transfers between devices, shift(): lax.ppermute(values[k], axis, turn(len(values), k))  24.5 us
    all_to_all x5, waiting for transfers between devices, exchange(): return lax.all_to_all(values, axis, 0, 0, tiled=True)  23.6 us
    ppermute x12, starting transfers between devices, shift(): lax.ppermute(values[k], axis, turn(len(values), k))  15.8 us
    ppermute x3, waiting for transfers between devices, gather_ring(): back = lax.ppermute(back, 'mp', turn(count, 1))  11.5 us
    ppermute x3, starting transfers between devices, gather_ring(): ahead = lax.ppermute(ahead, 'mp', turn(count, count - 1))  9.12 us
  transfers between devices with their start and end apart: 28, of which 18 were waited for; matrix products, arithmetic and copies ran while one was open for 6% of the time, Pallas kernels for 3%

profile of v9, /device:TPU:8, one launch (start us, length us, event | category | flops | bytes accessed | tf_op | source)
XLA Modules:
  0.0 236.2 jit_solution(15909429899936282253)
XLA Ops:
  0.6 4.5 %shard_map.153 = (bf16[192,1536]{1,0:T(8,128)(2,1)}, bf16[192,768]{1,0:T(8,128)(2,1)}, f32[192,768]{1,0:T(8,128)}, bf16[8,288,128]{2,1,0:T(8,128)(2,1)}) custom-call(bf16[192,1536]{1,0:T(8,128)(2,1)} %far_x.1, bf16[1536,768]{1,0:T(8,128)(2,1)} %far_one.1, bf16[768,1536]{1,0:T(8,128)(2,1)} %two_ref.1), custom_call_target="tpu_custom_call" | custom-call | tf_op jit(solution)/shard_map/pallas_call | solution.py:49
  5.2 8.6 %all-to-all-start = ((bf16[8,288,128]{2,1,0:T(8,128)(2,1)}), bf16[8,288,128]{2,1,0:T(8,128)(2,1)S(1)}, u32[]{:S(2)}, u32[]{:S(2)}) async-start(bf16[8,288,128]{2,1,0:T(8,128)(2,1)} %get-tuple-element.51), calls=%async_computation | async-start | bytes 1179648 | tf_op jit(solution)/shard_map/all_to_all | solution.py:33
  14.4 1.2 copy.42
  17.8 1.2 constant_dynamic-slice_fusion.3
  19.2 13.5 %all-to-all-done.refs_9_ = bf16[8,288,128]{2,1,0:T(8,128)(2,1)S(1)} async-done(((bf16[8,288,128]{2,1,0:T(8,128)(2,1)}), bf16[8,288,128]{2,1,0:T(8,128)(2,1)S(1)}, u32[]{:S(2)}, u32[]{:S(2)}) %all-to-all-start) | async-done | bytes 589856 | tf_op jit(solution)/shard_map/all_to_all | solution.py:33
  33.0 14.8 %all_to_all.45 = bf16[32,16,256]{2,1,0:T(8,128)(2,1)S(1)} all-to-all(bf16[32,16,256]{2,1,0:T(8,128)(2,1)S(1)} %bitcast.56), channel_id=1, replica_groups=mesh['line'=4,'column'=4,'core'=2,'mp'=8] {'line','column','core'}, dimensions={0} | all-to-all | bytes 524288 | tf_op jit(solution)/shard_map/all_to_all | solution.py:33
  48.8 2.7 %collective-permute-start.1 = (bf16[208,384]{1,0:T(8,128)(2,1)S(1)}, bf16[208,384]{1,0:T(8,128)(2,1)S(1)}, u32[]{:S(2)}, u32[]{:S(2)}) collective-permute-start(bf16[208,384]{1,0:T(8,128)(2,1)S(1)} %get-tuple-element.53.rest_0_.refs_4_), channel_id=1, source_target_pairs={{0,7},{1,0},{2,1},{3,2},{4,3},{5,4},{6,5},{7,6},{8,15},{9,8},{10,9... | collective-permute-start | bytes 479240 | tf_op jit(solution)/shard_map/ppermute | solution.py:83
  51.5 4.5 %collective-permute-done.rest_1_ = bf16[208,384]{1,0:T(8,128)(2,1)S(1)} collective-permute-done((bf16[208,384]{1,0:T(8,128)(2,1)S(1)}, bf16[208,384]{1,0:T(8,128)(2,1)S(1)}, u32[]{:S(2)}, u32[]{:S(2)}) %collective-permute-start) | collective-permute-done | bytes 159776 | tf_op jit(solution)/shard_map/ppermute | solution.py:82
  56.0 3.2 %collective-permute-start.3 = (bf16[208,384]{1,0:T(8,128)(2,1)S(1)}, bf16[208,384]{1,0:T(8,128)(2,1)S(1)}, u32[]{:S(2)}, u32[]{:S(2)}) collective-permute-start(bf16[208,384]{1,0:T(8,128)(2,1)S(1)} %collective-permute-done.1.rest_2_), channel_id=1, source_target_pairs={{0,7},{1,0},{2,1},{3,2},{4,3},{5,4},{6,5},{7,6},{8,15},{9,8},{10,9... | collective-permute-start | bytes 479240 | tf_op jit(solution)/shard_map/ppermute | solution.py:83
  59.3 3.7 %collective-permute-done.2.rest_3_ = bf16[208,384]{1,0:T(8,128)(2,1)S(1)} collective-permute-done((bf16[208,384]{1,0:T(8,128)(2,1)S(1)}, bf16[208,384]{1,0:T(8,128)(2,1)S(1)}, u32[]{:S(2)}, u32[]{:S(2)}) %collective-permute-start.2) | collective-permute-done | bytes 159776 | tf_op jit(solution)/shard_map/ppermute | solution.py:82
  63.0 3.2 %collective-permute-start.5 = (bf16[208,384]{1,0:T(8,128)(2,1)S(1)}, bf16[208,384]{1,0:T(8,128)(2,1)S(1)}, u32[]{:S(2)}, u32[]{:S(2)}) collective-permute-start(bf16[208,384]{1,0:T(8,128)(2,1)S(1)} %collective-permute-done.3.rest_4_), channel_id=1, source_target_pairs={{0,7},{1,0},{2,1},{3,2},{4,3},{5,4},{6,5},{7,6},{8,15},{9,8},{10,9... | collective-permute-start | bytes 479240 | tf_op jit(solution)/shard_map/ppermute | solution.py:83
  66.2 3.2 %collective-permute-done.4.rest_5_ = bf16[208,384]{1,0:T(8,128)(2,1)S(1)} collective-permute-done((bf16[208,384]{1,0:T(8,128)(2,1)S(1)}, bf16[208,384]{1,0:T(8,128)(2,1)S(1)}, u32[]{:S(2)}, u32[]{:S(2)}) %collective-permute-start.4) | collective-permute-done | bytes 159776 | tf_op jit(solution)/shard_map/ppermute | solution.py:82
  69.6 3.5 %collective-permute-start.7 = (bf16[96,384]{1,0:T(8,128)(2,1)S(1)}, bf16[96,384]{1,0:T(8,128)(2,1)S(1)}, u32[]{:S(2)}, u32[]{:S(2)}) collective-permute-start(bf16[96,384]{1,0:T(8,128)(2,1)S(1)} %slice.51), channel_id=1, source_target_pairs={{0,7},{1,0},{2,1},{3,2},{4,3},{5,4},{6,5},{7,6},{8,15},{9,8},{10,9... | collective-permute-start | bytes 221192 | tf_op jit(solution)/shard_map/ppermute | solution.py:87
  73.1 2.0 collective-permute-done.7.rest_8_
  75.9 6.5 %shard_map.156 = (bf16[1536,384]{1,0:T(8,128)(2,1)}, f32[2,3,96,384]{3,2,1,0:T(8,128)}, f32[2,384,384]{2,1,0:T(8,128)}, f32[2,384]{1,0:T(2,128)}, f32[2,2,384]{2...) custom-call(s32[1]{0:T(128)} %bitcast.1.here, ...), custom_call_target="tpu_custom_call" | custom-call | tf_op jit(solution)/shard_map/pallas_call | solution.py:49
  82.5 13.1 %all_to_all.46.parts_ref = f32[8,1,1536]{2,1,0:T(1,128)} all-to-all(f32[8,1,1536]{2,1,0:T(1,128)} %get-tuple-element.54), channel_id=1, replica_groups=mesh['line'=4,'column'=4,'core'=2,'mp'=8] {'mp'}, dimensions={0} | all-to-all | bytes 98304 | tf_op jit(solution)/shard_map/all_to_all | solution.py:33
  95.6 2.0 shard_map.157
  97.6 4.9 %all-to-all-start.3 = ((f32[32,1,128]{2,1,0:T(1,128)}), f32[32,1,128]{2,1,0:T(1,128)S(1)}, u32[]{:S(2)}, u32[]{:S(2)}) async-start(f32[32,1,128]{2,1,0:T(1,128)} %shard_map.157), calls=%async_computation.3 | async-start | bytes 32768 | tf_op jit(solution)/shard_map/all_to_all | solution.py:33
  102.5 1.2 copy.49.far_query_weights
  103.6 1.1 copy.50.far_key_weights
  104.8 1.2 copy.51.far_value_weights
  106.7 1.8 all-to-all-done.3
  109.2 6.3 %shard_map.158 = (f32[1,1]{1,0:T(1,128)}, f32[1,1536]{1,0:T(1,128)}, f32[1,192]{1,0:T(1,128)}, bf16[576,384]{1,0:T(8,128)(2,1)}, bf16[8,208,384]{2,1,0:T(8,128)(2,1)}) custom-call(s32[1]{0:T(128)} %bitcast.owner, f32[32,128]{1,0:T(8,128)} %bitcast.66, s32[32,1]{1,0:T(8,128)} %copy.48.pair_ref, f32[8,1,1536]{2,1,0:T(1,128)} %all_to_all.46.parts_ref, ...), custom_call_target="tpu_custom_call" | custom-call | tf_op jit(solution)/shard_map/pallas_call | solution.py:49
  115.5 4.4 %all-to-all-start.4 = ((bf16[8,208,384]{2,1,0:T(8,128)(2,1)}), bf16[8,208,384]{2,1,0:T(8,128)(2,1)}, u32[]{:S(2)}, u32[]{:S(2)}) async-start(bf16[8,208,384]{2,1,0:T(8,128)(2,1)} %get-tuple-element.76), calls=%async_computation.4 | async-start | bytes 2555904 | tf_op jit(solution)/shard_map/all_to_all | solution.py:33
  120.9 1.4 shard_map.159
  123.3 1.4 collective-permute-done.8.got_ref
  124.6 1.0 copy-done.3
  125.6 1.6 shard_map.160
  127.9 2.0 collective-permute-start.10
  130.0 1.2 collective-permute-start.11
  131.2 6.4 %collective-permute-done.9.refs_1_ = bf16[4,48,384]{2,1,0:T(8,128)(2,1)S(1)} collective-permute-done((bf16[4,48,384]{2,1,0:T(8,128)(2,1)S(1)}, bf16[4,48,384]{2,1,0:T(8,128)(2,1)S(1)}, u32[]{:S(2)}, u32[]{:S(2)}) %collective-permute-start.9) | collective-permute-done | bytes 147488 | tf_op jit(solution)/shard_map/ppermute | solution.py:764
  138.3 1.7 collective-permute-start.14
  140.6 2.0 collective-permute-start.12
  143.0 2.5 %collective-permute-done.13 = bf16[48,384]{1,0:T(8,128)(2,1)S(1)} collective-permute-done((bf16[48,384]{1,0:T(8,128)(2,1)S(1)}, bf16[48,384]{1,0:T(8,128)(2,1)S(1)}, u32[]{:S(2)}, u32[]{:S(2)}) %collective-permute-start.13) | collective-permute-done | bytes 36896 | tf_op jit(solution)/shard_map/ppermute | solution.py:764
  145.5 8.3 %all-to-all-done.4.refs_7_ = bf16[8,208,384]{2,1,0:T(8,128)(2,1)} async-done(((bf16[8,208,384]{2,1,0:T(8,128)(2,1)}), bf16[8,208,384]{2,1,0:T(8,128)(2,1)}, u32[]{:S(2)}, u32[]{:S(2)}) %all-to-all-start.4) | async-done | bytes 1277984 | tf_op jit(solution)/shard_map/all_to_all | solution.py:33
  153.9 1.9 shard_map.162
  155.7 13.1 %all_to_all.47 = bf16[32,16,192]{2,1,0:T(8,128)(2,1)S(1)} all-to-all(bf16[32,16,192]{2,1,0:T(8,128)(2,1)S(1)} %bitcast.59), channel_id=1, replica_groups=mesh['line'=4,'column'=4,'core'=2,'mp'=8] {'line','column','core'}, dimensions={0} | all-to-all | bytes 393216 | tf_op jit(solution)/shard_map/all_to_all | solution.py:33
  169.1 22.4 %all_to_all.48.parts_ref = bf16[8,288,128]{2,1,0:T(8,128)(2,1)S(1)} all-to-all(bf16[8,288,128]{2,1,0:T(8,128)(2,1)S(1)} %shard_map.163), channel_id=1, replica_groups=mesh['line'=4,'column'=4,'core'=2,'mp'=8] {'mp'}, dimensions={0} | all-to-all | bytes 1179648 | tf_op jit(solution)/shard_map/all_to_all | solution.py:33
  192.3 2.6 %shard_map.167 = (bf16[16,48,768]{2,1,0:T(8,128)(2,1)S(1)}, bf16[16,48,768]{2,1,0:T(8,128)(2,1)S(1)}) custom-call(bf16[768,1536]{1,0:T(8,128)(2,1)S(1)} %copy-done.1, f32[768,192]{1,0:T(8,128)S(1)} %bitcast.50, bf16[768,192]{1,0:T(8,128)(2,1)S(1)} %bitcast.52, bf16[768,192]{1,0:T(8,128)(2,1)S(1)} %bitcast.54, bf16[1536,192]{1,0:T(8,128)(2,1)S(1)} %get-tuple-element.77.grad_ref), custom_call_target="tpu_custom_call" | custom-call | tf_op jit(solution)/shard_map/pallas_call | solution.py:49
  195.4 1.0 shard_map.165
  196.4 1.4 collective-permute-done.19.refs_2_
  197.9 1.3 shard_map.168
  199.2 4.9 %all-to-all-start.8 = ((bf16[4,4,48,768]{3,2,1,0:T(8,128)(2,1)}), bf16[4,4,48,768]{3,2,1,0:T(8,128)(2,1)S(1)}, u32[]{:S(2)}, u32[]{:S(2)}) async-start(bf16[4,4,48,768]{3,2,1,0:T(8,128)(2,1)} %shard_map.168), calls=%async_computation.8 | async-start | bytes 2359296 | tf_op jit(solution)/shard_map/all_to_all | solution.py:33
  204.8 2.1 collective-permute-start.17
  208.9 11.9 %collective-permute-done.16.refs_1_ = bf16[4,48,768]{2,1,0:T(8,128)(2,1)S(1)} collective-permute-done((bf16[4,48,768]{2,1,0:T(8,128)(2,1)}, bf16[4,48,768]{2,1,0:T(8,128)(2,1)S(1)}, u32[]{:S(2)}, u32[]{:S(2)}) %collective-permute-start.16) | collective-permute-done | bytes 294944 | tf_op jit(solution)/shard_map/ppermute | solution.py:764
  222.1 4.8 %all-to-all-start.7 = ((bf16[4,48,768]{2,1,0:T(8,128)(2,1)}), bf16[4,48,768]{2,1,0:T(8,128)(2,1)S(1)}, u32[]{:S(2)}, u32[]{:S(2)}) async-start(bf16[4,48,768]{2,1,0:T(8,128)(2,1)} %shard_map.166), calls=%async_computation.7 | async-start | bytes 589824 | tf_op jit(solution)/shard_map/all_to_all | solution.py:33
  227.5 3.6 %collective-permute-start.21 = (bf16[48,768]{1,0:T(8,128)(2,1)S(1)}, bf16[48,768]{1,0:T(8,128)(2,1)S(1)}, u32[]{:S(2)}, u32[]{:S(2)}) collective-permute-start(bf16[48,768]{1,0:T(8,128)(2,1)S(1)} %get-tuple-element.87), channel_id=1, source_target_pairs={{0,32},{16,48},{32,0},{48,16},{1,33},{17,49},{33,1},{49,17},{2,34}... | collective-permute-start | bytes 221192 | tf_op jit(solution)/shard_map/ppermute | solution.py:764
  234.2 1.2 collective-permute-done.22.refs_3_
  (154 shorter events, 20.9 us)
Async XLA Ops:
  5.2 8.6 %copy-start.13 = (bf16[192,1536]{1,0:T(8,128)(2,1)S(1)}, bf16[192,1536]{1,0:T(8,128)(2,1)}, u32[]{:S(2)}) copy-start(bf16[192,1536]{1,0:T(8,128)(2,1)} %far_x.1) | copy-start | bytes 1769476
  5.2 9.3 %copy-start.15 = (bf16[192,1536]{1,0:T(8,128)(2,1)S(1)}, bf16[192,1536]{1,0:T(8,128)(2,1)}, u32[]{:S(2)}) copy-start(bf16[192,1536]{1,0:T(8,128)(2,1)} %get-tuple-element.49) | copy-start | bytes 1769476
  5.2 27.5 %all-to-all-start = ((bf16[8,288,128]{2,1,0:T(8,128)(2,1)}), bf16[8,288,128]{2,1,0:T(8,128)(2,1)S(1)}, u32[]{:S(2)}, u32[]{:S(2)}) async-start(bf16[8,288,128]{2,1,0:T(8,128)(2,1)} %get-tuple-element.51), calls=%async_computation | async-start | bytes 1179648 | tf_op jit(solution)/shard_map/all_to_all | solution.py:33
  48.2 27.1 %copy-start.5 = (bf16[208,384]{1,0:T(8,128)(2,1)}, bf16[208,384]{1,0:T(8,128)(2,1)S(1)}, u32[]{:S(2)}) copy-start(bf16[208,384]{1,0:T(8,128)(2,1)S(1)} %get-tuple-element.53.rest_0_.refs_4_) | copy-start | bytes 479236
  48.2 27.1 %copy-start.7 = (f32[1,384]{1,0:T(1,128)}, f32[1,384]{1,0:T(1,128)S(1)}, u32[]{:S(2)}) copy-start(f32[1,384]{1,0:T(1,128)S(1)} %get-tuple-element.52.valid_ref.refs_2_) | copy-start | bytes 4612
  48.2 7.8 %collective-permute-start = (bf16[208,384]{1,0:T(8,128)(2,1)S(1)}, bf16[208,384]{1,0:T(8,128)(2,1)S(1)}, u32[]{:S(2)}, u32[]{:S(2)}) collective-permute-start(bf16[208,384]{1,0:T(8,128)(2,1)S(1)} %get-tuple-element.53.rest_0_.refs_4_), channel_id=1, source_target_pairs={{0,1},{1,2},{2,3},{3,4},{4,5},{5,6},{6,7},{7,0},{8,9},{9,10},{10,1... | collective-permute-start | bytes 479240 | tf_op jit(solution)/shard_map/ppermute | solution.py:82
  48.8 7.2 %collective-permute-start.1 = (bf16[208,384]{1,0:T(8,128)(2,1)S(1)}, bf16[208,384]{1,0:T(8,128)(2,1)S(1)}, u32[]{:S(2)}, u32[]{:S(2)}) collective-permute-start(bf16[208,384]{1,0:T(8,128)(2,1)S(1)} %get-tuple-element.53.rest_0_.refs_4_), channel_id=1, source_target_pairs={{0,7},{1,0},{2,1},{3,2},{4,3},{5,4},{6,5},{7,6},{8,15},{9,8},{10,9... | collective-permute-start | bytes 479240 | tf_op jit(solution)/shard_map/ppermute | solution.py:83
  56.0 19.3 %copy-start.18 = (bf16[208,384]{1,0:T(8,128)(2,1)}, bf16[208,384]{1,0:T(8,128)(2,1)S(1)}, u32[]{:S(2)}) copy-start(bf16[208,384]{1,0:T(8,128)(2,1)S(1)} %collective-permute-done.rest_1_) | copy-start | bytes 479236
  56.0 7.0 %collective-permute-start.2 = (bf16[208,384]{1,0:T(8,128)(2,1)S(1)}, bf16[208,384]{1,0:T(8,128)(2,1)S(1)}, u32[]{:S(2)}, u32[]{:S(2)}) collective-permute-start(bf16[208,384]{1,0:T(8,128)(2,1)S(1)} %collective-permute-done.rest_1_), channel_id=1, source_target_pairs={{0,1},{1,2},{2,3},{3,4},{4,5},{5,6},{6,7},{7,0},{8,9},{9,10},{10,1... | collective-permute-start | bytes 479240 | tf_op jit(solution)/shard_map/ppermute | solution.py:82
  56.0 19.3 %copy-start.19 = (bf16[208,384]{1,0:T(8,128)(2,1)}, bf16[208,384]{1,0:T(8,128)(2,1)S(1)}, u32[]{:S(2)}) copy-start(bf16[208,384]{1,0:T(8,128)(2,1)S(1)} %collective-permute-done.1.rest_2_) | copy-start | bytes 479236
  56.0 7.0 %collective-permute-start.3 = (bf16[208,384]{1,0:T(8,128)(2,1)S(1)}, bf16[208,384]{1,0:T(8,128)(2,1)S(1)}, u32[]{:S(2)}, u32[]{:S(2)}) collective-permute-start(bf16[208,384]{1,0:T(8,128)(2,1)S(1)} %collective-permute-done.1.rest_2_), channel_id=1, source_target_pairs={{0,7},{1,0},{2,1},{3,2},{4,3},{5,4},{6,5},{7,6},{8,15},{9,8},{10,9... | collective-permute-start | bytes 479240 | tf_op jit(solution)/shard_map/ppermute | solution.py:83
  63.0 12.3 %copy-start.20 = (bf16[208,384]{1,0:T(8,128)(2,1)}, bf16[208,384]{1,0:T(8,128)(2,1)S(1)}, u32[]{:S(2)}) copy-start(bf16[208,384]{1,0:T(8,128)(2,1)S(1)} %collective-permute-done.2.rest_3_) | copy-start | bytes 479236
  63.0 6.5 %collective-permute-start.4 = (bf16[208,384]{1,0:T(8,128)(2,1)S(1)}, bf16[208,384]{1,0:T(8,128)(2,1)S(1)}, u32[]{:S(2)}, u32[]{:S(2)}) collective-permute-start(bf16[208,384]{1,0:T(8,128)(2,1)S(1)} %collective-permute-done.2.rest_3_), channel_id=1, source_target_pairs={{0,1},{1,2},{2,3},{3,4},{4,5},{5,6},{6,7},{7,0},{8,9},{9,10},{10,1... | collective-permute-start | bytes 479240 | tf_op jit(solution)/shard_map/ppermute | solution.py:82
  63.0 12.3 %copy-start.21 = (bf16[208,384]{1,0:T(8,128)(2,1)}, bf16[208,384]{1,0:T(8,128)(2,1)S(1)}, u32[]{:S(2)}) copy-start(bf16[208,384]{1,0:T(8,128)(2,1)S(1)} %collective-permute-done.3.rest_4_) | copy-start | bytes 479236
  63.0 6.6 %collective-permute-start.5 = (bf16[208,384]{1,0:T(8,128)(2,1)S(1)}, bf16[208,384]{1,0:T(8,128)(2,1)S(1)}, u32[]{:S(2)}, u32[]{:S(2)}) collective-permute-start(bf16[208,384]{1,0:T(8,128)(2,1)S(1)} %collective-permute-done.3.rest_4_), channel_id=1, source_target_pairs={{0,7},{1,0},{2,1},{3,2},{4,3},{5,4},{6,5},{7,6},{8,15},{9,8},{10,9... | collective-permute-start | bytes 479240 | tf_op jit(solution)/shard_map/ppermute | solution.py:83
  69.5 5.8 %copy-start.16 = (bf16[208,384]{1,0:T(8,128)(2,1)}, bf16[208,384]{1,0:T(8,128)(2,1)S(1)}, u32[]{:S(2)}) copy-start(bf16[208,384]{1,0:T(8,128)(2,1)S(1)} %collective-permute-done.4.rest_5_) | copy-start | bytes 479236
  69.5 5.8 %collective-permute-start.6 = (bf16[112,384]{1,0:T(8,128)(2,1)S(1)}, bf16[112,384]{1,0:T(8,128)(2,1)S(1)}, u32[]{:S(2)}, u32[]{:S(2)}) collective-permute-start(bf16[112,384]{1,0:T(8,128)(2,1)S(1)} %slice.50), channel_id=1, source_target_pairs={{0,1},{1,2},{2,3},{3,4},{4,5},{5,6},{6,7},{7,0},{8,9},{9,10},{10,1... | collective-permute-start | bytes 258056 | tf_op jit(solution)/shard_map/ppermute | solution.py:86
  69.6 5.7 %copy-start.17 = (bf16[208,384]{1,0:T(8,128)(2,1)}, bf16[208,384]{1,0:T(8,128)(2,1)S(1)}, u32[]{:S(2)}) copy-start(bf16[208,384]{1,0:T(8,128)(2,1)S(1)} %collective-permute-done.5.rest_6_) | copy-start | bytes 479236
  69.6 5.4 %collective-permute-start.7 = (bf16[96,384]{1,0:T(8,128)(2,1)S(1)}, bf16[96,384]{1,0:T(8,128)(2,1)S(1)}, u32[]{:S(2)}, u32[]{:S(2)}) collective-permute-start(bf16[96,384]{1,0:T(8,128)(2,1)S(1)} %slice.51), channel_id=1, source_target_pairs={{0,7},{1,0},{2,1},{3,2},{4,3},{5,4},{6,5},{7,6},{8,15},{9,8},{10,9... | collective-permute-start | bytes 221192 | tf_op jit(solution)/shard_map/ppermute | solution.py:87
  75.9 26.5 %copy-start.10 = (bf16[1536,192]{0,1:T(8,128)(2,1)S(1)}, bf16[1536,192]{0,1:T(8,128)(2,1)}, u32[]{:S(2)}) copy-start(bf16[1536,192]{0,1:T(8,128)(2,1)} %param.16) | copy-start | bytes 1769476
  82.5 21.1 %copy-start.11 = (bf16[1536,192]{0,1:T(8,128)(2,1)S(1)}, bf16[1536,192]{0,1:T(8,128)(2,1)}, u32[]{:S(2)}) copy-start(bf16[1536,192]{0,1:T(8,128)(2,1)} %param.17) | copy-start | bytes 1769476
  97.6 11.0 %all-to-all-start.3 = ((f32[32,1,128]{2,1,0:T(1,128)}), f32[32,1,128]{2,1,0:T(1,128)S(1)}, u32[]{:S(2)}, u32[]{:S(2)}) async-start(f32[32,1,128]{2,1,0:T(1,128)} %shard_map.157), calls=%async_computation.3 | async-start | bytes 32768 | tf_op jit(solution)/shard_map/all_to_all | solution.py:33
  103.6 2.4 %copy-start.29 = (s32[32]{0:T(128)S(1)}, s32[32]{0:T(128)}, u32[]{:S(2)}) copy-start(s32[32]{0:T(128)} %param.12) | copy-start | bytes 388
  115.4 4.4 %copy-start = (bf16[1536,384]{1,0:T(8,128)(2,1)S(1)}, bf16[1536,384]{1,0:T(8,128)(2,1)}, u32[]{:S(2)}) copy-start(bf16[1536,384]{1,0:T(8,128)(2,1)} %get-tuple-element.60.far_norm.norm_ref) | copy-start | bytes 3538948
  115.5 38.4 %all-to-all-start.4 = ((bf16[8,208,384]{2,1,0:T(8,128)(2,1)}), bf16[8,208,384]{2,1,0:T(8,128)(2,1)}, u32[]{:S(2)}, u32[]{:S(2)}) async-start(bf16[8,208,384]{2,1,0:T(8,128)(2,1)} %get-tuple-element.76), calls=%async_computation.4 | async-start | bytes 2555904 | tf_op jit(solution)/shard_map/all_to_all | solution.py:33
  119.9 2.4 %copy-start.25 = (f32[2,384]{1,0:T(2,128)S(1)}, f32[2,384]{1,0:T(2,128)}, u32[]{:S(2)}) copy-start(f32[2,384]{1,0:T(2,128)} %get-tuple-element.57.mass_ref) | copy-start | bytes 9220
  122.3 2.3 collective-permute-start.8
  127.2 26.6 %copy-start.6 = (bf16[208,384]{1,0:T(8,128)(2,1)S(1)}, bf16[208,384]{1,0:T(8,128)(2,1)}, u32[]{:S(2)}) copy-start(bf16[208,384]{1,0:T(8,128)(2,1)} %copy-done.5) | copy-start | bytes 479236
  127.2 26.6 %copy-start.8 = (f32[1,384]{1,0:T(1,128)S(1)}, f32[1,384]{1,0:T(1,128)}, u32[]{:S(2)}) copy-start(f32[1,384]{1,0:T(1,128)} %copy-done.7) | copy-start | bytes 4612
  127.3 26.6 %copy-start.9 = (f32[2,384]{1,0:T(2,128)S(1)}, f32[2,384]{1,0:T(2,128)}, u32[]{:S(2)}) copy-start(f32[2,384]{1,0:T(2,128)} %get-tuple-element.73.refs_3_) | copy-start | bytes 9220
  127.3 10.3 %collective-permute-start.9 = (bf16[4,48,384]{2,1,0:T(8,128)(2,1)S(1)}, bf16[4,48,384]{2,1,0:T(8,128)(2,1)S(1)}, u32[]{:S(2)}, u32[]{:S(2)}) collective-permute-start(bf16[4,48,384]{2,1,0:T(8,128)(2,1)S(1)} %get-tuple-element.65), channel_id=1, source_target_pairs={{0,16},{16,32},{32,48},{48,0},{1,17},{17,33},{33,49},{49,1},{2,18}... | collective-permute-start | bytes 442376 | tf_op jit(solution)/shard_map/ppermute | solution.py:764
  127.9 9.7 %collective-permute-start.10 = (bf16[4,48,384]{2,1,0:T(8,128)(2,1)S(1)}, bf16[4,48,384]{2,1,0:T(8,128)(2,1)S(1)}, u32[]{:S(2)}, u32[]{:S(2)}) collective-permute-start(bf16[4,48,384]{2,1,0:T(8,128)(2,1)S(1)} %get-tuple-element.66), channel_id=1, source_target_pairs={{0,32},{16,48},{32,0},{48,16},{1,33},{17,49},{33,1},{49,17},{2,34}... | collective-permute-start | bytes 442376 | tf_op jit(solution)/shard_map/ppermute | solution.py:764
  130.0 8.3 %collective-permute-start.11 = (bf16[4,48,384]{2,1,0:T(8,128)(2,1)S(1)}, bf16[4,48,384]{2,1,0:T(8,128)(2,1)S(1)}, u32[]{:S(2)}, u32[]{:S(2)}) collective-permute-start(bf16[4,48,384]{2,1,0:T(8,128)(2,1)S(1)} %get-tuple-element.67), channel_id=1, source_target_pairs={{0,48},{16,0},{32,16},{48,32},{1,49},{17,1},{33,17},{49,33},{2,50}... | collective-permute-start | bytes 442376 | tf_op jit(solution)/shard_map/ppermute | solution.py:764
  138.3 4.7 %collective-permute-start.14 = (bf16[48,384]{1,0:T(8,128)(2,1)S(1)}, bf16[48,384]{1,0:T(8,128)(2,1)S(1)}, u32[]{:S(2)}, u32[]{:S(2)}) collective-permute-start(bf16[48,384]{1,0:T(8,128)(2,1)S(1)} %get-tuple-element.71), channel_id=1, source_target_pairs={{0,192},{64,0},{128,64},{192,128},{1,193},{65,1},{129,65},{193,129... | collective-permute-start | bytes 110600 | tf_op jit(solution)/shard_map/ppermute | solution.py:764
  140.0 5.5 %collective-permute-start.13 = (bf16[48,384]{1,0:T(8,128)(2,1)S(1)}, bf16[48,384]{1,0:T(8,128)(2,1)S(1)}, u32[]{:S(2)}, u32[]{:S(2)}) collective-permute-start(bf16[48,384]{1,0:T(8,128)(2,1)S(1)} %get-tuple-element.70), channel_id=1, source_target_pairs={{0,128},{64,192},{128,0},{192,64},{1,129},{65,193},{129,1},{193,65... | collective-permute-start | bytes 110600 | tf_op jit(solution)/shard_map/ppermute | solution.py:764
  140.6 4.9 %collective-permute-start.12 = (bf16[48,384]{1,0:T(8,128)(2,1)S(1)}, bf16[48,384]{1,0:T(8,128)(2,1)S(1)}, u32[]{:S(2)}, u32[]{:S(2)}) collective-permute-start(bf16[48,384]{1,0:T(8,128)(2,1)S(1)} %get-tuple-element.69), channel_id=1, source_target_pairs={{0,64},{64,128},{128,192},{192,0},{1,65},{65,129},{129,193},{193,1... | collective-permute-start | bytes 110600 | tf_op jit(solution)/shard_map/ppermute | solution.py:764
  168.8 22.7 %copy-start.4 = (bf16[192,768]{1,0:T(8,128)(2,1)S(1)}, bf16[192,768]{1,0:T(8,128)(2,1)}, u32[]{:S(2)}) copy-start(bf16[192,768]{1,0:T(8,128)(2,1)} %get-tuple-element.62.hidden_ref) | copy-start | bytes 884740
  168.8 23.5 %copy-start.1 = (bf16[768,1536]{1,0:T(8,128)(2,1)S(1)}, bf16[768,1536]{1,0:T(8,128)(2,1)}, u32[]{:S(2)}) copy-start(bf16[768,1536]{1,0:T(8,128)(2,1)} %two_ref.1) | copy-start | bytes 7077892
  192.1 3.3 %collective-permute-start.15 = (bf16[16,48,768]{2,1,0:T(8,128)(2,1)S(1)}, bf16[16,48,768]{2,1,0:T(8,128)(2,1)S(1)}, u32[]{:S(2)}, u32[]{:S(2)}) collective-permute-start(bf16[16,48,768]{2,1,0:T(8,128)(2,1)S(1)} %get-tuple-element.78), channel_id=1, source_target_pairs={{0,8},{8,0},{1,9},{9,1},{2,10},{10,2},{3,11},{11,3},{4,12},{12,4},... | collective-permute-start | bytes 3538952 | tf_op jit(solution)/shard_map/ppermute | solution.py:813
  194.9 3.0 %collective-permute-start.19 = (bf16[16,48,768]{2,1,0:T(8,128)(2,1)S(1)}, bf16[16,48,768]{2,1,0:T(8,128)(2,1)S(1)}, u32[]{:S(2)}, u32[]{:S(2)}) collective-permute-start(bf16[16,48,768]{2,1,0:T(8,128)(2,1)S(1)} %get-tuple-element.84), channel_id=1, source_target_pairs={{0,8},{8,0},{1,9},{9,1},{2,10},{10,2},{3,11},{11,3},{4,12},{12,4},... | collective-permute-start | bytes 3538952 | tf_op jit(solution)/shard_map/ppermute | solution.py:824
  199.2 22.9 %all-to-all-start.8 = ((bf16[4,4,48,768]{3,2,1,0:T(8,128)(2,1)}), bf16[4,4,48,768]{3,2,1,0:T(8,128)(2,1)S(1)}, u32[]{:S(2)}, u32[]{:S(2)}) async-start(bf16[4,4,48,768]{3,2,1,0:T(8,128)(2,1)} %shard_map.168), calls=%async_computation.8 | async-start | bytes 2359296 | tf_op jit(solution)/shard_map/all_to_all | solution.py:33
  204.1 16.7 %collective-permute-start.16 = (bf16[4,48,768]{2,1,0:T(8,128)(2,1)}, bf16[4,48,768]{2,1,0:T(8,128)(2,1)S(1)}, u32[]{:S(2)}, u32[]{:S(2)}) collective-permute-start(bf16[4,48,768]{2,1,0:T(8,128)(2,1)} %get-tuple-element.80), channel_id=1, source_target_pairs={{0,16},{16,32},{32,48},{48,0},{1,17},{17,33},{33,49},{49,1},{2,18}... | collective-permute-start | bytes 884744 | tf_op jit(solution)/shard_map/ppermute | solution.py:764
  204.8 16.0 %collective-permute-start.17 = (bf16[4,48,768]{2,1,0:T(8,128)(2,1)S(1)}, bf16[4,48,768]{2,1,0:T(8,128)(2,1)S(1)}, u32[]{:S(2)}, u32[]{:S(2)}) collective-permute-start(bf16[4,48,768]{2,1,0:T(8,128)(2,1)S(1)} %get-tuple-element.81), channel_id=1, source_target_pairs={{0,32},{16,48},{32,0},{48,16},{1,33},{17,49},{33,1},{49,17},{2,34}... | collective-permute-start | bytes 884744 | tf_op jit(solution)/shard_map/ppermute | solution.py:764
  207.0 14.3 %collective-permute-start.18 = (bf16[4,48,768]{2,1,0:T(8,128)(2,1)S(1)}, bf16[4,48,768]{2,1,0:T(8,128)(2,1)S(1)}, u32[]{:S(2)}, u32[]{:S(2)}) collective-permute-start(bf16[4,48,768]{2,1,0:T(8,128)(2,1)S(1)} %get-tuple-element.82), channel_id=1, source_target_pairs={{0,48},{16,0},{32,16},{48,32},{1,49},{17,1},{33,17},{49,33},{2,50}... | collective-permute-start | bytes 884744 | tf_op jit(solution)/shard_map/ppermute | solution.py:764
  222.1 10.6 %all-to-all-start.7 = ((bf16[4,48,768]{2,1,0:T(8,128)(2,1)}), bf16[4,48,768]{2,1,0:T(8,128)(2,1)S(1)}, u32[]{:S(2)}, u32[]{:S(2)}) async-start(bf16[4,48,768]{2,1,0:T(8,128)(2,1)} %shard_map.166), calls=%async_computation.7 | async-start | bytes 589824 | tf_op jit(solution)/shard_map/all_to_all | solution.py:33
  227.0 6.4 %collective-permute-start.20 = (bf16[48,768]{1,0:T(8,128)(2,1)S(1)}, bf16[48,768]{1,0:T(8,128)(2,1)S(1)}, u32[]{:S(2)}, u32[]{:S(2)}) collective-permute-start(bf16[48,768]{1,0:T(8,128)(2,1)S(1)} %get-tuple-element.86), channel_id=1, source_target_pairs={{0,16},{16,32},{32,48},{48,0},{1,17},{17,33},{33,49},{49,1},{2,18}... | collective-permute-start | bytes 221192 | tf_op jit(solution)/shard_map/ppermute | solution.py:764
  227.5 6.7 %collective-permute-start.21 = (bf16[48,768]{1,0:T(8,128)(2,1)S(1)}, bf16[48,768]{1,0:T(8,128)(2,1)S(1)}, u32[]{:S(2)}, u32[]{:S(2)}) collective-permute-start(bf16[48,768]{1,0:T(8,128)(2,1)S(1)} %get-tuple-element.87), channel_id=1, source_target_pairs={{0,32},{16,48},{32,0},{48,16},{1,33},{17,49},{33,1},{49,17},{2,34}... | collective-permute-start | bytes 221192 | tf_op jit(solution)/shard_map/ppermute | solution.py:764
  231.1 4.4 %collective-permute-start.22 = (bf16[48,768]{1,0:T(8,128)(2,1)S(1)}, bf16[48,768]{1,0:T(8,128)(2,1)S(1)}, u32[]{:S(2)}, u32[]{:S(2)}) collective-permute-start(bf16[48,768]{1,0:T(8,128)(2,1)S(1)} %get-tuple-element.88), channel_id=1, source_target_pairs={{0,48},{16,0},{32,16},{48,32},{1,49},{17,1},{33,17},{49,33},{2,50}... | collective-permute-start | bytes 221192 | tf_op jit(solution)/shard_map/ppermute | solution.py:764
  (12 other events, 10.7 us)

commit v10 on v7

--- a/solution.py
+++ b/solution.py
@@ -245,7 +245,7 @@
         scores = contract(query_unit.astype(bf16), key_unit.astype(bf16), 0, 0)
         weights = jnp.exp(scores * (score_scale / HEAD)) * valid
         weights = weights * (1.0 / jnp.sum(weights, 1, keepdims=True))
-        attention_ref[h] = weights
+        attention_ref[h] = weights.astype(bf16)
         copies.append(
             pltpu.make_async_copy(attention_ref.at[h], far_attention.at[h], sems.at[2 + 2 * h])
         )
@@ -374,7 +374,7 @@
     for h in range(heads):
         up_head = up[h * HEAD : (h + 1) * HEAD]
         values = heads_ref[h, 2]
-        weights = attention_ref[h]
+        weights = attention_ref[h].astype(f32)
         pull = jnp.sum(up_head * values, 0, keepdims=True)
         pull_mean = jnp.sum(weights * pull, 1, keepdims=True)
         grad_scores = (weights * (pull - pull_mean) * (score_scale / HEAD)).astype(bf16)
@@ -668,7 +668,7 @@
         [
             ((width, length), bf16, "far"),
             ((heads, 3, HEAD, length), f32, "far"),
-            ((heads, length, length), f32, "far"),
+            ((heads, length, length), bf16, "far"),
             ((2, length), f32),
             ((heads, 2, length), f32),
             ((heads, length), f32),
@@ -688,7 +688,7 @@
             ((width, length), bf16),
             ((width, length), bf16),
             ((heads, 3, HEAD, length), f32),
-            ((heads, length, length), f32),
+            ((heads, length, length), bf16),
             ((inner, width), bf16),
             ((inner, width), bf16),
             ((inner, width), bf16),
@@ -730,7 +730,7 @@
         scratch=[
             (w_out.shape, bf16),
             (by_head.shape, f32),
-            (attention.shape, f32),
+            (attention.shape, bf16),
             (w_query.shape, bf16),
             (w_key.shape, bf16),
             (w_value.shape, bf16),

time: 237 us -> 237 us (level)
  no operation moved by 1% of the time
where the time goes in v10:
time: 237 us; the launch traced here: 236 us
  waiting for transfers between devices  64.6 us (27%)
  blocking collectives  63.1 us (27%)
  starting transfers between devices  56.8 us (24%)
  Pallas kernels  31.3 us (13%)
  local copies, waits for them, and re-layouts  15.8 us (7%)
    all_to_all x4, blocking collectives, exchange(): return lax.all_to_all(values, axis, 0, 0, tiled=True)  63.1 us
    pallas_call x18, Pallas kernels, call(): pl.pallas_call(kernel if skip else body, out_shape=[jax.ShapeDtypeStruct(...  31.3 us
    all_to_all x5, starting transfers between devices, exchange(): return lax.all_to_all(values, axis, 0, 0, tiled=True)  27.6 us
    ppermute x12, waiting for transfers between devices, shift(): lax.ppermute(values[k], axis, turn(len(values), k))  24.5 us
    all_to_all x5, waiting for transfers between devices, exchange(): return lax.all_to_all(values, axis, 0, 0, tiled=True)  23.7 us
    ppermute x12, starting transfers between devices, shift(): lax.ppermute(values[k], axis, turn(len(values), k))  15.8 us
    ppermute x3, waiting for transfers between devices, gather_ring(): back = lax.ppermute(back, 'mp', turn(count, 1))  11.4 us
    unnamed x72, local copies, waits for them, and re-layouts  8.6 us
  transfers between devices with their start and end apart: 28, of which 18 were waited for; matrix products, arithmetic and copies ran while one was open for 6% of the time, Pallas kernels for 3%

profile of v10, /device:TPU:8, one launch (start us, length us, event | category | flops | bytes accessed | tf_op | source)
XLA Modules:
  0.0 235.7 jit_solution(16250872200767718523)
XLA Ops:
  0.6 4.5 %shard_map.153 = (bf16[192,1536]{1,0:T(8,128)(2,1)}, bf16[192,768]{1,0:T(8,128)(2,1)}, f32[192,768]{1,0:T(8,128)}, bf16[8,288,128]{2,1,0:T(8,128)(2,1)}) custom-call(bf16[192,1536]{1,0:T(8,128)(2,1)} %far_x.1, bf16[1536,768]{1,0:T(8,128)(2,1)} %far_one.1, bf16[768,1536]{1,0:T(8,128)(2,1)} %two_ref.1), custom_call_target="tpu_custom_call" | custom-call | tf_op jit(solution)/shard_map/pallas_call | solution.py:49
  5.2 8.6 %all-to-all-start = ((bf16[8,288,128]{2,1,0:T(8,128)(2,1)}), bf16[8,288,128]{2,1,0:T(8,128)(2,1)S(1)}, u32[]{:S(2)}, u32[]{:S(2)}) async-start(bf16[8,288,128]{2,1,0:T(8,128)(2,1)} %get-tuple-element.51), calls=%async_computation | async-start | bytes 1179648 | tf_op jit(solution)/shard_map/all_to_all | solution.py:33
  14.4 1.2 copy.42
  17.8 1.2 constant_dynamic-slice_fusion.3
  19.2 13.5 %all-to-all-done.refs_9_ = bf16[8,288,128]{2,1,0:T(8,128)(2,1)S(1)} async-done(((bf16[8,288,128]{2,1,0:T(8,128)(2,1)}), bf16[8,288,128]{2,1,0:T(8,128)(2,1)S(1)}, u32[]{:S(2)}, u32[]{:S(2)}) %all-to-all-start) | async-done | bytes 589856 | tf_op jit(solution)/shard_map/all_to_all | solution.py:33
  33.0 14.8 %all_to_all.45 = bf16[32,16,256]{2,1,0:T(8,128)(2,1)S(1)} all-to-all(bf16[32,16,256]{2,1,0:T(8,128)(2,1)S(1)} %bitcast.56), channel_id=1, replica_groups=mesh['line'=4,'column'=4,'core'=2,'mp'=8] {'line','column','core'}, dimensions={0} | all-to-all | bytes 524288 | tf_op jit(solution)/shard_map/all_to_all | solution.py:33
  48.8 2.7 %collective-permute-start.1 = (bf16[208,384]{1,0:T(8,128)(2,1)S(1)}, bf16[208,384]{1,0:T(8,128)(2,1)S(1)}, u32[]{:S(2)}, u32[]{:S(2)}) collective-permute-start(bf16[208,384]{1,0:T(8,128)(2,1)S(1)} %get-tuple-element.53.rest_0_.refs_4_), channel_id=1, source_target_pairs={{0,7},{1,0},{2,1},{3,2},{4,3},{5,4},{6,5},{7,6},{8,15},{9,8},{10,9... | collective-permute-start | bytes 479240 | tf_op jit(solution)/shard_map/ppermute | solution.py:83
  51.5 4.5 %collective-permute-done.rest_1_ = bf16[208,384]{1,0:T(8,128)(2,1)S(1)} collective-permute-done((bf16[208,384]{1,0:T(8,128)(2,1)S(1)}, bf16[208,384]{1,0:T(8,128)(2,1)S(1)}, u32[]{:S(2)}, u32[]{:S(2)}) %collective-permute-start) | collective-permute-done | bytes 159776 | tf_op jit(solution)/shard_map/ppermute | solution.py:82
  56.0 3.2 %collective-permute-start.3 = (bf16[208,384]{1,0:T(8,128)(2,1)S(1)}, bf16[208,384]{1,0:T(8,128)(2,1)S(1)}, u32[]{:S(2)}, u32[]{:S(2)}) collective-permute-start(bf16[208,384]{1,0:T(8,128)(2,1)S(1)} %collective-permute-done.1.rest_2_), channel_id=1, source_target_pairs={{0,7},{1,0},{2,1},{3,2},{4,3},{5,4},{6,5},{7,6},{8,15},{9,8},{10,9... | collective-permute-start | bytes 479240 | tf_op jit(solution)/shard_map/ppermute | solution.py:83
  59.3 3.7 %collective-permute-done.2.rest_3_ = bf16[208,384]{1,0:T(8,128)(2,1)S(1)} collective-permute-done((bf16[208,384]{1,0:T(8,128)(2,1)S(1)}, bf16[208,384]{1,0:T(8,128)(2,1)S(1)}, u32[]{:S(2)}, u32[]{:S(2)}) %collective-permute-start.2) | collective-permute-done | bytes 159776 | tf_op jit(solution)/shard_map/ppermute | solution.py:82
  63.7 2.7 %collective-permute-start.5 = (bf16[208,384]{1,0:T(8,128)(2,1)S(1)}, bf16[208,384]{1,0:T(8,128)(2,1)S(1)}, u32[]{:S(2)}, u32[]{:S(2)}) collective-permute-start(bf16[208,384]{1,0:T(8,128)(2,1)S(1)} %collective-permute-done.3.rest_4_), channel_id=1, source_target_pairs={{0,7},{1,0},{2,1},{3,2},{4,3},{5,4},{6,5},{7,6},{8,15},{9,8},{10,9... | collective-permute-start | bytes 479240 | tf_op jit(solution)/shard_map/ppermute | solution.py:83
  66.3 3.2 %collective-permute-done.4.rest_5_ = bf16[208,384]{1,0:T(8,128)(2,1)S(1)} collective-permute-done((bf16[208,384]{1,0:T(8,128)(2,1)S(1)}, bf16[208,384]{1,0:T(8,128)(2,1)S(1)}, u32[]{:S(2)}, u32[]{:S(2)}) %collective-permute-start.4) | collective-permute-done | bytes 159776 | tf_op jit(solution)/shard_map/ppermute | solution.py:82
  69.6 3.5 %collective-permute-start.7 = (bf16[96,384]{1,0:T(8,128)(2,1)S(1)}, bf16[96,384]{1,0:T(8,128)(2,1)S(1)}, u32[]{:S(2)}, u32[]{:S(2)}) collective-permute-start(bf16[96,384]{1,0:T(8,128)(2,1)S(1)} %slice.51), channel_id=1, source_target_pairs={{0,7},{1,0},{2,1},{3,2},{4,3},{5,4},{6,5},{7,6},{8,15},{9,8},{10,9... | collective-permute-start | bytes 221192 | tf_op jit(solution)/shard_map/ppermute | solution.py:87
  73.1 2.0 collective-permute-done.7.rest_8_
  75.9 6.6 %shard_map.156 = (bf16[1536,384]{1,0:T(8,128)(2,1)}, f32[2,3,96,384]{3,2,1,0:T(8,128)}, bf16[2,384,384]{2,1,0:T(8,128)(2,1)}, f32[2,384]{1,0:T(2,128)}, f32[2,2,...) custom-call(s32[1]{0:T(128)} %bitcast.1.here, ...), custom_call_target="tpu_custom_call" | custom-call | tf_op jit(solution)/shard_map/pallas_call | solution.py:49
  82.5 12.9 %all_to_all.46.parts_ref = f32[8,1,1536]{2,1,0:T(1,128)S(1)} all-to-all(f32[8,1,1536]{2,1,0:T(1,128)} %get-tuple-element.54), channel_id=1, replica_groups=mesh['line'=4,'column'=4,'core'=2,'mp'=8] {'mp'}, dimensions={0} | all-to-all | bytes 98304 | tf_op jit(solution)/shard_map/all_to_all | solution.py:33
  96.3 1.0 shard_map.157
  97.4 4.9 %all-to-all-start.3 = ((f32[32,1,128]{2,1,0:T(1,128)}), f32[32,1,128]{2,1,0:T(1,128)S(1)}, u32[]{:S(2)}, u32[]{:S(2)}) async-start(f32[32,1,128]{2,1,0:T(1,128)} %shard_map.157), calls=%async_computation.3 | async-start | bytes 32768 | tf_op jit(solution)/shard_map/all_to_all | solution.py:33
  102.2 1.2 copy.49.far_query_weights
  103.4 1.2 copy.50.far_key_weights
  104.6 1.2 copy.51.far_value_weights
  106.5 1.9 all-to-all-done.3
  108.9 6.1 %shard_map.158 = (f32[1,1]{1,0:T(1,128)}, f32[1,1536]{1,0:T(1,128)}, f32[1,192]{1,0:T(1,128)}, bf16[576,384]{1,0:T(8,128)(2,1)}, bf16[8,208,384]{2,1,0:T(8,128)(2,1)}) custom-call(s32[1]{0:T(128)} %bitcast.owner, f32[32,128]{1,0:T(8,128)} %bitcast.66, s32[32,1]{1,0:T(8,128)} %copy.48.pair_ref, f32[8,1,1536]{2,1,0:T(1,128)} %copy-done.8, ...), custom_call_target="tpu_custom_call" | custom-call | tf_op jit(solution)/shard_map/pallas_call | solution.py:49
  115.0 4.4 %all-to-all-start.4 = ((bf16[8,208,384]{2,1,0:T(8,128)(2,1)}), bf16[8,208,384]{2,1,0:T(8,128)(2,1)}, u32[]{:S(2)}, u32[]{:S(2)}) async-start(bf16[8,208,384]{2,1,0:T(8,128)(2,1)} %get-tuple-element.76), calls=%async_computation.4 | async-start | bytes 2555904 | tf_op jit(solution)/shard_map/all_to_all | solution.py:33
  120.5 1.3 shard_map.159
  122.8 1.4 collective-permute-done.8.got_ref
  124.2 1.0 copy-done.3
  125.2 1.6 shard_map.160
  127.5 2.0 collective-permute-start.10
  129.5 1.2 collective-permute-start.11
  130.8 6.4 %collective-permute-done.9.refs_1_ = bf16[4,48,384]{2,1,0:T(8,128)(2,1)S(1)} collective-permute-done((bf16[4,48,384]{2,1,0:T(8,128)(2,1)S(1)}, bf16[4,48,384]{2,1,0:T(8,128)(2,1)S(1)}, u32[]{:S(2)}, u32[]{:S(2)}) %collective-permute-start.9) | collective-permute-done | bytes 147488 | tf_op jit(solution)/shard_map/ppermute | solution.py:763
  137.9 1.7 collective-permute-start.14
  140.2 2.0 collective-permute-start.12
  142.6 2.5 %collective-permute-done.13 = bf16[48,384]{1,0:T(8,128)(2,1)S(1)} collective-permute-done((bf16[48,384]{1,0:T(8,128)(2,1)S(1)}, bf16[48,384]{1,0:T(8,128)(2,1)S(1)}, u32[]{:S(2)}, u32[]{:S(2)}) %collective-permute-start.13) | collective-permute-done | bytes 36896 | tf_op jit(solution)/shard_map/ppermute | solution.py:763
  145.1 8.4 %all-to-all-done.4.refs_7_ = bf16[8,208,384]{2,1,0:T(8,128)(2,1)} async-done(((bf16[8,208,384]{2,1,0:T(8,128)(2,1)}), bf16[8,208,384]{2,1,0:T(8,128)(2,1)}, u32[]{:S(2)}, u32[]{:S(2)}) %all-to-all-start.4) | async-done | bytes 1277984 | tf_op jit(solution)/shard_map/all_to_all | solution.py:33
  153.4 1.8 shard_map.162
  155.3 13.0 %all_to_all.47 = bf16[32,16,192]{2,1,0:T(8,128)(2,1)S(1)} all-to-all(bf16[32,16,192]{2,1,0:T(8,128)(2,1)S(1)} %bitcast.59), channel_id=1, replica_groups=mesh['line'=4,'column'=4,'core'=2,'mp'=8] {'line','column','core'}, dimensions={0} | all-to-all | bytes 393216 | tf_op jit(solution)/shard_map/all_to_all | solution.py:33
  168.7 22.4 %all_to_all.48.parts_ref = bf16[8,288,128]{2,1,0:T(8,128)(2,1)S(1)} all-to-all(bf16[8,288,128]{2,1,0:T(8,128)(2,1)S(1)} %shard_map.163), channel_id=1, replica_groups=mesh['line'=4,'column'=4,'core'=2,'mp'=8] {'mp'}, dimensions={0} | all-to-all | bytes 1179648 | tf_op jit(solution)/shard_map/all_to_all | solution.py:33
  191.8 2.6 %shard_map.167 = (bf16[16,48,768]{2,1,0:T(8,128)(2,1)S(1)}, bf16[16,48,768]{2,1,0:T(8,128)(2,1)S(1)}) custom-call(bf16[768,1536]{1,0:T(8,128)(2,1)S(1)} %copy-done.1, f32[768,192]{1,0:T(8,128)S(1)} %bitcast.50, bf16[768,192]{1,0:T(8,128)(2,1)S(1)} %bitcast.52, bf16[768,192]{1,0:T(8,128)(2,1)S(1)} %bitcast.54, bf16[1536,192]{1,0:T(8,128)(2,1)S(1)} %get-tuple-element.77.grad_ref), custom_call_target="tpu_custom_call" | custom-call | tf_op jit(solution)/shard_map/pallas_call | solution.py:49
  194.9 1.0 shard_map.165
  196.0 1.4 collective-permute-done.19.refs_2_
  197.4 1.3 shard_map.168
  198.7 4.9 %all-to-all-start.8 = ((bf16[4,4,48,768]{3,2,1,0:T(8,128)(2,1)}), bf16[4,4,48,768]{3,2,1,0:T(8,128)(2,1)S(1)}, u32[]{:S(2)}, u32[]{:S(2)}) async-start(bf16[4,4,48,768]{3,2,1,0:T(8,128)(2,1)} %shard_map.168), calls=%async_computation.8 | async-start | bytes 2359296 | tf_op jit(solution)/shard_map/all_to_all | solution.py:33
  204.4 2.1 collective-permute-start.17
  208.4 11.9 %collective-permute-done.16.refs_1_ = bf16[4,48,768]{2,1,0:T(8,128)(2,1)S(1)} collective-permute-done((bf16[4,48,768]{2,1,0:T(8,128)(2,1)}, bf16[4,48,768]{2,1,0:T(8,128)(2,1)S(1)}, u32[]{:S(2)}, u32[]{:S(2)}) %collective-permute-start.16) | collective-permute-done | bytes 294944 | tf_op jit(solution)/shard_map/ppermute | solution.py:763
  221.6 4.8 %all-to-all-start.7 = ((bf16[4,48,768]{2,1,0:T(8,128)(2,1)}), bf16[4,48,768]{2,1,0:T(8,128)(2,1)S(1)}, u32[]{:S(2)}, u32[]{:S(2)}) async-start(bf16[4,48,768]{2,1,0:T(8,128)(2,1)} %shard_map.166), calls=%async_computation.7 | async-start | bytes 589824 | tf_op jit(solution)/shard_map/all_to_all | solution.py:33
  227.1 3.6 %collective-permute-start.21 = (bf16[48,768]{1,0:T(8,128)(2,1)S(1)}, bf16[48,768]{1,0:T(8,128)(2,1)S(1)}, u32[]{:S(2)}, u32[]{:S(2)}) collective-permute-start(bf16[48,768]{1,0:T(8,128)(2,1)S(1)} %get-tuple-element.87), channel_id=1, source_target_pairs={{0,32},{16,48},{32,0},{48,16},{1,33},{17,49},{33,1},{49,17},{2,34}... | collective-permute-start | bytes 221192 | tf_op jit(solution)/shard_map/ppermute | solution.py:763
  233.7 1.2 collective-permute-done.22.refs_3_
  (158 shorter events, 22.6 us)
Async XLA Ops:
  5.2 8.6 %copy-start.15 = (bf16[192,1536]{1,0:T(8,128)(2,1)S(1)}, bf16[192,1536]{1,0:T(8,128)(2,1)}, u32[]{:S(2)}) copy-start(bf16[192,1536]{1,0:T(8,128)(2,1)} %far_x.1) | copy-start | bytes 1769476
  5.2 9.3 %copy-start.17 = (bf16[192,1536]{1,0:T(8,128)(2,1)S(1)}, bf16[192,1536]{1,0:T(8,128)(2,1)}, u32[]{:S(2)}) copy-start(bf16[192,1536]{1,0:T(8,128)(2,1)} %get-tuple-element.49) | copy-start | bytes 1769476
  5.2 27.5 %all-to-all-start = ((bf16[8,288,128]{2,1,0:T(8,128)(2,1)}), bf16[8,288,128]{2,1,0:T(8,128)(2,1)S(1)}, u32[]{:S(2)}, u32[]{:S(2)}) async-start(bf16[8,288,128]{2,1,0:T(8,128)(2,1)} %get-tuple-element.51), calls=%async_computation | async-start | bytes 1179648 | tf_op jit(solution)/shard_map/all_to_all | solution.py:33
  48.2 27.1 %copy-start.5 = (bf16[208,384]{1,0:T(8,128)(2,1)}, bf16[208,384]{1,0:T(8,128)(2,1)S(1)}, u32[]{:S(2)}) copy-start(bf16[208,384]{1,0:T(8,128)(2,1)S(1)} %get-tuple-element.53.rest_0_.refs_4_) | copy-start | bytes 479236
  48.2 27.1 %copy-start.9 = (f32[1,384]{1,0:T(1,128)}, f32[1,384]{1,0:T(1,128)S(1)}, u32[]{:S(2)}) copy-start(f32[1,384]{1,0:T(1,128)S(1)} %get-tuple-element.52.valid_ref.refs_2_) | copy-start | bytes 4612
  48.2 7.8 %collective-permute-start = (bf16[208,384]{1,0:T(8,128)(2,1)S(1)}, bf16[208,384]{1,0:T(8,128)(2,1)S(1)}, u32[]{:S(2)}, u32[]{:S(2)}) collective-permute-start(bf16[208,384]{1,0:T(8,128)(2,1)S(1)} %get-tuple-element.53.rest_0_.refs_4_), channel_id=1, source_target_pairs={{0,1},{1,2},{2,3},{3,4},{4,5},{5,6},{6,7},{7,0},{8,9},{9,10},{10,1... | collective-permute-start | bytes 479240 | tf_op jit(solution)/shard_map/ppermute | solution.py:82
  48.8 7.2 %collective-permute-start.1 = (bf16[208,384]{1,0:T(8,128)(2,1)S(1)}, bf16[208,384]{1,0:T(8,128)(2,1)S(1)}, u32[]{:S(2)}, u32[]{:S(2)}) collective-permute-start(bf16[208,384]{1,0:T(8,128)(2,1)S(1)} %get-tuple-element.53.rest_0_.refs_4_), channel_id=1, source_target_pairs={{0,7},{1,0},{2,1},{3,2},{4,3},{5,4},{6,5},{7,6},{8,15},{9,8},{10,9... | collective-permute-start | bytes 479240 | tf_op jit(solution)/shard_map/ppermute | solution.py:83
  56.0 3.2 %copy-start.20 = (bf16[208,384]{1,0:T(8,128)(2,1)}, bf16[208,384]{1,0:T(8,128)(2,1)S(1)}, u32[]{:S(2)}) copy-start(bf16[208,384]{1,0:T(8,128)(2,1)S(1)} %collective-permute-done.rest_1_) | copy-start | bytes 479236
  56.0 7.0 %collective-permute-start.2 = (bf16[208,384]{1,0:T(8,128)(2,1)S(1)}, bf16[208,384]{1,0:T(8,128)(2,1)S(1)}, u32[]{:S(2)}, u32[]{:S(2)}) collective-permute-start(bf16[208,384]{1,0:T(8,128)(2,1)S(1)} %collective-permute-done.rest_1_), channel_id=1, source_target_pairs={{0,1},{1,2},{2,3},{3,4},{4,5},{5,6},{6,7},{7,0},{8,9},{9,10},{10,1... | collective-permute-start | bytes 479240 | tf_op jit(solution)/shard_map/ppermute | solution.py:82
  56.0 7.0 %copy-start.21 = (bf16[208,384]{1,0:T(8,128)(2,1)}, bf16[208,384]{1,0:T(8,128)(2,1)S(1)}, u32[]{:S(2)}) copy-start(bf16[208,384]{1,0:T(8,128)(2,1)S(1)} %collective-permute-done.1.rest_2_) | copy-start | bytes 479236
  56.0 7.0 %collective-permute-start.3 = (bf16[208,384]{1,0:T(8,128)(2,1)S(1)}, bf16[208,384]{1,0:T(8,128)(2,1)S(1)}, u32[]{:S(2)}, u32[]{:S(2)}) collective-permute-start(bf16[208,384]{1,0:T(8,128)(2,1)S(1)} %collective-permute-done.1.rest_2_), channel_id=1, source_target_pairs={{0,7},{1,0},{2,1},{3,2},{4,3},{5,4},{6,5},{7,6},{8,15},{9,8},{10,9... | collective-permute-start | bytes 479240 | tf_op jit(solution)/shard_map/ppermute | solution.py:83
  63.0 6.5 %collective-permute-start.4 = (bf16[208,384]{1,0:T(8,128)(2,1)S(1)}, bf16[208,384]{1,0:T(8,128)(2,1)S(1)}, u32[]{:S(2)}, u32[]{:S(2)}) collective-permute-start(bf16[208,384]{1,0:T(8,128)(2,1)S(1)} %collective-permute-done.2.rest_3_), channel_id=1, source_target_pairs={{0,1},{1,2},{2,3},{3,4},{4,5},{5,6},{6,7},{7,0},{8,9},{9,10},{10,1... | collective-permute-start | bytes 479240 | tf_op jit(solution)/shard_map/ppermute | solution.py:82
  63.7 11.6 %copy-start.23 = (bf16[208,384]{1,0:T(8,128)(2,1)}, bf16[208,384]{1,0:T(8,128)(2,1)S(1)}, u32[]{:S(2)}) copy-start(bf16[208,384]{1,0:T(8,128)(2,1)S(1)} %collective-permute-done.3.rest_4_) | copy-start | bytes 479236
  63.7 5.9 %collective-permute-start.5 = (bf16[208,384]{1,0:T(8,128)(2,1)S(1)}, bf16[208,384]{1,0:T(8,128)(2,1)S(1)}, u32[]{:S(2)}, u32[]{:S(2)}) collective-permute-start(bf16[208,384]{1,0:T(8,128)(2,1)S(1)} %collective-permute-done.3.rest_4_), channel_id=1, source_target_pairs={{0,7},{1,0},{2,1},{3,2},{4,3},{5,4},{6,5},{7,6},{8,15},{9,8},{10,9... | collective-permute-start | bytes 479240 | tf_op jit(solution)/shard_map/ppermute | solution.py:83
  69.5 5.8 %copy-start.18 = (bf16[208,384]{1,0:T(8,128)(2,1)}, bf16[208,384]{1,0:T(8,128)(2,1)S(1)}, u32[]{:S(2)}) copy-start(bf16[208,384]{1,0:T(8,128)(2,1)S(1)} %collective-permute-done.4.rest_5_) | copy-start | bytes 479236
  69.5 5.8 %collective-permute-start.6 = (bf16[112,384]{1,0:T(8,128)(2,1)S(1)}, bf16[112,384]{1,0:T(8,128)(2,1)S(1)}, u32[]{:S(2)}, u32[]{:S(2)}) collective-permute-start(bf16[112,384]{1,0:T(8,128)(2,1)S(1)} %slice.50), channel_id=1, source_target_pairs={{0,1},{1,2},{2,3},{3,4},{4,5},{5,6},{6,7},{7,0},{8,9},{9,10},{10,1... | collective-permute-start | bytes 258056 | tf_op jit(solution)/shard_map/ppermute | solution.py:86
  69.6 5.7 %copy-start.19 = (bf16[208,384]{1,0:T(8,128)(2,1)}, bf16[208,384]{1,0:T(8,128)(2,1)S(1)}, u32[]{:S(2)}) copy-start(bf16[208,384]{1,0:T(8,128)(2,1)S(1)} %collective-permute-done.5.rest_6_) | copy-start | bytes 479236
  69.6 5.4 %collective-permute-start.7 = (bf16[96,384]{1,0:T(8,128)(2,1)S(1)}, bf16[96,384]{1,0:T(8,128)(2,1)S(1)}, u32[]{:S(2)}, u32[]{:S(2)}) collective-permute-start(bf16[96,384]{1,0:T(8,128)(2,1)S(1)} %slice.51), channel_id=1, source_target_pairs={{0,7},{1,0},{2,1},{3,2},{4,3},{5,4},{6,5},{7,6},{8,15},{9,8},{10,9... | collective-permute-start | bytes 221192 | tf_op jit(solution)/shard_map/ppermute | solution.py:87
  75.9 26.3 %copy-start.12 = (bf16[1536,192]{0,1:T(8,128)(2,1)S(1)}, bf16[1536,192]{0,1:T(8,128)(2,1)}, u32[]{:S(2)}) copy-start(bf16[1536,192]{0,1:T(8,128)(2,1)} %param.16) | copy-start | bytes 1769476
  75.9 27.5 %copy-start.13 = (bf16[1536,192]{0,1:T(8,128)(2,1)S(1)}, bf16[1536,192]{0,1:T(8,128)(2,1)}, u32[]{:S(2)}) copy-start(bf16[1536,192]{0,1:T(8,128)(2,1)} %param.17) | copy-start | bytes 1769476
  95.4 9.2 %copy-start.8 = (f32[8,1,1536]{2,1,0:T(1,128)}, f32[8,1,1536]{2,1,0:T(1,128)S(1)}, u32[]{:S(2)}) copy-start(f32[8,1,1536]{2,1,0:T(1,128)S(1)} %all_to_all.46.parts_ref) | copy-start | bytes 147460
  97.4 11.0 %all-to-all-start.3 = ((f32[32,1,128]{2,1,0:T(1,128)}), f32[32,1,128]{2,1,0:T(1,128)S(1)}, u32[]{:S(2)}, u32[]{:S(2)}) async-start(f32[32,1,128]{2,1,0:T(1,128)} %shard_map.157), calls=%async_computation.3 | async-start | bytes 32768 | tf_op jit(solution)/shard_map/all_to_all | solution.py:33
  103.4 2.3 copy-start.31
  115.0 4.4 %copy-start = (bf16[1536,384]{1,0:T(8,128)(2,1)S(1)}, bf16[1536,384]{1,0:T(8,128)(2,1)}, u32[]{:S(2)}) copy-start(bf16[1536,384]{1,0:T(8,128)(2,1)} %get-tuple-element.60.far_norm.norm_ref) | copy-start | bytes 3538948
  115.0 38.4 %all-to-all-start.4 = ((bf16[8,208,384]{2,1,0:T(8,128)(2,1)}), bf16[8,208,384]{2,1,0:T(8,128)(2,1)}, u32[]{:S(2)}, u32[]{:S(2)}) async-start(bf16[8,208,384]{2,1,0:T(8,128)(2,1)} %get-tuple-element.76), calls=%async_computation.4 | async-start | bytes 2555904 | tf_op jit(solution)/shard_map/all_to_all | solution.py:33
  119.4 2.4 %copy-start.27 = (f32[2,384]{1,0:T(2,128)S(1)}, f32[2,384]{1,0:T(2,128)}, u32[]{:S(2)}) copy-start(f32[2,384]{1,0:T(2,128)} %get-tuple-element.57.mass_ref) | copy-start | bytes 9220
  121.8 2.3 collective-permute-start.8
  126.8 26.6 %copy-start.6 = (bf16[208,384]{1,0:T(8,128)(2,1)S(1)}, bf16[208,384]{1,0:T(8,128)(2,1)}, u32[]{:S(2)}) copy-start(bf16[208,384]{1,0:T(8,128)(2,1)} %copy-done.5) | copy-start | bytes 479236
  126.8 26.6 %copy-start.10 = (f32[1,384]{1,0:T(1,128)S(1)}, f32[1,384]{1,0:T(1,128)}, u32[]{:S(2)}) copy-start(f32[1,384]{1,0:T(1,128)} %copy-done.9) | copy-start | bytes 4612
  126.8 26.6 %copy-start.11 = (f32[2,384]{1,0:T(2,128)S(1)}, f32[2,384]{1,0:T(2,128)}, u32[]{:S(2)}) copy-start(f32[2,384]{1,0:T(2,128)} %get-tuple-element.73.refs_3_) | copy-start | bytes 9220
  126.8 10.3 %collective-permute-start.9 = (bf16[4,48,384]{2,1,0:T(8,128)(2,1)S(1)}, bf16[4,48,384]{2,1,0:T(8,128)(2,1)S(1)}, u32[]{:S(2)}, u32[]{:S(2)}) collective-permute-start(bf16[4,48,384]{2,1,0:T(8,128)(2,1)S(1)} %get-tuple-element.65), channel_id=1, source_target_pairs={{0,16},{16,32},{32,48},{48,0},{1,17},{17,33},{33,49},{49,1},{2,18}... | collective-permute-start | bytes 442376 | tf_op jit(solution)/shard_map/ppermute | solution.py:763
  127.5 9.7 %collective-permute-start.10 = (bf16[4,48,384]{2,1,0:T(8,128)(2,1)S(1)}, bf16[4,48,384]{2,1,0:T(8,128)(2,1)S(1)}, u32[]{:S(2)}, u32[]{:S(2)}) collective-permute-start(bf16[4,48,384]{2,1,0:T(8,128)(2,1)S(1)} %get-tuple-element.66), channel_id=1, source_target_pairs={{0,32},{16,48},{32,0},{48,16},{1,33},{17,49},{33,1},{49,17},{2,34}... | collective-permute-start | bytes 442376 | tf_op jit(solution)/shard_map/ppermute | solution.py:763
  129.5 8.2 %collective-permute-start.11 = (bf16[4,48,384]{2,1,0:T(8,128)(2,1)S(1)}, bf16[4,48,384]{2,1,0:T(8,128)(2,1)S(1)}, u32[]{:S(2)}, u32[]{:S(2)}) collective-permute-start(bf16[4,48,384]{2,1,0:T(8,128)(2,1)S(1)} %get-tuple-element.67), channel_id=1, source_target_pairs={{0,48},{16,0},{32,16},{48,32},{1,49},{17,1},{33,17},{49,33},{2,50}... | collective-permute-start | bytes 442376 | tf_op jit(solution)/shard_map/ppermute | solution.py:763
  137.9 4.7 %collective-permute-start.14 = (bf16[48,384]{1,0:T(8,128)(2,1)S(1)}, bf16[48,384]{1,0:T(8,128)(2,1)S(1)}, u32[]{:S(2)}, u32[]{:S(2)}) collective-permute-start(bf16[48,384]{1,0:T(8,128)(2,1)S(1)} %get-tuple-element.71), channel_id=1, source_target_pairs={{0,192},{64,0},{128,64},{192,128},{1,193},{65,1},{129,65},{193,129... | collective-permute-start | bytes 110600 | tf_op jit(solution)/shard_map/ppermute | solution.py:763
  139.6 5.5 %collective-permute-start.13 = (bf16[48,384]{1,0:T(8,128)(2,1)S(1)}, bf16[48,384]{1,0:T(8,128)(2,1)S(1)}, u32[]{:S(2)}, u32[]{:S(2)}) collective-permute-start(bf16[48,384]{1,0:T(8,128)(2,1)S(1)} %get-tuple-element.70), channel_id=1, source_target_pairs={{0,128},{64,192},{128,0},{192,64},{1,129},{65,193},{129,1},{193,65... | collective-permute-start | bytes 110600 | tf_op jit(solution)/shard_map/ppermute | solution.py:763
  140.2 4.9 %collective-permute-start.12 = (bf16[48,384]{1,0:T(8,128)(2,1)S(1)}, bf16[48,384]{1,0:T(8,128)(2,1)S(1)}, u32[]{:S(2)}, u32[]{:S(2)}) collective-permute-start(bf16[48,384]{1,0:T(8,128)(2,1)S(1)} %get-tuple-element.69), channel_id=1, source_target_pairs={{0,64},{64,128},{128,192},{192,0},{1,65},{65,129},{129,193},{193,1... | collective-permute-start | bytes 110600 | tf_op jit(solution)/shard_map/ppermute | solution.py:763
  168.3 22.7 %copy-start.4 = (bf16[192,768]{1,0:T(8,128)(2,1)S(1)}, bf16[192,768]{1,0:T(8,128)(2,1)}, u32[]{:S(2)}) copy-start(bf16[192,768]{1,0:T(8,128)(2,1)} %get-tuple-element.62.hidden_ref) | copy-start | bytes 884740
  168.3 23.5 %copy-start.1 = (bf16[768,1536]{1,0:T(8,128)(2,1)S(1)}, bf16[768,1536]{1,0:T(8,128)(2,1)}, u32[]{:S(2)}) copy-start(bf16[768,1536]{1,0:T(8,128)(2,1)} %two_ref.1) | copy-start | bytes 7077892
  191.6 3.3 %collective-permute-start.15 = (bf16[16,48,768]{2,1,0:T(8,128)(2,1)S(1)}, bf16[16,48,768]{2,1,0:T(8,128)(2,1)S(1)}, u32[]{:S(2)}, u32[]{:S(2)}) collective-permute-start(bf16[16,48,768]{2,1,0:T(8,128)(2,1)S(1)} %get-tuple-element.78), channel_id=1, source_target_pairs={{0,8},{8,0},{1,9},{9,1},{2,10},{10,2},{3,11},{11,3},{4,12},{12,4},... | collective-permute-start | bytes 3538952 | tf_op jit(solution)/shard_map/ppermute | solution.py:812
  194.4 3.0 %collective-permute-start.19 = (bf16[16,48,768]{2,1,0:T(8,128)(2,1)S(1)}, bf16[16,48,768]{2,1,0:T(8,128)(2,1)S(1)}, u32[]{:S(2)}, u32[]{:S(2)}) collective-permute-start(bf16[16,48,768]{2,1,0:T(8,128)(2,1)S(1)} %get-tuple-element.84), channel_id=1, source_target_pairs={{0,8},{8,0},{1,9},{9,1},{2,10},{10,2},{3,11},{11,3},{4,12},{12,4},... | collective-permute-start | bytes 3538952 | tf_op jit(solution)/shard_map/ppermute | solution.py:823
  198.7 22.9 %all-to-all-start.8 = ((bf16[4,4,48,768]{3,2,1,0:T(8,128)(2,1)}), bf16[4,4,48,768]{3,2,1,0:T(8,128)(2,1)S(1)}, u32[]{:S(2)}, u32[]{:S(2)}) async-start(bf16[4,4,48,768]{3,2,1,0:T(8,128)(2,1)} %shard_map.168), calls=%async_computation.8 | async-start | bytes 2359296 | tf_op jit(solution)/shard_map/all_to_all | solution.py:33
  203.6 16.7 %collective-permute-start.16 = (bf16[4,48,768]{2,1,0:T(8,128)(2,1)}, bf16[4,48,768]{2,1,0:T(8,128)(2,1)S(1)}, u32[]{:S(2)}, u32[]{:S(2)}) collective-permute-start(bf16[4,48,768]{2,1,0:T(8,128)(2,1)} %get-tuple-element.80), channel_id=1, source_target_pairs={{0,16},{16,32},{32,48},{48,0},{1,17},{17,33},{33,49},{49,1},{2,18}... | collective-permute-start | bytes 884744 | tf_op jit(solution)/shard_map/ppermute | solution.py:763
  204.4 16.0 %collective-permute-start.17 = (bf16[4,48,768]{2,1,0:T(8,128)(2,1)S(1)}, bf16[4,48,768]{2,1,0:T(8,128)(2,1)S(1)}, u32[]{:S(2)}, u32[]{:S(2)}) collective-permute-start(bf16[4,48,768]{2,1,0:T(8,128)(2,1)S(1)} %get-tuple-element.81), channel_id=1, source_target_pairs={{0,32},{16,48},{32,0},{48,16},{1,33},{17,49},{33,1},{49,17},{2,34}... | collective-permute-start | bytes 884744 | tf_op jit(solution)/shard_map/ppermute | solution.py:763
  206.5 14.3 %collective-permute-start.18 = (bf16[4,48,768]{2,1,0:T(8,128)(2,1)S(1)}, bf16[4,48,768]{2,1,0:T(8,128)(2,1)S(1)}, u32[]{:S(2)}, u32[]{:S(2)}) collective-permute-start(bf16[4,48,768]{2,1,0:T(8,128)(2,1)S(1)} %get-tuple-element.82), channel_id=1, source_target_pairs={{0,48},{16,0},{32,16},{48,32},{1,49},{17,1},{33,17},{49,33},{2,50}... | collective-permute-start | bytes 884744 | tf_op jit(solution)/shard_map/ppermute | solution.py:763
  221.6 10.6 %all-to-all-start.7 = ((bf16[4,48,768]{2,1,0:T(8,128)(2,1)}), bf16[4,48,768]{2,1,0:T(8,128)(2,1)S(1)}, u32[]{:S(2)}, u32[]{:S(2)}) async-start(bf16[4,48,768]{2,1,0:T(8,128)(2,1)} %shard_map.166), calls=%async_computation.7 | async-start | bytes 589824 | tf_op jit(solution)/shard_map/all_to_all | solution.py:33
  226.6 6.4 %collective-permute-start.20 = (bf16[48,768]{1,0:T(8,128)(2,1)S(1)}, bf16[48,768]{1,0:T(8,128)(2,1)S(1)}, u32[]{:S(2)}, u32[]{:S(2)}) collective-permute-start(bf16[48,768]{1,0:T(8,128)(2,1)S(1)} %get-tuple-element.86), channel_id=1, source_target_pairs={{0,16},{16,32},{32,48},{48,0},{1,17},{17,33},{33,49},{49,1},{2,18}... | collective-permute-start | bytes 221192 | tf_op jit(solution)/shard_map/ppermute | solution.py:763
  227.1 6.7 %collective-permute-start.21 = (bf16[48,768]{1,0:T(8,128)(2,1)S(1)}, bf16[48,768]{1,0:T(8,128)(2,1)S(1)}, u32[]{:S(2)}, u32[]{:S(2)}) collective-permute-start(bf16[48,768]{1,0:T(8,128)(2,1)S(1)} %get-tuple-element.87), channel_id=1, source_target_pairs={{0,32},{16,48},{32,0},{48,16},{1,33},{17,49},{33,1},{49,17},{2,34}... | collective-permute-start | bytes 221192 | tf_op jit(solution)/shard_map/ppermute | solution.py:763
  230.6 4.4 %collective-permute-start.22 = (bf16[48,768]{1,0:T(8,128)(2,1)S(1)}, bf16[48,768]{1,0:T(8,128)(2,1)S(1)}, u32[]{:S(2)}, u32[]{:S(2)}) collective-permute-start(bf16[48,768]{1,0:T(8,128)(2,1)S(1)} %get-tuple-element.88), channel_id=1, source_target_pairs={{0,48},{16,0},{32,16},{48,32},{1,49},{17,1},{33,17},{49,33},{2,50}... | collective-permute-start | bytes 221192 | tf_op jit(solution)/shard_map/ppermute | solution.py:763
  (14 other events, 12.3 us)
